TPU v7x, 32 devices: a whole 2x2x4 slice. The times are simulated.
32 devices in a mesh: obs: 8 (over z, x), par: 4 (over y, core).
Axes of the slice: x: 2, y: 2, z: 4, core: 2. Of those that a mesh axis runs over, the one named last changes fastest.
Arguments:
- operator: bfloat16 [4096, 65536], P('obs', 'par'), as said below
- targets: float32 [16, 4096], P(None, 'obs'), may hold values from -6 to 6
- start: float32 [16, 65536], P(None, 'par'), may hold values from -3 to 3
Outputs:
- solution: float32 [16, 65536], P(None, 'par')
- residual: float32 [16, 4096], P(None, 'obs')
Inputs may be any that keep to these rules, and one draw needn't show every extreme that they name: `operator`: entries are the product of an independent draw, a scale of each row and a scale of each column, divided by the square root of 65536.
All inputs are finite; a program needn't handle non-finite values.
Results may differ from a plain program's by a relative error of at most 0.00775.
Values may be sent and summed in bfloat16 or wider, within the bound.
No kernel may reach another device: no remote copies, remote signals or barrier semaphores. Data moves between devices by JAX's collectives and lax.ppermute only.
A program may use at most 64 MiB of HBM per device.

v0:
```python
import jax
import jax.numpy as jnp
from jax import lax
from jax.sharding import PartitionSpec as P

ITERS = 4


def shards(operator, targets, start):

    def forward_local(direc_bf):
        return lax.dot_general(
            direc_bf, operator, (((1,), (1,)), ((), ())), preferred_element_type=jnp.float32
        )

    def image_of(direc_bf):
        partial_terms = forward_local(direc_bf)
        return lax.psum(partial_terms, "par")

    def image_norm(image):
        local_sum = jnp.sum(image * image, axis=1, keepdims=True)
        return lax.psum(local_sum, "obs")

    def gradient_of(resid):
        whole_rows = resid.astype(jnp.bfloat16)
        partial_terms = jnp.dot(whole_rows, operator, preferred_element_type=jnp.float32)
        gradient = lax.psum(partial_terms, "obs")
        gamma = lax.psum(jnp.sum(gradient * gradient, axis=1, keepdims=True), "par")
        return (gradient, gamma)

    def whole_direction(direction):
        return direction.astype(jnp.bfloat16)

    first_image = image_of(start.astype(jnp.bfloat16))
    residual = targets - first_image
    gradient, gamma = gradient_of(residual)
    solution = start
    direction = gradient

    def advance(index, carry):
        solution, residual, direction, gamma = carry
        image = image_of(whole_direction(direction))
        delta = image_norm(image)
        alpha = gamma / delta
        solution = solution + alpha * direction
        residual = residual - alpha * image
        gradient, gamma_new = gradient_of(residual)
        direction = gradient + gamma_new / gamma * direction
        return (solution, residual, direction, gamma_new)

    solution, residual, direction, gamma = lax.fori_loop(
        0, ITERS, advance, (solution, residual, direction, gamma)
    )
    return (solution, residual)


def solution(mesh):
    placed = (P("obs", "par"), P(None, "obs"), P(None, "par"))
    return jax.shard_map(
        shards,
        mesh=mesh,
        in_specs=placed,
        out_specs=(P(None, "par"), P(None, "obs")),
        check_vma=False,
    )
```

profile of v0, /device:TPU:0, one launch (start us, length us, event | category | flops | bytes accessed | tf_op | source)
XLA Modules:
  0.0 677.5 jit_solution(3642669001123234071)
XLA Ops:
  7.2 0.0 all-reduce.3.cloned.1.call-start
  7.2 1.2 copy.24
  8.4 10.2 %fusion.4 = f32[16,512]{1,0:T(8,128)S(1)} fusion(bf16[512,16384]{1,0:T(8,128)(2,1)} %param.5, f32[16,16384]{1,0:T(8,128)S(1)} %copy.24), kind=kOutput, calls=%fused_computation.12 | convolution fusion | flops 268697600 | bytes 17858560 | tf_op jit(solution)/shard_map/dot_general | solution.py:12
  18.6 12.9 %psum.49 = f32[16,512]{1,0:T(8,128)S(1)} all-reduce(f32[16,512]{1,0:T(8,128)S(1)} %fusion.4), channel_id=1, replica_groups=mesh['obs'=8,'par'=4] {'par'}, use_global_device_ids=true, to_apply=%region_0.0 | all-reduce | flops 8192 | bytes 65536 | tf_op jit(solution)/shard_map/psum | solution.py:18
  31.5 0.0 copy-done.4
  31.6 9.0 %fusion.6 = f32[16,16384]{1,0:T(8,128)} fusion(bf16[512,16384]{1,0:T(8,128)(2,1)} %param.5, f32[16,512]{1,0:T(8,128)S(1)} %sub.6), kind=kOutput, calls=%fused_computation.14 | convolution fusion | flops 268443648 | bytes 17858560 | tf_op jit(solution)/shard_map/dot_general | solution.py:26
  40.6 0.0 all-reduce.3.cloned.1.call-update
  40.6 78.5 %all-reduce.3.cloned.1.call-done = f32[16,16384]{1,0:T(8,128)} async-done(((f32[16,16384]{1,0:T(8,128)}), f32[16,16384]{1,0:T(8,128)}) %all-reduce.3.cloned.1.call-update) | async-done | bytes 1048592 | tf_op jit(solution)/shard_map/psum | solution.py:27
  119.1 1.5 multiply_reduce_fusion.2
  120.6 6.1 psum.51
  126.6 543.4 %while.16 = (s32[]{:T(128)}, f32[16,16384]{1,0:T(8,128)S(1)}, f32[16,512]{1,0:T(8,128)S(1)}, f32[16,16384]{1,0:T(8,128)}, f32[16,1]{0,1:T(1,128)S(1)}, /*index=5*/bf16[512,16384]{1,0:T(8,128)(2,1)}, s32[]{:T(128)}) while((s32[]{:T(128)}, f32[16,16384]{1,0:T(8,128)S(1)}, f32[16,512]{1,0:T(8,128)S(1)}, f32[16,16384]{1,0:T(8,128)}, ...), condition=%wide.region_11.0_spmd, body=%wide.region_4.0_spmd.sunk | while | flops 539017216 | bytes 56886508 | solution.py:51
  126.6 0.0 all-reduce.5.cloned.1.call-start
  126.7 10.6 %fusion.22 = f32[16,512]{1,0:T(8,128)S(1)} fusion(bf16[512,16384]{1,0:T(8,128)(2,1)} %get-tuple-element.111, f32[16,16384]{1,0:T(8,128)} %get-tuple-element.102), kind=kOutput, calls=%fused_computation.3.clone.1 | convolution fusion | flops 268697600 | bytes 17858560 | tf_op jit(solution)/shard_map/while/body/eval_jaxpr/dot_general | solution.py:12
  137.3 10.9 %psum.56 = f32[16,512]{1,0:T(8,128)S(1)} all-reduce(f32[16,512]{1,0:T(8,128)S(1)} %fusion.22), channel_id=1, replica_groups=mesh['obs'=8,'par'=4] {'par'}, use_global_device_ids=true, to_apply=%region_5.0 | all-reduce | flops 8192 | bytes 65536 | tf_op jit(solution)/shard_map/while/body/eval_jaxpr/psum | solution.py:18
  148.1 0.1 multiply_reduce_fusion.5
  148.3 20.0 %psum.57 = f32[16,1]{0,1:T(1,128)S(1)} all-reduce(f32[16,1]{0,1:T(1,128)S(1)} %bitcast.23), channel_id=1, replica_groups=mesh['obs'=8,'par'=4] {'obs'}, use_global_device_ids=true, to_apply=%region_7.0 | all-reduce | flops 16 | bytes 128 | tf_op jit(solution)/shard_map/while/body/eval_jaxpr/psum | solution.py:22
  168.3 0.1 multiply_subtract_fusion.2
  168.4 9.0 %fusion.23 = f32[16,16384]{1,0:T(8,128)} fusion(bf16[512,16384]{1,0:T(8,128)(2,1)} %get-tuple-element.111, f32[16,512]{1,0:T(8,128)S(1)} %multiply_subtract_fusion.2), kind=kOutput, calls=%fused_computation.7.clone.1 | convolution fusion | flops 268443648 | bytes 17858560 | tf_op jit(solution)/shard_map/while/body/eval_jaxpr/dot_general | solution.py:26
  177.4 0.0 all-reduce.5.cloned.1.call-update
  177.4 74.9 %all-reduce.5.cloned.1.call-done = f32[16,16384]{1,0:T(8,128)} async-done(((f32[16,16384]{1,0:T(8,128)}), f32[16,16384]{1,0:T(8,128)}) %all-reduce.5.cloned.1.call-update) | async-done | bytes 1048592 | tf_op jit(solution)/shard_map/while/body/eval_jaxpr/psum | solution.py:27
  252.4 1.5 multiply_reduce_fusion.6
  253.9 5.9 psum.59
  259.7 1.8 multiply_add_fusion.3
  261.5 1.0 copy-done.1
  262.5 0.0 all-reduce.5.cloned.1.call-start
  262.5 10.6 %fusion.22 = f32[16,512]{1,0:T(8,128)S(1)} fusion(bf16[512,16384]{1,0:T(8,128)(2,1)} %get-tuple-element.111, f32[16,16384]{1,0:T(8,128)} %get-tuple-element.102), kind=kOutput, calls=%fused_computation.3.clone.1 | convolution fusion | flops 268697600 | bytes 17858560 | tf_op jit(solution)/shard_map/while/body/eval_jaxpr/dot_general | solution.py:12
  273.1 10.9 %psum.56 = f32[16,512]{1,0:T(8,128)S(1)} all-reduce(f32[16,512]{1,0:T(8,128)S(1)} %fusion.22), channel_id=1, replica_groups=mesh['obs'=8,'par'=4] {'par'}, use_global_device_ids=true, to_apply=%region_5.0 | all-reduce | flops 8192 | bytes 65536 | tf_op jit(solution)/shard_map/while/body/eval_jaxpr/psum | solution.py:18
  284.0 0.1 multiply_reduce_fusion.5
  284.1 20.0 %psum.57 = f32[16,1]{0,1:T(1,128)S(1)} all-reduce(f32[16,1]{0,1:T(1,128)S(1)} %bitcast.23), channel_id=1, replica_groups=mesh['obs'=8,'par'=4] {'obs'}, use_global_device_ids=true, to_apply=%region_7.0 | all-reduce | flops 16 | bytes 128 | tf_op jit(solution)/shard_map/while/body/eval_jaxpr/psum | solution.py:22
  304.1 0.1 multiply_subtract_fusion.2
  304.2 9.0 %fusion.23 = f32[16,16384]{1,0:T(8,128)} fusion(bf16[512,16384]{1,0:T(8,128)(2,1)} %get-tuple-element.111, f32[16,512]{1,0:T(8,128)S(1)} %multiply_subtract_fusion.2), kind=kOutput, calls=%fused_computation.7.clone.1 | convolution fusion | flops 268443648 | bytes 17858560 | tf_op jit(solution)/shard_map/while/body/eval_jaxpr/dot_general | solution.py:26
  313.3 0.0 all-reduce.5.cloned.1.call-update
  313.3 74.9 %all-reduce.5.cloned.1.call-done = f32[16,16384]{1,0:T(8,128)} async-done(((f32[16,16384]{1,0:T(8,128)}), f32[16,16384]{1,0:T(8,128)}) %all-reduce.5.cloned.1.call-update) | async-done | bytes 1048592 | tf_op jit(solution)/shard_map/while/body/eval_jaxpr/psum | solution.py:27
  388.2 1.5 multiply_reduce_fusion.6
  389.7 5.9 psum.59
  395.6 0.0 copy-done
  395.6 1.8 multiply_add_fusion.3
  397.3 1.0 copy-done.1
  398.3 10.6 %fusion.22 = f32[16,512]{1,0:T(8,128)S(1)} fusion(bf16[512,16384]{1,0:T(8,128)(2,1)} %get-tuple-element.111, f32[16,16384]{1,0:T(8,128)} %get-tuple-element.102), kind=kOutput, calls=%fused_computation.3.clone.1 | convolution fusion | flops 268697600 | bytes 17858560 | tf_op jit(solution)/shard_map/while/body/eval_jaxpr/dot_general | solution.py:12
  408.9 10.9 %psum.56 = f32[16,512]{1,0:T(8,128)S(1)} all-reduce(f32[16,512]{1,0:T(8,128)S(1)} %fusion.22), channel_id=1, replica_groups=mesh['obs'=8,'par'=4] {'par'}, use_global_device_ids=true, to_apply=%region_5.0 | all-reduce | flops 8192 | bytes 65536 | tf_op jit(solution)/shard_map/while/body/eval_jaxpr/psum | solution.py:18
  419.8 0.1 multiply_reduce_fusion.5
  419.9 20.0 %psum.57 = f32[16,1]{0,1:T(1,128)S(1)} all-reduce(f32[16,1]{0,1:T(1,128)S(1)} %bitcast.23), channel_id=1, replica_groups=mesh['obs'=8,'par'=4] {'obs'}, use_global_device_ids=true, to_apply=%region_7.0 | all-reduce | flops 16 | bytes 128 | tf_op jit(solution)/shard_map/while/body/eval_jaxpr/psum | solution.py:22
  440.0 0.1 multiply_subtract_fusion.2
  440.1 9.0 %fusion.23 = f32[16,16384]{1,0:T(8,128)} fusion(bf16[512,16384]{1,0:T(8,128)(2,1)} %get-tuple-element.111, f32[16,512]{1,0:T(8,128)S(1)} %multiply_subtract_fusion.2), kind=kOutput, calls=%fused_computation.7.clone.1 | convolution fusion | flops 268443648 | bytes 17858560 | tf_op jit(solution)/shard_map/while/body/eval_jaxpr/dot_general | solution.py:26
  449.1 0.0 all-reduce.5.cloned.1.call-update
  449.1 74.9 %all-reduce.5.cloned.1.call-done = f32[16,16384]{1,0:T(8,128)} async-done(((f32[16,16384]{1,0:T(8,128)}), f32[16,16384]{1,0:T(8,128)}) %all-reduce.5.cloned.1.call-update) | async-done | bytes 1048592 | tf_op jit(solution)/shard_map/while/body/eval_jaxpr/psum | solution.py:27
  524.1 1.5 multiply_reduce_fusion.6
  525.5 5.9 psum.59
  531.4 1.8 multiply_add_fusion.3
  533.2 1.0 copy-done.1
  534.2 10.6 %fusion.22 = f32[16,512]{1,0:T(8,128)S(1)} fusion(bf16[512,16384]{1,0:T(8,128)(2,1)} %get-tuple-element.111, f32[16,16384]{1,0:T(8,128)} %get-tuple-element.102), kind=kOutput, calls=%fused_computation.3.clone.1 | convolution fusion | flops 268697600 | bytes 17858560 | tf_op jit(solution)/shard_map/while/body/eval_jaxpr/dot_general | solution.py:12
  544.8 10.9 %psum.56 = f32[16,512]{1,0:T(8,128)S(1)} all-reduce(f32[16,512]{1,0:T(8,128)S(1)} %fusion.22), channel_id=1, replica_groups=mesh['obs'=8,'par'=4] {'par'}, use_global_device_ids=true, to_apply=%region_5.0 | all-reduce | flops 8192 | bytes 65536 | tf_op jit(solution)/shard_map/while/body/eval_jaxpr/psum | solution.py:18
  555.6 0.1 multiply_reduce_fusion.5
  555.8 20.0 %psum.57 = f32[16,1]{0,1:T(1,128)S(1)} all-reduce(f32[16,1]{0,1:T(1,128)S(1)} %bitcast.23), channel_id=1, replica_groups=mesh['obs'=8,'par'=4] {'obs'}, use_global_device_ids=true, to_apply=%region_7.0 | all-reduce | flops 16 | bytes 128 | tf_op jit(solution)/shard_map/while/body/eval_jaxpr/psum | solution.py:22
  575.8 0.1 multiply_subtract_fusion.2
  575.9 9.0 %fusion.23 = f32[16,16384]{1,0:T(8,128)} fusion(bf16[512,16384]{1,0:T(8,128)(2,1)} %get-tuple-element.111, f32[16,512]{1,0:T(8,128)S(1)} %multiply_subtract_fusion.2), kind=kOutput, calls=%fused_computation.7.clone.1 | convolution fusion | flops 268443648 | bytes 17858560 | tf_op jit(solution)/shard_map/while/body/eval_jaxpr/dot_general | solution.py:26
  584.9 0.0 all-reduce.5.cloned.1.call-update
  585.0 74.9 %all-reduce.5.cloned.1.call-done = f32[16,16384]{1,0:T(8,128)} async-done(((f32[16,16384]{1,0:T(8,128)}), f32[16,16384]{1,0:T(8,128)}) %all-reduce.5.cloned.1.call-update) | async-done | bytes 1048592 | tf_op jit(solution)/shard_map/while/body/eval_jaxpr/psum | solution.py:27
  659.9 1.5 multiply_reduce_fusion.6
  661.4 5.9 psum.59
  667.3 1.8 multiply_add_fusion.3
  669.0 0.0 copy-start.1
  669.0 1.0 copy-done.1
  670.0 1.0 copy-done.2
  (29 shorter events, 0.1 us)
Async XLA Ops:
  7.2 24.4 %copy-start.4 = (f32[16,512]{1,0:T(8,128)S(1)}, f32[16,512]{1,0:T(8,128)}, u32[]{:S(2)}) copy-start(f32[16,512]{1,0:T(8,128)} %param.6) | copy-start | bytes 98308
  7.2 111.9 %all-reduce.3.cloned.1.call-start = ((), (), s32[]{:S(2)}) async-start(), calls=%async_computation | async-start | bytes 2097152 | tf_op jit(solution)/shard_map/psum | solution.py:27
  126.6 125.8 %all-reduce.5.cloned.1.call-start = ((), (), s32[]{:S(2)}) async-start(), calls=%async_computation.1 | async-start | bytes 2097152 | tf_op jit(solution)/shard_map/while/body/eval_jaxpr/psum | solution.py:27
  126.7 133.1 %copy-start = (f32[16,16384]{1,0:T(8,128)S(1)}, f32[16,16384]{1,0:T(8,128)}, u32[]{:S(2)}) copy-start(f32[16,16384]{1,0:T(8,128)} %get-tuple-element.102) | copy-start | bytes 3145732 | tf_op jit(solution)/shard_map/while
  261.5 1.0 copy-start.1
  262.5 125.7 %all-reduce.5.cloned.1.call-start = ((), (), s32[]{:S(2)}) async-start(), calls=%async_computation.1 | async-start | bytes 2097152 | tf_op jit(solution)/shard_map/while/body/eval_jaxpr/psum | solution.py:27
  262.5 133.1 %copy-start = (f32[16,16384]{1,0:T(8,128)S(1)}, f32[16,16384]{1,0:T(8,128)}, u32[]{:S(2)}) copy-start(f32[16,16384]{1,0:T(8,128)} %get-tuple-element.102) | copy-start | bytes 3145732 | tf_op jit(solution)/shard_map/while
  397.3 1.0 copy-start.1
  398.3 125.7 %all-reduce.5.cloned.1.call-start = ((), (), s32[]{:S(2)}) async-start(), calls=%async_computation.1 | async-start | bytes 2097152 | tf_op jit(solution)/shard_map/while/body/eval_jaxpr/psum | solution.py:27
  398.3 133.1 %copy-start = (f32[16,16384]{1,0:T(8,128)S(1)}, f32[16,16384]{1,0:T(8,128)}, u32[]{:S(2)}) copy-start(f32[16,16384]{1,0:T(8,128)} %get-tuple-element.102) | copy-start | bytes 3145732 | tf_op jit(solution)/shard_map/while
  533.2 1.0 copy-start.1
  534.2 125.7 %all-reduce.5.cloned.1.call-start = ((), (), s32[]{:S(2)}) async-start(), calls=%async_computation.1 | async-start | bytes 2097152 | tf_op jit(solution)/shard_map/while/body/eval_jaxpr/psum | solution.py:27
  534.2 133.1 %copy-start = (f32[16,16384]{1,0:T(8,128)S(1)}, f32[16,16384]{1,0:T(8,128)}, u32[]{:S(2)}) copy-start(f32[16,16384]{1,0:T(8,128)} %get-tuple-element.102) | copy-start | bytes 3145732 | tf_op jit(solution)/shard_map/while
  669.0 1.0 copy-start.1
  670.0 1.0 copy-start.2
  670.0 1.0 copy-start.3
Sparse Core Ops, SparseCore 0:
  40.7 78.2 all-reduce.2
  177.6 74.7 all-reduce.4
  313.4 74.7 all-reduce.4
  449.2 74.7 all-reduce.4
  585.1 74.7 all-reduce.4
where the time goes:
time: 678 us
  waiting for transfers between devices  378 us (56%)
  blocking collectives  166 us (24%)
  matrix products  97.7 us (14%)
  other arithmetic  15.2 us (2%)
  between operations  13.7 us (2%)
    psum x5, waiting for transfers between devices, gradient_of(): gradient = lax.psum(partial_terms, 'obs')  378 us
    psum x4, blocking collectives, image_norm(): return lax.psum(local_sum, 'obs')  80.1 us
    psum x5, blocking collectives, image_of(): return lax.psum(partial_terms, 'par')  56.4 us
    dot_general x5, matrix products, forward_local(): lax.dot_general(direc_bf, operator, (((1,), (1,)), ((), ())), preferred_e...  52.5 us
    dot_general x5, matrix products, gradient_of(): jnp.dot(whole_rows, operator, preferred_element_type=jnp.float32)  45.2 us
    psum x5, blocking collectives, gradient_of(): gamma = lax.psum(jnp.sum(gradient * gradient, axis=1, keepdims=True), 'par')  29.6 us
  transfers between devices with their start and end apart: 5, of which 5 were waited for; matrix products, arithmetic and copies ran while one was open for 0% of the time, Pallas kernels for 0%

commit v1 on v0

v1 whole, which is shorter than its diff:
```python
import functools

import jax
import jax.numpy as jnp
from jax import lax
from jax.experimental import pallas as pl
from jax.experimental.pallas import tpu as pltpu
from jax.sharding import PartitionSpec as P

ITERS = 4
LANES = 128
F32 = jnp.float32
BF16 = jnp.bfloat16
VMEM = pl.BlockSpec(memory_space=pltpu.VMEM)
SMEM = pl.BlockSpec(memory_space=pltpu.SMEM)
HBM = pl.BlockSpec(memory_space=pl.ANY)


def params(mebibytes=32):
    return pltpu.CompilerParams(vmem_limit_bytes=mebibytes << 20)


def cost(scen, rows, columns):
    return pl.CostEstimate(
        flops=2 * 16 * scen * rows * columns, bytes_accessed=2 * rows * columns, transcendentals=0
    )


def load_kernel(chunk, op_hbm, start_hbm, op_ref, image_ref, start_ref, sems):
    pieces = op_ref.shape[1] // chunk
    copies = [pltpu.make_async_copy(start_hbm, start_ref, sems.at[pieces])]
    for k in range(pieces):
        at = pl.ds(k * chunk, chunk)
        copies.append(pltpu.make_async_copy(op_hbm.at[:, at], op_ref.at[:, at], sems.at[k]))
    for copy in copies:
        copy.start()
    copies[0].wait()
    total = jnp.zeros(image_ref.shape, F32)
    for k in range(pieces):
        copies[k + 1].wait()
        at = pl.ds(k * chunk, chunk)
        total += lax.dot_general(
            start_ref[:, at].astype(BF16), op_ref[:, at], (((1,), (1,)), ((), ())), preferred_element_type=F32
        )
    image_ref[...] = total


def load(operator, start):
    rows, columns = operator.shape
    scen = start.shape[0]
    chunk = min(2048, columns)
    return pl.pallas_call(
        functools.partial(load_kernel, chunk),
        out_shape=(
            jax.ShapeDtypeStruct(operator.shape, BF16),
            jax.ShapeDtypeStruct((scen, rows), F32),
        ),
        in_specs=[HBM, HBM],
        out_specs=(VMEM, VMEM),
        scratch_shapes=[pltpu.VMEM(start.shape, F32), pltpu.SemaphoreType.DMA((columns // chunk + 1,))],
        compiler_params=params(),
        cost_estimate=cost(scen, rows, columns),
    )(operator, start)


def backward_kernel(chunk, at_ref, op_ref, w_ref, norm_ref, out_ref):
    width = out_ref.shape[1] - (LANES if norm_ref is not None else 0)
    scen = out_ref.shape[0]
    w = w_ref[...]
    base = at_ref[0] * width
    for k in range(width // chunk):
        at = pl.ds(pl.multiple_of(base + k * chunk, chunk), chunk)
        both = jnp.dot(w, op_ref[:, at], preferred_element_type=F32)
        out_ref[:, k * chunk : (k + 1) * chunk] = (both[:scen] + both[scen:]).astype(out_ref.dtype)
    if norm_ref is not None:
        out_ref[:, width:] = norm_ref[...]


def backward(at, op, w, norm, width):
    scen = w.shape[0] // 2
    chunk = min(1024, width)
    if norm is None:
        body = lambda at_ref, op_ref, w_ref, out_ref: backward_kernel(chunk, at_ref, op_ref, w_ref, None, out_ref)
        out = jax.ShapeDtypeStruct((scen, width), F32)
        more = ()
    else:
        body = functools.partial(backward_kernel, chunk)
        out = jax.ShapeDtypeStruct((scen, width + LANES), BF16)
        more = (norm,)
    return pl.pallas_call(
        body,
        out_shape=out,
        in_specs=[SMEM, VMEM, VMEM] + [VMEM] * len(more),
        out_specs=VMEM,
        compiler_params=params(),
        cost_estimate=cost(scen, op.shape[0], width),
    )(at.reshape(1), op, w, *more)


def forward_kernel(at_ref, op_ref, v_ref, sum_ref, out_ref):
    width = v_ref.shape[1]
    rows = op_ref.shape[0]
    v = v_ref[...]
    at = pl.ds(pl.multiple_of(at_ref[0] * width, width), width)
    image = lax.dot_general(v, op_ref[:, at], (((1,), (1,)), ((), ())), preferred_element_type=F32)
    wide = v.astype(F32)
    square = wide * wide
    norm = square[:, :LANES]
    for k in range(1, width // LANES):
        norm += square[:, k * LANES : (k + 1) * LANES]
    if sum_ref is not None:
        image += sum_ref[:, :rows]
        norm += sum_ref[:, rows:]
    out_ref[:, :rows] = image
    out_ref[:, rows:] = norm


def forward(at, op, v, total):
    scen, width = v.shape
    rows = op.shape[0]
    if total is None:
        body = lambda at_ref, op_ref, v_ref, out_ref: forward_kernel(at_ref, op_ref, v_ref, None, out_ref)
        more = ()
    else:
        body = forward_kernel
        more = (total,)
    return pl.pallas_call(
        body,
        out_shape=jax.ShapeDtypeStruct((scen, rows + LANES), F32),
        in_specs=[SMEM, VMEM, VMEM] + [VMEM] * len(more),
        out_specs=VMEM,
        compiler_params=params(),
        cost_estimate=cost(scen, rows, width),
    )(at.reshape(1), op, v, *more)


def exchange(value, axis, size, distance):
    return lax.ppermute(value, axis, [(i, i ^ distance) for i in range(size)])


def stages(size, stride=1):
    while stride < size:
        members = 4 if size // stride % 4 == 0 else 2
        yield stride, members
        stride *= members


def tree(parts):
    if len(parts) == 2:
        return parts[0] + parts[1]
    return (parts[0] + parts[1]) + (parts[2] + parts[3])


def sum_over(value, axis, size, stride=1):
    for stride, members in stages(size, stride):
        value = tree([value] + [exchange(value, axis, size, k * stride) for k in range(1, members)])
    return value


def rounded(value):
    return lax.reduce_precision(value, exponent_bits=8, mantissa_bits=7)


def split3(value):
    high = rounded(value)
    rest = value - high
    middle = rounded(rest)
    return high.astype(BF16), middle.astype(BF16), rounded(rest - middle).astype(BF16)


def norm_block(value):
    terms = split3(value)
    lane = lax.broadcasted_iota(jnp.int32, (value.shape[0], LANES), 1)
    block = jnp.zeros((value.shape[0], LANES), BF16)
    for k, term in enumerate(terms):
        block = jnp.where(lane == k, term, block)
    return block


def norm_of(block):
    wide = block.astype(F32)
    return (wide[:, 0:1] + wide[:, 1:2]) + wide[:, 2:3]


def shards(n_obs, n_par, operator, targets, start):
    rows, columns = operator.shape
    near = 4 if n_obs % 4 == 0 else n_obs
    width = columns // near
    me = lax.axis_index("obs")
    own = me % near

    def gradient_sum(w, norm):
        sent = {d: backward(own ^ d, op, w, norm_block(norm), width) for d in reversed(range(1, near))}
        got = {d: exchange(sent[d], "obs", n_obs, d) for d in sent}
        mine = backward(own, op, w, None, width)
        total = tree([mine] + [got[d][:, :width].astype(F32) for d in range(1, near)])
        norms = tree([norm] + [norm_of(got[d][:, width:]) for d in range(1, near)])
        for stride, members in stages(n_obs, near):
            total = rounded(total)
            both = jnp.concatenate([total.astype(BF16), norm_block(norms)], axis=1)
            got = [exchange(both, "obs", n_obs, k * stride) for k in range(1, members)]
            total = tree([total] + [part[:, :width].astype(F32) for part in got])
            norms = tree([norms] + [norm_of(part[:, width:]) for part in got])
        return total, norms

    def image_of(mine):
        got = {d: exchange(mine, "obs", n_obs, d) for d in reversed(range(1, near))}
        total = forward(own, op, mine, None)
        for d in got:
            total = forward(own ^ d, op, got[d], total)
        total = sum_over(total, "par", n_par)
        got[0] = mine
        return total[:, :rows], got, jnp.sum(total[:, rows:], axis=1, keepdims=True)

    def whole(pieces):
        ordered = [None] * near
        stacked = jnp.stack([pieces[d] for d in range(near)])
        for k in range(near):
            ordered[k] = lax.dynamic_index_in_dim(stacked, own ^ k, 0, keepdims=False)
        return jnp.concatenate(ordered, axis=1)

    def high_low(value):
        high = rounded(value)
        return jnp.concatenate([high, rounded(value - high)], axis=0).astype(BF16)

    op, first = load(operator, start)
    residual = targets - sum_over(first, "par", n_par)
    gradient, _ = gradient_sum(high_low(residual), jnp.zeros((start.shape[0], 1), F32))
    solution = start
    for index in range(ITERS):
        product, pieces, gamma_new = image_of(rounded(gradient).astype(BF16))
        if index == 0:
            image = product
            direction = whole(pieces).astype(F32)
        else:
            beta = gamma_new / gamma
            image = product + beta * image
            direction = whole(pieces).astype(F32) + beta * direction
        gamma = gamma_new
        delta = jnp.sum(image * image, axis=1, keepdims=True)
        if index < ITERS - 1:
            change, delta = gradient_sum(high_low(image), delta)
        else:
            delta = sum_over(jnp.broadcast_to(delta, (delta.shape[0], LANES)), "obs", n_obs)[:, :1]
        alpha = gamma / delta
        if index < ITERS - 1:
            gradient = gradient - alpha * change
        solution = solution + alpha * direction
        residual = residual - alpha * image
    return (solution, residual)


def solution(mesh):
    return jax.shard_map(
        functools.partial(shards, mesh.shape["obs"], mesh.shape["par"]),
        mesh=mesh,
        in_specs=(P("obs", "par"), P(None, "obs"), P(None, "par")),
        out_specs=(P(None, "par"), P(None, "obs")),
        check_vma=False,
    )
```

time: 678 us -> 214 us (0.32)
  waiting for transfers between devices: 378 us -> 56.6 us
  blocking collectives: 166 us -> 0 us
  matrix products: 97.7 us -> 0 us
  starting transfers between devices: 0.08 us -> 55.2 us
  local copies, waits for them, and re-layouts: 6.15 us -> 54.4 us
  Pallas kernels: 0 us -> 38.7 us
  between operations: 13.7 us -> 1.09 us
  other arithmetic: 15.2 us -> 7.4 us
    psum x5 -> x0, waiting for transfers between devices: 378 us -> none  [gradient_of(): gradient = lax.psum(partial_terms, 'obs')]
    psum x14 -> x0, blocking collectives: 166 us -> none  [the longest x4 80.1 us: image_norm(): return lax.psum(local_sum, 'obs')]
    dot_general x10 -> x0, matrix products: 97.7 us -> none  [the longest x5 52.5 us: forward_local(): lax.dot_general(direc_bf, operator, (((1,), (1,)), ((), ())), preferred_e...]
    ppermute x0 -> x47, waiting for transfers between devices: none -> 56.6 us  [exchange(): return lax.ppermute(value, axis, [(i, i ^ distance) for i in range(size)])]
    ppermute x0 -> x47, starting transfers between devices: none -> 55.2 us  [exchange(): return lax.ppermute(value, axis, [(i, i ^ distance) for i in range(size)])]
    unnamed x7 -> x28, local copies, waits for them, and re-layouts: 2.2 us -> 53.7 us
    pallas_call x0 -> x33, Pallas kernels: none -> 38.7 us  [the longest x16 19 us: forward(): pl.pallas_call(body, out_shape=jax.ShapeDtypeStruct((scen, rows + LANES),...]
  transfers between devices with their start and end apart: 5 -> 47, of which waited for: 5 -> 25; matrix products, arithmetic and copies ran while one was open for 0% -> 0% of each run, Pallas kernels for 0% -> 10%
where the time goes in v1:
time: 214 us; the launch traced here: 213 us
  waiting for transfers between devices  56.6 us (26%)
  starting transfers between devices  55.2 us (26%)
  local copies, waits for them, and re-layouts  54.4 us (25%)
  Pallas kernels  38.7 us (18%)
  other arithmetic  7.4 us (3%)
    ppermute x47, waiting for transfers between devices, exchange(): return lax.ppermute(value, axis, [(i, i ^ distance) for i in range(size)])  56.6 us
    ppermute x47, starting transfers between devices, exchange(): return lax.ppermute(value, axis, [(i, i ^ distance) for i in range(size)])  55.2 us
    unnamed x28, local copies, waits for them, and re-layouts  53.7 us
    pallas_call x16, Pallas kernels, forward(): pl.pallas_call(body, out_shape=jax.ShapeDtypeStruct((scen, rows + LANES),...  19 us
    pallas_call x16, Pallas kernels, backward(): pl.pallas_call(body, out_shape=out, in_specs=[SMEM, VMEM, VMEM] + [VMEM]...  12.9 us
    pallas_call x1, Pallas kernels, load(): pl.pallas_call(functools.partial(load_kernel, chunk), out_shape=(jax.Shap...  6.83 us
  transfers between devices with their start and end apart: 47, of which 25 were waited for; matrix products, arithmetic and copies ran while one was open for 0% of the time, Pallas kernels for 10%

profile of v1, /device:TPU:0, one launch (start us, length us, event | category | flops | bytes accessed | tf_op | source)
XLA Modules:
  0.0 213.3 jit_solution(17664721976226380796)
XLA Ops:
  0.6 1.2 copy-done.9
  1.9 6.8 %shard_map.50 = (bf16[512,16384]{1,0:T(8,128)(2,1)S(1)}, f32[16,512]{1,0:T(8,128)S(1)}) custom-call(bf16[512,16384]{1,0:T(8,128)(2,1)} %op_hbm.1, f32[16,16384]{1,0:T(8,128)S(1)} %copy-done.9), custom_call_target="tpu_custom_call" | custom-call | flops 4294967296 | bytes 16777216 | tf_op jit(solution)/shard_map/pallas_call | solution.py:52
  8.7 5.7 %copy-done = bf16[512,16384]{1,0:T(8,128)(2,1)} copy-done((bf16[512,16384]{1,0:T(8,128)(2,1)}, bf16[512,16384]{1,0:T(8,128)(2,1)S(1)}, u32[]{:S(2)}) %copy-start) | copy-done | bytes 16777240
  14.9 2.5 %collective-permute-start.1 = (f32[16,512]{1,0:T(8,128)S(1)}, f32[16,512]{1,0:T(8,128)S(1)}, u32[]{:S(2)}, u32[]{:S(2)}) collective-permute-start(f32[16,512]{1,0:T(8,128)S(1)} %get-tuple-element.5), channel_id=1, source_target_pairs={{0,2},{1,3},{2,0},{3,1},{4,6},{5,7},{6,4},{7,5},{8,10},{9,11},{10,... | collective-permute-start | bytes 98312 | tf_op jit(solution)/shard_map/ppermute | solution.py:138
  17.6 1.9 collective-permute-done.1
  19.5 1.3 collective-permute-done.2
  21.4 5.8 %copy-done.1 = bf16[512,16384]{1,0:T(8,128)(2,1)S(1)} copy-done((bf16[512,16384]{1,0:T(8,128)(2,1)S(1)}, bf16[512,16384]{1,0:T(8,128)(2,1)}, u32[]{:S(2)}) %copy-start.1) | copy-done | bytes 16777240
  28.0 1.5 collective-permute-start.3
  30.3 1.6 collective-permute-start.4
  33.9 2.6 %collective-permute-done.4 = bf16[16,4224]{1,0:T(8,128)(2,1)S(1)} collective-permute-done((bf16[16,4224]{1,0:T(8,128)(2,1)S(1)}, bf16[16,4224]{1,0:T(8,128)(2,1)S(1)}, u32[]{:S(2)}, u32[]{:S(2)}) %collective-permute-start.4) | collective-permute-done | bytes 135200 | tf_op jit(solution)/shard_map/ppermute | solution.py:138
  36.5 2.2 %collective-permute-done.5 = bf16[16,4224]{1,0:T(8,128)(2,1)S(1)} collective-permute-done((bf16[16,4224]{1,0:T(8,128)(2,1)S(1)}, bf16[16,4224]{1,0:T(8,128)(2,1)S(1)}, u32[]{:S(2)}, u32[]{:S(2)}) %collective-permute-start.5) | collective-permute-done | bytes 135200 | tf_op jit(solution)/shard_map/ppermute | solution.py:138
  39.1 2.7 %collective-permute-start.6 = (bf16[16,4224]{1,0:T(8,128)(2,1)S(1)}, bf16[16,4224]{1,0:T(8,128)(2,1)S(1)}, u32[]{:S(2)}, u32[]{:S(2)}) collective-permute-start(bf16[16,4224]{1,0:T(8,128)(2,1)S(1)} %pad_maximum_fusion.4), channel_id=1, source_target_pairs={{0,16},{4,20},{8,24},{12,28},{16,0},{20,4},{24,8},{28,12},{1,17},{... | collective-permute-start | bytes 405512 | tf_op jit(solution)/shard_map/ppermute | solution.py:138
  41.8 5.5 %collective-permute-done.6 = bf16[16,4224]{1,0:T(8,128)(2,1)S(1)} collective-permute-done((bf16[16,4224]{1,0:T(8,128)(2,1)S(1)}, bf16[16,4224]{1,0:T(8,128)(2,1)S(1)}, u32[]{:S(2)}, u32[]{:S(2)}) %collective-permute-start.6) | collective-permute-done | bytes 135200 | tf_op jit(solution)/shard_map/ppermute | solution.py:138
  47.3 2.0 collective-permute-start.9
  49.3 1.5 collective-permute-start.8
  50.7 1.2 shard_map.55.sum_ref
  52.1 2.2 %collective-permute-done.9.v_ref = bf16[16,4096]{1,0:T(8,128)(2,1)S(1)} collective-permute-done((bf16[16,4096]{1,0:T(8,128)(2,1)S(1)}, bf16[16,4096]{1,0:T(8,128)(2,1)S(1)}, u32[]{:S(2)}, u32[]{:S(2)}) %collective-permute-start.9) | collective-permute-done | bytes 131104 | tf_op jit(solution)/shard_map/ppermute | solution.py:138
  54.2 1.2 shard_map.56.sum_ref
  56.0 1.2 shard_map.57.sum_ref
  57.2 1.2 shard_map.58
  60.3 2.3 %collective-permute-done.11 = f32[16,640]{1,0:T(8,128)S(1)} collective-permute-done((f32[16,640]{1,0:T(8,128)S(1)}, f32[16,640]{1,0:T(8,128)S(1)}, u32[]{:S(2)}, u32[]{:S(2)}) %collective-permute-start.11) | collective-permute-done | bytes 40992 | tf_op jit(solution)/shard_map/ppermute | solution.py:138
  65.0 1.4 collective-permute-start.13
  68.0 1.3 collective-permute-start.15
  69.4 5.8 %copy-done.2 = bf16[512,16384]{1,0:T(8,128)(2,1)S(1)} copy-done((bf16[512,16384]{1,0:T(8,128)(2,1)S(1)}, bf16[512,16384]{1,0:T(8,128)(2,1)}, u32[]{:S(2)}) %copy-start.2) | copy-done | bytes 16777240
  76.4 2.5 %collective-permute-start.16 = (bf16[16,4224]{1,0:T(8,128)(2,1)S(1)}, bf16[16,4224]{1,0:T(8,128)(2,1)S(1)}, u32[]{:S(2)}, u32[]{:S(2)}) collective-permute-start(bf16[16,4224]{1,0:T(8,128)(2,1)S(1)} %pad_maximum_fusion.5), channel_id=1, source_target_pairs={{0,16},{4,20},{8,24},{12,28},{16,0},{20,4},{24,8},{28,12},{1,17},{... | collective-permute-start | bytes 405512 | tf_op jit(solution)/shard_map/ppermute | solution.py:138
  79.1 6.1 %collective-permute-done.16 = bf16[16,4224]{1,0:T(8,128)(2,1)S(1)} collective-permute-done((bf16[16,4224]{1,0:T(8,128)(2,1)S(1)}, bf16[16,4224]{1,0:T(8,128)(2,1)S(1)}, u32[]{:S(2)}, u32[]{:S(2)}) %collective-permute-start.16) | collective-permute-done | bytes 135200 | tf_op jit(solution)/shard_map/ppermute | solution.py:138
  85.5 1.5 collective-permute-start.19
  87.0 1.4 collective-permute-start.18
  88.4 5.8 %copy-done.3 = bf16[512,16384]{1,0:T(8,128)(2,1)S(1)} copy-done((bf16[512,16384]{1,0:T(8,128)(2,1)S(1)}, bf16[512,16384]{1,0:T(8,128)(2,1)}, u32[]{:S(2)}) %copy-start.3) | copy-done | bytes 16777240
  96.2 1.2 shard_map.64.sum_ref
  97.4 1.2 shard_map.65.sum_ref
  98.6 1.7 collective-permute-done.17.v_ref
  100.4 1.2 shard_map.66
  103.4 2.3 %collective-permute-done.21 = f32[16,640]{1,0:T(8,128)S(1)} collective-permute-done((f32[16,640]{1,0:T(8,128)S(1)}, f32[16,640]{1,0:T(8,128)S(1)}, u32[]{:S(2)}, u32[]{:S(2)}) %collective-permute-start.21) | collective-permute-done | bytes 40992 | tf_op jit(solution)/shard_map/ppermute | solution.py:138
  106.6 5.8 %copy-done.4 = bf16[512,16384]{1,0:T(8,128)(2,1)S(1)} copy-done((bf16[512,16384]{1,0:T(8,128)(2,1)S(1)}, bf16[512,16384]{1,0:T(8,128)(2,1)}, u32[]{:S(2)}) %copy-start.4) | copy-done | bytes 16777240
  116.4 1.9 collective-permute-start.25
  118.4 5.8 %copy-done.5 = bf16[512,16384]{1,0:T(8,128)(2,1)S(1)} copy-done((bf16[512,16384]{1,0:T(8,128)(2,1)S(1)}, bf16[512,16384]{1,0:T(8,128)(2,1)}, u32[]{:S(2)}) %copy-start.5) | copy-done | bytes 16777240
  125.4 2.2 %collective-permute-start.26 = (bf16[16,4224]{1,0:T(8,128)(2,1)S(1)}, bf16[16,4224]{1,0:T(8,128)(2,1)S(1)}, u32[]{:S(2)}, u32[]{:S(2)}) collective-permute-start(bf16[16,4224]{1,0:T(8,128)(2,1)S(1)} %pad_maximum_fusion.6), channel_id=1, source_target_pairs={{0,16},{4,20},{8,24},{12,28},{16,0},{20,4},{24,8},{28,12},{1,17},{... | collective-permute-start | bytes 405512 | tf_op jit(solution)/shard_map/ppermute | solution.py:138
  127.8 6.2 %collective-permute-done.26 = bf16[16,4224]{1,0:T(8,128)(2,1)S(1)} collective-permute-done((bf16[16,4224]{1,0:T(8,128)(2,1)S(1)}, bf16[16,4224]{1,0:T(8,128)(2,1)S(1)}, u32[]{:S(2)}, u32[]{:S(2)}) %collective-permute-start.26) | collective-permute-done | bytes 135200 | tf_op jit(solution)/shard_map/ppermute | solution.py:138
  135.2 1.6 collective-permute-start.28
  136.9 5.8 %copy-done.6 = bf16[512,16384]{1,0:T(8,128)(2,1)S(1)} copy-done((bf16[512,16384]{1,0:T(8,128)(2,1)S(1)}, bf16[512,16384]{1,0:T(8,128)(2,1)}, u32[]{:S(2)}) %copy-start.6) | copy-done | bytes 16777240
  143.8 1.2 collective-permute-start.27
  145.0 1.2 shard_map.72.sum_ref
  146.2 1.2 shard_map.73.sum_ref
  147.4 1.4 collective-permute-done.27.v_ref
  148.8 1.2 shard_map.74
  151.9 2.1 collective-permute-done.31
  156.7 1.2 collective-permute-start.33
  159.1 1.9 collective-permute-start.35
  161.1 5.8 %copy-done.7 = bf16[512,16384]{1,0:T(8,128)(2,1)S(1)} copy-done((bf16[512,16384]{1,0:T(8,128)(2,1)S(1)}, bf16[512,16384]{1,0:T(8,128)(2,1)}, u32[]{:S(2)}) %copy-start.7) | copy-done | bytes 16777240
  169.0 2.0 collective-permute-start.36
  171.1 6.7 %collective-permute-done.36 = bf16[16,4224]{1,0:T(8,128)(2,1)S(1)} collective-permute-done((bf16[16,4224]{1,0:T(8,128)(2,1)}, bf16[16,4224]{1,0:T(8,128)(2,1)S(1)}, u32[]{:S(2)}, u32[]{:S(2)}) %collective-permute-start.36) | collective-permute-done | bytes 135200 | tf_op jit(solution)/shard_map/ppermute | solution.py:138
  179.1 1.8 collective-permute-start.38
  180.9 5.8 %copy-done.8 = bf16[512,16384]{1,0:T(8,128)(2,1)S(1)} copy-done((bf16[512,16384]{1,0:T(8,128)(2,1)S(1)}, bf16[512,16384]{1,0:T(8,128)(2,1)}, u32[]{:S(2)}) %copy-start.8) | copy-done | bytes 16777240
  188.7 1.2 shard_map.80.sum_ref
  189.9 1.2 shard_map.81.sum_ref
  191.1 1.7 collective-permute-done.37.v_ref
  192.8 1.2 shard_map.82
  195.9 2.1 collective-permute-done.41
  200.2 2.3 %collective-permute-start.45 = (f32[16,128]{0,1:T(8,128)S(1)}, f32[16,128]{0,1:T(8,128)S(1)}, u32[]{:S(2)}, u32[]{:S(2)}) collective-permute-start(f32[16,128]{0,1:T(8,128)S(1)} %broadcast_in_dim.280), channel_id=1, source_target_pairs={{0,12},{4,8},{8,4},{12,0},{16,28},{20,24},{24,20},{28,16},{1,13},{... | collective-permute-start | bytes 24584 | tf_op jit(solution)/shard_map/ppermute | solution.py:138
  204.5 1.3 collective-permute-done.45
  205.8 3.0 %collective-permute-start.46 = (f32[16,128]{0,1:T(8,128)S(1)}, f32[16,128]{0,1:T(8,128)S(1)}, u32[]{:S(2)}, u32[]{:S(2)}) collective-permute-start(f32[16,128]{0,1:T(8,128)S(1)} %add_add_fusion), channel_id=1, source_target_pairs={{0,16},{4,20},{8,24},{12,28},{16,0},{20,4},{24,8},{28,12},{1,17},{... | collective-permute-start | bytes 24584 | tf_op jit(solution)/shard_map/ppermute | solution.py:138
  208.8 2.2 %collective-permute-done.46 = f32[16,128]{0,1:T(8,128)S(1)} collective-permute-done((f32[16,128]{0,1:T(8,128)S(1)}, f32[16,128]{0,1:T(8,128)S(1)}, u32[]{:S(2)}, u32[]{:S(2)}) %collective-permute-start.46) | collective-permute-done | bytes 8224 | tf_op jit(solution)/shard_map/ppermute | solution.py:138
  211.7 1.6 fusion.3
  (180 shorter events, 44.5 us)
Async XLA Ops:
  0.6 1.2 copy-start.9
  1.9 18.9 %copy-start.13 = (f32[16,512]{1,0:T(8,128)S(1)}, f32[16,512]{1,0:T(8,128)}, u32[]{:S(2)}) copy-start(f32[16,512]{1,0:T(8,128)} %param.4) | copy-start | bytes 98308
  8.7 5.7 %copy-start = (bf16[512,16384]{1,0:T(8,128)(2,1)}, bf16[512,16384]{1,0:T(8,128)(2,1)S(1)}, u32[]{:S(2)}) copy-start(bf16[512,16384]{1,0:T(8,128)(2,1)S(1)} %get-tuple-element.4.op_ref) | copy-start | bytes 50331652
  14.4 3.1 %collective-permute-start = (f32[16,512]{1,0:T(8,128)S(1)}, f32[16,512]{1,0:T(8,128)S(1)}, u32[]{:S(2)}, u32[]{:S(2)}) collective-permute-start(f32[16,512]{1,0:T(8,128)S(1)} %get-tuple-element.5), channel_id=1, source_target_pairs={{0,1},{1,0},{2,3},{3,2},{4,5},{5,4},{6,7},{7,6},{8,9},{9,8},{10,11... | collective-permute-start | bytes 98312 | tf_op jit(solution)/shard_map/ppermute | solution.py:138
  14.9 4.6 %collective-permute-start.1 = (f32[16,512]{1,0:T(8,128)S(1)}, f32[16,512]{1,0:T(8,128)S(1)}, u32[]{:S(2)}, u32[]{:S(2)}) collective-permute-start(f32[16,512]{1,0:T(8,128)S(1)} %get-tuple-element.5), channel_id=1, source_target_pairs={{0,2},{1,3},{2,0},{3,1},{4,6},{5,7},{6,4},{7,5},{8,10},{9,11},{10,... | collective-permute-start | bytes 98312 | tf_op jit(solution)/shard_map/ppermute | solution.py:138
  17.4 3.3 %collective-permute-start.2 = (f32[16,512]{1,0:T(8,128)S(1)}, f32[16,512]{1,0:T(8,128)S(1)}, u32[]{:S(2)}, u32[]{:S(2)}) collective-permute-start(f32[16,512]{1,0:T(8,128)S(1)} %get-tuple-element.5), channel_id=1, source_target_pairs={{0,3},{1,2},{2,1},{3,0},{4,7},{5,6},{6,5},{7,4},{8,11},{9,10},{10,... | collective-permute-start | bytes 98312 | tf_op jit(solution)/shard_map/ppermute | solution.py:138
  20.8 0.6 copy-start.11
  21.4 5.8 %copy-start.1 = (bf16[512,16384]{1,0:T(8,128)(2,1)S(1)}, bf16[512,16384]{1,0:T(8,128)(2,1)}, u32[]{:S(2)}) copy-start(bf16[512,16384]{1,0:T(8,128)(2,1)} %copy-done) | copy-start | bytes 50331652
  28.0 5.9 %collective-permute-start.3 = (bf16[16,4224]{1,0:T(8,128)(2,1)S(1)}, bf16[16,4224]{1,0:T(8,128)(2,1)S(1)}, u32[]{:S(2)}, u32[]{:S(2)}) collective-permute-start(bf16[16,4224]{1,0:T(8,128)(2,1)S(1)} %shard_map.52), channel_id=1, source_target_pairs={{0,4},{4,0},{8,12},{12,8},{16,20},{20,16},{24,28},{28,24},{1,5},{5... | collective-permute-start | bytes 405512 | tf_op jit(solution)/shard_map/ppermute | solution.py:138
  30.3 6.3 %collective-permute-start.4 = (bf16[16,4224]{1,0:T(8,128)(2,1)S(1)}, bf16[16,4224]{1,0:T(8,128)(2,1)S(1)}, u32[]{:S(2)}, u32[]{:S(2)}) collective-permute-start(bf16[16,4224]{1,0:T(8,128)(2,1)S(1)} %shard_map.53), channel_id=1, source_target_pairs={{0,8},{4,12},{8,0},{12,4},{16,24},{20,28},{24,16},{28,20},{1,9},{5... | collective-permute-start | bytes 405512 | tf_op jit(solution)/shard_map/ppermute | solution.py:138
  32.7 6.1 %collective-permute-start.5 = (bf16[16,4224]{1,0:T(8,128)(2,1)S(1)}, bf16[16,4224]{1,0:T(8,128)(2,1)S(1)}, u32[]{:S(2)}, u32[]{:S(2)}) collective-permute-start(bf16[16,4224]{1,0:T(8,128)(2,1)S(1)} %shard_map.54), channel_id=1, source_target_pairs={{0,12},{4,8},{8,4},{12,0},{16,28},{20,24},{24,20},{28,16},{1,13},{... | collective-permute-start | bytes 405512 | tf_op jit(solution)/shard_map/ppermute | solution.py:138
  39.1 8.1 %collective-permute-start.6 = (bf16[16,4224]{1,0:T(8,128)(2,1)S(1)}, bf16[16,4224]{1,0:T(8,128)(2,1)S(1)}, u32[]{:S(2)}, u32[]{:S(2)}) collective-permute-start(bf16[16,4224]{1,0:T(8,128)(2,1)S(1)} %pad_maximum_fusion.4), channel_id=1, source_target_pairs={{0,16},{4,20},{8,24},{12,28},{16,0},{20,4},{24,8},{28,12},{1,17},{... | collective-permute-start | bytes 405512 | tf_op jit(solution)/shard_map/ppermute | solution.py:138
  47.3 6.9 %collective-permute-start.9 = (bf16[16,4096]{1,0:T(8,128)(2,1)S(1)}, bf16[16,4096]{1,0:T(8,128)(2,1)S(1)}, u32[]{:S(2)}, u32[]{:S(2)}) collective-permute-start(bf16[16,4096]{1,0:T(8,128)(2,1)S(1)} %reduce-precision_convert_fusion.3.v_ref), channel_id=1, source_target_pairs={{0,12},{4,8},{8,4},{12,0},{16,28},{20,24},{24,20},{28,16},{1,13},{... | collective-permute-start | bytes 393224 | tf_op jit(solution)/shard_map/ppermute | solution.py:138
  49.3 6.8 %collective-permute-start.8 = (bf16[16,4096]{1,0:T(8,128)(2,1)S(1)}, bf16[16,4096]{1,0:T(8,128)(2,1)S(1)}, u32[]{:S(2)}, u32[]{:S(2)}) collective-permute-start(bf16[16,4096]{1,0:T(8,128)(2,1)S(1)} %reduce-precision_convert_fusion.3.v_ref), channel_id=1, source_target_pairs={{0,8},{4,12},{8,0},{12,4},{16,24},{20,28},{24,16},{28,20},{1,9},{5... | collective-permute-start | bytes 393224 | tf_op jit(solution)/shard_map/ppermute | solution.py:138
  51.9 5.3 %collective-permute-start.7 = (bf16[16,4096]{1,0:T(8,128)(2,1)S(1)}, bf16[16,4096]{1,0:T(8,128)(2,1)S(1)}, u32[]{:S(2)}, u32[]{:S(2)}) collective-permute-start(bf16[16,4096]{1,0:T(8,128)(2,1)S(1)} %reduce-precision_convert_fusion.3.v_ref), channel_id=1, source_target_pairs={{0,4},{4,0},{8,12},{12,8},{16,20},{20,16},{24,28},{28,24},{1,5},{5... | collective-permute-start | bytes 393224 | tf_op jit(solution)/shard_map/ppermute | solution.py:138
  58.4 1.9 collective-permute-start.10
  58.4 4.2 %collective-permute-start.11 = (f32[16,640]{1,0:T(8,128)S(1)}, f32[16,640]{1,0:T(8,128)S(1)}, u32[]{:S(2)}, u32[]{:S(2)}) collective-permute-start(f32[16,640]{1,0:T(8,128)S(1)} %shard_map.58), channel_id=1, source_target_pairs={{0,2},{1,3},{2,0},{3,1},{4,6},{5,7},{6,4},{7,5},{8,10},{9,11},{10,... | collective-permute-start | bytes 122888 | tf_op jit(solution)/shard_map/ppermute | solution.py:138
  59.3 3.8 %collective-permute-start.12 = (f32[16,640]{1,0:T(8,128)S(1)}, f32[16,640]{1,0:T(8,128)S(1)}, u32[]{:S(2)}, u32[]{:S(2)}) collective-permute-start(f32[16,640]{1,0:T(8,128)S(1)} %shard_map.58), channel_id=1, source_target_pairs={{0,3},{1,2},{2,1},{3,0},{4,7},{5,6},{6,5},{7,4},{8,11},{9,10},{10,... | collective-permute-start | bytes 122888 | tf_op jit(solution)/shard_map/ppermute | solution.py:138
  65.0 10.9 %collective-permute-start.13 = (bf16[16,4224]{1,0:T(8,128)(2,1)S(1)}, bf16[16,4224]{1,0:T(8,128)(2,1)S(1)}, u32[]{:S(2)}, u32[]{:S(2)}) collective-permute-start(bf16[16,4224]{1,0:T(8,128)(2,1)S(1)} %shard_map.59), channel_id=1, source_target_pairs={{0,4},{4,0},{8,12},{12,8},{16,20},{20,16},{24,28},{28,24},{1,5},{5... | collective-permute-start | bytes 405512 | tf_op jit(solution)/shard_map/ppermute | solution.py:138
  67.1 8.8 %collective-permute-start.14 = (bf16[16,4224]{1,0:T(8,128)(2,1)S(1)}, bf16[16,4224]{1,0:T(8,128)(2,1)S(1)}, u32[]{:S(2)}, u32[]{:S(2)}) collective-permute-start(bf16[16,4224]{1,0:T(8,128)(2,1)S(1)} %shard_map.60), channel_id=1, source_target_pairs={{0,8},{4,12},{8,0},{12,4},{16,24},{20,28},{24,16},{28,20},{1,9},{5... | collective-permute-start | bytes 405512 | tf_op jit(solution)/shard_map/ppermute | solution.py:138
  68.0 7.9 %collective-permute-start.15 = (bf16[16,4224]{1,0:T(8,128)(2,1)S(1)}, bf16[16,4224]{1,0:T(8,128)(2,1)S(1)}, u32[]{:S(2)}, u32[]{:S(2)}) collective-permute-start(bf16[16,4224]{1,0:T(8,128)(2,1)S(1)} %shard_map.61), channel_id=1, source_target_pairs={{0,12},{4,8},{8,4},{12,0},{16,28},{20,24},{24,20},{28,16},{1,13},{... | collective-permute-start | bytes 405512 | tf_op jit(solution)/shard_map/ppermute | solution.py:138
  69.4 5.8 %copy-start.2 = (bf16[512,16384]{1,0:T(8,128)(2,1)S(1)}, bf16[512,16384]{1,0:T(8,128)(2,1)}, u32[]{:S(2)}) copy-start(bf16[512,16384]{1,0:T(8,128)(2,1)} %copy-done) | copy-start | bytes 50331652
  76.4 8.8 %collective-permute-start.16 = (bf16[16,4224]{1,0:T(8,128)(2,1)S(1)}, bf16[16,4224]{1,0:T(8,128)(2,1)S(1)}, u32[]{:S(2)}, u32[]{:S(2)}) collective-permute-start(bf16[16,4224]{1,0:T(8,128)(2,1)S(1)} %pad_maximum_fusion.5), channel_id=1, source_target_pairs={{0,16},{4,20},{8,24},{12,28},{16,0},{20,4},{24,8},{28,12},{1,17},{... | collective-permute-start | bytes 405512 | tf_op jit(solution)/shard_map/ppermute | solution.py:138
  85.5 10.7 %collective-permute-start.19 = (bf16[16,4096]{1,0:T(8,128)(2,1)S(1)}, bf16[16,4096]{1,0:T(8,128)(2,1)S(1)}, u32[]{:S(2)}, u32[]{:S(2)}) collective-permute-start(bf16[16,4096]{1,0:T(8,128)(2,1)S(1)} %get-tuple-element.26.v_ref), channel_id=1, source_target_pairs={{0,12},{4,8},{8,4},{12,0},{16,28},{20,24},{24,20},{28,16},{1,13},{... | collective-permute-start | bytes 393224 | tf_op jit(solution)/shard_map/ppermute | solution.py:138
  87.0 10.4 %collective-permute-start.18 = (bf16[16,4096]{1,0:T(8,128)(2,1)S(1)}, bf16[16,4096]{1,0:T(8,128)(2,1)S(1)}, u32[]{:S(2)}, u32[]{:S(2)}) collective-permute-start(bf16[16,4096]{1,0:T(8,128)(2,1)S(1)} %get-tuple-element.26.v_ref), channel_id=1, source_target_pairs={{0,8},{4,12},{8,0},{12,4},{16,24},{20,28},{24,16},{28,20},{1,9},{5... | collective-permute-start | bytes 393224 | tf_op jit(solution)/shard_map/ppermute | solution.py:138
  88.4 5.8 %copy-start.3 = (bf16[512,16384]{1,0:T(8,128)(2,1)S(1)}, bf16[512,16384]{1,0:T(8,128)(2,1)}, u32[]{:S(2)}) copy-start(bf16[512,16384]{1,0:T(8,128)(2,1)} %copy-done) | copy-start | bytes 50331652
  95.4 5.0 %collective-permute-start.17 = (bf16[16,4096]{1,0:T(8,128)(2,1)S(1)}, bf16[16,4096]{1,0:T(8,128)(2,1)S(1)}, u32[]{:S(2)}, u32[]{:S(2)}) collective-permute-start(bf16[16,4096]{1,0:T(8,128)(2,1)S(1)} %get-tuple-element.26.v_ref), channel_id=1, source_target_pairs={{0,4},{4,0},{8,12},{12,8},{16,20},{20,16},{24,28},{28,24},{1,5},{5... | collective-permute-start | bytes 393224 | tf_op jit(solution)/shard_map/ppermute | solution.py:138
  101.6 1.9 collective-permute-start.20
  101.6 4.2 %collective-permute-start.21 = (f32[16,640]{1,0:T(8,128)S(1)}, f32[16,640]{1,0:T(8,128)S(1)}, u32[]{:S(2)}, u32[]{:S(2)}) collective-permute-start(f32[16,640]{1,0:T(8,128)S(1)} %shard_map.66), channel_id=1, source_target_pairs={{0,2},{1,3},{2,0},{3,1},{4,6},{5,7},{6,4},{7,5},{8,10},{9,11},{10,... | collective-permute-start | bytes 122888 | tf_op jit(solution)/shard_map/ppermute | solution.py:138
  102.6 3.6 %collective-permute-start.22 = (f32[16,640]{1,0:T(8,128)S(1)}, f32[16,640]{1,0:T(8,128)S(1)}, u32[]{:S(2)}, u32[]{:S(2)}) collective-permute-start(f32[16,640]{1,0:T(8,128)S(1)} %shard_map.66), channel_id=1, source_target_pairs={{0,3},{1,2},{2,1},{3,0},{4,7},{5,6},{6,5},{7,4},{8,11},{9,10},{10,... | collective-permute-start | bytes 122888 | tf_op jit(solution)/shard_map/ppermute | solution.py:138
  106.6 5.8 %copy-start.4 = (bf16[512,16384]{1,0:T(8,128)(2,1)S(1)}, bf16[512,16384]{1,0:T(8,128)(2,1)}, u32[]{:S(2)}) copy-start(bf16[512,16384]{1,0:T(8,128)(2,1)} %copy-done) | copy-start | bytes 50331652
  114.0 10.9 %collective-permute-start.23 = (bf16[16,4224]{1,0:T(8,128)(2,1)S(1)}, bf16[16,4224]{1,0:T(8,128)(2,1)S(1)}, u32[]{:S(2)}, u32[]{:S(2)}) collective-permute-start(bf16[16,4224]{1,0:T(8,128)(2,1)S(1)} %shard_map.67), channel_id=1, source_target_pairs={{0,4},{4,0},{8,12},{12,8},{16,20},{20,16},{24,28},{28,24},{1,5},{5... | collective-permute-start | bytes 405512 | tf_op jit(solution)/shard_map/ppermute | solution.py:138
  115.7 9.3 %collective-permute-start.24 = (bf16[16,4224]{1,0:T(8,128)(2,1)S(1)}, bf16[16,4224]{1,0:T(8,128)(2,1)S(1)}, u32[]{:S(2)}, u32[]{:S(2)}) collective-permute-start(bf16[16,4224]{1,0:T(8,128)(2,1)S(1)} %shard_map.68), channel_id=1, source_target_pairs={{0,8},{4,12},{8,0},{12,4},{16,24},{20,28},{24,16},{28,20},{1,9},{5... | collective-permute-start | bytes 405512 | tf_op jit(solution)/shard_map/ppermute | solution.py:138
  116.4 8.6 %collective-permute-start.25 = (bf16[16,4224]{1,0:T(8,128)(2,1)S(1)}, bf16[16,4224]{1,0:T(8,128)(2,1)S(1)}, u32[]{:S(2)}, u32[]{:S(2)}) collective-permute-start(bf16[16,4224]{1,0:T(8,128)(2,1)S(1)} %shard_map.69), channel_id=1, source_target_pairs={{0,12},{4,8},{8,4},{12,0},{16,28},{20,24},{24,20},{28,16},{1,13},{... | collective-permute-start | bytes 405512 | tf_op jit(solution)/shard_map/ppermute | solution.py:138
  118.4 5.8 %copy-start.5 = (bf16[512,16384]{1,0:T(8,128)(2,1)S(1)}, bf16[512,16384]{1,0:T(8,128)(2,1)}, u32[]{:S(2)}) copy-start(bf16[512,16384]{1,0:T(8,128)(2,1)} %copy-done) | copy-start | bytes 50331652
  125.4 8.6 %collective-permute-start.26 = (bf16[16,4224]{1,0:T(8,128)(2,1)S(1)}, bf16[16,4224]{1,0:T(8,128)(2,1)S(1)}, u32[]{:S(2)}, u32[]{:S(2)}) collective-permute-start(bf16[16,4224]{1,0:T(8,128)(2,1)S(1)} %pad_maximum_fusion.6), channel_id=1, source_target_pairs={{0,16},{4,20},{8,24},{12,28},{16,0},{20,4},{24,8},{28,12},{1,17},{... | collective-permute-start | bytes 405512 | tf_op jit(solution)/shard_map/ppermute | solution.py:138
  134.4 10.6 %collective-permute-start.29 = (bf16[16,4096]{1,0:T(8,128)(2,1)S(1)}, bf16[16,4096]{1,0:T(8,128)(2,1)S(1)}, u32[]{:S(2)}, u32[]{:S(2)}) collective-permute-start(bf16[16,4096]{1,0:T(8,128)(2,1)S(1)} %get-tuple-element.21.v_ref), channel_id=1, source_target_pairs={{0,12},{4,8},{8,4},{12,0},{16,28},{20,24},{24,20},{28,16},{1,13},{... | collective-permute-start | bytes 393224 | tf_op jit(solution)/shard_map/ppermute | solution.py:138
  135.2 11.0 %collective-permute-start.28 = (bf16[16,4096]{1,0:T(8,128)(2,1)S(1)}, bf16[16,4096]{1,0:T(8,128)(2,1)S(1)}, u32[]{:S(2)}, u32[]{:S(2)}) collective-permute-start(bf16[16,4096]{1,0:T(8,128)(2,1)S(1)} %get-tuple-element.21.v_ref), channel_id=1, source_target_pairs={{0,8},{4,12},{8,0},{12,4},{16,24},{20,28},{24,16},{28,20},{1,9},{5... | collective-permute-start | bytes 393224 | tf_op jit(solution)/shard_map/ppermute | solution.py:138
  136.9 5.8 %copy-start.6 = (bf16[512,16384]{1,0:T(8,128)(2,1)S(1)}, bf16[512,16384]{1,0:T(8,128)(2,1)}, u32[]{:S(2)}) copy-start(bf16[512,16384]{1,0:T(8,128)(2,1)} %copy-done) | copy-start | bytes 50331652
  143.8 5.0 %collective-permute-start.27 = (bf16[16,4096]{1,0:T(8,128)(2,1)S(1)}, bf16[16,4096]{1,0:T(8,128)(2,1)S(1)}, u32[]{:S(2)}, u32[]{:S(2)}) collective-permute-start(bf16[16,4096]{1,0:T(8,128)(2,1)S(1)} %get-tuple-element.21.v_ref), channel_id=1, source_target_pairs={{0,4},{4,0},{8,12},{12,8},{16,20},{20,16},{24,28},{28,24},{1,5},{5... | collective-permute-start | bytes 393224 | tf_op jit(solution)/shard_map/ppermute | solution.py:138
  150.0 2.0 collective-permute-start.30
  150.0 4.1 %collective-permute-start.31 = (f32[16,640]{1,0:T(8,128)S(1)}, f32[16,640]{1,0:T(8,128)S(1)}, u32[]{:S(2)}, u32[]{:S(2)}) collective-permute-start(f32[16,640]{1,0:T(8,128)S(1)} %shard_map.74), channel_id=1, source_target_pairs={{0,2},{1,3},{2,0},{3,1},{4,6},{5,7},{6,4},{7,5},{8,10},{9,11},{10,... | collective-permute-start | bytes 122888 | tf_op jit(solution)/shard_map/ppermute | solution.py:138
  151.1 3.6 %collective-permute-start.32 = (f32[16,640]{1,0:T(8,128)S(1)}, f32[16,640]{1,0:T(8,128)S(1)}, u32[]{:S(2)}, u32[]{:S(2)}) collective-permute-start(f32[16,640]{1,0:T(8,128)S(1)} %shard_map.74), channel_id=1, source_target_pairs={{0,3},{1,2},{2,1},{3,0},{4,7},{5,6},{6,5},{7,4},{8,11},{9,10},{10,... | collective-permute-start | bytes 122888 | tf_op jit(solution)/shard_map/ppermute | solution.py:138
  156.7 11.2 %collective-permute-start.33 = (bf16[16,4224]{1,0:T(8,128)(2,1)S(1)}, bf16[16,4224]{1,0:T(8,128)(2,1)S(1)}, u32[]{:S(2)}, u32[]{:S(2)}) collective-permute-start(bf16[16,4224]{1,0:T(8,128)(2,1)S(1)} %shard_map.75), channel_id=1, source_target_pairs={{0,4},{4,0},{8,12},{12,8},{16,20},{20,16},{24,28},{28,24},{1,5},{5... | collective-permute-start | bytes 405512 | tf_op jit(solution)/shard_map/ppermute | solution.py:138
  158.7 9.2 %collective-permute-start.34 = (bf16[16,4224]{1,0:T(8,128)(2,1)S(1)}, bf16[16,4224]{1,0:T(8,128)(2,1)S(1)}, u32[]{:S(2)}, u32[]{:S(2)}) collective-permute-start(bf16[16,4224]{1,0:T(8,128)(2,1)S(1)} %shard_map.76), channel_id=1, source_target_pairs={{0,8},{4,12},{8,0},{12,4},{16,24},{20,28},{24,16},{28,20},{1,9},{5... | collective-permute-start | bytes 405512 | tf_op jit(solution)/shard_map/ppermute | solution.py:138
  159.1 8.8 %collective-permute-start.35 = (bf16[16,4224]{1,0:T(8,128)(2,1)S(1)}, bf16[16,4224]{1,0:T(8,128)(2,1)S(1)}, u32[]{:S(2)}, u32[]{:S(2)}) collective-permute-start(bf16[16,4224]{1,0:T(8,128)(2,1)S(1)} %shard_map.77), channel_id=1, source_target_pairs={{0,12},{4,8},{8,4},{12,0},{16,28},{20,24},{24,20},{28,16},{1,13},{... | collective-permute-start | bytes 405512 | tf_op jit(solution)/shard_map/ppermute | solution.py:138
  161.1 5.8 %copy-start.7 = (bf16[512,16384]{1,0:T(8,128)(2,1)S(1)}, bf16[512,16384]{1,0:T(8,128)(2,1)}, u32[]{:S(2)}) copy-start(bf16[512,16384]{1,0:T(8,128)(2,1)} %copy-done) | copy-start | bytes 50331652
  169.0 8.8 %collective-permute-start.36 = (bf16[16,4224]{1,0:T(8,128)(2,1)}, bf16[16,4224]{1,0:T(8,128)(2,1)S(1)}, u32[]{:S(2)}, u32[]{:S(2)}) collective-permute-start(bf16[16,4224]{1,0:T(8,128)(2,1)} %pad_maximum_fusion.7), channel_id=1, source_target_pairs={{0,16},{4,20},{8,24},{12,28},{16,0},{20,4},{24,8},{28,12},{1,17},{... | collective-permute-start | bytes 405512 | tf_op jit(solution)/shard_map/ppermute | solution.py:138
  178.0 10.7 %collective-permute-start.39 = (bf16[16,4096]{1,0:T(8,128)(2,1)S(1)}, bf16[16,4096]{1,0:T(8,128)(2,1)S(1)}, u32[]{:S(2)}, u32[]{:S(2)}) collective-permute-start(bf16[16,4096]{1,0:T(8,128)(2,1)S(1)} %reduce-precision_convert_fusion.v_ref), channel_id=1, source_target_pairs={{0,12},{4,8},{8,4},{12,0},{16,28},{20,24},{24,20},{28,16},{1,13},{... | collective-permute-start | bytes 393224 | tf_op jit(solution)/shard_map/ppermute | solution.py:138
  179.1 10.9 %collective-permute-start.38 = (bf16[16,4096]{1,0:T(8,128)(2,1)S(1)}, bf16[16,4096]{1,0:T(8,128)(2,1)S(1)}, u32[]{:S(2)}, u32[]{:S(2)}) collective-permute-start(bf16[16,4096]{1,0:T(8,128)(2,1)S(1)} %reduce-precision_convert_fusion.v_ref), channel_id=1, source_target_pairs={{0,8},{4,12},{8,0},{12,4},{16,24},{20,28},{24,16},{28,20},{1,9},{5... | collective-permute-start | bytes 393224 | tf_op jit(solution)/shard_map/ppermute | solution.py:138
  180.9 5.8 %copy-start.8 = (bf16[512,16384]{1,0:T(8,128)(2,1)S(1)}, bf16[512,16384]{1,0:T(8,128)(2,1)}, u32[]{:S(2)}) copy-start(bf16[512,16384]{1,0:T(8,128)(2,1)} %copy-done) | copy-start | bytes 50331652
  187.8 5.0 %collective-permute-start.37 = (bf16[16,4096]{1,0:T(8,128)(2,1)S(1)}, bf16[16,4096]{1,0:T(8,128)(2,1)S(1)}, u32[]{:S(2)}, u32[]{:S(2)}) collective-permute-start(bf16[16,4096]{1,0:T(8,128)(2,1)S(1)} %reduce-precision_convert_fusion.v_ref), channel_id=1, source_target_pairs={{0,4},{4,0},{8,12},{12,8},{16,20},{20,16},{24,28},{28,24},{1,5},{5... | collective-permute-start | bytes 393224 | tf_op jit(solution)/shard_map/ppermute | solution.py:138
  189.9 21.1 %copy-start.12 = (f32[16,512]{1,0:T(8,128)S(1)}, f32[16,512]{1,0:T(8,128)}, u32[]{:S(2)}) copy-start(f32[16,512]{1,0:T(8,128)} %copy-done.11) | copy-start | bytes 98308
  189.9 21.8 %copy-start.10 = (f32[16,16384]{1,0:T(8,128)S(1)}, f32[16,16384]{1,0:T(8,128)}, u32[]{:S(2)}) copy-start(f32[16,16384]{1,0:T(8,128)} %start_hbm.1) | copy-start | bytes 3145732
  194.0 1.9 collective-permute-start.40
  194.0 4.1 %collective-permute-start.41 = (f32[16,640]{1,0:T(8,128)S(1)}, f32[16,640]{1,0:T(8,128)S(1)}, u32[]{:S(2)}, u32[]{:S(2)}) collective-permute-start(f32[16,640]{1,0:T(8,128)S(1)} %shard_map.82), channel_id=1, source_target_pairs={{0,2},{1,3},{2,0},{3,1},{4,6},{5,7},{6,4},{7,5},{8,10},{9,11},{10,... | collective-permute-start | bytes 122888 | tf_op jit(solution)/shard_map/ppermute | solution.py:138
  195.1 3.6 %collective-permute-start.42 = (f32[16,640]{1,0:T(8,128)S(1)}, f32[16,640]{1,0:T(8,128)S(1)}, u32[]{:S(2)}, u32[]{:S(2)}) collective-permute-start(f32[16,640]{1,0:T(8,128)S(1)} %shard_map.82), channel_id=1, source_target_pairs={{0,3},{1,2},{2,1},{3,0},{4,7},{5,6},{6,5},{7,4},{8,11},{9,10},{10,... | collective-permute-start | bytes 122888 | tf_op jit(solution)/shard_map/ppermute | solution.py:138
  199.0 4.3 %collective-permute-start.43 = (f32[16,128]{0,1:T(8,128)S(1)}, f32[16,128]{0,1:T(8,128)S(1)}, u32[]{:S(2)}, u32[]{:S(2)}) collective-permute-start(f32[16,128]{0,1:T(8,128)S(1)} %broadcast_in_dim.280), channel_id=1, source_target_pairs={{0,4},{4,0},{8,12},{12,8},{16,20},{20,16},{24,28},{28,24},{1,5},{5... | collective-permute-start | bytes 24584 | tf_op jit(solution)/shard_map/ppermute | solution.py:138
  199.9 4.5 %collective-permute-start.44 = (f32[16,128]{0,1:T(8,128)S(1)}, f32[16,128]{0,1:T(8,128)S(1)}, u32[]{:S(2)}, u32[]{:S(2)}) collective-permute-start(f32[16,128]{0,1:T(8,128)S(1)} %broadcast_in_dim.280), channel_id=1, source_target_pairs={{0,8},{4,12},{8,0},{12,4},{16,24},{20,28},{24,16},{28,20},{1,9},{5... | collective-permute-start | bytes 24584 | tf_op jit(solution)/shard_map/ppermute | solution.py:138
  200.2 5.5 %collective-permute-start.45 = (f32[16,128]{0,1:T(8,128)S(1)}, f32[16,128]{0,1:T(8,128)S(1)}, u32[]{:S(2)}, u32[]{:S(2)}) collective-permute-start(f32[16,128]{0,1:T(8,128)S(1)} %broadcast_in_dim.280), channel_id=1, source_target_pairs={{0,12},{4,8},{8,4},{12,0},{16,28},{20,24},{24,20},{28,16},{1,13},{... | collective-permute-start | bytes 24584 | tf_op jit(solution)/shard_map/ppermute | solution.py:138
  205.8 5.2 %collective-permute-start.46 = (f32[16,128]{0,1:T(8,128)S(1)}, f32[16,128]{0,1:T(8,128)S(1)}, u32[]{:S(2)}, u32[]{:S(2)}) collective-permute-start(f32[16,128]{0,1:T(8,128)S(1)} %add_add_fusion), channel_id=1, source_target_pairs={{0,16},{4,20},{8,24},{12,28},{16,0},{20,4},{24,8},{28,12},{1,17},{... | collective-permute-start | bytes 24584 | tf_op jit(solution)/shard_map/ppermute | solution.py:138

commit v2 on v0

v2 whole, which is shorter than its diff:
```python
import functools

import jax
import jax.numpy as jnp
from jax import lax
from jax.experimental import pallas as pl
from jax.experimental.pallas import tpu as pltpu
from jax.sharding import PartitionSpec as P

ITERS = 4
LANES = 128
F32 = jnp.float32
BF16 = jnp.bfloat16
VMEM = pl.BlockSpec(memory_space=pltpu.VMEM)
ANY = pl.BlockSpec(memory_space=pl.ANY)


def shape(*sizes, dtype=F32):
    return jax.ShapeDtypeStruct(sizes, dtype)


def call(body, out, args, specs=None, scratch=(), flops=0, bytes_accessed=1 << 18):
    return pl.pallas_call(
        body,
        out_shape=out,
        in_specs=specs if specs is not None else [VMEM] * len(args),
        out_specs=jax.tree.map(lambda _: VMEM, out),
        scratch_shapes=scratch,
        compiler_params=pltpu.CompilerParams(vmem_limit_bytes=24 << 20),
        cost_estimate=pl.CostEstimate(flops=flops, bytes_accessed=bytes_accessed, transcendentals=0),
    )(*args)


def operator_cost(rows, columns):
    return {"flops": 512 * rows * columns, "bytes_accessed": 2 * rows * columns}


def tree(parts):
    if len(parts) == 1:
        return parts[0]
    if len(parts) == 2:
        return parts[0] + parts[1]
    return (parts[0] + parts[1]) + (parts[2] + parts[3])


def lane_total(value):
    return jnp.broadcast_to(jnp.sum(value, axis=1, keepdims=True), (value.shape[0], LANES))


def pack_norm(value):
    high = value.astype(BF16).astype(F32)
    rest = value - high
    middle = rest.astype(BF16).astype(F32)
    lane = lax.broadcasted_iota(jnp.int32, value.shape, 1)
    zero = jnp.zeros_like(value)
    return jnp.where(
        lane == 0, high, jnp.where(lane == 1, middle, jnp.where(lane == 2, rest - middle, zero))
    ).astype(BF16)


def unpack_norm(block):
    return lane_total(block.astype(F32))


def split(value, out_ref):
    scen = value.shape[0]
    high = value.astype(BF16)
    out_ref[:scen, :] = high
    out_ref[scen:, :] = (value - high.astype(F32)).astype(BF16)


def load_kernel(chunk, op_hbm, start_hbm, op_ref, image_ref, start_ref, sems):
    pieces = op_ref.shape[1] // chunk
    copies = [pltpu.make_async_copy(start_hbm, start_ref, sems.at[pieces])]
    for k in range(pieces):
        at = pl.ds(k * chunk, chunk)
        copies.append(pltpu.make_async_copy(op_hbm.at[:, at], op_ref.at[:, at], sems.at[k]))
    for copy in copies:
        copy.start()
    copies[0].wait()
    total = jnp.zeros(image_ref.shape, F32)
    for k in range(pieces):
        copies[k + 1].wait()
        at = pl.ds(k * chunk, chunk)
        total += lax.dot_general(
            start_ref[:, at].astype(BF16), op_ref[:, at], (((1,), (1,)), ((), ())), preferred_element_type=F32
        )
    image_ref[...] = total


def load(operator, start):
    rows, columns = operator.shape
    chunk = min(2048, columns)
    return call(
        functools.partial(load_kernel, chunk),
        (shape(rows, columns, dtype=BF16), shape(start.shape[0], rows)),
        (operator, start),
        [ANY, ANY],
        [pltpu.VMEM(start.shape, F32), pltpu.SemaphoreType.DMA((columns // chunk + 1,))],
        **operator_cost(rows, columns),
    )


def place(near, distance):
    return (lax.axis_index("obs") & (near - 1)) ^ distance


def backward_kernel(near, distance, chunk, op_ref, w_ref, *refs):
    out_ref = refs[-1]
    scen = out_ref.shape[0]
    width = out_ref.shape[1] - LANES * (len(refs) - 1)
    w = w_ref[...]
    base = place(near, distance) * width
    for k in range(width // chunk):
        at = pl.ds(pl.multiple_of(base + k * chunk, chunk), chunk)
        both = jnp.dot(w, op_ref[:, at], preferred_element_type=F32)
        out_ref[:, k * chunk : (k + 1) * chunk] = (both[:scen] + both[scen:]).astype(out_ref.dtype)
    for norm_ref in refs[:-1]:
        out_ref[:, width:] = norm_ref[...]


def backward(near, distance, op, w, *norm):
    width = op.shape[1] // near
    scen = w.shape[0] // 2
    out = shape(scen, width + LANES, dtype=BF16) if norm else shape(scen, width)
    return call(
        functools.partial(backward_kernel, near, distance, min(1024, width)),
        out,
        (op, w, *norm),
        **operator_cost(op.shape[0], width),
    )


def forward_kernel(near, distance, op_ref, v_ref, *refs):
    out_ref = refs[-1]
    width = v_ref.shape[1]
    rows = op_ref.shape[0]
    v = v_ref[...]
    at = pl.ds(pl.multiple_of(place(near, distance) * width, width), width)
    image = lax.dot_general(v, op_ref[:, at], (((1,), (1,)), ((), ())), preferred_element_type=F32)
    wide = v.astype(F32)
    square = wide * wide
    norm = square[:, :LANES]
    for k in range(1, width // LANES):
        norm += square[:, k * LANES : (k + 1) * LANES]
    for sum_ref in refs[:-1]:
        image += sum_ref[:, :rows]
        norm += sum_ref[:, rows:]
    out_ref[:, :rows] = image
    out_ref[:, rows:] = norm


def forward(near, distance, op, v, *total):
    scen, width = v.shape
    rows = op.shape[0]
    return call(
        functools.partial(forward_kernel, near, distance),
        shape(scen, rows + LANES),
        (op, v, *total),
        **operator_cost(rows, width),
    )


def first_kernel(targets_ref, *refs):
    *part_refs, residual_ref, w_ref, norm_ref, packed_ref = refs
    residual = targets_ref[...] - tree([ref[...] for ref in part_refs])
    residual_ref[...] = residual
    norm_ref[...] = jnp.zeros(norm_ref.shape, F32)
    packed_ref[...] = jnp.zeros(packed_ref.shape, BF16)
    split(residual, w_ref)


def image_kernel(later, last, *refs):
    outs = 4 + (not last) * 2
    ins, (image_ref, gamma_ref, beta_ref, norm_ref, *more_refs) = refs[:-outs], refs[-outs:]
    if later:
        old_ref, old_gamma_ref, *ins = ins
    total = tree([ref[...] for ref in ins])
    rows = image_ref.shape[1]
    image = total[:, :rows]
    gamma = lane_total(total[:, rows:])
    beta = jnp.zeros_like(gamma)
    if later:
        beta = gamma / old_gamma_ref[...]
        image += jnp.concatenate([beta] * (rows // LANES), axis=1) * old_ref[...]
    image_ref[...] = image
    gamma_ref[...] = gamma
    beta_ref[...] = beta
    norm = lane_total(image * image)
    norm_ref[...] = norm
    if not last:
        packed_ref, w_ref = more_refs
        packed_ref[...] = pack_norm(norm)
        split(image, w_ref)


def near_kernel(mine_ref, norm_ref, *refs):
    *got_refs, out_ref = refs
    width = mine_ref.shape[1]
    total = tree([mine_ref[...]] + [ref[:, :width].astype(F32) for ref in got_refs])
    norm = tree([norm_ref[...]] + [unpack_norm(ref[:, width:]) for ref in got_refs])
    out_ref[:, :width] = total.astype(BF16)
    out_ref[:, width:] = pack_norm(norm)


def far_kernel(*refs):
    *got_refs, out_ref = refs
    width = out_ref.shape[1] - LANES
    out_ref[:, :width] = tree([ref[:, :width].astype(F32) for ref in got_refs]).astype(BF16)
    out_ref[:, width:] = pack_norm(tree([unpack_norm(ref[:, width:]) for ref in got_refs]))


def gradient_kernel(later, *refs):
    *ins, gradient_ref, rounded_ref, alpha_ref = refs
    if later:
        old_ref, gamma_ref, *ins = ins
    width = gradient_ref.shape[1]
    total = tree([ref[:, :width].astype(F32) for ref in ins])
    if later:
        alpha = gamma_ref[...] / tree([unpack_norm(ref[:, width:]) for ref in ins])
        alpha_ref[...] = alpha
        total = old_ref[...] - jnp.concatenate([alpha] * (width // LANES), axis=1) * total
    else:
        alpha_ref[...] = jnp.zeros(alpha_ref.shape, F32)
    gradient_ref[...] = total
    rounded_ref[...] = total.astype(BF16)


def directions_kernel(near, width, start_ref, *refs):
    *ins, direction_ref, solution_ref = refs
    alphas = ins[: ITERS - 1]
    betas = ins[ITERS - 1 : 2 * ITERS - 1]
    pieces = ins[2 * ITERS - 1 :]
    for d in range(near):
        base = place(near, d) * width
        for k in range(width // LANES):
            at = pl.ds(pl.multiple_of(base + k * LANES, LANES), LANES)
            here = slice(k * LANES, (k + 1) * LANES)
            solution = start_ref[:, at]
            direction = pieces[d][:, here].astype(F32)
            for index in range(1, ITERS):
                solution += alphas[index - 1][...] * direction
                direction = pieces[index * near + d][:, here].astype(F32) + betas[index][...] * direction
            direction_ref[:, at] = direction
            solution_ref[:, at] = solution


def last_kernel(parts, gamma_ref, direction_ref, base_ref, residual_ref, *refs):
    *ins, out_ref, out_residual_ref = refs
    norms = ins[:parts]
    alphas = ins[parts : parts + ITERS - 1]
    images = ins[parts + ITERS - 1 :]
    alpha = gamma_ref[...] / tree([ref[...] for ref in norms])

    def step(k, _):
        at = pl.ds(pl.multiple_of(k * LANES, LANES), LANES)
        out_ref[:, at] = base_ref[:, at] + alpha * direction_ref[:, at]
        return 0

    lax.fori_loop(0, out_ref.shape[1] // LANES, step, 0, unroll=8)
    residual = residual_ref[...]
    rows = residual.shape[1]
    for index in range(ITERS):
        factor = alpha if index == ITERS - 1 else alphas[index][...]
        residual -= jnp.concatenate([factor] * (rows // LANES), axis=1) * images[index][...]
    out_residual_ref[...] = residual


def exchange(value, axis, size, distance):
    return lax.ppermute(value, axis, [(i, i ^ distance) for i in range(size)])


def stages(size, stride=1):
    found = []
    while stride < size:
        members = 4 if size // stride % 4 == 0 else 2
        found.append((stride, members))
        stride *= members
    return found


def exchanged(value, axis, size, stride, members):
    return [value] + [exchange(value, axis, size, k * stride) for k in range(1, members)]


def parts_over(value, axis, size):
    parts = [value]
    for stride, members in stages(size):
        parts = exchanged(tree(parts), axis, size, stride, members)
    return parts


def shards(n_obs, n_par, operator, targets, start):
    rows, columns = operator.shape
    scen = start.shape[0]
    near = 4 if n_obs % 4 == 0 else n_obs
    width = columns // near
    lanes = shape(scen, LANES)
    image_shape = shape(scen, rows)
    term_shape = shape(2 * scen, rows, dtype=BF16)

    def gradient_parts(w, norm, packed):
        sent = {d: backward(near, d, op, w, packed) for d in reversed(range(1, near))}
        got = {d: exchange(sent[d], "obs", n_obs, d) for d in sent}
        mine = backward(near, 0, op, w)
        both = shape(scen, width + LANES, dtype=BF16)
        value = call(near_kernel, both, (mine, norm, *(got[d] for d in range(1, near))))
        parts = [value]
        for index, (stride, members) in enumerate(stages(n_obs, near)):
            if index:
                value = call(far_kernel, both, parts)
            parts = exchanged(value, "obs", n_obs, stride, members)
        return parts

    def image_parts(mine):
        got = {d: exchange(mine, "obs", n_obs, d) for d in reversed(range(1, near))}
        total = forward(near, 0, op, mine)
        for d in got:
            total = forward(near, d, op, got[d], total)
        return parts_over(total, "par", n_par), [mine] + [got[d] for d in range(1, near)]

    op, first = load(operator, start)
    packed_lanes = shape(scen, LANES, dtype=BF16)
    residual, w, norm, packed = call(
        first_kernel, (image_shape, term_shape, lanes, packed_lanes), (targets, *parts_over(first, "par", n_par))
    )
    images, alphas, betas, pieces = [], [], [], []
    gradient = gamma = None
    for index in range(ITERS):
        parts = gradient_parts(w, norm, packed)
        gradient, rounded, alpha = call(
            functools.partial(gradient_kernel, index > 0),
            (shape(scen, width), shape(scen, width, dtype=BF16), lanes),
            ((gradient, gamma) if index else ()) + tuple(parts),
        )
        alphas += [alpha] if index else []
        parts, got = image_parts(rounded)
        pieces += got
        last = index == ITERS - 1
        image, gamma, beta, norm, *more = call(
            functools.partial(image_kernel, index > 0, last),
            (image_shape, lanes, lanes, lanes) + (() if last else (packed_lanes, term_shape)),
            ((image, gamma) if index else ()) + tuple(parts),
        )
        if not last:
            packed, w = more
        images.append(image)
        betas.append(beta)

    norms = parts_over(norm, "obs", n_obs)
    direction, base = call(
        functools.partial(directions_kernel, near, width),
        (shape(scen, columns), shape(scen, columns)),
        (start, *alphas, *betas, *pieces),
        flops=1 << 22,
        bytes_accessed=6 << 20,
    )
    return call(
        functools.partial(last_kernel, len(norms)),
        (shape(scen, columns), image_shape),
        (gamma, direction, base, residual, *norms, *alphas, *images),
    )


def solution(mesh):
    return jax.shard_map(
        functools.partial(shards, mesh.shape["obs"], mesh.shape["par"]),
        mesh=mesh,
        in_specs=(P("obs", "par"), P(None, "obs"), P(None, "par")),
        out_specs=(P(None, "par"), P(None, "obs")),
        check_vma=False,
    )
```

time: 678 us -> 173 us (0.26)
  waiting for transfers between devices: 378 us -> 71.5 us
  blocking collectives: 166 us -> 0 us
  matrix products: 97.7 us -> 0 us
  starting transfers between devices: 0.08 us -> 55.2 us
  Pallas kernels: 0 us -> 44 us
  other arithmetic: 15.2 us -> 0.01 us
  between operations: 13.7 us -> 0.75 us
    psum x5 -> x0, waiting for transfers between devices: 378 us -> none  [gradient_of(): gradient = lax.psum(partial_terms, 'obs')]
    psum x14 -> x0, blocking collectives: 166 us -> none  [the longest x4 80.1 us: image_norm(): return lax.psum(local_sum, 'obs')]
    dot_general x10 -> x0, matrix products: 97.7 us -> none  [the longest x5 52.5 us: forward_local(): lax.dot_general(direc_bf, operator, (((1,), (1,)), ((), ())), preferred_e...]
    ppermute x0 -> x47, waiting for transfers between devices: none -> 71.5 us  [exchange(): return lax.ppermute(value, axis, [(i, i ^ distance) for i in range(size)])]
    ppermute x0 -> x47, starting transfers between devices: none -> 55.2 us  [exchange(): return lax.ppermute(value, axis, [(i, i ^ distance) for i in range(size)])]
    pallas_call x0 -> x48, Pallas kernels: none -> 44 us  [call(): pl.pallas_call(body, out_shape=out, in_specs=specs if specs is not None e...]
    reduce_sum x9 -> x0, other arithmetic: 7.81 us -> none  [the longest x5 7.34 us: gradient_of(): gamma = lax.psum(jnp.sum(gradient * gradient, axis=1, keepdims=True), 'par')]
    add x4 -> x1, other arithmetic: 7.02 us -> 0.01 us  [tree(): return parts[0] + parts[1] + (parts[2] + parts[3])]
  transfers between devices with their start and end apart: 5 -> 47, of which waited for: 5 -> 34; matrix products, arithmetic and copies ran while one was open for 0% -> 0% of each run, Pallas kernels for 0% -> 11%
where the time goes in v2:
time: 173 us
  waiting for transfers between devices  71.5 us (41%)
  starting transfers between devices  55.2 us (32%)
  Pallas kernels  44 us (25%)
    ppermute x47, waiting for transfers between devices, exchange(): return lax.ppermute(value, axis, [(i, i ^ distance) for i in range(size)])  71.5 us
    ppermute x47, starting transfers between devices, exchange(): return lax.ppermute(value, axis, [(i, i ^ distance) for i in range(size)])  55.2 us
    pallas_call x48, Pallas kernels, call(): pl.pallas_call(body, out_shape=out, in_specs=specs if specs is not None e...  44 us
  transfers between devices with their start and end apart: 47, of which 34 were waited for; matrix products, arithmetic and copies ran while one was open for 0% of the time, Pallas kernels for 11%

profile of v2, /device:TPU:0, one launch (start us, length us, event | category | flops | bytes accessed | tf_op | source)
XLA Modules:
  0.0 172.6 jit_solution(10025040624598817721)
XLA Ops:
  0.6 1.2 copy-done
  1.9 6.8 %shard_map.50 = (bf16[512,16384]{1,0:T(8,128)(2,1)S(1)}, f32[16,512]{1,0:T(8,128)S(1)}) custom-call(bf16[512,16384]{1,0:T(8,128)(2,1)} %op_hbm.1, f32[16,16384]{1,0:T(8,128)S(1)} %copy-done), custom_call_target="tpu_custom_call" | custom-call | flops 4294967296 | bytes 16777216 | tf_op jit(solution)/shard_map/pallas_call | solution.py:23
  8.7 2.5 %collective-permute-start.2 = (f32[16,512]{1,0:T(8,128)S(1)}, f32[16,512]{1,0:T(8,128)S(1)}, u32[]{:S(2)}, u32[]{:S(2)}) collective-permute-start(f32[16,512]{1,0:T(8,128)S(1)} %get-tuple-element.43.refs_0_), channel_id=1, source_target_pairs={{0,3},{1,2},{2,1},{3,0},{4,7},{5,6},{6,5},{7,4},{8,11},{9,10},{10,... | collective-permute-start | bytes 98312 | tf_op jit(solution)/shard_map/ppermute | solution.py:270
  13.0 2.2 %collective-permute-done.1.refs_2_ = f32[16,512]{1,0:T(8,128)S(1)} collective-permute-done((f32[16,512]{1,0:T(8,128)S(1)}, f32[16,512]{1,0:T(8,128)S(1)}, u32[]{:S(2)}, u32[]{:S(2)}) %collective-permute-start.1) | collective-permute-done | bytes 32800 | tf_op jit(solution)/shard_map/ppermute | solution.py:270
  17.6 1.5 collective-permute-start.3
  19.1 1.6 collective-permute-start.4
  22.9 2.7 %collective-permute-done.4.refs_1_ = bf16[16,4224]{1,0:T(8,128)(2,1)S(1)} collective-permute-done((bf16[16,4224]{1,0:T(8,128)(2,1)S(1)}, bf16[16,4224]{1,0:T(8,128)(2,1)S(1)}, u32[]{:S(2)}, u32[]{:S(2)}) %collective-permute-start.4) | collective-permute-done | bytes 135200 | tf_op jit(solution)/shard_map/ppermute | solution.py:270
  25.6 1.4 collective-permute-done.5.refs_2_
  27.2 2.6 %collective-permute-start.6 = (bf16[16,4224]{1,0:T(8,128)(2,1)S(1)}, bf16[16,4224]{1,0:T(8,128)(2,1)S(1)}, u32[]{:S(2)}, u32[]{:S(2)}) collective-permute-start(bf16[16,4224]{1,0:T(8,128)(2,1)S(1)} %shard_map.56.refs_0_), channel_id=1, source_target_pairs={{0,16},{4,20},{8,24},{12,28},{16,0},{20,4},{24,8},{28,12},{1,17},{... | collective-permute-start | bytes 405512 | tf_op jit(solution)/shard_map/ppermute | solution.py:270
  29.8 5.7 %collective-permute-done.6.refs_1_ = bf16[16,4224]{1,0:T(8,128)(2,1)S(1)} collective-permute-done((bf16[16,4224]{1,0:T(8,128)(2,1)S(1)}, bf16[16,4224]{1,0:T(8,128)(2,1)S(1)}, u32[]{:S(2)}, u32[]{:S(2)}) %collective-permute-start.6) | collective-permute-done | bytes 135200 | tf_op jit(solution)/shard_map/ppermute | solution.py:270
  37.0 1.4 collective-permute-start.8
  38.4 1.2 shard_map.58.refs_0_
  39.5 1.2 collective-permute-start.7
  40.8 2.7 %collective-permute-done.9.v_ref.refs_10_ = bf16[16,4096]{1,0:T(8,128)(2,1)S(1)} collective-permute-done((bf16[16,4096]{1,0:T(8,128)(2,1)S(1)}, bf16[16,4096]{1,0:T(8,128)(2,1)S(1)}, u32[]{:S(2)}, u32[]{:S(2)}) %collective-permute-start.9) | collective-permute-done | bytes 131104 | tf_op jit(solution)/shard_map/ppermute | solution.py:270
  43.4 1.2 shard_map.59.refs_0_
  44.6 1.2 shard_map.60.refs_0_
  45.8 1.2 shard_map.61.refs_0_
  47.0 1.4 collective-permute-start.11
  48.9 2.0 %collective-permute-done.12.refs_3_ = f32[16,640]{1,0:T(8,128)S(1)} collective-permute-done((f32[16,640]{1,0:T(8,128)S(1)}, f32[16,640]{1,0:T(8,128)S(1)}, u32[]{:S(2)}, u32[]{:S(2)}) %collective-permute-start.12) | collective-permute-done | bytes 40992 | tf_op jit(solution)/shard_map/ppermute | solution.py:270
  55.2 2.2 %collective-permute-start.15 = (bf16[16,4224]{1,0:T(8,128)(2,1)S(1)}, bf16[16,4224]{1,0:T(8,128)(2,1)S(1)}, u32[]{:S(2)}, u32[]{:S(2)}) collective-permute-start(bf16[16,4224]{1,0:T(8,128)(2,1)S(1)} %shard_map.66), channel_id=1, source_target_pairs={{0,12},{4,8},{8,4},{12,0},{16,28},{20,24},{24,20},{28,16},{1,13},{... | collective-permute-start | bytes 405512 | tf_op jit(solution)/shard_map/ppermute | solution.py:270
  58.1 1.3 collective-permute-done.13.refs_0_
  59.5 1.6 collective-permute-done.14.refs_1_
  61.1 2.4 %collective-permute-done.15.refs_2_ = bf16[16,4224]{1,0:T(8,128)(2,1)S(1)} collective-permute-done((bf16[16,4224]{1,0:T(8,128)(2,1)S(1)}, bf16[16,4224]{1,0:T(8,128)(2,1)S(1)}, u32[]{:S(2)}, u32[]{:S(2)}) %collective-permute-start.15) | collective-permute-done | bytes 135200 | tf_op jit(solution)/shard_map/ppermute | solution.py:270
  63.7 2.2 %collective-permute-start.16 = (bf16[16,4224]{1,0:T(8,128)(2,1)S(1)}, bf16[16,4224]{1,0:T(8,128)(2,1)S(1)}, u32[]{:S(2)}, u32[]{:S(2)}) collective-permute-start(bf16[16,4224]{1,0:T(8,128)(2,1)S(1)} %shard_map.67.refs_2_), channel_id=1, source_target_pairs={{0,16},{4,20},{8,24},{12,28},{16,0},{20,4},{24,8},{28,12},{1,17},{... | collective-permute-start | bytes 405512 | tf_op jit(solution)/shard_map/ppermute | solution.py:270
  66.0 6.4 %collective-permute-done.16.refs_3_ = bf16[16,4224]{1,0:T(8,128)(2,1)S(1)} collective-permute-done((bf16[16,4224]{1,0:T(8,128)(2,1)S(1)}, bf16[16,4224]{1,0:T(8,128)(2,1)S(1)}, u32[]{:S(2)}, u32[]{:S(2)}) %collective-permute-start.16) | collective-permute-done | bytes 135200 | tf_op jit(solution)/shard_map/ppermute | solution.py:270
  72.5 1.3 collective-permute-start.19
  73.9 1.3 collective-permute-start.18
  75.2 1.4 shard_map.69.refs_0_
  77.4 2.0 %collective-permute-done.19.v_ref.refs_14_ = bf16[16,4096]{1,0:T(8,128)(2,1)S(1)} collective-permute-done((bf16[16,4096]{1,0:T(8,128)(2,1)S(1)}, bf16[16,4096]{1,0:T(8,128)(2,1)S(1)}, u32[]{:S(2)}, u32[]{:S(2)}) %collective-permute-start.19) | collective-permute-done | bytes 131104 | tf_op jit(solution)/shard_map/ppermute | solution.py:270
  79.5 1.2 shard_map.70.refs_0_
  80.7 1.2 shard_map.71.refs_0_
  81.9 1.2 shard_map.72.refs_2_
  85.0 1.6 collective-permute-done.22.refs_5_
  92.2 1.4 collective-permute-start.25
  94.4 1.3 collective-permute-done.23.refs_0_
  95.7 1.9 %collective-permute-done.24.refs_1_ = bf16[16,4224]{1,0:T(8,128)(2,1)S(1)} collective-permute-done((bf16[16,4224]{1,0:T(8,128)(2,1)S(1)}, bf16[16,4224]{1,0:T(8,128)(2,1)S(1)}, u32[]{:S(2)}, u32[]{:S(2)}) %collective-permute-start.24) | collective-permute-done | bytes 135200 | tf_op jit(solution)/shard_map/ppermute | solution.py:270
  97.7 2.1 %collective-permute-done.25.refs_2_ = bf16[16,4224]{1,0:T(8,128)(2,1)S(1)} collective-permute-done((bf16[16,4224]{1,0:T(8,128)(2,1)S(1)}, bf16[16,4224]{1,0:T(8,128)(2,1)S(1)}, u32[]{:S(2)}, u32[]{:S(2)}) %collective-permute-start.25) | collective-permute-done | bytes 135200 | tf_op jit(solution)/shard_map/ppermute | solution.py:270
  100.0 2.7 %collective-permute-start.26 = (bf16[16,4224]{1,0:T(8,128)(2,1)S(1)}, bf16[16,4224]{1,0:T(8,128)(2,1)S(1)}, u32[]{:S(2)}, u32[]{:S(2)}) collective-permute-start(bf16[16,4224]{1,0:T(8,128)(2,1)S(1)} %shard_map.78.refs_2_), channel_id=1, source_target_pairs={{0,16},{4,20},{8,24},{12,28},{16,0},{20,4},{24,8},{28,12},{1,17},{... | collective-permute-start | bytes 405512 | tf_op jit(solution)/shard_map/ppermute | solution.py:270
  102.7 5.8 %collective-permute-done.26.refs_3_ = bf16[16,4224]{1,0:T(8,128)(2,1)S(1)} collective-permute-done((bf16[16,4224]{1,0:T(8,128)(2,1)S(1)}, bf16[16,4224]{1,0:T(8,128)(2,1)S(1)}, u32[]{:S(2)}, u32[]{:S(2)}) %collective-permute-start.26) | collective-permute-done | bytes 135200 | tf_op jit(solution)/shard_map/ppermute | solution.py:270
  109.7 1.5 collective-permute-start.28
  113.4 2.2 %collective-permute-done.29.v_ref.refs_18_ = bf16[16,4096]{1,0:T(8,128)(2,1)S(1)} collective-permute-done((bf16[16,4096]{1,0:T(8,128)(2,1)S(1)}, bf16[16,4096]{1,0:T(8,128)(2,1)S(1)}, u32[]{:S(2)}, u32[]{:S(2)}) %collective-permute-start.29) | collective-permute-done | bytes 131104 | tf_op jit(solution)/shard_map/ppermute | solution.py:270
  115.6 1.2 shard_map.81.refs_0_
  116.8 1.2 shard_map.82.refs_0_
  118.0 1.2 shard_map.83.refs_2_
  119.7 1.4 collective-permute-start.30
  121.1 1.6 collective-permute-done.32.refs_5_
  128.2 1.4 collective-permute-start.35
  130.4 1.3 collective-permute-done.33.refs_0_
  131.7 2.1 %collective-permute-done.34.refs_1_ = bf16[16,4224]{1,0:T(8,128)(2,1)S(1)} collective-permute-done((bf16[16,4224]{1,0:T(8,128)(2,1)S(1)}, bf16[16,4224]{1,0:T(8,128)(2,1)S(1)}, u32[]{:S(2)}, u32[]{:S(2)}) %collective-permute-start.34) | collective-permute-done | bytes 135200 | tf_op jit(solution)/shard_map/ppermute | solution.py:270
  133.8 1.9 %collective-permute-done.35.refs_2_ = bf16[16,4224]{1,0:T(8,128)(2,1)S(1)} collective-permute-done((bf16[16,4224]{1,0:T(8,128)(2,1)S(1)}, bf16[16,4224]{1,0:T(8,128)(2,1)S(1)}, u32[]{:S(2)}, u32[]{:S(2)}) %collective-permute-start.35) | collective-permute-done | bytes 135200 | tf_op jit(solution)/shard_map/ppermute | solution.py:270
  135.8 2.8 %collective-permute-start.36 = (bf16[16,4224]{1,0:T(8,128)(2,1)S(1)}, bf16[16,4224]{1,0:T(8,128)(2,1)S(1)}, u32[]{:S(2)}, u32[]{:S(2)}) collective-permute-start(bf16[16,4224]{1,0:T(8,128)(2,1)S(1)} %shard_map.89.refs_2_), channel_id=1, source_target_pairs={{0,16},{4,20},{8,24},{12,28},{16,0},{20,4},{24,8},{28,12},{1,17},{... | collective-permute-start | bytes 405512 | tf_op jit(solution)/shard_map/ppermute | solution.py:270
  138.6 5.9 %collective-permute-done.36.refs_3_ = bf16[16,4224]{1,0:T(8,128)(2,1)S(1)} collective-permute-done((bf16[16,4224]{1,0:T(8,128)(2,1)S(1)}, bf16[16,4224]{1,0:T(8,128)(2,1)S(1)}, u32[]{:S(2)}, u32[]{:S(2)}) %collective-permute-start.36) | collective-permute-done | bytes 135200 | tf_op jit(solution)/shard_map/ppermute | solution.py:270
  145.4 1.3 collective-permute-start.39
  146.6 1.3 collective-permute-start.38
  148.0 1.4 shard_map.91.refs_0_
  150.3 2.2 %collective-permute-done.39.v_ref.refs_22_ = bf16[16,4096]{1,0:T(8,128)(2,1)S(1)} collective-permute-done((bf16[16,4096]{1,0:T(8,128)(2,1)S(1)}, bf16[16,4096]{1,0:T(8,128)(2,1)S(1)}, u32[]{:S(2)}, u32[]{:S(2)}) %collective-permute-start.39) | collective-permute-done | bytes 131104 | tf_op jit(solution)/shard_map/ppermute | solution.py:270
  152.4 1.2 shard_map.92.refs_0_
  153.6 1.2 shard_map.93.refs_0_
  154.8 1.2 shard_map.94.refs_2_
  157.9 1.6 collective-permute-done.42.refs_5_
  160.5 1.5 collective-permute-start.45
  166.7 2.5 %collective-permute-start.46 = (f32[16,128]{1,0:T(8,128)S(1)}, f32[16,128]{1,0:T(8,128)S(1)}, u32[]{:S(2)}, u32[]{:S(2)}) collective-permute-start(f32[16,128]{1,0:T(8,128)S(1)} %add_add_fusion.refs_0_), channel_id=1, source_target_pairs={{0,16},{4,20},{8,24},{12,28},{16,0},{20,4},{24,8},{28,12},{1,17},{... | collective-permute-start | bytes 24584 | tf_op jit(solution)/shard_map/ppermute | solution.py:270
  169.8 1.5 collective-permute-done.46.refs_1_
  171.3 1.4 shard_map.97
  (85 shorter events, 43.8 us)
Async XLA Ops:
  0.6 1.2 copy-start
  1.9 13.3 %copy-start.2 = (f32[16,512]{1,0:T(8,128)S(1)}, f32[16,512]{1,0:T(8,128)}, u32[]{:S(2)}) copy-start(f32[16,512]{1,0:T(8,128)} %targets_ref.1) | copy-start | bytes 98308
  8.7 4.3 %collective-permute-start.2 = (f32[16,512]{1,0:T(8,128)S(1)}, f32[16,512]{1,0:T(8,128)S(1)}, u32[]{:S(2)}, u32[]{:S(2)}) collective-permute-start(f32[16,512]{1,0:T(8,128)S(1)} %get-tuple-element.43.refs_0_), channel_id=1, source_target_pairs={{0,3},{1,2},{2,1},{3,0},{4,7},{5,6},{6,5},{7,4},{8,11},{9,10},{10,... | collective-permute-start | bytes 98312 | tf_op jit(solution)/shard_map/ppermute | solution.py:270
  11.2 4.0 %collective-permute-start.1 = (f32[16,512]{1,0:T(8,128)S(1)}, f32[16,512]{1,0:T(8,128)S(1)}, u32[]{:S(2)}, u32[]{:S(2)}) collective-permute-start(f32[16,512]{1,0:T(8,128)S(1)} %get-tuple-element.43.refs_0_), channel_id=1, source_target_pairs={{0,2},{1,3},{2,0},{3,1},{4,6},{5,7},{6,4},{7,5},{8,10},{9,11},{10,... | collective-permute-start | bytes 98312 | tf_op jit(solution)/shard_map/ppermute | solution.py:270
  11.8 3.3 %collective-permute-start = (f32[16,512]{1,0:T(8,128)S(1)}, f32[16,512]{1,0:T(8,128)S(1)}, u32[]{:S(2)}, u32[]{:S(2)}) collective-permute-start(f32[16,512]{1,0:T(8,128)S(1)} %get-tuple-element.43.refs_0_), channel_id=1, source_target_pairs={{0,1},{1,0},{2,3},{3,2},{4,5},{5,4},{6,7},{7,6},{8,9},{9,8},{10,11... | collective-permute-start | bytes 98312 | tf_op jit(solution)/shard_map/ppermute | solution.py:270
  17.6 5.3 %collective-permute-start.3 = (bf16[16,4224]{1,0:T(8,128)(2,1)S(1)}, bf16[16,4224]{1,0:T(8,128)(2,1)S(1)}, u32[]{:S(2)}, u32[]{:S(2)}) collective-permute-start(bf16[16,4224]{1,0:T(8,128)(2,1)S(1)} %shard_map.53), channel_id=1, source_target_pairs={{0,4},{4,0},{8,12},{12,8},{16,20},{20,16},{24,28},{28,24},{1,5},{5... | collective-permute-start | bytes 405512 | tf_op jit(solution)/shard_map/ppermute | solution.py:270
  19.1 6.5 %collective-permute-start.4 = (bf16[16,4224]{1,0:T(8,128)(2,1)S(1)}, bf16[16,4224]{1,0:T(8,128)(2,1)S(1)}, u32[]{:S(2)}, u32[]{:S(2)}) collective-permute-start(bf16[16,4224]{1,0:T(8,128)(2,1)S(1)} %shard_map.54), channel_id=1, source_target_pairs={{0,8},{4,12},{8,0},{12,4},{16,24},{20,28},{24,16},{28,20},{1,9},{5... | collective-permute-start | bytes 405512 | tf_op jit(solution)/shard_map/ppermute | solution.py:270
  20.7 6.3 %collective-permute-start.5 = (bf16[16,4224]{1,0:T(8,128)(2,1)S(1)}, bf16[16,4224]{1,0:T(8,128)(2,1)S(1)}, u32[]{:S(2)}, u32[]{:S(2)}) collective-permute-start(bf16[16,4224]{1,0:T(8,128)(2,1)S(1)} %shard_map.55), channel_id=1, source_target_pairs={{0,12},{4,8},{8,4},{12,0},{16,28},{20,24},{24,20},{28,16},{1,13},{... | collective-permute-start | bytes 405512 | tf_op jit(solution)/shard_map/ppermute | solution.py:270
  27.2 8.3 %collective-permute-start.6 = (bf16[16,4224]{1,0:T(8,128)(2,1)S(1)}, bf16[16,4224]{1,0:T(8,128)(2,1)S(1)}, u32[]{:S(2)}, u32[]{:S(2)}) collective-permute-start(bf16[16,4224]{1,0:T(8,128)(2,1)S(1)} %shard_map.56.refs_0_), channel_id=1, source_target_pairs={{0,16},{4,20},{8,24},{12,28},{16,0},{20,4},{24,8},{28,12},{1,17},{... | collective-permute-start | bytes 405512 | tf_op jit(solution)/shard_map/ppermute | solution.py:270
  36.1 7.3 %collective-permute-start.9 = (bf16[16,4096]{1,0:T(8,128)(2,1)S(1)}, bf16[16,4096]{1,0:T(8,128)(2,1)S(1)}, u32[]{:S(2)}, u32[]{:S(2)}) collective-permute-start(bf16[16,4096]{1,0:T(8,128)(2,1)S(1)} %get-tuple-element.47.v_ref.refs_7_), channel_id=1, source_target_pairs={{0,12},{4,8},{8,4},{12,0},{16,28},{20,24},{24,20},{28,16},{1,13},{... | collective-permute-start | bytes 393224 | tf_op jit(solution)/shard_map/ppermute | solution.py:270
  37.0 7.6 %collective-permute-start.8 = (bf16[16,4096]{1,0:T(8,128)(2,1)S(1)}, bf16[16,4096]{1,0:T(8,128)(2,1)S(1)}, u32[]{:S(2)}, u32[]{:S(2)}) collective-permute-start(bf16[16,4096]{1,0:T(8,128)(2,1)S(1)} %get-tuple-element.47.v_ref.refs_7_), channel_id=1, source_target_pairs={{0,8},{4,12},{8,0},{12,4},{16,24},{20,28},{24,16},{28,20},{1,9},{5... | collective-permute-start | bytes 393224 | tf_op jit(solution)/shard_map/ppermute | solution.py:270
  39.5 6.3 %collective-permute-start.7 = (bf16[16,4096]{1,0:T(8,128)(2,1)S(1)}, bf16[16,4096]{1,0:T(8,128)(2,1)S(1)}, u32[]{:S(2)}, u32[]{:S(2)}) collective-permute-start(bf16[16,4096]{1,0:T(8,128)(2,1)S(1)} %get-tuple-element.47.v_ref.refs_7_), channel_id=1, source_target_pairs={{0,4},{4,0},{8,12},{12,8},{16,20},{20,16},{24,28},{28,24},{1,5},{5... | collective-permute-start | bytes 393224 | tf_op jit(solution)/shard_map/ppermute | solution.py:270
  47.0 3.8 %collective-permute-start.12 = (f32[16,640]{1,0:T(8,128)S(1)}, f32[16,640]{1,0:T(8,128)S(1)}, u32[]{:S(2)}, u32[]{:S(2)}) collective-permute-start(f32[16,640]{1,0:T(8,128)S(1)} %shard_map.61.refs_0_), channel_id=1, source_target_pairs={{0,3},{1,2},{2,1},{3,0},{4,7},{5,6},{6,5},{7,4},{8,11},{9,10},{10,... | collective-permute-start | bytes 122888 | tf_op jit(solution)/shard_map/ppermute | solution.py:270
  47.0 4.3 %collective-permute-start.11 = (f32[16,640]{1,0:T(8,128)S(1)}, f32[16,640]{1,0:T(8,128)S(1)}, u32[]{:S(2)}, u32[]{:S(2)}) collective-permute-start(f32[16,640]{1,0:T(8,128)S(1)} %shard_map.61.refs_0_), channel_id=1, source_target_pairs={{0,2},{1,3},{2,0},{3,1},{4,6},{5,7},{6,4},{7,5},{8,10},{9,11},{10,... | collective-permute-start | bytes 122888 | tf_op jit(solution)/shard_map/ppermute | solution.py:270
  48.4 3.0 %collective-permute-start.10 = (f32[16,640]{1,0:T(8,128)S(1)}, f32[16,640]{1,0:T(8,128)S(1)}, u32[]{:S(2)}, u32[]{:S(2)}) collective-permute-start(f32[16,640]{1,0:T(8,128)S(1)} %shard_map.61.refs_0_), channel_id=1, source_target_pairs={{0,1},{1,0},{2,3},{3,2},{4,5},{5,4},{6,7},{7,6},{8,9},{9,8},{10,11... | collective-permute-start | bytes 122888 | tf_op jit(solution)/shard_map/ppermute | solution.py:270
  53.9 5.6 %collective-permute-start.13 = (bf16[16,4224]{1,0:T(8,128)(2,1)S(1)}, bf16[16,4224]{1,0:T(8,128)(2,1)S(1)}, u32[]{:S(2)}, u32[]{:S(2)}) collective-permute-start(bf16[16,4224]{1,0:T(8,128)(2,1)S(1)} %shard_map.64), channel_id=1, source_target_pairs={{0,4},{4,0},{8,12},{12,8},{16,20},{20,16},{24,28},{28,24},{1,5},{5... | collective-permute-start | bytes 405512 | tf_op jit(solution)/shard_map/ppermute | solution.py:270
  54.6 6.5 %collective-permute-start.14 = (bf16[16,4224]{1,0:T(8,128)(2,1)S(1)}, bf16[16,4224]{1,0:T(8,128)(2,1)S(1)}, u32[]{:S(2)}, u32[]{:S(2)}) collective-permute-start(bf16[16,4224]{1,0:T(8,128)(2,1)S(1)} %shard_map.65), channel_id=1, source_target_pairs={{0,8},{4,12},{8,0},{12,4},{16,24},{20,28},{24,16},{28,20},{1,9},{5... | collective-permute-start | bytes 405512 | tf_op jit(solution)/shard_map/ppermute | solution.py:270
  55.2 8.4 %collective-permute-start.15 = (bf16[16,4224]{1,0:T(8,128)(2,1)S(1)}, bf16[16,4224]{1,0:T(8,128)(2,1)S(1)}, u32[]{:S(2)}, u32[]{:S(2)}) collective-permute-start(bf16[16,4224]{1,0:T(8,128)(2,1)S(1)} %shard_map.66), channel_id=1, source_target_pairs={{0,12},{4,8},{8,4},{12,0},{16,28},{20,24},{24,20},{28,16},{1,13},{... | collective-permute-start | bytes 405512 | tf_op jit(solution)/shard_map/ppermute | solution.py:270
  63.7 8.7 %collective-permute-start.16 = (bf16[16,4224]{1,0:T(8,128)(2,1)S(1)}, bf16[16,4224]{1,0:T(8,128)(2,1)S(1)}, u32[]{:S(2)}, u32[]{:S(2)}) collective-permute-start(bf16[16,4224]{1,0:T(8,128)(2,1)S(1)} %shard_map.67.refs_2_), channel_id=1, source_target_pairs={{0,16},{4,20},{8,24},{12,28},{16,0},{20,4},{24,8},{28,12},{1,17},{... | collective-permute-start | bytes 405512 | tf_op jit(solution)/shard_map/ppermute | solution.py:270
  72.5 7.0 %collective-permute-start.19 = (bf16[16,4096]{1,0:T(8,128)(2,1)S(1)}, bf16[16,4096]{1,0:T(8,128)(2,1)S(1)}, u32[]{:S(2)}, u32[]{:S(2)}) collective-permute-start(bf16[16,4096]{1,0:T(8,128)(2,1)S(1)} %get-tuple-element.54.v_ref.refs_11_), channel_id=1, source_target_pairs={{0,12},{4,8},{8,4},{12,0},{16,28},{20,24},{24,20},{28,16},{1,13},{... | collective-permute-start | bytes 393224 | tf_op jit(solution)/shard_map/ppermute | solution.py:270
  73.9 6.8 %collective-permute-start.18 = (bf16[16,4096]{1,0:T(8,128)(2,1)S(1)}, bf16[16,4096]{1,0:T(8,128)(2,1)S(1)}, u32[]{:S(2)}, u32[]{:S(2)}) collective-permute-start(bf16[16,4096]{1,0:T(8,128)(2,1)S(1)} %get-tuple-element.54.v_ref.refs_11_), channel_id=1, source_target_pairs={{0,8},{4,12},{8,0},{12,4},{16,24},{20,28},{24,16},{28,20},{1,9},{5... | collective-permute-start | bytes 393224 | tf_op jit(solution)/shard_map/ppermute | solution.py:270
  76.6 5.3 %collective-permute-start.17 = (bf16[16,4096]{1,0:T(8,128)(2,1)S(1)}, bf16[16,4096]{1,0:T(8,128)(2,1)S(1)}, u32[]{:S(2)}, u32[]{:S(2)}) collective-permute-start(bf16[16,4096]{1,0:T(8,128)(2,1)S(1)} %get-tuple-element.54.v_ref.refs_11_), channel_id=1, source_target_pairs={{0,4},{4,0},{8,12},{12,8},{16,20},{20,16},{24,28},{28,24},{1,5},{5... | collective-permute-start | bytes 393224 | tf_op jit(solution)/shard_map/ppermute | solution.py:270
  83.1 3.4 %collective-permute-start.22 = (f32[16,640]{1,0:T(8,128)S(1)}, f32[16,640]{1,0:T(8,128)S(1)}, u32[]{:S(2)}, u32[]{:S(2)}) collective-permute-start(f32[16,640]{1,0:T(8,128)S(1)} %shard_map.72.refs_2_), channel_id=1, source_target_pairs={{0,3},{1,2},{2,1},{3,0},{4,7},{5,6},{6,5},{7,4},{8,11},{9,10},{10,... | collective-permute-start | bytes 122888 | tf_op jit(solution)/shard_map/ppermute | solution.py:270
  83.1 4.5 %collective-permute-start.21 = (f32[16,640]{1,0:T(8,128)S(1)}, f32[16,640]{1,0:T(8,128)S(1)}, u32[]{:S(2)}, u32[]{:S(2)}) collective-permute-start(f32[16,640]{1,0:T(8,128)S(1)} %shard_map.72.refs_2_), channel_id=1, source_target_pairs={{0,2},{1,3},{2,0},{3,1},{4,6},{5,7},{6,4},{7,5},{8,10},{9,11},{10,... | collective-permute-start | bytes 122888 | tf_op jit(solution)/shard_map/ppermute | solution.py:270
  84.1 3.4 %collective-permute-start.20 = (f32[16,640]{1,0:T(8,128)S(1)}, f32[16,640]{1,0:T(8,128)S(1)}, u32[]{:S(2)}, u32[]{:S(2)}) collective-permute-start(f32[16,640]{1,0:T(8,128)S(1)} %shard_map.72.refs_2_), channel_id=1, source_target_pairs={{0,1},{1,0},{2,3},{3,2},{4,5},{5,4},{6,7},{7,6},{8,9},{9,8},{10,11... | collective-permute-start | bytes 122888 | tf_op jit(solution)/shard_map/ppermute | solution.py:270
  90.1 5.6 %collective-permute-start.23 = (bf16[16,4224]{1,0:T(8,128)(2,1)S(1)}, bf16[16,4224]{1,0:T(8,128)(2,1)S(1)}, u32[]{:S(2)}, u32[]{:S(2)}) collective-permute-start(bf16[16,4224]{1,0:T(8,128)(2,1)S(1)} %shard_map.75), channel_id=1, source_target_pairs={{0,4},{4,0},{8,12},{12,8},{16,20},{20,16},{24,28},{28,24},{1,5},{5... | collective-permute-start | bytes 405512 | tf_op jit(solution)/shard_map/ppermute | solution.py:270
  91.2 6.5 %collective-permute-start.24 = (bf16[16,4224]{1,0:T(8,128)(2,1)S(1)}, bf16[16,4224]{1,0:T(8,128)(2,1)S(1)}, u32[]{:S(2)}, u32[]{:S(2)}) collective-permute-start(bf16[16,4224]{1,0:T(8,128)(2,1)S(1)} %shard_map.76), channel_id=1, source_target_pairs={{0,8},{4,12},{8,0},{12,4},{16,24},{20,28},{24,16},{28,20},{1,9},{5... | collective-permute-start | bytes 405512 | tf_op jit(solution)/shard_map/ppermute | solution.py:270
  92.2 7.6 %collective-permute-start.25 = (bf16[16,4224]{1,0:T(8,128)(2,1)S(1)}, bf16[16,4224]{1,0:T(8,128)(2,1)S(1)}, u32[]{:S(2)}, u32[]{:S(2)}) collective-permute-start(bf16[16,4224]{1,0:T(8,128)(2,1)S(1)} %shard_map.77), channel_id=1, source_target_pairs={{0,12},{4,8},{8,4},{12,0},{16,28},{20,24},{24,20},{28,16},{1,13},{... | collective-permute-start | bytes 405512 | tf_op jit(solution)/shard_map/ppermute | solution.py:270
  100.0 8.5 %collective-permute-start.26 = (bf16[16,4224]{1,0:T(8,128)(2,1)S(1)}, bf16[16,4224]{1,0:T(8,128)(2,1)S(1)}, u32[]{:S(2)}, u32[]{:S(2)}) collective-permute-start(bf16[16,4224]{1,0:T(8,128)(2,1)S(1)} %shard_map.78.refs_2_), channel_id=1, source_target_pairs={{0,16},{4,20},{8,24},{12,28},{16,0},{20,4},{24,8},{28,12},{1,17},{... | collective-permute-start | bytes 405512 | tf_op jit(solution)/shard_map/ppermute | solution.py:270
  108.6 7.0 %collective-permute-start.29 = (bf16[16,4096]{1,0:T(8,128)(2,1)S(1)}, bf16[16,4096]{1,0:T(8,128)(2,1)S(1)}, u32[]{:S(2)}, u32[]{:S(2)}) collective-permute-start(bf16[16,4096]{1,0:T(8,128)(2,1)S(1)} %get-tuple-element.61.v_ref.refs_15_), channel_id=1, source_target_pairs={{0,12},{4,8},{8,4},{12,0},{16,28},{20,24},{24,20},{28,16},{1,13},{... | collective-permute-start | bytes 393224 | tf_op jit(solution)/shard_map/ppermute | solution.py:270
  109.7 7.1 %collective-permute-start.28 = (bf16[16,4096]{1,0:T(8,128)(2,1)S(1)}, bf16[16,4096]{1,0:T(8,128)(2,1)S(1)}, u32[]{:S(2)}, u32[]{:S(2)}) collective-permute-start(bf16[16,4096]{1,0:T(8,128)(2,1)S(1)} %get-tuple-element.61.v_ref.refs_15_), channel_id=1, source_target_pairs={{0,8},{4,12},{8,0},{12,4},{16,24},{20,28},{24,16},{28,20},{1,9},{5... | collective-permute-start | bytes 393224 | tf_op jit(solution)/shard_map/ppermute | solution.py:270
  112.4 5.6 %collective-permute-start.27 = (bf16[16,4096]{1,0:T(8,128)(2,1)S(1)}, bf16[16,4096]{1,0:T(8,128)(2,1)S(1)}, u32[]{:S(2)}, u32[]{:S(2)}) collective-permute-start(bf16[16,4096]{1,0:T(8,128)(2,1)S(1)} %get-tuple-element.61.v_ref.refs_15_), channel_id=1, source_target_pairs={{0,4},{4,0},{8,12},{12,8},{16,20},{20,16},{24,28},{28,24},{1,5},{5... | collective-permute-start | bytes 393224 | tf_op jit(solution)/shard_map/ppermute | solution.py:270
  119.2 3.4 %collective-permute-start.32 = (f32[16,640]{1,0:T(8,128)S(1)}, f32[16,640]{1,0:T(8,128)S(1)}, u32[]{:S(2)}, u32[]{:S(2)}) collective-permute-start(f32[16,640]{1,0:T(8,128)S(1)} %shard_map.83.refs_2_), channel_id=1, source_target_pairs={{0,3},{1,2},{2,1},{3,0},{4,7},{5,6},{6,5},{7,4},{8,11},{9,10},{10,... | collective-permute-start | bytes 122888 | tf_op jit(solution)/shard_map/ppermute | solution.py:270
  119.2 4.3 %collective-permute-start.31 = (f32[16,640]{1,0:T(8,128)S(1)}, f32[16,640]{1,0:T(8,128)S(1)}, u32[]{:S(2)}, u32[]{:S(2)}) collective-permute-start(f32[16,640]{1,0:T(8,128)S(1)} %shard_map.83.refs_2_), channel_id=1, source_target_pairs={{0,2},{1,3},{2,0},{3,1},{4,6},{5,7},{6,4},{7,5},{8,10},{9,11},{10,... | collective-permute-start | bytes 122888 | tf_op jit(solution)/shard_map/ppermute | solution.py:270
  119.7 3.8 %collective-permute-start.30 = (f32[16,640]{1,0:T(8,128)S(1)}, f32[16,640]{1,0:T(8,128)S(1)}, u32[]{:S(2)}, u32[]{:S(2)}) collective-permute-start(f32[16,640]{1,0:T(8,128)S(1)} %shard_map.83.refs_2_), channel_id=1, source_target_pairs={{0,1},{1,0},{2,3},{3,2},{4,5},{5,4},{6,7},{7,6},{8,9},{9,8},{10,11... | collective-permute-start | bytes 122888 | tf_op jit(solution)/shard_map/ppermute | solution.py:270
  126.1 5.6 %collective-permute-start.33 = (bf16[16,4224]{1,0:T(8,128)(2,1)S(1)}, bf16[16,4224]{1,0:T(8,128)(2,1)S(1)}, u32[]{:S(2)}, u32[]{:S(2)}) collective-permute-start(bf16[16,4224]{1,0:T(8,128)(2,1)S(1)} %shard_map.86), channel_id=1, source_target_pairs={{0,4},{4,0},{8,12},{12,8},{16,20},{20,16},{24,28},{28,24},{1,5},{5... | collective-permute-start | bytes 405512 | tf_op jit(solution)/shard_map/ppermute | solution.py:270
  127.3 6.5 %collective-permute-start.34 = (bf16[16,4224]{1,0:T(8,128)(2,1)S(1)}, bf16[16,4224]{1,0:T(8,128)(2,1)S(1)}, u32[]{:S(2)}, u32[]{:S(2)}) collective-permute-start(bf16[16,4224]{1,0:T(8,128)(2,1)S(1)} %shard_map.87), channel_id=1, source_target_pairs={{0,8},{4,12},{8,0},{12,4},{16,24},{20,28},{24,16},{28,20},{1,9},{5... | collective-permute-start | bytes 405512 | tf_op jit(solution)/shard_map/ppermute | solution.py:270
  128.2 7.4 %collective-permute-start.35 = (bf16[16,4224]{1,0:T(8,128)(2,1)S(1)}, bf16[16,4224]{1,0:T(8,128)(2,1)S(1)}, u32[]{:S(2)}, u32[]{:S(2)}) collective-permute-start(bf16[16,4224]{1,0:T(8,128)(2,1)S(1)} %shard_map.88), channel_id=1, source_target_pairs={{0,12},{4,8},{8,4},{12,0},{16,28},{20,24},{24,20},{28,16},{1,13},{... | collective-permute-start | bytes 405512 | tf_op jit(solution)/shard_map/ppermute | solution.py:270
  135.8 8.7 %collective-permute-start.36 = (bf16[16,4224]{1,0:T(8,128)(2,1)S(1)}, bf16[16,4224]{1,0:T(8,128)(2,1)S(1)}, u32[]{:S(2)}, u32[]{:S(2)}) collective-permute-start(bf16[16,4224]{1,0:T(8,128)(2,1)S(1)} %shard_map.89.refs_2_), channel_id=1, source_target_pairs={{0,16},{4,20},{8,24},{12,28},{16,0},{20,4},{24,8},{28,12},{1,17},{... | collective-permute-start | bytes 405512 | tf_op jit(solution)/shard_map/ppermute | solution.py:270
  145.4 7.1 %collective-permute-start.39 = (bf16[16,4096]{1,0:T(8,128)(2,1)S(1)}, bf16[16,4096]{1,0:T(8,128)(2,1)S(1)}, u32[]{:S(2)}, u32[]{:S(2)}) collective-permute-start(bf16[16,4096]{1,0:T(8,128)(2,1)S(1)} %get-tuple-element.68.v_ref.refs_19_), channel_id=1, source_target_pairs={{0,12},{4,8},{8,4},{12,0},{16,28},{20,24},{24,20},{28,16},{1,13},{... | collective-permute-start | bytes 393224 | tf_op jit(solution)/shard_map/ppermute | solution.py:270
  146.6 7.0 %collective-permute-start.38 = (bf16[16,4096]{1,0:T(8,128)(2,1)S(1)}, bf16[16,4096]{1,0:T(8,128)(2,1)S(1)}, u32[]{:S(2)}, u32[]{:S(2)}) collective-permute-start(bf16[16,4096]{1,0:T(8,128)(2,1)S(1)} %get-tuple-element.68.v_ref.refs_19_), channel_id=1, source_target_pairs={{0,8},{4,12},{8,0},{12,4},{16,24},{20,28},{24,16},{28,20},{1,9},{5... | collective-permute-start | bytes 393224 | tf_op jit(solution)/shard_map/ppermute | solution.py:270
  149.4 5.5 %collective-permute-start.37 = (bf16[16,4096]{1,0:T(8,128)(2,1)S(1)}, bf16[16,4096]{1,0:T(8,128)(2,1)S(1)}, u32[]{:S(2)}, u32[]{:S(2)}) collective-permute-start(bf16[16,4096]{1,0:T(8,128)(2,1)S(1)} %get-tuple-element.68.v_ref.refs_19_), channel_id=1, source_target_pairs={{0,4},{4,0},{8,12},{12,8},{16,20},{20,16},{24,28},{28,24},{1,5},{5... | collective-permute-start | bytes 393224 | tf_op jit(solution)/shard_map/ppermute | solution.py:270
  153.6 15.6 %copy-start.1 = (f32[16,16384]{1,0:T(8,128)S(1)}, f32[16,16384]{1,0:T(8,128)}, u32[]{:S(2)}) copy-start(f32[16,16384]{1,0:T(8,128)} %start_ref.1) | copy-start | bytes 3145732
  156.0 3.4 %collective-permute-start.42 = (f32[16,640]{1,0:T(8,128)S(1)}, f32[16,640]{1,0:T(8,128)S(1)}, u32[]{:S(2)}, u32[]{:S(2)}) collective-permute-start(f32[16,640]{1,0:T(8,128)S(1)} %shard_map.94.refs_2_), channel_id=1, source_target_pairs={{0,3},{1,2},{2,1},{3,0},{4,7},{5,6},{6,5},{7,4},{8,11},{9,10},{10,... | collective-permute-start | bytes 122888 | tf_op jit(solution)/shard_map/ppermute | solution.py:270
  156.0 4.3 %collective-permute-start.41 = (f32[16,640]{1,0:T(8,128)S(1)}, f32[16,640]{1,0:T(8,128)S(1)}, u32[]{:S(2)}, u32[]{:S(2)}) collective-permute-start(f32[16,640]{1,0:T(8,128)S(1)} %shard_map.94.refs_2_), channel_id=1, source_target_pairs={{0,2},{1,3},{2,0},{3,1},{4,6},{5,7},{6,4},{7,5},{8,10},{9,11},{10,... | collective-permute-start | bytes 122888 | tf_op jit(solution)/shard_map/ppermute | solution.py:270
  156.8 3.6 %collective-permute-start.40 = (f32[16,640]{1,0:T(8,128)S(1)}, f32[16,640]{1,0:T(8,128)S(1)}, u32[]{:S(2)}, u32[]{:S(2)}) collective-permute-start(f32[16,640]{1,0:T(8,128)S(1)} %shard_map.94.refs_2_), channel_id=1, source_target_pairs={{0,1},{1,0},{2,3},{3,2},{4,5},{5,4},{6,7},{7,6},{8,9},{9,8},{10,11... | collective-permute-start | bytes 122888 | tf_op jit(solution)/shard_map/ppermute | solution.py:270
  160.5 4.6 %collective-permute-start.45 = (f32[16,128]{1,0:T(8,128)S(1)}, f32[16,128]{1,0:T(8,128)S(1)}, u32[]{:S(2)}, u32[]{:S(2)}) collective-permute-start(f32[16,128]{1,0:T(8,128)S(1)} %get-tuple-element.80), channel_id=1, source_target_pairs={{0,12},{4,8},{8,4},{12,0},{16,28},{20,24},{24,20},{28,16},{1,13},{... | collective-permute-start | bytes 24584 | tf_op jit(solution)/shard_map/ppermute | solution.py:270
  162.1 3.7 %collective-permute-start.44 = (f32[16,128]{1,0:T(8,128)S(1)}, f32[16,128]{1,0:T(8,128)S(1)}, u32[]{:S(2)}, u32[]{:S(2)}) collective-permute-start(f32[16,128]{1,0:T(8,128)S(1)} %get-tuple-element.80), channel_id=1, source_target_pairs={{0,8},{4,12},{8,0},{12,4},{16,24},{20,28},{24,16},{28,20},{1,9},{5... | collective-permute-start | bytes 24584 | tf_op jit(solution)/shard_map/ppermute | solution.py:270
  163.0 3.7 %collective-permute-start.43 = (f32[16,128]{1,0:T(8,128)S(1)}, f32[16,128]{1,0:T(8,128)S(1)}, u32[]{:S(2)}, u32[]{:S(2)}) collective-permute-start(f32[16,128]{1,0:T(8,128)S(1)} %get-tuple-element.80), channel_id=1, source_target_pairs={{0,4},{4,0},{8,12},{12,8},{16,20},{20,16},{24,28},{28,24},{1,5},{5... | collective-permute-start | bytes 24584 | tf_op jit(solution)/shard_map/ppermute | solution.py:270
  166.7 4.5 %collective-permute-start.46 = (f32[16,128]{1,0:T(8,128)S(1)}, f32[16,128]{1,0:T(8,128)S(1)}, u32[]{:S(2)}, u32[]{:S(2)}) collective-permute-start(f32[16,128]{1,0:T(8,128)S(1)} %add_add_fusion.refs_0_), channel_id=1, source_target_pairs={{0,16},{4,20},{8,24},{12,28},{16,0},{20,4},{24,8},{28,12},{1,17},{... | collective-permute-start | bytes 24584 | tf_op jit(solution)/shard_map/ppermute | solution.py:270

commit v3 on v2

--- a/solution.py
+++ b/solution.py
@@ -8,6 +8,7 @@
 from jax.sharding import PartitionSpec as P
 
 ITERS = 4
+ADD_FLOPS = 1 << 28
 LANES = 128
 F32 = jnp.float32
 BF16 = jnp.bfloat16
@@ -19,20 +20,16 @@
     return jax.ShapeDtypeStruct(sizes, dtype)
 
 
-def call(body, out, args, specs=None, scratch=(), flops=0, bytes_accessed=1 << 18):
+def call(body, out, args, specs=None, scratch=(), flops=0, limit=24 << 20):
     return pl.pallas_call(
         body,
         out_shape=out,
         in_specs=specs if specs is not None else [VMEM] * len(args),
         out_specs=jax.tree.map(lambda _: VMEM, out),
         scratch_shapes=scratch,
-        compiler_params=pltpu.CompilerParams(vmem_limit_bytes=24 << 20),
-        cost_estimate=pl.CostEstimate(flops=flops, bytes_accessed=bytes_accessed, transcendentals=0),
+        compiler_params=pltpu.CompilerParams(vmem_limit_bytes=limit),
+        cost_estimate=pl.CostEstimate(flops=flops, bytes_accessed=1024, transcendentals=0),
     )(*args)
-
-
-def operator_cost(rows, columns):
-    return {"flops": 512 * rows * columns, "bytes_accessed": 2 * rows * columns}
 
 
 def tree(parts):
@@ -97,7 +94,6 @@
         (operator, start),
         [ANY, ANY],
         [pltpu.VMEM(start.shape, F32), pltpu.SemaphoreType.DMA((columns // chunk + 1,))],
-        **operator_cost(rows, columns),
     )
 
 
@@ -127,7 +123,6 @@
         functools.partial(backward_kernel, near, distance, min(1024, width)),
         out,
         (op, w, *norm),
-        **operator_cost(op.shape[0], width),
     )
 
 
@@ -157,7 +152,6 @@
         functools.partial(forward_kernel, near, distance),
         shape(scen, rows + LANES),
         (op, v, *total),
-        **operator_cost(rows, width),
     )
 
 
@@ -194,11 +188,15 @@
         split(image, w_ref)
 
 
-def near_kernel(mine_ref, norm_ref, *refs):
+def add_kernel(sum_ref, got_ref, out_ref):
+    out_ref[...] = sum_ref[...] + got_ref[:, : out_ref.shape[1]].astype(F32)
+
+
+def near_kernel(order, sum_ref, norm_ref, *refs):
     *got_refs, out_ref = refs
-    width = mine_ref.shape[1]
-    total = tree([mine_ref[...]] + [ref[:, :width].astype(F32) for ref in got_refs])
-    norm = tree([norm_ref[...]] + [unpack_norm(ref[:, width:]) for ref in got_refs])
+    width = sum_ref.shape[1]
+    total = sum_ref[...] + got_refs[-1][:, :width].astype(F32)
+    norm = tree([norm_ref[...]] + [unpack_norm(ref[:, width:]) for _, ref in sorted(zip(order, got_refs), key=lambda pair: pair[0])])
     out_ref[:, :width] = total.astype(BF16)
     out_ref[:, width:] = pack_norm(norm)
 
@@ -300,11 +298,13 @@
     term_shape = shape(2 * scen, rows, dtype=BF16)
 
     def gradient_parts(w, norm, packed):
-        sent = {d: backward(near, d, op, w, packed) for d in reversed(range(1, near))}
-        got = {d: exchange(sent[d], "obs", n_obs, d) for d in sent}
-        mine = backward(near, 0, op, w)
+        order = (3, 1, 2) if near == 4 else tuple(range(1, near))
+        got = {d: exchange(backward(near, d, op, w, packed), "obs", n_obs, d) for d in order}
+        total = backward(near, 0, op, w)
+        for d in order[:-1]:
+            total = call(add_kernel, shape(scen, width), (total, got[d]), flops=ADD_FLOPS)
         both = shape(scen, width + LANES, dtype=BF16)
-        value = call(near_kernel, both, (mine, norm, *(got[d] for d in range(1, near))))
+        value = call(functools.partial(near_kernel, order), both, (total, norm, *(got[d] for d in order)))
         parts = [value]
         for index, (stride, members) in enumerate(stages(n_obs, near)):
             if index:
@@ -313,7 +313,7 @@
         return parts
 
     def image_parts(mine):
-        got = {d: exchange(mine, "obs", n_obs, d) for d in reversed(range(1, near))}
+        got = {d: exchange(mine, "obs", n_obs, d) for d in range(1, near)}
         total = forward(near, 0, op, mine)
         for d in got:
             total = forward(near, d, op, got[d], total)
@@ -352,8 +352,6 @@
         functools.partial(directions_kernel, near, width),
         (shape(scen, columns), shape(scen, columns)),
         (start, *alphas, *betas, *pieces),
-        flops=1 << 22,
-        bytes_accessed=6 << 20,
     )
     return call(
         functools.partial(last_kernel, len(norms)),

time: 173 us -> 169 us (0.977)
  waiting for transfers between devices: 71.5 us -> 66.4 us
    ppermute x47, waiting for transfers between devices: 71.5 us -> 66.4 us  [exchange(): return lax.ppermute(value, axis, [(i, i ^ distance) for i in range(size)])]
    pallas_call x48 -> x56, Pallas kernels: 44 us -> 43.6 us  [call(): pl.pallas_call(body, out_shape=out, in_specs=specs if specs is not None e...]
  transfers between devices with their start and end apart: 47 -> 47, of which waited for: 34 -> 39; matrix products, arithmetic and copies ran while one was open for 0% -> 0% of each run, Pallas kernels for 11% -> 15%
where the time goes in v3:
time: 169 us
  waiting for transfers between devices  66.4 us (39%)
  starting transfers between devices  56.6 us (33%)
  Pallas kernels  43.6 us (26%)
    ppermute x47, waiting for transfers between devices, exchange(): return lax.ppermute(value, axis, [(i, i ^ distance) for i in range(size)])  66.4 us
    ppermute x47, starting transfers between devices, exchange(): return lax.ppermute(value, axis, [(i, i ^ distance) for i in range(size)])  56.6 us
    pallas_call x56, Pallas kernels, call(): pl.pallas_call(body, out_shape=out, in_specs=specs if specs is not None e...  43.6 us
  transfers between devices with their start and end apart: 47, of which 39 were waited for; matrix products, arithmetic and copies ran while one was open for 0% of the time, Pallas kernels for 15%

profile of v3, /device:TPU:0, one launch (start us, length us, event | category | flops | bytes accessed | tf_op | source)
XLA Modules:
  0.0 168.7 jit_solution(1864857100116084805)
XLA Ops:
  0.6 1.2 copy-done
  1.9 6.8 %shard_map.50 = (bf16[512,16384]{1,0:T(8,128)(2,1)S(1)}, f32[16,512]{1,0:T(8,128)S(1)}) custom-call(bf16[512,16384]{1,0:T(8,128)(2,1)} %op_hbm.1, f32[16,16384]{1,0:T(8,128)S(1)} %copy-done), custom_call_target="tpu_custom_call" | custom-call | bytes 1024 | tf_op jit(solution)/shard_map/pallas_call | solution.py:24
  9.2 2.6 %collective-permute-start.1 = (f32[16,512]{1,0:T(8,128)S(1)}, f32[16,512]{1,0:T(8,128)S(1)}, u32[]{:S(2)}, u32[]{:S(2)}) collective-permute-start(f32[16,512]{1,0:T(8,128)S(1)} %get-tuple-element.43.refs_0_), channel_id=1, source_target_pairs={{0,2},{1,3},{2,0},{3,1},{4,6},{5,7},{6,4},{7,5},{8,10},{9,11},{10,... | collective-permute-start | bytes 98312 | tf_op jit(solution)/shard_map/ppermute | solution.py:268
  11.9 1.9 %collective-permute-done.1.refs_2_ = f32[16,512]{1,0:T(8,128)S(1)} collective-permute-done((f32[16,512]{1,0:T(8,128)S(1)}, f32[16,512]{1,0:T(8,128)S(1)}, u32[]{:S(2)}, u32[]{:S(2)}) %collective-permute-start.1) | collective-permute-done | bytes 32800 | tf_op jit(solution)/shard_map/ppermute | solution.py:268
  13.8 1.4 collective-permute-done.2.refs_3_
  16.0 2.5 %collective-permute-start.3 = (bf16[16,4224]{1,0:T(8,128)(2,1)S(1)}, bf16[16,4224]{1,0:T(8,128)(2,1)S(1)}, u32[]{:S(2)}, u32[]{:S(2)}) collective-permute-start(bf16[16,4224]{1,0:T(8,128)(2,1)S(1)} %shard_map.53), channel_id=1, source_target_pairs={{0,12},{4,8},{8,4},{12,0},{16,28},{20,24},{24,20},{28,16},{1,13},{... | collective-permute-start | bytes 405512 | tf_op jit(solution)/shard_map/ppermute | solution.py:268
  22.7 2.8 %collective-permute-done.4.got_ref.refs_1_ = bf16[16,4224]{1,0:T(8,128)(2,1)S(1)} collective-permute-done((bf16[16,4224]{1,0:T(8,128)(2,1)S(1)}, bf16[16,4224]{1,0:T(8,128)(2,1)S(1)}, u32[]{:S(2)}, u32[]{:S(2)}) %collective-permute-start.4) | collective-permute-done | bytes 135200 | tf_op jit(solution)/shard_map/ppermute | solution.py:268
  25.8 2.7 %collective-permute-start.6 = (bf16[16,4224]{1,0:T(8,128)(2,1)S(1)}, bf16[16,4224]{1,0:T(8,128)(2,1)S(1)}, u32[]{:S(2)}, u32[]{:S(2)}) collective-permute-start(bf16[16,4224]{1,0:T(8,128)(2,1)S(1)} %shard_map.58.refs_0_), channel_id=1, source_target_pairs={{0,16},{4,20},{8,24},{12,28},{16,0},{20,4},{24,8},{28,12},{1,17},{... | collective-permute-start | bytes 405512 | tf_op jit(solution)/shard_map/ppermute | solution.py:268
  28.5 6.3 %collective-permute-done.6.refs_1_ = bf16[16,4224]{1,0:T(8,128)(2,1)S(1)} collective-permute-done((bf16[16,4224]{1,0:T(8,128)(2,1)S(1)}, bf16[16,4224]{1,0:T(8,128)(2,1)S(1)}, u32[]{:S(2)}, u32[]{:S(2)}) %collective-permute-start.6) | collective-permute-done | bytes 135200 | tf_op jit(solution)/shard_map/ppermute | solution.py:268
  35.4 1.7 %collective-permute-start.9 = (bf16[16,4096]{1,0:T(8,128)(2,1)S(1)}, bf16[16,4096]{1,0:T(8,128)(2,1)S(1)}, u32[]{:S(2)}, u32[]{:S(2)}) collective-permute-start(bf16[16,4096]{1,0:T(8,128)(2,1)S(1)} %get-tuple-element.47.v_ref.refs_7_), channel_id=1, source_target_pairs={{0,4},{4,0},{8,12},{12,8},{16,20},{20,16},{24,28},{28,24},{1,5},{5... | collective-permute-start | bytes 393224 | tf_op jit(solution)/shard_map/ppermute | solution.py:268
  37.7 1.1 collective-permute-start.7
  38.9 1.2 shard_map.60.refs_0_
  41.0 1.2 shard_map.61.refs_0_
  42.6 1.2 shard_map.62.refs_0_
  44.6 1.2 shard_map.63.refs_0_
  46.7 1.0 collective-permute-start.12
  47.7 2.4 %collective-permute-done.11.refs_2_ = f32[16,640]{1,0:T(8,128)S(1)} collective-permute-done((f32[16,640]{1,0:T(8,128)S(1)}, f32[16,640]{1,0:T(8,128)S(1)}, u32[]{:S(2)}, u32[]{:S(2)}) %collective-permute-start.11) | collective-permute-done | bytes 40992 | tf_op jit(solution)/shard_map/ppermute | solution.py:268
  51.4 2.0 %collective-permute-start.13 = (bf16[16,4224]{1,0:T(8,128)(2,1)S(1)}, bf16[16,4224]{1,0:T(8,128)(2,1)S(1)}, u32[]{:S(2)}, u32[]{:S(2)}) collective-permute-start(bf16[16,4224]{1,0:T(8,128)(2,1)S(1)} %shard_map.66), channel_id=1, source_target_pairs={{0,12},{4,8},{8,4},{12,0},{16,28},{20,24},{24,20},{28,16},{1,13},{... | collective-permute-start | bytes 405512 | tf_op jit(solution)/shard_map/ppermute | solution.py:268
  55.3 1.2 collective-permute-start.15
  58.1 2.8 %collective-permute-done.14.got_ref.refs_1_ = bf16[16,4224]{1,0:T(8,128)(2,1)S(1)} collective-permute-done((bf16[16,4224]{1,0:T(8,128)(2,1)S(1)}, bf16[16,4224]{1,0:T(8,128)(2,1)S(1)}, u32[]{:S(2)}, u32[]{:S(2)}) %collective-permute-start.14) | collective-permute-done | bytes 135200 | tf_op jit(solution)/shard_map/ppermute | solution.py:268
  61.0 2.9 %collective-permute-start.16 = (bf16[16,4224]{1,0:T(8,128)(2,1)S(1)}, bf16[16,4224]{1,0:T(8,128)(2,1)S(1)}, u32[]{:S(2)}, u32[]{:S(2)}) collective-permute-start(bf16[16,4224]{1,0:T(8,128)(2,1)S(1)} %shard_map.71.refs_2_), channel_id=1, source_target_pairs={{0,16},{4,20},{8,24},{12,28},{16,0},{20,4},{24,8},{28,12},{1,17},{... | collective-permute-start | bytes 405512 | tf_op jit(solution)/shard_map/ppermute | solution.py:268
  63.9 6.4 %collective-permute-done.16.refs_3_ = bf16[16,4224]{1,0:T(8,128)(2,1)S(1)} collective-permute-done((bf16[16,4224]{1,0:T(8,128)(2,1)S(1)}, bf16[16,4224]{1,0:T(8,128)(2,1)S(1)}, u32[]{:S(2)}, u32[]{:S(2)}) %collective-permute-start.16) | collective-permute-done | bytes 135200 | tf_op jit(solution)/shard_map/ppermute | solution.py:268
  70.5 1.6 collective-permute-start.19
  72.8 1.2 collective-permute-start.17
  74.0 1.4 shard_map.73.refs_0_
  76.0 1.2 shard_map.74.refs_0_
  77.6 1.2 shard_map.75.refs_0_
  79.8 1.2 shard_map.76.refs_2_
  81.0 1.0 collective-permute-start.21
  82.8 2.3 %collective-permute-done.21.refs_4_ = f32[16,640]{1,0:T(8,128)S(1)} collective-permute-done((f32[16,640]{1,0:T(8,128)S(1)}, f32[16,640]{1,0:T(8,128)S(1)}, u32[]{:S(2)}, u32[]{:S(2)}) %collective-permute-start.21) | collective-permute-done | bytes 40992 | tf_op jit(solution)/shard_map/ppermute | solution.py:268
  86.6 1.9 %collective-permute-start.23 = (bf16[16,4224]{1,0:T(8,128)(2,1)S(1)}, bf16[16,4224]{1,0:T(8,128)(2,1)S(1)}, u32[]{:S(2)}, u32[]{:S(2)}) collective-permute-start(bf16[16,4224]{1,0:T(8,128)(2,1)S(1)} %shard_map.79), channel_id=1, source_target_pairs={{0,12},{4,8},{8,4},{12,0},{16,28},{20,24},{24,20},{28,16},{1,13},{... | collective-permute-start | bytes 405512 | tf_op jit(solution)/shard_map/ppermute | solution.py:268
  90.4 1.3 collective-permute-start.25
  93.2 2.8 %collective-permute-done.24.got_ref.refs_1_ = bf16[16,4224]{1,0:T(8,128)(2,1)S(1)} collective-permute-done((bf16[16,4224]{1,0:T(8,128)(2,1)S(1)}, bf16[16,4224]{1,0:T(8,128)(2,1)S(1)}, u32[]{:S(2)}, u32[]{:S(2)}) %collective-permute-start.24) | collective-permute-done | bytes 135200 | tf_op jit(solution)/shard_map/ppermute | solution.py:268
  96.1 2.9 %collective-permute-start.26 = (bf16[16,4224]{1,0:T(8,128)(2,1)S(1)}, bf16[16,4224]{1,0:T(8,128)(2,1)S(1)}, u32[]{:S(2)}, u32[]{:S(2)}) collective-permute-start(bf16[16,4224]{1,0:T(8,128)(2,1)S(1)} %shard_map.84.refs_2_), channel_id=1, source_target_pairs={{0,16},{4,20},{8,24},{12,28},{16,0},{20,4},{24,8},{28,12},{1,17},{... | collective-permute-start | bytes 405512 | tf_op jit(solution)/shard_map/ppermute | solution.py:268
  99.0 6.5 %collective-permute-done.26.refs_3_ = bf16[16,4224]{1,0:T(8,128)(2,1)S(1)} collective-permute-done((bf16[16,4224]{1,0:T(8,128)(2,1)S(1)}, bf16[16,4224]{1,0:T(8,128)(2,1)S(1)}, u32[]{:S(2)}, u32[]{:S(2)}) %collective-permute-start.26) | collective-permute-done | bytes 135200 | tf_op jit(solution)/shard_map/ppermute | solution.py:268
  105.6 1.5 collective-permute-start.29
  107.9 1.3 collective-permute-start.27
  109.2 1.2 shard_map.86.refs_0_
  111.1 1.2 shard_map.87.refs_0_
  112.7 1.2 shard_map.88.refs_0_
  113.9 1.1 collective-permute-done.27.v_ref.refs_18_
  114.9 1.2 shard_map.89.refs_2_
  116.1 1.1 collective-permute-start.31
  118.0 2.2 %collective-permute-done.31.refs_4_ = f32[16,640]{1,0:T(8,128)S(1)} collective-permute-done((f32[16,640]{1,0:T(8,128)S(1)}, f32[16,640]{1,0:T(8,128)S(1)}, u32[]{:S(2)}, u32[]{:S(2)}) %collective-permute-start.31) | collective-permute-done | bytes 40992 | tf_op jit(solution)/shard_map/ppermute | solution.py:268
  121.7 1.8 %collective-permute-start.33 = (bf16[16,4224]{1,0:T(8,128)(2,1)S(1)}, bf16[16,4224]{1,0:T(8,128)(2,1)S(1)}, u32[]{:S(2)}, u32[]{:S(2)}) collective-permute-start(bf16[16,4224]{1,0:T(8,128)(2,1)S(1)} %shard_map.92), channel_id=1, source_target_pairs={{0,12},{4,8},{8,4},{12,0},{16,28},{20,24},{24,20},{28,16},{1,13},{... | collective-permute-start | bytes 405512 | tf_op jit(solution)/shard_map/ppermute | solution.py:268
  125.5 1.4 collective-permute-start.35
  128.4 2.8 %collective-permute-done.34.got_ref.refs_1_ = bf16[16,4224]{1,0:T(8,128)(2,1)S(1)} collective-permute-done((bf16[16,4224]{1,0:T(8,128)(2,1)S(1)}, bf16[16,4224]{1,0:T(8,128)(2,1)S(1)}, u32[]{:S(2)}, u32[]{:S(2)}) %collective-permute-start.34) | collective-permute-done | bytes 135200 | tf_op jit(solution)/shard_map/ppermute | solution.py:268
  131.3 2.8 %collective-permute-start.36 = (bf16[16,4224]{1,0:T(8,128)(2,1)S(1)}, bf16[16,4224]{1,0:T(8,128)(2,1)S(1)}, u32[]{:S(2)}, u32[]{:S(2)}) collective-permute-start(bf16[16,4224]{1,0:T(8,128)(2,1)S(1)} %shard_map.97.refs_2_), channel_id=1, source_target_pairs={{0,16},{4,20},{8,24},{12,28},{16,0},{20,4},{24,8},{28,12},{1,17},{... | collective-permute-start | bytes 405512 | tf_op jit(solution)/shard_map/ppermute | solution.py:268
  134.1 6.6 %collective-permute-done.36.refs_3_ = bf16[16,4224]{1,0:T(8,128)(2,1)S(1)} collective-permute-done((bf16[16,4224]{1,0:T(8,128)(2,1)S(1)}, bf16[16,4224]{1,0:T(8,128)(2,1)S(1)}, u32[]{:S(2)}, u32[]{:S(2)}) %collective-permute-start.36) | collective-permute-done | bytes 135200 | tf_op jit(solution)/shard_map/ppermute | solution.py:268
  141.5 1.3 collective-permute-start.39
  143.5 1.4 collective-permute-start.37
  145.0 1.4 shard_map.99.refs_0_
  146.7 1.2 shard_map.100.refs_0_
  148.4 1.2 shard_map.101.refs_0_
  149.6 1.1 collective-permute-done.37.v_ref.refs_22_
  150.7 1.2 shard_map.102.refs_2_
  151.9 1.1 collective-permute-start.41
  153.8 2.2 %collective-permute-done.41.refs_4_ = f32[16,640]{1,0:T(8,128)S(1)} collective-permute-done((f32[16,640]{1,0:T(8,128)S(1)}, f32[16,640]{1,0:T(8,128)S(1)}, u32[]{:S(2)}, u32[]{:S(2)}) %collective-permute-start.41) | collective-permute-done | bytes 40992 | tf_op jit(solution)/shard_map/ppermute | solution.py:268
  157.2 1.9 %collective-permute-start.45 = (f32[16,128]{1,0:T(8,128)S(1)}, f32[16,128]{1,0:T(8,128)S(1)}, u32[]{:S(2)}, u32[]{:S(2)}) collective-permute-start(f32[16,128]{1,0:T(8,128)S(1)} %get-tuple-element.80), channel_id=1, source_target_pairs={{0,12},{4,8},{8,4},{12,0},{16,28},{20,24},{24,20},{28,16},{1,13},{... | collective-permute-start | bytes 24584 | tf_op jit(solution)/shard_map/ppermute | solution.py:268
  159.1 1.1 collective-permute-start.43
  160.4 1.4 collective-permute-done.45
  162.7 3.0 %collective-permute-start.46 = (f32[16,128]{1,0:T(8,128)S(1)}, f32[16,128]{1,0:T(8,128)S(1)}, u32[]{:S(2)}, u32[]{:S(2)}) collective-permute-start(f32[16,128]{1,0:T(8,128)S(1)} %add_add_fusion.refs_0_), channel_id=1, source_target_pairs={{0,16},{4,20},{8,24},{12,28},{16,0},{20,4},{24,8},{28,12},{1,17},{... | collective-permute-start | bytes 24584 | tf_op jit(solution)/shard_map/ppermute | solution.py:268
  166.3 1.1 collective-permute-done.46.refs_1_
  167.3 1.4 shard_map.105
  (93 shorter events, 38.1 us)
Async XLA Ops:
  0.6 1.2 copy-start
  1.9 13.3 %copy-start.2 = (f32[16,512]{1,0:T(8,128)S(1)}, f32[16,512]{1,0:T(8,128)}, u32[]{:S(2)}) copy-start(f32[16,512]{1,0:T(8,128)} %targets_ref.1) | copy-start | bytes 98308
  8.7 3.2 %collective-permute-start = (f32[16,512]{1,0:T(8,128)S(1)}, f32[16,512]{1,0:T(8,128)S(1)}, u32[]{:S(2)}, u32[]{:S(2)}) collective-permute-start(f32[16,512]{1,0:T(8,128)S(1)} %get-tuple-element.43.refs_0_), channel_id=1, source_target_pairs={{0,1},{1,0},{2,3},{3,2},{4,5},{5,4},{6,7},{7,6},{8,9},{9,8},{10,11... | collective-permute-start | bytes 98312 | tf_op jit(solution)/shard_map/ppermute | solution.py:268
  9.2 4.6 %collective-permute-start.1 = (f32[16,512]{1,0:T(8,128)S(1)}, f32[16,512]{1,0:T(8,128)S(1)}, u32[]{:S(2)}, u32[]{:S(2)}) collective-permute-start(f32[16,512]{1,0:T(8,128)S(1)} %get-tuple-element.43.refs_0_), channel_id=1, source_target_pairs={{0,2},{1,3},{2,0},{3,1},{4,6},{5,7},{6,4},{7,5},{8,10},{9,11},{10,... | collective-permute-start | bytes 98312 | tf_op jit(solution)/shard_map/ppermute | solution.py:268
  11.8 3.3 %collective-permute-start.2 = (f32[16,512]{1,0:T(8,128)S(1)}, f32[16,512]{1,0:T(8,128)S(1)}, u32[]{:S(2)}, u32[]{:S(2)}) collective-permute-start(f32[16,512]{1,0:T(8,128)S(1)} %get-tuple-element.43.refs_0_), channel_id=1, source_target_pairs={{0,3},{1,2},{2,1},{3,0},{4,7},{5,6},{6,5},{7,4},{8,11},{9,10},{10,... | collective-permute-start | bytes 98312 | tf_op jit(solution)/shard_map/ppermute | solution.py:268
  16.0 6.7 %collective-permute-start.3 = (bf16[16,4224]{1,0:T(8,128)(2,1)S(1)}, bf16[16,4224]{1,0:T(8,128)(2,1)S(1)}, u32[]{:S(2)}, u32[]{:S(2)}) collective-permute-start(bf16[16,4224]{1,0:T(8,128)(2,1)S(1)} %shard_map.53), channel_id=1, source_target_pairs={{0,12},{4,8},{8,4},{12,0},{16,28},{20,24},{24,20},{28,16},{1,13},{... | collective-permute-start | bytes 405512 | tf_op jit(solution)/shard_map/ppermute | solution.py:268
  19.3 6.2 %collective-permute-start.4 = (bf16[16,4224]{1,0:T(8,128)(2,1)S(1)}, bf16[16,4224]{1,0:T(8,128)(2,1)S(1)}, u32[]{:S(2)}, u32[]{:S(2)}) collective-permute-start(bf16[16,4224]{1,0:T(8,128)(2,1)S(1)} %shard_map.55), channel_id=1, source_target_pairs={{0,4},{4,0},{8,12},{12,8},{16,20},{20,16},{24,28},{28,24},{1,5},{5... | collective-permute-start | bytes 405512 | tf_op jit(solution)/shard_map/ppermute | solution.py:268
  20.6 5.1 %collective-permute-start.5 = (bf16[16,4224]{1,0:T(8,128)(2,1)S(1)}, bf16[16,4224]{1,0:T(8,128)(2,1)S(1)}, u32[]{:S(2)}, u32[]{:S(2)}) collective-permute-start(bf16[16,4224]{1,0:T(8,128)(2,1)S(1)} %shard_map.57), channel_id=1, source_target_pairs={{0,8},{4,12},{8,0},{12,4},{16,24},{20,28},{24,16},{28,20},{1,9},{5... | collective-permute-start | bytes 405512 | tf_op jit(solution)/shard_map/ppermute | solution.py:268
  25.8 8.9 %collective-permute-start.6 = (bf16[16,4224]{1,0:T(8,128)(2,1)S(1)}, bf16[16,4224]{1,0:T(8,128)(2,1)S(1)}, u32[]{:S(2)}, u32[]{:S(2)}) collective-permute-start(bf16[16,4224]{1,0:T(8,128)(2,1)S(1)} %shard_map.58.refs_0_), channel_id=1, source_target_pairs={{0,16},{4,20},{8,24},{12,28},{16,0},{20,4},{24,8},{28,12},{1,17},{... | collective-permute-start | bytes 405512 | tf_op jit(solution)/shard_map/ppermute | solution.py:268
  35.4 5.6 %collective-permute-start.9 = (bf16[16,4096]{1,0:T(8,128)(2,1)S(1)}, bf16[16,4096]{1,0:T(8,128)(2,1)S(1)}, u32[]{:S(2)}, u32[]{:S(2)}) collective-permute-start(bf16[16,4096]{1,0:T(8,128)(2,1)S(1)} %get-tuple-element.47.v_ref.refs_7_), channel_id=1, source_target_pairs={{0,4},{4,0},{8,12},{12,8},{16,20},{20,16},{24,28},{28,24},{1,5},{5... | collective-permute-start | bytes 393224 | tf_op jit(solution)/shard_map/ppermute | solution.py:268
  37.1 5.5 %collective-permute-start.8 = (bf16[16,4096]{1,0:T(8,128)(2,1)S(1)}, bf16[16,4096]{1,0:T(8,128)(2,1)S(1)}, u32[]{:S(2)}, u32[]{:S(2)}) collective-permute-start(bf16[16,4096]{1,0:T(8,128)(2,1)S(1)} %get-tuple-element.47.v_ref.refs_7_), channel_id=1, source_target_pairs={{0,8},{4,12},{8,0},{12,4},{16,24},{20,28},{24,16},{28,20},{1,9},{5... | collective-permute-start | bytes 393224 | tf_op jit(solution)/shard_map/ppermute | solution.py:268
  37.7 6.9 %collective-permute-start.7 = (bf16[16,4096]{1,0:T(8,128)(2,1)S(1)}, bf16[16,4096]{1,0:T(8,128)(2,1)S(1)}, u32[]{:S(2)}, u32[]{:S(2)}) collective-permute-start(bf16[16,4096]{1,0:T(8,128)(2,1)S(1)} %get-tuple-element.47.v_ref.refs_7_), channel_id=1, source_target_pairs={{0,12},{4,8},{8,4},{12,0},{16,28},{20,24},{24,20},{28,16},{1,13},{... | collective-permute-start | bytes 393224 | tf_op jit(solution)/shard_map/ppermute | solution.py:268
  45.8 1.9 %collective-permute-start.10 = (f32[16,640]{1,0:T(8,128)S(1)}, f32[16,640]{1,0:T(8,128)S(1)}, u32[]{:S(2)}, u32[]{:S(2)}) collective-permute-start(f32[16,640]{1,0:T(8,128)S(1)} %shard_map.63.refs_0_), channel_id=1, source_target_pairs={{0,1},{1,0},{2,3},{3,2},{4,5},{5,4},{6,7},{7,6},{8,9},{9,8},{10,11... | collective-permute-start | bytes 122888 | tf_op jit(solution)/shard_map/ppermute | solution.py:268
  45.8 4.2 %collective-permute-start.11 = (f32[16,640]{1,0:T(8,128)S(1)}, f32[16,640]{1,0:T(8,128)S(1)}, u32[]{:S(2)}, u32[]{:S(2)}) collective-permute-start(f32[16,640]{1,0:T(8,128)S(1)} %shard_map.63.refs_0_), channel_id=1, source_target_pairs={{0,2},{1,3},{2,0},{3,1},{4,6},{5,7},{6,4},{7,5},{8,10},{9,11},{10,... | collective-permute-start | bytes 122888 | tf_op jit(solution)/shard_map/ppermute | solution.py:268
  46.7 3.9 %collective-permute-start.12 = (f32[16,640]{1,0:T(8,128)S(1)}, f32[16,640]{1,0:T(8,128)S(1)}, u32[]{:S(2)}, u32[]{:S(2)}) collective-permute-start(f32[16,640]{1,0:T(8,128)S(1)} %shard_map.63.refs_0_), channel_id=1, source_target_pairs={{0,3},{1,2},{2,1},{3,0},{4,7},{5,6},{6,5},{7,4},{8,11},{9,10},{10,... | collective-permute-start | bytes 122888 | tf_op jit(solution)/shard_map/ppermute | solution.py:268
  51.4 6.6 %collective-permute-start.13 = (bf16[16,4224]{1,0:T(8,128)(2,1)S(1)}, bf16[16,4224]{1,0:T(8,128)(2,1)S(1)}, u32[]{:S(2)}, u32[]{:S(2)}) collective-permute-start(bf16[16,4224]{1,0:T(8,128)(2,1)S(1)} %shard_map.66), channel_id=1, source_target_pairs={{0,12},{4,8},{8,4},{12,0},{16,28},{20,24},{24,20},{28,16},{1,13},{... | collective-permute-start | bytes 405512 | tf_op jit(solution)/shard_map/ppermute | solution.py:268
  54.2 6.6 %collective-permute-start.14 = (bf16[16,4224]{1,0:T(8,128)(2,1)S(1)}, bf16[16,4224]{1,0:T(8,128)(2,1)S(1)}, u32[]{:S(2)}, u32[]{:S(2)}) collective-permute-start(bf16[16,4224]{1,0:T(8,128)(2,1)S(1)} %shard_map.68), channel_id=1, source_target_pairs={{0,4},{4,0},{8,12},{12,8},{16,20},{20,16},{24,28},{28,24},{1,5},{5... | collective-permute-start | bytes 405512 | tf_op jit(solution)/shard_map/ppermute | solution.py:268
  55.3 5.5 %collective-permute-start.15 = (bf16[16,4224]{1,0:T(8,128)(2,1)S(1)}, bf16[16,4224]{1,0:T(8,128)(2,1)S(1)}, u32[]{:S(2)}, u32[]{:S(2)}) collective-permute-start(bf16[16,4224]{1,0:T(8,128)(2,1)S(1)} %shard_map.70), channel_id=1, source_target_pairs={{0,8},{4,12},{8,0},{12,4},{16,24},{20,28},{24,16},{28,20},{1,9},{5... | collective-permute-start | bytes 405512 | tf_op jit(solution)/shard_map/ppermute | solution.py:268
  61.0 9.4 %collective-permute-start.16 = (bf16[16,4224]{1,0:T(8,128)(2,1)S(1)}, bf16[16,4224]{1,0:T(8,128)(2,1)S(1)}, u32[]{:S(2)}, u32[]{:S(2)}) collective-permute-start(bf16[16,4224]{1,0:T(8,128)(2,1)S(1)} %shard_map.71.refs_2_), channel_id=1, source_target_pairs={{0,16},{4,20},{8,24},{12,28},{16,0},{20,4},{24,8},{28,12},{1,17},{... | collective-permute-start | bytes 405512 | tf_op jit(solution)/shard_map/ppermute | solution.py:268
  70.5 5.5 %collective-permute-start.19 = (bf16[16,4096]{1,0:T(8,128)(2,1)S(1)}, bf16[16,4096]{1,0:T(8,128)(2,1)S(1)}, u32[]{:S(2)}, u32[]{:S(2)}) collective-permute-start(bf16[16,4096]{1,0:T(8,128)(2,1)S(1)} %get-tuple-element.54.v_ref.refs_11_), channel_id=1, source_target_pairs={{0,4},{4,0},{8,12},{12,8},{16,20},{20,16},{24,28},{28,24},{1,5},{5... | collective-permute-start | bytes 393224 | tf_op jit(solution)/shard_map/ppermute | solution.py:268
  72.1 5.5 %collective-permute-start.18 = (bf16[16,4096]{1,0:T(8,128)(2,1)S(1)}, bf16[16,4096]{1,0:T(8,128)(2,1)S(1)}, u32[]{:S(2)}, u32[]{:S(2)}) collective-permute-start(bf16[16,4096]{1,0:T(8,128)(2,1)S(1)} %get-tuple-element.54.v_ref.refs_11_), channel_id=1, source_target_pairs={{0,8},{4,12},{8,0},{12,4},{16,24},{20,28},{24,16},{28,20},{1,9},{5... | collective-permute-start | bytes 393224 | tf_op jit(solution)/shard_map/ppermute | solution.py:268
  72.8 7.0 %collective-permute-start.17 = (bf16[16,4096]{1,0:T(8,128)(2,1)S(1)}, bf16[16,4096]{1,0:T(8,128)(2,1)S(1)}, u32[]{:S(2)}, u32[]{:S(2)}) collective-permute-start(bf16[16,4096]{1,0:T(8,128)(2,1)S(1)} %get-tuple-element.54.v_ref.refs_11_), channel_id=1, source_target_pairs={{0,12},{4,8},{8,4},{12,0},{16,28},{20,24},{24,20},{28,16},{1,13},{... | collective-permute-start | bytes 393224 | tf_op jit(solution)/shard_map/ppermute | solution.py:268
  81.0 1.9 %collective-permute-start.20 = (f32[16,640]{1,0:T(8,128)S(1)}, f32[16,640]{1,0:T(8,128)S(1)}, u32[]{:S(2)}, u32[]{:S(2)}) collective-permute-start(f32[16,640]{1,0:T(8,128)S(1)} %shard_map.76.refs_2_), channel_id=1, source_target_pairs={{0,1},{1,0},{2,3},{3,2},{4,5},{5,4},{6,7},{7,6},{8,9},{9,8},{10,11... | collective-permute-start | bytes 122888 | tf_op jit(solution)/shard_map/ppermute | solution.py:268
  81.0 4.2 %collective-permute-start.21 = (f32[16,640]{1,0:T(8,128)S(1)}, f32[16,640]{1,0:T(8,128)S(1)}, u32[]{:S(2)}, u32[]{:S(2)}) collective-permute-start(f32[16,640]{1,0:T(8,128)S(1)} %shard_map.76.refs_2_), channel_id=1, source_target_pairs={{0,2},{1,3},{2,0},{3,1},{4,6},{5,7},{6,4},{7,5},{8,10},{9,11},{10,... | collective-permute-start | bytes 122888 | tf_op jit(solution)/shard_map/ppermute | solution.py:268
  81.9 3.7 %collective-permute-start.22 = (f32[16,640]{1,0:T(8,128)S(1)}, f32[16,640]{1,0:T(8,128)S(1)}, u32[]{:S(2)}, u32[]{:S(2)}) collective-permute-start(f32[16,640]{1,0:T(8,128)S(1)} %shard_map.76.refs_2_), channel_id=1, source_target_pairs={{0,3},{1,2},{2,1},{3,0},{4,7},{5,6},{6,5},{7,4},{8,11},{9,10},{10,... | collective-permute-start | bytes 122888 | tf_op jit(solution)/shard_map/ppermute | solution.py:268
  86.6 6.6 %collective-permute-start.23 = (bf16[16,4224]{1,0:T(8,128)(2,1)S(1)}, bf16[16,4224]{1,0:T(8,128)(2,1)S(1)}, u32[]{:S(2)}, u32[]{:S(2)}) collective-permute-start(bf16[16,4224]{1,0:T(8,128)(2,1)S(1)} %shard_map.79), channel_id=1, source_target_pairs={{0,12},{4,8},{8,4},{12,0},{16,28},{20,24},{24,20},{28,16},{1,13},{... | collective-permute-start | bytes 405512 | tf_op jit(solution)/shard_map/ppermute | solution.py:268
  89.2 6.8 %collective-permute-start.24 = (bf16[16,4224]{1,0:T(8,128)(2,1)S(1)}, bf16[16,4224]{1,0:T(8,128)(2,1)S(1)}, u32[]{:S(2)}, u32[]{:S(2)}) collective-permute-start(bf16[16,4224]{1,0:T(8,128)(2,1)S(1)} %shard_map.81), channel_id=1, source_target_pairs={{0,4},{4,0},{8,12},{12,8},{16,20},{20,16},{24,28},{28,24},{1,5},{5... | collective-permute-start | bytes 405512 | tf_op jit(solution)/shard_map/ppermute | solution.py:268
  90.4 5.6 %collective-permute-start.25 = (bf16[16,4224]{1,0:T(8,128)(2,1)S(1)}, bf16[16,4224]{1,0:T(8,128)(2,1)S(1)}, u32[]{:S(2)}, u32[]{:S(2)}) collective-permute-start(bf16[16,4224]{1,0:T(8,128)(2,1)S(1)} %shard_map.83), channel_id=1, source_target_pairs={{0,8},{4,12},{8,0},{12,4},{16,24},{20,28},{24,16},{28,20},{1,9},{5... | collective-permute-start | bytes 405512 | tf_op jit(solution)/shard_map/ppermute | solution.py:268
  96.1 9.4 %collective-permute-start.26 = (bf16[16,4224]{1,0:T(8,128)(2,1)S(1)}, bf16[16,4224]{1,0:T(8,128)(2,1)S(1)}, u32[]{:S(2)}, u32[]{:S(2)}) collective-permute-start(bf16[16,4224]{1,0:T(8,128)(2,1)S(1)} %shard_map.84.refs_2_), channel_id=1, source_target_pairs={{0,16},{4,20},{8,24},{12,28},{16,0},{20,4},{24,8},{28,12},{1,17},{... | collective-permute-start | bytes 405512 | tf_op jit(solution)/shard_map/ppermute | solution.py:268
  105.6 5.4 %collective-permute-start.29 = (bf16[16,4096]{1,0:T(8,128)(2,1)S(1)}, bf16[16,4096]{1,0:T(8,128)(2,1)S(1)}, u32[]{:S(2)}, u32[]{:S(2)}) collective-permute-start(bf16[16,4096]{1,0:T(8,128)(2,1)S(1)} %get-tuple-element.61.v_ref.refs_15_), channel_id=1, source_target_pairs={{0,4},{4,0},{8,12},{12,8},{16,20},{20,16},{24,28},{28,24},{1,5},{5... | collective-permute-start | bytes 393224 | tf_op jit(solution)/shard_map/ppermute | solution.py:268
  107.1 5.6 %collective-permute-start.28 = (bf16[16,4096]{1,0:T(8,128)(2,1)S(1)}, bf16[16,4096]{1,0:T(8,128)(2,1)S(1)}, u32[]{:S(2)}, u32[]{:S(2)}) collective-permute-start(bf16[16,4096]{1,0:T(8,128)(2,1)S(1)} %get-tuple-element.61.v_ref.refs_15_), channel_id=1, source_target_pairs={{0,8},{4,12},{8,0},{12,4},{16,24},{20,28},{24,16},{28,20},{1,9},{5... | collective-permute-start | bytes 393224 | tf_op jit(solution)/shard_map/ppermute | solution.py:268
  107.9 7.1 %collective-permute-start.27 = (bf16[16,4096]{1,0:T(8,128)(2,1)S(1)}, bf16[16,4096]{1,0:T(8,128)(2,1)S(1)}, u32[]{:S(2)}, u32[]{:S(2)}) collective-permute-start(bf16[16,4096]{1,0:T(8,128)(2,1)S(1)} %get-tuple-element.61.v_ref.refs_15_), channel_id=1, source_target_pairs={{0,12},{4,8},{8,4},{12,0},{16,28},{20,24},{24,20},{28,16},{1,13},{... | collective-permute-start | bytes 393224 | tf_op jit(solution)/shard_map/ppermute | solution.py:268
  116.1 1.9 %collective-permute-start.30 = (f32[16,640]{1,0:T(8,128)S(1)}, f32[16,640]{1,0:T(8,128)S(1)}, u32[]{:S(2)}, u32[]{:S(2)}) collective-permute-start(f32[16,640]{1,0:T(8,128)S(1)} %shard_map.89.refs_2_), channel_id=1, source_target_pairs={{0,1},{1,0},{2,3},{3,2},{4,5},{5,4},{6,7},{7,6},{8,9},{9,8},{10,11... | collective-permute-start | bytes 122888 | tf_op jit(solution)/shard_map/ppermute | solution.py:268
  116.1 4.1 %collective-permute-start.31 = (f32[16,640]{1,0:T(8,128)S(1)}, f32[16,640]{1,0:T(8,128)S(1)}, u32[]{:S(2)}, u32[]{:S(2)}) collective-permute-start(f32[16,640]{1,0:T(8,128)S(1)} %shard_map.89.refs_2_), channel_id=1, source_target_pairs={{0,2},{1,3},{2,0},{3,1},{4,6},{5,7},{6,4},{7,5},{8,10},{9,11},{10,... | collective-permute-start | bytes 122888 | tf_op jit(solution)/shard_map/ppermute | solution.py:268
  117.2 3.6 %collective-permute-start.32 = (f32[16,640]{1,0:T(8,128)S(1)}, f32[16,640]{1,0:T(8,128)S(1)}, u32[]{:S(2)}, u32[]{:S(2)}) collective-permute-start(f32[16,640]{1,0:T(8,128)S(1)} %shard_map.89.refs_2_), channel_id=1, source_target_pairs={{0,3},{1,2},{2,1},{3,0},{4,7},{5,6},{6,5},{7,4},{8,11},{9,10},{10,... | collective-permute-start | bytes 122888 | tf_op jit(solution)/shard_map/ppermute | solution.py:268
  121.7 6.6 %collective-permute-start.33 = (bf16[16,4224]{1,0:T(8,128)(2,1)S(1)}, bf16[16,4224]{1,0:T(8,128)(2,1)S(1)}, u32[]{:S(2)}, u32[]{:S(2)}) collective-permute-start(bf16[16,4224]{1,0:T(8,128)(2,1)S(1)} %shard_map.92), channel_id=1, source_target_pairs={{0,12},{4,8},{8,4},{12,0},{16,28},{20,24},{24,20},{28,16},{1,13},{... | collective-permute-start | bytes 405512 | tf_op jit(solution)/shard_map/ppermute | solution.py:268
  124.3 6.9 %collective-permute-start.34 = (bf16[16,4224]{1,0:T(8,128)(2,1)S(1)}, bf16[16,4224]{1,0:T(8,128)(2,1)S(1)}, u32[]{:S(2)}, u32[]{:S(2)}) collective-permute-start(bf16[16,4224]{1,0:T(8,128)(2,1)S(1)} %shard_map.94), channel_id=1, source_target_pairs={{0,4},{4,0},{8,12},{12,8},{16,20},{20,16},{24,28},{28,24},{1,5},{5... | collective-permute-start | bytes 405512 | tf_op jit(solution)/shard_map/ppermute | solution.py:268
  125.5 5.7 %collective-permute-start.35 = (bf16[16,4224]{1,0:T(8,128)(2,1)S(1)}, bf16[16,4224]{1,0:T(8,128)(2,1)S(1)}, u32[]{:S(2)}, u32[]{:S(2)}) collective-permute-start(bf16[16,4224]{1,0:T(8,128)(2,1)S(1)} %shard_map.96), channel_id=1, source_target_pairs={{0,8},{4,12},{8,0},{12,4},{16,24},{20,28},{24,16},{28,20},{1,9},{5... | collective-permute-start | bytes 405512 | tf_op jit(solution)/shard_map/ppermute | solution.py:268
  131.3 9.4 %collective-permute-start.36 = (bf16[16,4224]{1,0:T(8,128)(2,1)S(1)}, bf16[16,4224]{1,0:T(8,128)(2,1)S(1)}, u32[]{:S(2)}, u32[]{:S(2)}) collective-permute-start(bf16[16,4224]{1,0:T(8,128)(2,1)S(1)} %shard_map.97.refs_2_), channel_id=1, source_target_pairs={{0,16},{4,20},{8,24},{12,28},{16,0},{20,4},{24,8},{28,12},{1,17},{... | collective-permute-start | bytes 405512 | tf_op jit(solution)/shard_map/ppermute | solution.py:268
  141.5 5.2 %collective-permute-start.39 = (bf16[16,4096]{1,0:T(8,128)(2,1)S(1)}, bf16[16,4096]{1,0:T(8,128)(2,1)S(1)}, u32[]{:S(2)}, u32[]{:S(2)}) collective-permute-start(bf16[16,4096]{1,0:T(8,128)(2,1)S(1)} %get-tuple-element.68.v_ref.refs_19_), channel_id=1, source_target_pairs={{0,4},{4,0},{8,12},{12,8},{16,20},{20,16},{24,28},{28,24},{1,5},{5... | collective-permute-start | bytes 393224 | tf_op jit(solution)/shard_map/ppermute | solution.py:268
  142.8 5.5 %collective-permute-start.38 = (bf16[16,4096]{1,0:T(8,128)(2,1)S(1)}, bf16[16,4096]{1,0:T(8,128)(2,1)S(1)}, u32[]{:S(2)}, u32[]{:S(2)}) collective-permute-start(bf16[16,4096]{1,0:T(8,128)(2,1)S(1)} %get-tuple-element.68.v_ref.refs_19_), channel_id=1, source_target_pairs={{0,8},{4,12},{8,0},{12,4},{16,24},{20,28},{24,16},{28,20},{1,9},{5... | collective-permute-start | bytes 393224 | tf_op jit(solution)/shard_map/ppermute | solution.py:268
  143.5 7.2 %collective-permute-start.37 = (bf16[16,4096]{1,0:T(8,128)(2,1)S(1)}, bf16[16,4096]{1,0:T(8,128)(2,1)S(1)}, u32[]{:S(2)}, u32[]{:S(2)}) collective-permute-start(bf16[16,4096]{1,0:T(8,128)(2,1)S(1)} %get-tuple-element.68.v_ref.refs_19_), channel_id=1, source_target_pairs={{0,12},{4,8},{8,4},{12,0},{16,28},{20,24},{24,20},{28,16},{1,13},{... | collective-permute-start | bytes 393224 | tf_op jit(solution)/shard_map/ppermute | solution.py:268
  147.9 17.8 %copy-start.1 = (f32[16,16384]{1,0:T(8,128)S(1)}, f32[16,16384]{1,0:T(8,128)}, u32[]{:S(2)}) copy-start(f32[16,16384]{1,0:T(8,128)} %start_ref.1) | copy-start | bytes 3145732
  151.9 1.9 %collective-permute-start.40 = (f32[16,640]{1,0:T(8,128)S(1)}, f32[16,640]{1,0:T(8,128)S(1)}, u32[]{:S(2)}, u32[]{:S(2)}) collective-permute-start(f32[16,640]{1,0:T(8,128)S(1)} %shard_map.102.refs_2_), channel_id=1, source_target_pairs={{0,1},{1,0},{2,3},{3,2},{4,5},{5,4},{6,7},{7,6},{8,9},{9,8},{10,11... | collective-permute-start | bytes 122888 | tf_op jit(solution)/shard_map/ppermute | solution.py:268
  151.9 4.1 %collective-permute-start.41 = (f32[16,640]{1,0:T(8,128)S(1)}, f32[16,640]{1,0:T(8,128)S(1)}, u32[]{:S(2)}, u32[]{:S(2)}) collective-permute-start(f32[16,640]{1,0:T(8,128)S(1)} %shard_map.102.refs_2_), channel_id=1, source_target_pairs={{0,2},{1,3},{2,0},{3,1},{4,6},{5,7},{6,4},{7,5},{8,10},{9,11},{10,... | collective-permute-start | bytes 122888 | tf_op jit(solution)/shard_map/ppermute | solution.py:268
  153.0 3.6 %collective-permute-start.42 = (f32[16,640]{1,0:T(8,128)S(1)}, f32[16,640]{1,0:T(8,128)S(1)}, u32[]{:S(2)}, u32[]{:S(2)}) collective-permute-start(f32[16,640]{1,0:T(8,128)S(1)} %shard_map.102.refs_2_), channel_id=1, source_target_pairs={{0,3},{1,2},{2,1},{3,0},{4,7},{5,6},{6,5},{7,4},{8,11},{9,10},{10,... | collective-permute-start | bytes 122888 | tf_op jit(solution)/shard_map/ppermute | solution.py:268
  156.7 3.7 %collective-permute-start.44 = (f32[16,128]{1,0:T(8,128)S(1)}, f32[16,128]{1,0:T(8,128)S(1)}, u32[]{:S(2)}, u32[]{:S(2)}) collective-permute-start(f32[16,128]{1,0:T(8,128)S(1)} %get-tuple-element.80), channel_id=1, source_target_pairs={{0,8},{4,12},{8,0},{12,4},{16,24},{20,28},{24,16},{28,20},{1,9},{5... | collective-permute-start | bytes 24584 | tf_op jit(solution)/shard_map/ppermute | solution.py:268
  157.2 4.5 %collective-permute-start.45 = (f32[16,128]{1,0:T(8,128)S(1)}, f32[16,128]{1,0:T(8,128)S(1)}, u32[]{:S(2)}, u32[]{:S(2)}) collective-permute-start(f32[16,128]{1,0:T(8,128)S(1)} %get-tuple-element.80), channel_id=1, source_target_pairs={{0,12},{4,8},{8,4},{12,0},{16,28},{20,24},{24,20},{28,16},{1,13},{... | collective-permute-start | bytes 24584 | tf_op jit(solution)/shard_map/ppermute | solution.py:268
  159.1 3.7 %collective-permute-start.43 = (f32[16,128]{1,0:T(8,128)S(1)}, f32[16,128]{1,0:T(8,128)S(1)}, u32[]{:S(2)}, u32[]{:S(2)}) collective-permute-start(f32[16,128]{1,0:T(8,128)S(1)} %get-tuple-element.80), channel_id=1, source_target_pairs={{0,4},{4,0},{8,12},{12,8},{16,20},{20,16},{24,28},{28,24},{1,5},{5... | collective-permute-start | bytes 24584 | tf_op jit(solution)/shard_map/ppermute | solution.py:268
  162.7 4.6 %collective-permute-start.46 = (f32[16,128]{1,0:T(8,128)S(1)}, f32[16,128]{1,0:T(8,128)S(1)}, u32[]{:S(2)}, u32[]{:S(2)}) collective-permute-start(f32[16,128]{1,0:T(8,128)S(1)} %add_add_fusion.refs_0_), channel_id=1, source_target_pairs={{0,16},{4,20},{8,24},{12,28},{16,0},{20,4},{24,8},{28,12},{1,17},{... | collective-permute-start | bytes 24584 | tf_op jit(solution)/shard_map/ppermute | solution.py:268

commit v4 on v3

--- a/solution.py
+++ b/solution.py
@@ -8,6 +8,7 @@
 from jax.sharding import PartitionSpec as P
 
 ITERS = 4
+EARLY = 4
 ADD_FLOPS = 1 << 28
 LANES = 128
 F32 = jnp.float32
@@ -20,14 +21,15 @@
     return jax.ShapeDtypeStruct(sizes, dtype)
 
 
-def call(body, out, args, specs=None, scratch=(), flops=0, limit=24 << 20):
+def call(body, out, args, specs=None, scratch=(), flops=0, aliases=None, out_specs=None):
     return pl.pallas_call(
         body,
         out_shape=out,
         in_specs=specs if specs is not None else [VMEM] * len(args),
-        out_specs=jax.tree.map(lambda _: VMEM, out),
+        out_specs=out_specs or jax.tree.map(lambda _: VMEM, out),
+        input_output_aliases=aliases or {},
         scratch_shapes=scratch,
-        compiler_params=pltpu.CompilerParams(vmem_limit_bytes=limit),
+        compiler_params=pltpu.CompilerParams(vmem_limit_bytes=24 << 20),
         cost_estimate=pl.CostEstimate(flops=flops, bytes_accessed=1024, transcendentals=0),
     )(*args)
 
@@ -35,9 +37,8 @@
 def tree(parts):
     if len(parts) == 1:
         return parts[0]
-    if len(parts) == 2:
-        return parts[0] + parts[1]
-    return (parts[0] + parts[1]) + (parts[2] + parts[3])
+    half = len(parts) // 2
+    return tree(parts[:half]) + tree(parts[half:])
 
 
 def lane_total(value):
@@ -66,47 +67,70 @@
     out_ref[scen:, :] = (value - high.astype(F32)).astype(BF16)
 
 
-def load_kernel(chunk, op_hbm, start_hbm, op_ref, image_ref, start_ref, sems):
-    pieces = op_ref.shape[1] // chunk
-    copies = [pltpu.make_async_copy(start_hbm, start_ref, sems.at[pieces])]
-    for k in range(pieces):
+def bring(chunk, first, last, op_hbm, op_ref, sems):
+    copies = []
+    for k in range(first, last):
         at = pl.ds(k * chunk, chunk)
         copies.append(pltpu.make_async_copy(op_hbm.at[:, at], op_ref.at[:, at], sems.at[k]))
-    for copy in copies:
-        copy.start()
-    copies[0].wait()
+        copies[-1].start()
+    return copies
+
+
+def early_kernel(chunk, last, op_hbm, op_ref, sems):
+    for copy in bring(chunk, 0, last, op_hbm, op_ref, sems):
+        copy.wait()
+
+
+def load_kernel(chunk, first, last, op_hbm, start_ref, early_ref, op_ref, image_ref, sems):
+    del early_ref
+    copies = bring(chunk, first, last, op_hbm, op_ref, sems)
     total = jnp.zeros(image_ref.shape, F32)
-    for k in range(pieces):
-        copies[k + 1].wait()
+    for k in range(last):
+        if k >= first:
+            copies[k - first].wait()
         at = pl.ds(k * chunk, chunk)
         total += lax.dot_general(
             start_ref[:, at].astype(BF16), op_ref[:, at], (((1,), (1,)), ((), ())), preferred_element_type=F32
         )
-    image_ref[...] = total
+    image_ref[...] = total.astype(BF16)
 
 
 def load(operator, start):
     rows, columns = operator.shape
-    chunk = min(2048, columns)
+    chunk = min(1024, columns)
+    pieces = columns // chunk
+    first = pieces * EARLY // 16
+    whole = shape(rows, columns, dtype=BF16)
+    sems = [pltpu.SemaphoreType.DMA((pieces,))]
+    early = call(functools.partial(early_kernel, chunk, first), whole, (operator,), [ANY], sems)
     return call(
-        functools.partial(load_kernel, chunk),
-        (shape(rows, columns, dtype=BF16), shape(start.shape[0], rows)),
-        (operator, start),
-        [ANY, ANY],
-        [pltpu.VMEM(start.shape, F32), pltpu.SemaphoreType.DMA((columns // chunk + 1,))],
-    )
-
-
-def place(near, distance):
-    return (lax.axis_index("obs") & (near - 1)) ^ distance
-
-
-def backward_kernel(near, distance, chunk, op_ref, w_ref, *refs):
+        functools.partial(load_kernel, chunk, first, pieces),
+        (whole, shape(start.shape[0], rows, dtype=BF16)),
+        (operator, start, early),
+        [ANY, VMEM, VMEM],
+        sems,
+        aliases={2: 0},
+    )
+
+
+def place(n_obs, near, distance):
+    me = lax.axis_index("obs")
+    own = me & (near - 1)
+    if mirrored(n_obs, near):
+        own = own ^ (((me >> 2) & 1) << 1)
+    return own ^ distance
+
+
+def mirrored(n_obs, near):
+    return n_obs == 2 * near and near == 4
+
+
+def backward_kernel(n_obs, near, distance, chunk, op_ref, w_ref, *refs):
     out_ref = refs[-1]
     scen = out_ref.shape[0]
     width = out_ref.shape[1] - LANES * (len(refs) - 1)
     w = w_ref[...]
-    base = place(near, distance) * width
+    base = place(n_obs, near, distance) * width
     for k in range(width // chunk):
         at = pl.ds(pl.multiple_of(base + k * chunk, chunk), chunk)
         both = jnp.dot(w, op_ref[:, at], preferred_element_type=F32)
@@ -115,23 +139,23 @@
         out_ref[:, width:] = norm_ref[...]
 
 
-def backward(near, distance, op, w, *norm):
+def backward(n_obs, near, distance, op, w, *norm):
     width = op.shape[1] // near
     scen = w.shape[0] // 2
     out = shape(scen, width + LANES, dtype=BF16) if norm else shape(scen, width)
     return call(
-        functools.partial(backward_kernel, near, distance, min(1024, width)),
+        functools.partial(backward_kernel, n_obs, near, distance, min(1024, width)),
         out,
         (op, w, *norm),
     )
 
 
-def forward_kernel(near, distance, op_ref, v_ref, *refs):
+def forward_kernel(n_obs, near, distance, op_ref, v_ref, *refs):
     out_ref = refs[-1]
     width = v_ref.shape[1]
     rows = op_ref.shape[0]
     v = v_ref[...]
-    at = pl.ds(pl.multiple_of(place(near, distance) * width, width), width)
+    at = pl.ds(pl.multiple_of(place(n_obs, near, distance) * width, width), width)
     image = lax.dot_general(v, op_ref[:, at], (((1,), (1,)), ((), ())), preferred_element_type=F32)
     wide = v.astype(F32)
     square = wide * wide
@@ -141,23 +165,25 @@
     for sum_ref in refs[:-1]:
         image += sum_ref[:, :rows]
         norm += sum_ref[:, rows:]
-    out_ref[:, :rows] = image
+    if out_ref.dtype == BF16:
+        norm = pack_norm(lane_total(norm))
+    out_ref[:, :rows] = image.astype(out_ref.dtype)
     out_ref[:, rows:] = norm
 
 
-def forward(near, distance, op, v, *total):
+def forward(n_obs, near, distance, dtype, op, v, *total):
     scen, width = v.shape
     rows = op.shape[0]
     return call(
-        functools.partial(forward_kernel, near, distance),
-        shape(scen, rows + LANES),
+        functools.partial(forward_kernel, n_obs, near, distance),
+        shape(scen, rows + LANES, dtype=dtype),
         (op, v, *total),
     )
 
 
 def first_kernel(targets_ref, *refs):
     *part_refs, residual_ref, w_ref, norm_ref, packed_ref = refs
-    residual = targets_ref[...] - tree([ref[...] for ref in part_refs])
+    residual = targets_ref[...] - tree([ref[...].astype(F32) for ref in part_refs])
     residual_ref[...] = residual
     norm_ref[...] = jnp.zeros(norm_ref.shape, F32)
     packed_ref[...] = jnp.zeros(packed_ref.shape, BF16)
@@ -169,10 +195,9 @@
     ins, (image_ref, gamma_ref, beta_ref, norm_ref, *more_refs) = refs[:-outs], refs[-outs:]
     if later:
         old_ref, old_gamma_ref, *ins = ins
-    total = tree([ref[...] for ref in ins])
     rows = image_ref.shape[1]
-    image = total[:, :rows]
-    gamma = lane_total(total[:, rows:])
+    image = tree([ref[:, :rows].astype(F32) for ref in ins])
+    gamma = tree([unpack_norm(ref[:, rows:]) for ref in ins])
     beta = jnp.zeros_like(gamma)
     if later:
         beta = gamma / old_gamma_ref[...]
@@ -201,11 +226,12 @@
     out_ref[:, width:] = pack_norm(norm)
 
 
-def far_kernel(*refs):
+def far_kernel(normed, *refs):
     *got_refs, out_ref = refs
-    width = out_ref.shape[1] - LANES
+    width = out_ref.shape[1] - normed * LANES
     out_ref[:, :width] = tree([ref[:, :width].astype(F32) for ref in got_refs]).astype(BF16)
-    out_ref[:, width:] = pack_norm(tree([unpack_norm(ref[:, width:]) for ref in got_refs]))
+    if normed:
+        out_ref[:, width:] = pack_norm(tree([unpack_norm(ref[:, width:]) for ref in got_refs]))
 
 
 def gradient_kernel(later, *refs):
@@ -224,13 +250,13 @@
     rounded_ref[...] = total.astype(BF16)
 
 
-def directions_kernel(near, width, start_ref, *refs):
+def directions_kernel(n_obs, near, width, start_ref, *refs):
     *ins, direction_ref, solution_ref = refs
     alphas = ins[: ITERS - 1]
     betas = ins[ITERS - 1 : 2 * ITERS - 1]
     pieces = ins[2 * ITERS - 1 :]
     for d in range(near):
-        base = place(near, d) * width
+        base = place(n_obs, near, d) * width
         for k in range(width // LANES):
             at = pl.ds(pl.multiple_of(base + k * LANES, LANES), LANES)
             here = slice(k * LANES, (k + 1) * LANES)
@@ -243,25 +269,27 @@
             solution_ref[:, at] = solution
 
 
-def last_kernel(parts, gamma_ref, direction_ref, base_ref, residual_ref, *refs):
-    *ins, out_ref, out_residual_ref = refs
+def last_kernel(parts, chunk, gamma_ref, direction_ref, base_ref, residual_ref, *refs):
+    *ins, out_hbm, out_residual_ref, out_ref, sems = refs
     norms = ins[:parts]
     alphas = ins[parts : parts + ITERS - 1]
     images = ins[parts + ITERS - 1 :]
     alpha = gamma_ref[...] / tree([ref[...] for ref in norms])
-
-    def step(k, _):
-        at = pl.ds(pl.multiple_of(k * LANES, LANES), LANES)
-        out_ref[:, at] = base_ref[:, at] + alpha * direction_ref[:, at]
-        return 0
-
-    lax.fori_loop(0, out_ref.shape[1] // LANES, step, 0, unroll=8)
+    wide = jnp.concatenate([alpha] * (chunk // LANES), axis=1)
+    copies = []
+    for k in range(out_ref.shape[1] // chunk):
+        at = pl.ds(k * chunk, chunk)
+        out_ref[:, at] = base_ref[:, at] + wide * direction_ref[:, at]
+        copies.append(pltpu.make_async_copy(out_ref.at[:, at], out_hbm.at[:, at], sems.at[k]))
+        copies[-1].start()
     residual = residual_ref[...]
     rows = residual.shape[1]
     for index in range(ITERS):
         factor = alpha if index == ITERS - 1 else alphas[index][...]
         residual -= jnp.concatenate([factor] * (rows // LANES), axis=1) * images[index][...]
     out_residual_ref[...] = residual
+    for copy in copies:
+        copy.wait()
 
 
 def exchange(value, axis, size, distance):
@@ -281,11 +309,32 @@
     return [value] + [exchange(value, axis, size, k * stride) for k in range(1, members)]
 
 
-def parts_over(value, axis, size):
+def parts_over(value, axis, size, normed):
     parts = [value]
-    for stride, members in stages(size):
-        parts = exchanged(tree(parts), axis, size, stride, members)
+    for index, (stride, members) in enumerate(stages(size)):
+        if index:
+            value = call(functools.partial(far_kernel, normed), jax.ShapeDtypeStruct(value.shape, BF16), parts)
+        parts = exchanged(value, axis, size, stride, members)
     return parts
+
+
+def norm_kernel(mine_ref, *refs):
+    first_ref, *got_refs, out_ref = refs
+    own = jnp.where((lax.axis_index("par") & 1) == 0, mine_ref[...], first_ref[...])
+    out_ref[...] = tree([own] + [ref[...] for ref in got_refs])
+
+
+def norm_parts(norm, n_obs, n_par):
+    half = n_obs // 2
+    got = []
+    for k in range(half):
+        pairs = []
+        for at in range(n_obs):
+            for member in range(n_par):
+                there = at ^ (half + k if member % 2 or not k else k)
+                pairs.append((at * n_par + member, there * n_par + member))
+        got.append(lax.ppermute(norm, ("obs", "par"), pairs))
+    return exchanged(call(norm_kernel, jax.ShapeDtypeStruct(norm.shape, F32), (norm, *got)), "par", n_par, 1, 2)
 
 
 def shards(n_obs, n_par, operator, targets, start):
@@ -299,8 +348,8 @@
 
     def gradient_parts(w, norm, packed):
         order = (3, 1, 2) if near == 4 else tuple(range(1, near))
-        got = {d: exchange(backward(near, d, op, w, packed), "obs", n_obs, d) for d in order}
-        total = backward(near, 0, op, w)
+        got = {d: exchange(backward(n_obs, near, d, op, w, packed), "obs", n_obs, d) for d in order}
+        total = backward(n_obs, near, 0, op, w)
         for d in order[:-1]:
             total = call(add_kernel, shape(scen, width), (total, got[d]), flops=ADD_FLOPS)
         both = shape(scen, width + LANES, dtype=BF16)
@@ -308,21 +357,23 @@
         parts = [value]
         for index, (stride, members) in enumerate(stages(n_obs, near)):
             if index:
-                value = call(far_kernel, both, parts)
+                value = call(functools.partial(far_kernel, True), both, parts)
+            if mirrored(n_obs, near):
+                stride += 2
             parts = exchanged(value, "obs", n_obs, stride, members)
         return parts
 
     def image_parts(mine):
         got = {d: exchange(mine, "obs", n_obs, d) for d in range(1, near)}
-        total = forward(near, 0, op, mine)
+        total = forward(n_obs, near, 0, F32, op, mine)
         for d in got:
-            total = forward(near, d, op, got[d], total)
-        return parts_over(total, "par", n_par), [mine] + [got[d] for d in range(1, near)]
+            total = forward(n_obs, near, d, BF16 if d == near - 1 else F32, op, got[d], total)
+        return parts_over(total, "par", n_par, True), [mine] + [got[d] for d in range(1, near)]
 
     op, first = load(operator, start)
     packed_lanes = shape(scen, LANES, dtype=BF16)
     residual, w, norm, packed = call(
-        first_kernel, (image_shape, term_shape, lanes, packed_lanes), (targets, *parts_over(first, "par", n_par))
+        first_kernel, (image_shape, term_shape, lanes, packed_lanes), (targets, *parts_over(first, "par", n_par, False))
     )
     images, alphas, betas, pieces = [], [], [], []
     gradient = gamma = None
@@ -347,16 +398,19 @@
         images.append(image)
         betas.append(beta)
 
-    norms = parts_over(norm, "obs", n_obs)
+    norms = norm_parts(norm, n_obs, n_par)
     direction, base = call(
-        functools.partial(directions_kernel, near, width),
+        functools.partial(directions_kernel, n_obs, near, width),
         (shape(scen, columns), shape(scen, columns)),
         (start, *alphas, *betas, *pieces),
     )
+    chunk = min(2048, columns)
     return call(
-        functools.partial(last_kernel, len(norms)),
+        functools.partial(last_kernel, len(norms), chunk),
         (shape(scen, columns), image_shape),
         (gamma, direction, base, residual, *norms, *alphas, *images),
+        scratch=[pltpu.VMEM((scen, columns), F32), pltpu.SemaphoreType.DMA((columns // chunk,))],
+        out_specs=(ANY, VMEM),
     )
 
 

time: 169 us -> 159 us (0.941)
  waiting for transfers between devices: 66.4 us -> 55.6 us
    ppermute x47 -> x44, waiting for transfers between devices: 66.4 us -> 53 us  [exchange(): return lax.ppermute(value, axis, [(i, i ^ distance) for i in range(size)])]
    ppermute x0 -> x4, starting transfers between devices: none -> 5.48 us  [norm_parts(): got.append(lax.ppermute(norm, ('obs', 'par'), pairs))]
    ppermute x47 -> x44, starting transfers between devices: 56.6 us -> 51.6 us  [exchange(): return lax.ppermute(value, axis, [(i, i ^ distance) for i in range(size)])]
    ppermute x0 -> x4, waiting for transfers between devices: none -> 2.56 us  [norm_parts(): got.append(lax.ppermute(norm, ('obs', 'par'), pairs))]
    pallas_call x56 -> x58, Pallas kernels: 43.6 us -> 44.8 us  [call(): pl.pallas_call(body, out_shape=out, in_specs=specs if specs is not None e...]
  transfers between devices with their start and end apart: 47 -> 48, of which waited for: 39 -> 38; matrix products, arithmetic and copies ran while one was open for 0% -> 0% of each run, Pallas kernels for 15% -> 16%
where the time goes in v4:
time: 159 us
  starting transfers between devices  57.1 us (36%)
  waiting for transfers between devices  55.6 us (35%)
  Pallas kernels  44.8 us (28%)
    ppermute x44, waiting for transfers between devices, exchange(): return lax.ppermute(value, axis, [(i, i ^ distance) for i in range(size)])  53 us
    ppermute x44, starting transfers between devices, exchange(): return lax.ppermute(value, axis, [(i, i ^ distance) for i in range(size)])  51.6 us
    pallas_call x58, Pallas kernels, call(): pl.pallas_call(body, out_shape=out, in_specs=specs if specs is not None e...  44.8 us
    ppermute x4, starting transfers between devices, norm_parts(): got.append(lax.ppermute(norm, ('obs', 'par'), pairs))  5.48 us
  transfers between devices with their start and end apart: 48, of which 38 were waited for; matrix products, arithmetic and copies ran while one was open for 0% of the time, Pallas kernels for 16%

profile of v4, /device:TPU:0, one launch (start us, length us, event | category | flops | bytes accessed | tf_op | source)
XLA Modules:
  0.0 158.6 jit_solution(9410091820335952849)
XLA Ops:
  0.6 2.4 %shard_map.50.early_ref = bf16[512,16384]{1,0:T(8,128)(2,1)S(1)} custom-call(bf16[512,16384]{1,0:T(8,128)(2,1)} %op_hbm.3), custom_call_target="tpu_custom_call" | custom-call | bytes 1024 | tf_op jit(solution)/shard_map/pallas_call | solution.py:25
  3.1 5.2 %shard_map.51 = (bf16[512,16384]{1,0:T(8,128)(2,1)S(1)}, bf16[16,512]{1,0:T(8,128)(2,1)S(1)}) custom-call(bf16[512,16384]{1,0:T(8,128)(2,1)} %op_hbm.3, f32[16,16384]{1,0:T(8,128)S(1)} %copy-done, bf16[512,16384]{1,0:T(8,128)(2,1)S(1)} %shard_map.50.early_ref), custom_call_target="tpu_custom_call", output_to_operand_aliasing={{0}: (2, {})} | custom-call | bytes 1024 | tf_op jit(solution)/shard_map/pallas_call | solution.py:25
  8.3 2.5 %collective-permute-start.2 = (bf16[16,512]{1,0:T(8,128)(2,1)S(1)}, bf16[16,512]{1,0:T(8,128)(2,1)S(1)}, u32[]{:S(2)}, u32[]{:S(2)}) collective-permute-start(bf16[16,512]{1,0:T(8,128)(2,1)S(1)} %get-tuple-element.43.refs_0_), channel_id=1, source_target_pairs={{0,3},{1,2},{2,1},{3,0},{4,7},{5,6},{6,5},{7,4},{8,11},{9,10},{10,... | collective-permute-start | bytes 49160 | tf_op jit(solution)/shard_map/ppermute | solution.py:296
  12.2 2.3 %collective-permute-done.1.refs_2_ = bf16[16,512]{1,0:T(8,128)(2,1)S(1)} collective-permute-done((bf16[16,512]{1,0:T(8,128)(2,1)S(1)}, bf16[16,512]{1,0:T(8,128)(2,1)S(1)}, u32[]{:S(2)}, u32[]{:S(2)}) %collective-permute-start.1) | collective-permute-done | bytes 16416 | tf_op jit(solution)/shard_map/ppermute | solution.py:296
  15.4 2.5 %collective-permute-start.3 = (bf16[16,4224]{1,0:T(8,128)(2,1)S(1)}, bf16[16,4224]{1,0:T(8,128)(2,1)S(1)}, u32[]{:S(2)}, u32[]{:S(2)}) collective-permute-start(bf16[16,4224]{1,0:T(8,128)(2,1)S(1)} %shard_map.54), channel_id=1, source_target_pairs={{0,12},{4,8},{8,4},{12,0},{16,28},{20,24},{24,20},{28,16},{1,13},{... | collective-permute-start | bytes 405512 | tf_op jit(solution)/shard_map/ppermute | solution.py:296
  21.5 2.7 %collective-permute-done.4.got_ref.refs_1_ = bf16[16,4224]{1,0:T(8,128)(2,1)S(1)} collective-permute-done((bf16[16,4224]{1,0:T(8,128)(2,1)S(1)}, bf16[16,4224]{1,0:T(8,128)(2,1)S(1)}, u32[]{:S(2)}, u32[]{:S(2)}) %collective-permute-start.4) | collective-permute-done | bytes 135200 | tf_op jit(solution)/shard_map/ppermute | solution.py:296
  25.1 2.9 %collective-permute-start.6 = (bf16[16,4224]{1,0:T(8,128)(2,1)S(1)}, bf16[16,4224]{1,0:T(8,128)(2,1)S(1)}, u32[]{:S(2)}, u32[]{:S(2)}) collective-permute-start(bf16[16,4224]{1,0:T(8,128)(2,1)S(1)} %shard_map.59.refs_0_), channel_id=1, source_target_pairs={{0,24},{4,28},{8,16},{12,20},{16,8},{20,12},{24,0},{28,4},{1,25},{... | collective-permute-start | bytes 405512 | tf_op jit(solution)/shard_map/ppermute | solution.py:296
  28.0 4.0 %collective-permute-done.6.refs_1_ = bf16[16,4224]{1,0:T(8,128)(2,1)S(1)} collective-permute-done((bf16[16,4224]{1,0:T(8,128)(2,1)S(1)}, bf16[16,4224]{1,0:T(8,128)(2,1)S(1)}, u32[]{:S(2)}, u32[]{:S(2)}) %collective-permute-start.6) | collective-permute-done | bytes 135200 | tf_op jit(solution)/shard_map/ppermute | solution.py:296
  32.7 1.5 collective-permute-start.9
  34.2 2.3 %collective-permute-start.8 = (bf16[16,4096]{1,0:T(8,128)(2,1)S(1)}, bf16[16,4096]{1,0:T(8,128)(2,1)S(1)}, u32[]{:S(2)}, u32[]{:S(2)}) collective-permute-start(bf16[16,4096]{1,0:T(8,128)(2,1)S(1)} %get-tuple-element.47.v_ref.refs_7_), channel_id=1, source_target_pairs={{0,8},{4,12},{8,0},{12,4},{16,24},{20,28},{24,16},{28,20},{1,9},{5... | collective-permute-start | bytes 393224 | tf_op jit(solution)/shard_map/ppermute | solution.py:296
  36.5 1.2 shard_map.61.refs_0_
  37.7 1.2 shard_map.62.refs_0_
  38.9 1.6 collective-permute-done.8.v_ref.refs_9_
  40.4 1.2 shard_map.63.refs_0_
  42.4 1.2 shard_map.64.refs_0_
  44.4 1.1 collective-permute-start.10
  45.4 1.3 collective-permute-done.12.refs_3_
  48.4 2.4 %collective-permute-start.13 = (bf16[16,4224]{1,0:T(8,128)(2,1)S(1)}, bf16[16,4224]{1,0:T(8,128)(2,1)S(1)}, u32[]{:S(2)}, u32[]{:S(2)}) collective-permute-start(bf16[16,4224]{1,0:T(8,128)(2,1)S(1)} %shard_map.67), channel_id=1, source_target_pairs={{0,12},{4,8},{8,4},{12,0},{16,28},{20,24},{24,20},{28,16},{1,13},{... | collective-permute-start | bytes 405512 | tf_op jit(solution)/shard_map/ppermute | solution.py:296
  54.8 2.8 %collective-permute-done.14.got_ref.refs_1_ = bf16[16,4224]{1,0:T(8,128)(2,1)S(1)} collective-permute-done((bf16[16,4224]{1,0:T(8,128)(2,1)S(1)}, bf16[16,4224]{1,0:T(8,128)(2,1)S(1)}, u32[]{:S(2)}, u32[]{:S(2)}) %collective-permute-start.14) | collective-permute-done | bytes 135200 | tf_op jit(solution)/shard_map/ppermute | solution.py:296
  58.0 2.8 %collective-permute-start.16 = (bf16[16,4224]{1,0:T(8,128)(2,1)S(1)}, bf16[16,4224]{1,0:T(8,128)(2,1)S(1)}, u32[]{:S(2)}, u32[]{:S(2)}) collective-permute-start(bf16[16,4224]{1,0:T(8,128)(2,1)S(1)} %shard_map.72.refs_2_), channel_id=1, source_target_pairs={{0,24},{4,28},{8,16},{12,20},{16,8},{20,12},{24,0},{28,4},{1,25},{... | collective-permute-start | bytes 405512 | tf_op jit(solution)/shard_map/ppermute | solution.py:296
  60.8 4.1 %collective-permute-done.16.refs_3_ = bf16[16,4224]{1,0:T(8,128)(2,1)S(1)} collective-permute-done((bf16[16,4224]{1,0:T(8,128)(2,1)S(1)}, bf16[16,4224]{1,0:T(8,128)(2,1)S(1)}, u32[]{:S(2)}, u32[]{:S(2)}) %collective-permute-start.16) | collective-permute-done | bytes 135200 | tf_op jit(solution)/shard_map/ppermute | solution.py:296
  65.1 1.6 collective-permute-start.19
  66.6 2.7 %collective-permute-start.18 = (bf16[16,4096]{1,0:T(8,128)(2,1)S(1)}, bf16[16,4096]{1,0:T(8,128)(2,1)S(1)}, u32[]{:S(2)}, u32[]{:S(2)}) collective-permute-start(bf16[16,4096]{1,0:T(8,128)(2,1)S(1)} %get-tuple-element.54.v_ref.refs_11_), channel_id=1, source_target_pairs={{0,8},{4,12},{8,0},{12,4},{16,24},{20,28},{24,16},{28,20},{1,9},{5... | collective-permute-start | bytes 393224 | tf_op jit(solution)/shard_map/ppermute | solution.py:296
  69.4 1.4 shard_map.74.refs_0_
  70.7 1.2 shard_map.75.refs_0_
  71.9 1.8 %collective-permute-done.18.v_ref.refs_13_ = bf16[16,4096]{1,0:T(8,128)(2,1)S(1)} collective-permute-done((bf16[16,4096]{1,0:T(8,128)(2,1)S(1)}, bf16[16,4096]{1,0:T(8,128)(2,1)S(1)}, u32[]{:S(2)}, u32[]{:S(2)}) %collective-permute-start.18) | collective-permute-done | bytes 131104 | tf_op jit(solution)/shard_map/ppermute | solution.py:296
  73.7 1.2 shard_map.76.refs_0_
  75.2 1.2 shard_map.77.refs_2_
  76.4 1.0 collective-permute-start.21
  77.4 0.9 collective-permute-start.20
  78.3 1.3 collective-permute-done.22.refs_5_
  81.4 2.6 %collective-permute-start.23 = (bf16[16,4224]{1,0:T(8,128)(2,1)S(1)}, bf16[16,4224]{1,0:T(8,128)(2,1)S(1)}, u32[]{:S(2)}, u32[]{:S(2)}) collective-permute-start(bf16[16,4224]{1,0:T(8,128)(2,1)S(1)} %shard_map.80), channel_id=1, source_target_pairs={{0,12},{4,8},{8,4},{12,0},{16,28},{20,24},{24,20},{28,16},{1,13},{... | collective-permute-start | bytes 405512 | tf_op jit(solution)/shard_map/ppermute | solution.py:296
  88.1 2.8 %collective-permute-done.24.got_ref.refs_1_ = bf16[16,4224]{1,0:T(8,128)(2,1)S(1)} collective-permute-done((bf16[16,4224]{1,0:T(8,128)(2,1)S(1)}, bf16[16,4224]{1,0:T(8,128)(2,1)S(1)}, u32[]{:S(2)}, u32[]{:S(2)}) %collective-permute-start.24) | collective-permute-done | bytes 135200 | tf_op jit(solution)/shard_map/ppermute | solution.py:296
  91.2 2.2 %collective-permute-start.26 = (bf16[16,4224]{1,0:T(8,128)(2,1)S(1)}, bf16[16,4224]{1,0:T(8,128)(2,1)S(1)}, u32[]{:S(2)}, u32[]{:S(2)}) collective-permute-start(bf16[16,4224]{1,0:T(8,128)(2,1)S(1)} %shard_map.85.refs_2_), channel_id=1, source_target_pairs={{0,24},{4,28},{8,16},{12,20},{16,8},{20,12},{24,0},{28,4},{1,25},{... | collective-permute-start | bytes 405512 | tf_op jit(solution)/shard_map/ppermute | solution.py:296
  93.4 4.7 %collective-permute-done.26.refs_3_ = bf16[16,4224]{1,0:T(8,128)(2,1)S(1)} collective-permute-done((bf16[16,4224]{1,0:T(8,128)(2,1)S(1)}, bf16[16,4224]{1,0:T(8,128)(2,1)S(1)}, u32[]{:S(2)}, u32[]{:S(2)}) %collective-permute-start.26) | collective-permute-done | bytes 135200 | tf_op jit(solution)/shard_map/ppermute | solution.py:296
  98.2 1.9 %collective-permute-start.29 = (bf16[16,4096]{1,0:T(8,128)(2,1)S(1)}, bf16[16,4096]{1,0:T(8,128)(2,1)S(1)}, u32[]{:S(2)}, u32[]{:S(2)}) collective-permute-start(bf16[16,4096]{1,0:T(8,128)(2,1)S(1)} %get-tuple-element.61.v_ref.refs_15_), channel_id=1, source_target_pairs={{0,4},{4,0},{8,12},{12,8},{16,20},{20,16},{24,28},{28,24},{1,5},{5... | collective-permute-start | bytes 393224 | tf_op jit(solution)/shard_map/ppermute | solution.py:296
  100.1 2.6 %collective-permute-start.28 = (bf16[16,4096]{1,0:T(8,128)(2,1)S(1)}, bf16[16,4096]{1,0:T(8,128)(2,1)S(1)}, u32[]{:S(2)}, u32[]{:S(2)}) collective-permute-start(bf16[16,4096]{1,0:T(8,128)(2,1)S(1)} %get-tuple-element.61.v_ref.refs_15_), channel_id=1, source_target_pairs={{0,8},{4,12},{8,0},{12,4},{16,24},{20,28},{24,16},{28,20},{1,9},{5... | collective-permute-start | bytes 393224 | tf_op jit(solution)/shard_map/ppermute | solution.py:296
  102.7 1.2 shard_map.87.refs_0_
  103.9 1.2 shard_map.88.refs_0_
  105.1 1.9 %collective-permute-done.28.v_ref.refs_17_ = bf16[16,4096]{1,0:T(8,128)(2,1)S(1)} collective-permute-done((bf16[16,4096]{1,0:T(8,128)(2,1)S(1)}, bf16[16,4096]{1,0:T(8,128)(2,1)S(1)}, u32[]{:S(2)}, u32[]{:S(2)}) %collective-permute-start.28) | collective-permute-done | bytes 131104 | tf_op jit(solution)/shard_map/ppermute | solution.py:296
  107.0 1.2 shard_map.89.refs_0_
  108.6 1.2 shard_map.90.refs_2_
  110.6 1.1 collective-permute-start.30
  111.7 1.3 collective-permute-done.32.refs_5_
  114.7 2.2 %collective-permute-start.33 = (bf16[16,4224]{1,0:T(8,128)(2,1)S(1)}, bf16[16,4224]{1,0:T(8,128)(2,1)S(1)}, u32[]{:S(2)}, u32[]{:S(2)}) collective-permute-start(bf16[16,4224]{1,0:T(8,128)(2,1)S(1)} %shard_map.93), channel_id=1, source_target_pairs={{0,12},{4,8},{8,4},{12,0},{16,28},{20,24},{24,20},{28,16},{1,13},{... | collective-permute-start | bytes 405512 | tf_op jit(solution)/shard_map/ppermute | solution.py:296
  121.2 2.8 %collective-permute-done.34.got_ref.refs_1_ = bf16[16,4224]{1,0:T(8,128)(2,1)S(1)} collective-permute-done((bf16[16,4224]{1,0:T(8,128)(2,1)S(1)}, bf16[16,4224]{1,0:T(8,128)(2,1)S(1)}, u32[]{:S(2)}, u32[]{:S(2)}) %collective-permute-start.34) | collective-permute-done | bytes 135200 | tf_op jit(solution)/shard_map/ppermute | solution.py:296
  124.4 2.0 %collective-permute-start.36 = (bf16[16,4224]{1,0:T(8,128)(2,1)S(1)}, bf16[16,4224]{1,0:T(8,128)(2,1)S(1)}, u32[]{:S(2)}, u32[]{:S(2)}) collective-permute-start(bf16[16,4224]{1,0:T(8,128)(2,1)S(1)} %shard_map.98.refs_2_), channel_id=1, source_target_pairs={{0,24},{4,28},{8,16},{12,20},{16,8},{20,12},{24,0},{28,4},{1,25},{... | collective-permute-start | bytes 405512 | tf_op jit(solution)/shard_map/ppermute | solution.py:296
  126.4 5.0 %collective-permute-done.36.refs_3_ = bf16[16,4224]{1,0:T(8,128)(2,1)S(1)} collective-permute-done((bf16[16,4224]{1,0:T(8,128)(2,1)S(1)}, bf16[16,4224]{1,0:T(8,128)(2,1)S(1)}, u32[]{:S(2)}, u32[]{:S(2)}) %collective-permute-start.36) | collective-permute-done | bytes 135200 | tf_op jit(solution)/shard_map/ppermute | solution.py:296
  131.4 0.8 shard_map.99
  132.2 1.5 collective-permute-start.39
  133.8 2.4 %collective-permute-start.38 = (bf16[16,4096]{1,0:T(8,128)(2,1)S(1)}, bf16[16,4096]{1,0:T(8,128)(2,1)S(1)}, u32[]{:S(2)}, u32[]{:S(2)}) collective-permute-start(bf16[16,4096]{1,0:T(8,128)(2,1)S(1)} %get-tuple-element.68.v_ref.refs_19_), channel_id=1, source_target_pairs={{0,8},{4,12},{8,0},{12,4},{16,24},{20,28},{24,16},{28,20},{1,9},{5... | collective-permute-start | bytes 393224 | tf_op jit(solution)/shard_map/ppermute | solution.py:296
  136.4 1.4 shard_map.100.refs_0_
  137.8 1.2 shard_map.101.refs_0_
  139.0 1.2 collective-permute-done.38.v_ref.refs_21_
  140.2 1.2 shard_map.102.refs_0_
  142.2 1.2 shard_map.103.refs_2_
  143.4 0.9 collective-permute-start.41
  144.3 1.0 collective-permute-start.40
  145.3 1.3 collective-permute-done.42.refs_5_
  147.5 2.2 %collective-permute-start.46 = (f32[16,128]{1,0:T(8,128)S(1)}, f32[16,128]{1,0:T(8,128)S(1)}, u32[]{:S(2)}, u32[]{:S(2)}) collective-permute-start(f32[16,128]{1,0:T(8,128)S(1)} %get-tuple-element.80.mine_ref), channel_id=1, source_target_pairs={{0,12},{1,29},{2,14},{3,31},{4,8},{5,25},{6,10},{7,27},{8,4},{9,21... | collective-permute-start | bytes 24584 | tf_op jit(solution)/shard_map/ppermute | solution.py:336
  150.1 0.9 collective-permute-start.44
  151.0 2.0 %collective-permute-start.43 = (f32[16,128]{1,0:T(8,128)S(1)}, f32[16,128]{1,0:T(8,128)S(1)}, u32[]{:S(2)}, u32[]{:S(2)}) collective-permute-start(f32[16,128]{1,0:T(8,128)S(1)} %get-tuple-element.80.mine_ref), channel_id=1, source_target_pairs={{0,16},{1,17},{2,18},{3,19},{4,20},{5,21},{6,22},{7,23},{8,24},{9,... | collective-permute-start | bytes 24584 | tf_op jit(solution)/shard_map/ppermute | solution.py:336
  153.8 1.8 %collective-permute-done.43.refs_0_ = f32[16,128]{1,0:T(8,128)S(1)} collective-permute-done((f32[16,128]{1,0:T(8,128)S(1)}, f32[16,128]{1,0:T(8,128)S(1)}, u32[]{:S(2)}, u32[]{:S(2)}) %collective-permute-start.43) | collective-permute-done | bytes 8224 | tf_op jit(solution)/shard_map/ppermute | solution.py:336
  156.7 1.7 %shard_map.107 = (f32[16,16384]{1,0:T(8,128)}, f32[16,512]{1,0:T(8,128)}) custom-call(f32[16,128]{1,0:T(8,128)S(1)} %get-tuple-element.69.gamma_ref, f32[16,16384]{1,0:T(8,128)S(1)} %get-tuple-element.77.direction_ref, f32[16,16384]{1,0:T(8,128)S(1)} %get-tuple-element.78.base_ref, f32[16,512]{1,0:T(8,128)S(1)} %get-tuple-element.79.residual_ref, ...), custom_call_target="tpu_custom_call" | custom-call | bytes 1024 | tf_op jit(solution)/shard_map/pallas_call | solution.py:25
  (96 shorter events, 33.7 us)
Async XLA Ops:
  0.6 2.5 %copy-start = (f32[16,16384]{1,0:T(8,128)S(1)}, f32[16,16384]{1,0:T(8,128)}, u32[]{:S(2)}) copy-start(f32[16,16384]{1,0:T(8,128)} %start_ref.3) | copy-start | bytes 3145732
  3.1 11.4 %copy-start.2 = (f32[16,512]{1,0:T(8,128)S(1)}, f32[16,512]{1,0:T(8,128)}, u32[]{:S(2)}) copy-start(f32[16,512]{1,0:T(8,128)} %targets_ref.1) | copy-start | bytes 98308
  8.3 3.9 %collective-permute-start.2 = (bf16[16,512]{1,0:T(8,128)(2,1)S(1)}, bf16[16,512]{1,0:T(8,128)(2,1)S(1)}, u32[]{:S(2)}, u32[]{:S(2)}) collective-permute-start(bf16[16,512]{1,0:T(8,128)(2,1)S(1)} %get-tuple-element.43.refs_0_), channel_id=1, source_target_pairs={{0,3},{1,2},{2,1},{3,0},{4,7},{5,6},{6,5},{7,4},{8,11},{9,10},{10,... | collective-permute-start | bytes 49160 | tf_op jit(solution)/shard_map/ppermute | solution.py:296
  10.8 3.7 %collective-permute-start.1 = (bf16[16,512]{1,0:T(8,128)(2,1)S(1)}, bf16[16,512]{1,0:T(8,128)(2,1)S(1)}, u32[]{:S(2)}, u32[]{:S(2)}) collective-permute-start(bf16[16,512]{1,0:T(8,128)(2,1)S(1)} %get-tuple-element.43.refs_0_), channel_id=1, source_target_pairs={{0,2},{1,3},{2,0},{3,1},{4,6},{5,7},{6,4},{7,5},{8,10},{9,11},{10,... | collective-permute-start | bytes 49160 | tf_op jit(solution)/shard_map/ppermute | solution.py:296
  11.4 3.1 %collective-permute-start = (bf16[16,512]{1,0:T(8,128)(2,1)S(1)}, bf16[16,512]{1,0:T(8,128)(2,1)S(1)}, u32[]{:S(2)}, u32[]{:S(2)}) collective-permute-start(bf16[16,512]{1,0:T(8,128)(2,1)S(1)} %get-tuple-element.43.refs_0_), channel_id=1, source_target_pairs={{0,1},{1,0},{2,3},{3,2},{4,5},{5,4},{6,7},{7,6},{8,9},{9,8},{10,11... | collective-permute-start | bytes 49160 | tf_op jit(solution)/shard_map/ppermute | solution.py:296
  15.4 6.1 %collective-permute-start.3 = (bf16[16,4224]{1,0:T(8,128)(2,1)S(1)}, bf16[16,4224]{1,0:T(8,128)(2,1)S(1)}, u32[]{:S(2)}, u32[]{:S(2)}) collective-permute-start(bf16[16,4224]{1,0:T(8,128)(2,1)S(1)} %shard_map.54), channel_id=1, source_target_pairs={{0,12},{4,8},{8,4},{12,0},{16,28},{20,24},{24,20},{28,16},{1,13},{... | collective-permute-start | bytes 405512 | tf_op jit(solution)/shard_map/ppermute | solution.py:296
  18.7 5.5 %collective-permute-start.4 = (bf16[16,4224]{1,0:T(8,128)(2,1)S(1)}, bf16[16,4224]{1,0:T(8,128)(2,1)S(1)}, u32[]{:S(2)}, u32[]{:S(2)}) collective-permute-start(bf16[16,4224]{1,0:T(8,128)(2,1)S(1)} %shard_map.56), channel_id=1, source_target_pairs={{0,4},{4,0},{8,12},{12,8},{16,20},{20,16},{24,28},{28,24},{1,5},{5... | collective-permute-start | bytes 405512 | tf_op jit(solution)/shard_map/ppermute | solution.py:296
  20.0 5.0 %collective-permute-start.5 = (bf16[16,4224]{1,0:T(8,128)(2,1)S(1)}, bf16[16,4224]{1,0:T(8,128)(2,1)S(1)}, u32[]{:S(2)}, u32[]{:S(2)}) collective-permute-start(bf16[16,4224]{1,0:T(8,128)(2,1)S(1)} %shard_map.58), channel_id=1, source_target_pairs={{0,8},{4,12},{8,0},{12,4},{16,24},{20,28},{24,16},{28,20},{1,9},{5... | collective-permute-start | bytes 405512 | tf_op jit(solution)/shard_map/ppermute | solution.py:296
  25.1 6.9 %collective-permute-start.6 = (bf16[16,4224]{1,0:T(8,128)(2,1)S(1)}, bf16[16,4224]{1,0:T(8,128)(2,1)S(1)}, u32[]{:S(2)}, u32[]{:S(2)}) collective-permute-start(bf16[16,4224]{1,0:T(8,128)(2,1)S(1)} %shard_map.59.refs_0_), channel_id=1, source_target_pairs={{0,24},{4,28},{8,16},{12,20},{16,8},{20,12},{24,0},{28,4},{1,25},{... | collective-permute-start | bytes 405512 | tf_op jit(solution)/shard_map/ppermute | solution.py:296
  32.7 5.0 %collective-permute-start.9 = (bf16[16,4096]{1,0:T(8,128)(2,1)S(1)}, bf16[16,4096]{1,0:T(8,128)(2,1)S(1)}, u32[]{:S(2)}, u32[]{:S(2)}) collective-permute-start(bf16[16,4096]{1,0:T(8,128)(2,1)S(1)} %get-tuple-element.47.v_ref.refs_7_), channel_id=1, source_target_pairs={{0,4},{4,0},{8,12},{12,8},{16,20},{20,16},{24,28},{28,24},{1,5},{5... | collective-permute-start | bytes 393224 | tf_op jit(solution)/shard_map/ppermute | solution.py:296
  34.2 6.3 %collective-permute-start.8 = (bf16[16,4096]{1,0:T(8,128)(2,1)S(1)}, bf16[16,4096]{1,0:T(8,128)(2,1)S(1)}, u32[]{:S(2)}, u32[]{:S(2)}) collective-permute-start(bf16[16,4096]{1,0:T(8,128)(2,1)S(1)} %get-tuple-element.47.v_ref.refs_7_), channel_id=1, source_target_pairs={{0,8},{4,12},{8,0},{12,4},{16,24},{20,28},{24,16},{28,20},{1,9},{5... | collective-permute-start | bytes 393224 | tf_op jit(solution)/shard_map/ppermute | solution.py:296
  36.5 5.9 %collective-permute-start.7 = (bf16[16,4096]{1,0:T(8,128)(2,1)S(1)}, bf16[16,4096]{1,0:T(8,128)(2,1)S(1)}, u32[]{:S(2)}, u32[]{:S(2)}) collective-permute-start(bf16[16,4096]{1,0:T(8,128)(2,1)S(1)} %get-tuple-element.47.v_ref.refs_7_), channel_id=1, source_target_pairs={{0,12},{4,8},{8,4},{12,0},{16,28},{20,24},{24,20},{28,16},{1,13},{... | collective-permute-start | bytes 393224 | tf_op jit(solution)/shard_map/ppermute | solution.py:296
  43.5 3.2 %collective-permute-start.12 = (bf16[16,640]{1,0:T(8,128)(2,1)S(1)}, bf16[16,640]{1,0:T(8,128)(2,1)S(1)}, u32[]{:S(2)}, u32[]{:S(2)}) collective-permute-start(bf16[16,640]{1,0:T(8,128)(2,1)S(1)} %shard_map.64.refs_0_), channel_id=1, source_target_pairs={{0,3},{1,2},{2,1},{3,0},{4,7},{5,6},{6,5},{7,4},{8,11},{9,10},{10,... | collective-permute-start | bytes 61448 | tf_op jit(solution)/shard_map/ppermute | solution.py:296
  43.5 3.9 %collective-permute-start.11 = (bf16[16,640]{1,0:T(8,128)(2,1)S(1)}, bf16[16,640]{1,0:T(8,128)(2,1)S(1)}, u32[]{:S(2)}, u32[]{:S(2)}) collective-permute-start(bf16[16,640]{1,0:T(8,128)(2,1)S(1)} %shard_map.64.refs_0_), channel_id=1, source_target_pairs={{0,2},{1,3},{2,0},{3,1},{4,6},{5,7},{6,4},{7,5},{8,10},{9,11},{10,... | collective-permute-start | bytes 61448 | tf_op jit(solution)/shard_map/ppermute | solution.py:296
  44.4 3.1 %collective-permute-start.10 = (bf16[16,640]{1,0:T(8,128)(2,1)S(1)}, bf16[16,640]{1,0:T(8,128)(2,1)S(1)}, u32[]{:S(2)}, u32[]{:S(2)}) collective-permute-start(bf16[16,640]{1,0:T(8,128)(2,1)S(1)} %shard_map.64.refs_0_), channel_id=1, source_target_pairs={{0,1},{1,0},{2,3},{3,2},{4,5},{5,4},{6,7},{7,6},{8,9},{9,8},{10,11... | collective-permute-start | bytes 61448 | tf_op jit(solution)/shard_map/ppermute | solution.py:296
  48.4 6.5 %collective-permute-start.13 = (bf16[16,4224]{1,0:T(8,128)(2,1)S(1)}, bf16[16,4224]{1,0:T(8,128)(2,1)S(1)}, u32[]{:S(2)}, u32[]{:S(2)}) collective-permute-start(bf16[16,4224]{1,0:T(8,128)(2,1)S(1)} %shard_map.67), channel_id=1, source_target_pairs={{0,12},{4,8},{8,4},{12,0},{16,28},{20,24},{24,20},{28,16},{1,13},{... | collective-permute-start | bytes 405512 | tf_op jit(solution)/shard_map/ppermute | solution.py:296
  51.5 6.1 %collective-permute-start.14 = (bf16[16,4224]{1,0:T(8,128)(2,1)S(1)}, bf16[16,4224]{1,0:T(8,128)(2,1)S(1)}, u32[]{:S(2)}, u32[]{:S(2)}) collective-permute-start(bf16[16,4224]{1,0:T(8,128)(2,1)S(1)} %shard_map.69), channel_id=1, source_target_pairs={{0,4},{4,0},{8,12},{12,8},{16,20},{20,16},{24,28},{28,24},{1,5},{5... | collective-permute-start | bytes 405512 | tf_op jit(solution)/shard_map/ppermute | solution.py:296
  52.9 5.0 %collective-permute-start.15 = (bf16[16,4224]{1,0:T(8,128)(2,1)S(1)}, bf16[16,4224]{1,0:T(8,128)(2,1)S(1)}, u32[]{:S(2)}, u32[]{:S(2)}) collective-permute-start(bf16[16,4224]{1,0:T(8,128)(2,1)S(1)} %shard_map.71), channel_id=1, source_target_pairs={{0,8},{4,12},{8,0},{12,4},{16,24},{20,28},{24,16},{28,20},{1,9},{5... | collective-permute-start | bytes 405512 | tf_op jit(solution)/shard_map/ppermute | solution.py:296
  58.0 6.9 %collective-permute-start.16 = (bf16[16,4224]{1,0:T(8,128)(2,1)S(1)}, bf16[16,4224]{1,0:T(8,128)(2,1)S(1)}, u32[]{:S(2)}, u32[]{:S(2)}) collective-permute-start(bf16[16,4224]{1,0:T(8,128)(2,1)S(1)} %shard_map.72.refs_2_), channel_id=1, source_target_pairs={{0,24},{4,28},{8,16},{12,20},{16,8},{20,12},{24,0},{28,4},{1,25},{... | collective-permute-start | bytes 405512 | tf_op jit(solution)/shard_map/ppermute | solution.py:296
  65.1 5.7 %collective-permute-start.19 = (bf16[16,4096]{1,0:T(8,128)(2,1)S(1)}, bf16[16,4096]{1,0:T(8,128)(2,1)S(1)}, u32[]{:S(2)}, u32[]{:S(2)}) collective-permute-start(bf16[16,4096]{1,0:T(8,128)(2,1)S(1)} %get-tuple-element.54.v_ref.refs_11_), channel_id=1, source_target_pairs={{0,4},{4,0},{8,12},{12,8},{16,20},{20,16},{24,28},{28,24},{1,5},{5... | collective-permute-start | bytes 393224 | tf_op jit(solution)/shard_map/ppermute | solution.py:296
  66.6 7.1 %collective-permute-start.18 = (bf16[16,4096]{1,0:T(8,128)(2,1)S(1)}, bf16[16,4096]{1,0:T(8,128)(2,1)S(1)}, u32[]{:S(2)}, u32[]{:S(2)}) collective-permute-start(bf16[16,4096]{1,0:T(8,128)(2,1)S(1)} %get-tuple-element.54.v_ref.refs_11_), channel_id=1, source_target_pairs={{0,8},{4,12},{8,0},{12,4},{16,24},{20,28},{24,16},{28,20},{1,9},{5... | collective-permute-start | bytes 393224 | tf_op jit(solution)/shard_map/ppermute | solution.py:296
  69.4 5.9 %collective-permute-start.17 = (bf16[16,4096]{1,0:T(8,128)(2,1)S(1)}, bf16[16,4096]{1,0:T(8,128)(2,1)S(1)}, u32[]{:S(2)}, u32[]{:S(2)}) collective-permute-start(bf16[16,4096]{1,0:T(8,128)(2,1)S(1)} %get-tuple-element.54.v_ref.refs_11_), channel_id=1, source_target_pairs={{0,12},{4,8},{8,4},{12,0},{16,28},{20,24},{24,20},{28,16},{1,13},{... | collective-permute-start | bytes 393224 | tf_op jit(solution)/shard_map/ppermute | solution.py:296
  76.4 3.2 %collective-permute-start.22 = (bf16[16,640]{1,0:T(8,128)(2,1)S(1)}, bf16[16,640]{1,0:T(8,128)(2,1)S(1)}, u32[]{:S(2)}, u32[]{:S(2)}) collective-permute-start(bf16[16,640]{1,0:T(8,128)(2,1)S(1)} %shard_map.77.refs_2_), channel_id=1, source_target_pairs={{0,3},{1,2},{2,1},{3,0},{4,7},{5,6},{6,5},{7,4},{8,11},{9,10},{10,... | collective-permute-start | bytes 61448 | tf_op jit(solution)/shard_map/ppermute | solution.py:296
  76.4 4.0 %collective-permute-start.21 = (bf16[16,640]{1,0:T(8,128)(2,1)S(1)}, bf16[16,640]{1,0:T(8,128)(2,1)S(1)}, u32[]{:S(2)}, u32[]{:S(2)}) collective-permute-start(bf16[16,640]{1,0:T(8,128)(2,1)S(1)} %shard_map.77.refs_2_), channel_id=1, source_target_pairs={{0,2},{1,3},{2,0},{3,1},{4,6},{5,7},{6,4},{7,5},{8,10},{9,11},{10,... | collective-permute-start | bytes 61448 | tf_op jit(solution)/shard_map/ppermute | solution.py:296
  77.4 3.1 %collective-permute-start.20 = (bf16[16,640]{1,0:T(8,128)(2,1)S(1)}, bf16[16,640]{1,0:T(8,128)(2,1)S(1)}, u32[]{:S(2)}, u32[]{:S(2)}) collective-permute-start(bf16[16,640]{1,0:T(8,128)(2,1)S(1)} %shard_map.77.refs_2_), channel_id=1, source_target_pairs={{0,1},{1,0},{2,3},{3,2},{4,5},{5,4},{6,7},{7,6},{8,9},{9,8},{10,11... | collective-permute-start | bytes 61448 | tf_op jit(solution)/shard_map/ppermute | solution.py:296
  81.4 6.6 %collective-permute-start.23 = (bf16[16,4224]{1,0:T(8,128)(2,1)S(1)}, bf16[16,4224]{1,0:T(8,128)(2,1)S(1)}, u32[]{:S(2)}, u32[]{:S(2)}) collective-permute-start(bf16[16,4224]{1,0:T(8,128)(2,1)S(1)} %shard_map.80), channel_id=1, source_target_pairs={{0,12},{4,8},{8,4},{12,0},{16,28},{20,24},{24,20},{28,16},{1,13},{... | collective-permute-start | bytes 405512 | tf_op jit(solution)/shard_map/ppermute | solution.py:296
  84.8 6.0 %collective-permute-start.24 = (bf16[16,4224]{1,0:T(8,128)(2,1)S(1)}, bf16[16,4224]{1,0:T(8,128)(2,1)S(1)}, u32[]{:S(2)}, u32[]{:S(2)}) collective-permute-start(bf16[16,4224]{1,0:T(8,128)(2,1)S(1)} %shard_map.82), channel_id=1, source_target_pairs={{0,4},{4,0},{8,12},{12,8},{16,20},{20,16},{24,28},{28,24},{1,5},{5... | collective-permute-start | bytes 405512 | tf_op jit(solution)/shard_map/ppermute | solution.py:296
  86.0 5.1 %collective-permute-start.25 = (bf16[16,4224]{1,0:T(8,128)(2,1)S(1)}, bf16[16,4224]{1,0:T(8,128)(2,1)S(1)}, u32[]{:S(2)}, u32[]{:S(2)}) collective-permute-start(bf16[16,4224]{1,0:T(8,128)(2,1)S(1)} %shard_map.84), channel_id=1, source_target_pairs={{0,8},{4,12},{8,0},{12,4},{16,24},{20,28},{24,16},{28,20},{1,9},{5... | collective-permute-start | bytes 405512 | tf_op jit(solution)/shard_map/ppermute | solution.py:296
  91.2 6.9 %collective-permute-start.26 = (bf16[16,4224]{1,0:T(8,128)(2,1)S(1)}, bf16[16,4224]{1,0:T(8,128)(2,1)S(1)}, u32[]{:S(2)}, u32[]{:S(2)}) collective-permute-start(bf16[16,4224]{1,0:T(8,128)(2,1)S(1)} %shard_map.85.refs_2_), channel_id=1, source_target_pairs={{0,24},{4,28},{8,16},{12,20},{16,8},{20,12},{24,0},{28,4},{1,25},{... | collective-permute-start | bytes 405512 | tf_op jit(solution)/shard_map/ppermute | solution.py:296
  98.2 5.7 %collective-permute-start.29 = (bf16[16,4096]{1,0:T(8,128)(2,1)S(1)}, bf16[16,4096]{1,0:T(8,128)(2,1)S(1)}, u32[]{:S(2)}, u32[]{:S(2)}) collective-permute-start(bf16[16,4096]{1,0:T(8,128)(2,1)S(1)} %get-tuple-element.61.v_ref.refs_15_), channel_id=1, source_target_pairs={{0,4},{4,0},{8,12},{12,8},{16,20},{20,16},{24,28},{28,24},{1,5},{5... | collective-permute-start | bytes 393224 | tf_op jit(solution)/shard_map/ppermute | solution.py:296
  100.1 6.9 %collective-permute-start.28 = (bf16[16,4096]{1,0:T(8,128)(2,1)S(1)}, bf16[16,4096]{1,0:T(8,128)(2,1)S(1)}, u32[]{:S(2)}, u32[]{:S(2)}) collective-permute-start(bf16[16,4096]{1,0:T(8,128)(2,1)S(1)} %get-tuple-element.61.v_ref.refs_15_), channel_id=1, source_target_pairs={{0,8},{4,12},{8,0},{12,4},{16,24},{20,28},{24,16},{28,20},{1,9},{5... | collective-permute-start | bytes 393224 | tf_op jit(solution)/shard_map/ppermute | solution.py:296
  102.7 5.9 %collective-permute-start.27 = (bf16[16,4096]{1,0:T(8,128)(2,1)S(1)}, bf16[16,4096]{1,0:T(8,128)(2,1)S(1)}, u32[]{:S(2)}, u32[]{:S(2)}) collective-permute-start(bf16[16,4096]{1,0:T(8,128)(2,1)S(1)} %get-tuple-element.61.v_ref.refs_15_), channel_id=1, source_target_pairs={{0,12},{4,8},{8,4},{12,0},{16,28},{20,24},{24,20},{28,16},{1,13},{... | collective-permute-start | bytes 393224 | tf_op jit(solution)/shard_map/ppermute | solution.py:296
  109.8 3.2 %collective-permute-start.32 = (bf16[16,640]{1,0:T(8,128)(2,1)S(1)}, bf16[16,640]{1,0:T(8,128)(2,1)S(1)}, u32[]{:S(2)}, u32[]{:S(2)}) collective-permute-start(bf16[16,640]{1,0:T(8,128)(2,1)S(1)} %shard_map.90.refs_2_), channel_id=1, source_target_pairs={{0,3},{1,2},{2,1},{3,0},{4,7},{5,6},{6,5},{7,4},{8,11},{9,10},{10,... | collective-permute-start | bytes 61448 | tf_op jit(solution)/shard_map/ppermute | solution.py:296
  109.8 3.9 %collective-permute-start.31 = (bf16[16,640]{1,0:T(8,128)(2,1)S(1)}, bf16[16,640]{1,0:T(8,128)(2,1)S(1)}, u32[]{:S(2)}, u32[]{:S(2)}) collective-permute-start(bf16[16,640]{1,0:T(8,128)(2,1)S(1)} %shard_map.90.refs_2_), channel_id=1, source_target_pairs={{0,2},{1,3},{2,0},{3,1},{4,6},{5,7},{6,4},{7,5},{8,10},{9,11},{10,... | collective-permute-start | bytes 61448 | tf_op jit(solution)/shard_map/ppermute | solution.py:296
  110.6 3.1 %collective-permute-start.30 = (bf16[16,640]{1,0:T(8,128)(2,1)S(1)}, bf16[16,640]{1,0:T(8,128)(2,1)S(1)}, u32[]{:S(2)}, u32[]{:S(2)}) collective-permute-start(bf16[16,640]{1,0:T(8,128)(2,1)S(1)} %shard_map.90.refs_2_), channel_id=1, source_target_pairs={{0,1},{1,0},{2,3},{3,2},{4,5},{5,4},{6,7},{7,6},{8,9},{9,8},{10,11... | collective-permute-start | bytes 61448 | tf_op jit(solution)/shard_map/ppermute | solution.py:296
  114.7 6.5 %collective-permute-start.33 = (bf16[16,4224]{1,0:T(8,128)(2,1)S(1)}, bf16[16,4224]{1,0:T(8,128)(2,1)S(1)}, u32[]{:S(2)}, u32[]{:S(2)}) collective-permute-start(bf16[16,4224]{1,0:T(8,128)(2,1)S(1)} %shard_map.93), channel_id=1, source_target_pairs={{0,12},{4,8},{8,4},{12,0},{16,28},{20,24},{24,20},{28,16},{1,13},{... | collective-permute-start | bytes 405512 | tf_op jit(solution)/shard_map/ppermute | solution.py:296
  117.7 6.2 %collective-permute-start.34 = (bf16[16,4224]{1,0:T(8,128)(2,1)S(1)}, bf16[16,4224]{1,0:T(8,128)(2,1)S(1)}, u32[]{:S(2)}, u32[]{:S(2)}) collective-permute-start(bf16[16,4224]{1,0:T(8,128)(2,1)S(1)} %shard_map.95), channel_id=1, source_target_pairs={{0,4},{4,0},{8,12},{12,8},{16,20},{20,16},{24,28},{28,24},{1,5},{5... | collective-permute-start | bytes 405512 | tf_op jit(solution)/shard_map/ppermute | solution.py:296
  119.3 5.0 %collective-permute-start.35 = (bf16[16,4224]{1,0:T(8,128)(2,1)S(1)}, bf16[16,4224]{1,0:T(8,128)(2,1)S(1)}, u32[]{:S(2)}, u32[]{:S(2)}) collective-permute-start(bf16[16,4224]{1,0:T(8,128)(2,1)S(1)} %shard_map.97), channel_id=1, source_target_pairs={{0,8},{4,12},{8,0},{12,4},{16,24},{20,28},{24,16},{28,20},{1,9},{5... | collective-permute-start | bytes 405512 | tf_op jit(solution)/shard_map/ppermute | solution.py:296
  124.4 7.0 %collective-permute-start.36 = (bf16[16,4224]{1,0:T(8,128)(2,1)S(1)}, bf16[16,4224]{1,0:T(8,128)(2,1)S(1)}, u32[]{:S(2)}, u32[]{:S(2)}) collective-permute-start(bf16[16,4224]{1,0:T(8,128)(2,1)S(1)} %shard_map.98.refs_2_), channel_id=1, source_target_pairs={{0,24},{4,28},{8,16},{12,20},{16,8},{20,12},{24,0},{28,4},{1,25},{... | collective-permute-start | bytes 405512 | tf_op jit(solution)/shard_map/ppermute | solution.py:296
  132.2 5.6 %collective-permute-start.39 = (bf16[16,4096]{1,0:T(8,128)(2,1)S(1)}, bf16[16,4096]{1,0:T(8,128)(2,1)S(1)}, u32[]{:S(2)}, u32[]{:S(2)}) collective-permute-start(bf16[16,4096]{1,0:T(8,128)(2,1)S(1)} %get-tuple-element.68.v_ref.refs_19_), channel_id=1, source_target_pairs={{0,4},{4,0},{8,12},{12,8},{16,20},{20,16},{24,28},{28,24},{1,5},{5... | collective-permute-start | bytes 393224 | tf_op jit(solution)/shard_map/ppermute | solution.py:296
  133.8 6.5 %collective-permute-start.38 = (bf16[16,4096]{1,0:T(8,128)(2,1)S(1)}, bf16[16,4096]{1,0:T(8,128)(2,1)S(1)}, u32[]{:S(2)}, u32[]{:S(2)}) collective-permute-start(bf16[16,4096]{1,0:T(8,128)(2,1)S(1)} %get-tuple-element.68.v_ref.refs_19_), channel_id=1, source_target_pairs={{0,8},{4,12},{8,0},{12,4},{16,24},{20,28},{24,16},{28,20},{1,9},{5... | collective-permute-start | bytes 393224 | tf_op jit(solution)/shard_map/ppermute | solution.py:296
  136.1 6.1 %collective-permute-start.37 = (bf16[16,4096]{1,0:T(8,128)(2,1)S(1)}, bf16[16,4096]{1,0:T(8,128)(2,1)S(1)}, u32[]{:S(2)}, u32[]{:S(2)}) collective-permute-start(bf16[16,4096]{1,0:T(8,128)(2,1)S(1)} %get-tuple-element.68.v_ref.refs_19_), channel_id=1, source_target_pairs={{0,12},{4,8},{8,4},{12,0},{16,28},{20,24},{24,20},{28,16},{1,13},{... | collective-permute-start | bytes 393224 | tf_op jit(solution)/shard_map/ppermute | solution.py:296
  139.0 16.7 %copy-start.1 = (f32[16,16384]{1,0:T(8,128)S(1)}, f32[16,16384]{1,0:T(8,128)}, u32[]{:S(2)}) copy-start(f32[16,16384]{1,0:T(8,128)} %start_ref.3) | copy-start | bytes 3145732
  143.4 3.2 %collective-permute-start.42 = (bf16[16,640]{1,0:T(8,128)(2,1)S(1)}, bf16[16,640]{1,0:T(8,128)(2,1)S(1)}, u32[]{:S(2)}, u32[]{:S(2)}) collective-permute-start(bf16[16,640]{1,0:T(8,128)(2,1)S(1)} %shard_map.103.refs_2_), channel_id=1, source_target_pairs={{0,3},{1,2},{2,1},{3,0},{4,7},{5,6},{6,5},{7,4},{8,11},{9,10},{10,... | collective-permute-start | bytes 61448 | tf_op jit(solution)/shard_map/ppermute | solution.py:296
  143.4 4.0 %collective-permute-start.41 = (bf16[16,640]{1,0:T(8,128)(2,1)S(1)}, bf16[16,640]{1,0:T(8,128)(2,1)S(1)}, u32[]{:S(2)}, u32[]{:S(2)}) collective-permute-start(bf16[16,640]{1,0:T(8,128)(2,1)S(1)} %shard_map.103.refs_2_), channel_id=1, source_target_pairs={{0,2},{1,3},{2,0},{3,1},{4,6},{5,7},{6,4},{7,5},{8,10},{9,11},{10,... | collective-permute-start | bytes 61448 | tf_op jit(solution)/shard_map/ppermute | solution.py:296
  144.3 3.1 %collective-permute-start.40 = (bf16[16,640]{1,0:T(8,128)(2,1)S(1)}, bf16[16,640]{1,0:T(8,128)(2,1)S(1)}, u32[]{:S(2)}, u32[]{:S(2)}) collective-permute-start(bf16[16,640]{1,0:T(8,128)(2,1)S(1)} %shard_map.103.refs_2_), channel_id=1, source_target_pairs={{0,1},{1,0},{2,3},{3,2},{4,5},{5,4},{6,7},{7,6},{8,9},{9,8},{10,11... | collective-permute-start | bytes 61448 | tf_op jit(solution)/shard_map/ppermute | solution.py:296
  147.5 5.5 %collective-permute-start.46 = (f32[16,128]{1,0:T(8,128)S(1)}, f32[16,128]{1,0:T(8,128)S(1)}, u32[]{:S(2)}, u32[]{:S(2)}) collective-permute-start(f32[16,128]{1,0:T(8,128)S(1)} %get-tuple-element.80.mine_ref), channel_id=1, source_target_pairs={{0,12},{1,29},{2,14},{3,31},{4,8},{5,25},{6,10},{7,27},{8,4},{9,21... | collective-permute-start | bytes 24584 | tf_op jit(solution)/shard_map/ppermute | solution.py:336
  149.7 3.7 %collective-permute-start.45 = (f32[16,128]{1,0:T(8,128)S(1)}, f32[16,128]{1,0:T(8,128)S(1)}, u32[]{:S(2)}, u32[]{:S(2)}) collective-permute-start(f32[16,128]{1,0:T(8,128)S(1)} %get-tuple-element.80.mine_ref), channel_id=1, source_target_pairs={{0,8},{1,25},{2,10},{3,27},{4,12},{5,29},{6,14},{7,31},{8,0},{9,17... | collective-permute-start | bytes 24584 | tf_op jit(solution)/shard_map/ppermute | solution.py:336
  150.1 3.7 %collective-permute-start.44 = (f32[16,128]{1,0:T(8,128)S(1)}, f32[16,128]{1,0:T(8,128)S(1)}, u32[]{:S(2)}, u32[]{:S(2)}) collective-permute-start(f32[16,128]{1,0:T(8,128)S(1)} %get-tuple-element.80.mine_ref), channel_id=1, source_target_pairs={{0,4},{1,21},{2,6},{3,23},{4,0},{5,17},{6,2},{7,19},{8,12},{9,29},... | collective-permute-start | bytes 24584 | tf_op jit(solution)/shard_map/ppermute | solution.py:336
  151.0 4.5 %collective-permute-start.43 = (f32[16,128]{1,0:T(8,128)S(1)}, f32[16,128]{1,0:T(8,128)S(1)}, u32[]{:S(2)}, u32[]{:S(2)}) collective-permute-start(f32[16,128]{1,0:T(8,128)S(1)} %get-tuple-element.80.mine_ref), channel_id=1, source_target_pairs={{0,16},{1,17},{2,18},{3,19},{4,20},{5,21},{6,22},{7,23},{8,24},{9,... | collective-permute-start | bytes 24584 | tf_op jit(solution)/shard_map/ppermute | solution.py:336
  155.6 1.2 collective-permute-start.47

commit v5 on v4

--- a/solution.py
+++ b/solution.py
@@ -347,7 +347,7 @@
     term_shape = shape(2 * scen, rows, dtype=BF16)
 
     def gradient_parts(w, norm, packed):
-        order = (3, 1, 2) if near == 4 else tuple(range(1, near))
+        order = (2, 1, 3) if near == 4 else tuple(range(1, near))
         got = {d: exchange(backward(n_obs, near, d, op, w, packed), "obs", n_obs, d) for d in order}
         total = backward(n_obs, near, 0, op, w)
         for d in order[:-1]:

time: 159 us -> 152 us (0.956)
  waiting for transfers between devices: 55.6 us -> 50.8 us
  starting transfers between devices: 57.1 us -> 55.2 us
    ppermute x44, waiting for transfers between devices: 53 us -> 48.4 us  [exchange(): return lax.ppermute(value, axis, [(i, i ^ distance) for i in range(size)])]
    ppermute x44, starting transfers between devices: 51.6 us -> 49.6 us  [exchange(): return lax.ppermute(value, axis, [(i, i ^ distance) for i in range(size)])]
  transfers between devices with their start and end apart: 48 -> 48, of which waited for: 38 -> 31; matrix products, arithmetic and copies ran while one was open for 0% -> 0% of each run, Pallas kernels for 16% -> 16%
where the time goes in v5:
time: 152 us
  starting transfers between devices  55.2 us (36%)
  waiting for transfers between devices  50.8 us (33%)
  Pallas kernels  44.9 us (30%)
    ppermute x44, starting transfers between devices, exchange(): return lax.ppermute(value, axis, [(i, i ^ distance) for i in range(size)])  49.6 us
    ppermute x44, waiting for transfers between devices, exchange(): return lax.ppermute(value, axis, [(i, i ^ distance) for i in range(size)])  48.4 us
    pallas_call x58, Pallas kernels, call(): pl.pallas_call(body, out_shape=out, in_specs=specs if specs is not None e...  44.9 us
    ppermute x4, starting transfers between devices, norm_parts(): got.append(lax.ppermute(norm, ('obs', 'par'), pairs))  5.59 us
  transfers between devices with their start and end apart: 48, of which 31 were waited for; matrix products, arithmetic and copies ran while one was open for 0% of the time, Pallas kernels for 16%

profile of v5, /device:TPU:0, one launch (start us, length us, event | category | flops | bytes accessed | tf_op | source)
XLA Modules:
  0.0 152.0 jit_solution(4682079462269076437)
XLA Ops:
  0.6 2.4 %shard_map.50.early_ref = bf16[512,16384]{1,0:T(8,128)(2,1)S(1)} custom-call(bf16[512,16384]{1,0:T(8,128)(2,1)} %op_hbm.3), custom_call_target="tpu_custom_call" | custom-call | bytes 1024 | tf_op jit(solution)/shard_map/pallas_call | solution.py:25
  3.1 5.2 %shard_map.51 = (bf16[512,16384]{1,0:T(8,128)(2,1)S(1)}, bf16[16,512]{1,0:T(8,128)(2,1)S(1)}) custom-call(bf16[512,16384]{1,0:T(8,128)(2,1)} %op_hbm.3, f32[16,16384]{1,0:T(8,128)S(1)} %copy-done, bf16[512,16384]{1,0:T(8,128)(2,1)S(1)} %shard_map.50.early_ref), custom_call_target="tpu_custom_call", output_to_operand_aliasing={{0}: (2, {})} | custom-call | bytes 1024 | tf_op jit(solution)/shard_map/pallas_call | solution.py:25
  8.3 2.5 %collective-permute-start.2 = (bf16[16,512]{1,0:T(8,128)(2,1)S(1)}, bf16[16,512]{1,0:T(8,128)(2,1)S(1)}, u32[]{:S(2)}, u32[]{:S(2)}) collective-permute-start(bf16[16,512]{1,0:T(8,128)(2,1)S(1)} %get-tuple-element.43.refs_0_), channel_id=1, source_target_pairs={{0,3},{1,2},{2,1},{3,0},{4,7},{5,6},{6,5},{7,4},{8,11},{9,10},{10,... | collective-permute-start | bytes 49160 | tf_op jit(solution)/shard_map/ppermute | solution.py:296
  12.2 2.3 %collective-permute-done.1.refs_2_ = bf16[16,512]{1,0:T(8,128)(2,1)S(1)} collective-permute-done((bf16[16,512]{1,0:T(8,128)(2,1)S(1)}, bf16[16,512]{1,0:T(8,128)(2,1)S(1)}, u32[]{:S(2)}, u32[]{:S(2)}) %collective-permute-start.1) | collective-permute-done | bytes 16416 | tf_op jit(solution)/shard_map/ppermute | solution.py:296
  15.4 1.6 %collective-permute-start.3 = (bf16[16,4224]{1,0:T(8,128)(2,1)S(1)}, bf16[16,4224]{1,0:T(8,128)(2,1)S(1)}, u32[]{:S(2)}, u32[]{:S(2)}) collective-permute-start(bf16[16,4224]{1,0:T(8,128)(2,1)S(1)} %shard_map.54), channel_id=1, source_target_pairs={{0,8},{4,12},{8,0},{12,4},{16,24},{20,28},{24,16},{28,20},{1,9},{5... | collective-permute-start | bytes 405512 | tf_op jit(solution)/shard_map/ppermute | solution.py:296
  17.7 1.5 collective-permute-start.4
  21.3 3.4 %collective-permute-done.4.got_ref.refs_1_ = bf16[16,4224]{1,0:T(8,128)(2,1)S(1)} collective-permute-done((bf16[16,4224]{1,0:T(8,128)(2,1)S(1)}, bf16[16,4224]{1,0:T(8,128)(2,1)S(1)}, u32[]{:S(2)}, u32[]{:S(2)}) %collective-permute-start.4) | collective-permute-done | bytes 135200 | tf_op jit(solution)/shard_map/ppermute | solution.py:296
  24.7 1.2 collective-permute-done.5.refs_2_
  26.1 2.5 %collective-permute-start.6 = (bf16[16,4224]{1,0:T(8,128)(2,1)S(1)}, bf16[16,4224]{1,0:T(8,128)(2,1)S(1)}, u32[]{:S(2)}, u32[]{:S(2)}) collective-permute-start(bf16[16,4224]{1,0:T(8,128)(2,1)S(1)} %shard_map.59.refs_0_), channel_id=1, source_target_pairs={{0,24},{4,28},{8,16},{12,20},{16,8},{20,12},{24,0},{28,4},{1,25},{... | collective-permute-start | bytes 405512 | tf_op jit(solution)/shard_map/ppermute | solution.py:296
  28.6 4.4 %collective-permute-done.6.refs_1_ = bf16[16,4224]{1,0:T(8,128)(2,1)S(1)} collective-permute-done((bf16[16,4224]{1,0:T(8,128)(2,1)S(1)}, bf16[16,4224]{1,0:T(8,128)(2,1)S(1)}, u32[]{:S(2)}, u32[]{:S(2)}) %collective-permute-start.6) | collective-permute-done | bytes 135200 | tf_op jit(solution)/shard_map/ppermute | solution.py:296
  33.6 1.2 collective-permute-start.9
  35.6 1.6 %collective-permute-start.7 = (bf16[16,4096]{1,0:T(8,128)(2,1)S(1)}, bf16[16,4096]{1,0:T(8,128)(2,1)S(1)}, u32[]{:S(2)}, u32[]{:S(2)}) collective-permute-start(bf16[16,4096]{1,0:T(8,128)(2,1)S(1)} %get-tuple-element.47.v_ref.refs_7_), channel_id=1, source_target_pairs={{0,12},{4,8},{8,4},{12,0},{16,28},{20,24},{24,20},{28,16},{1,13},{... | collective-permute-start | bytes 393224 | tf_op jit(solution)/shard_map/ppermute | solution.py:296
  37.1 1.2 shard_map.61.refs_0_
  38.6 1.2 shard_map.62.refs_0_
  39.9 1.2 shard_map.63.refs_0_
  41.5 1.2 shard_map.64.refs_0_
  43.4 1.2 collective-permute-start.10
  44.5 1.3 collective-permute-done.12.refs_3_
  47.4 1.3 collective-permute-start.13
  51.1 1.4 collective-permute-start.15
  53.4 4.1 %collective-permute-done.14.got_ref.refs_1_ = bf16[16,4224]{1,0:T(8,128)(2,1)S(1)} collective-permute-done((bf16[16,4224]{1,0:T(8,128)(2,1)S(1)}, bf16[16,4224]{1,0:T(8,128)(2,1)S(1)}, u32[]{:S(2)}, u32[]{:S(2)}) %collective-permute-start.14) | collective-permute-done | bytes 135200 | tf_op jit(solution)/shard_map/ppermute | solution.py:296
  57.6 2.5 %collective-permute-start.16 = (bf16[16,4224]{1,0:T(8,128)(2,1)S(1)}, bf16[16,4224]{1,0:T(8,128)(2,1)S(1)}, u32[]{:S(2)}, u32[]{:S(2)}) collective-permute-start(bf16[16,4224]{1,0:T(8,128)(2,1)S(1)} %shard_map.72.refs_2_), channel_id=1, source_target_pairs={{0,24},{4,28},{8,16},{12,20},{16,8},{20,12},{24,0},{28,4},{1,25},{... | collective-permute-start | bytes 405512 | tf_op jit(solution)/shard_map/ppermute | solution.py:296
  60.1 4.3 %collective-permute-done.16.refs_3_ = bf16[16,4224]{1,0:T(8,128)(2,1)S(1)} collective-permute-done((bf16[16,4224]{1,0:T(8,128)(2,1)S(1)}, bf16[16,4224]{1,0:T(8,128)(2,1)S(1)}, u32[]{:S(2)}, u32[]{:S(2)}) %collective-permute-start.16) | collective-permute-done | bytes 135200 | tf_op jit(solution)/shard_map/ppermute | solution.py:296
  64.6 1.0 collective-permute-start.19
  66.3 1.9 %collective-permute-start.17 = (bf16[16,4096]{1,0:T(8,128)(2,1)S(1)}, bf16[16,4096]{1,0:T(8,128)(2,1)S(1)}, u32[]{:S(2)}, u32[]{:S(2)}) collective-permute-start(bf16[16,4096]{1,0:T(8,128)(2,1)S(1)} %get-tuple-element.54.v_ref.refs_11_), channel_id=1, source_target_pairs={{0,12},{4,8},{8,4},{12,0},{16,28},{20,24},{24,20},{28,16},{1,13},{... | collective-permute-start | bytes 393224 | tf_op jit(solution)/shard_map/ppermute | solution.py:296
  68.2 1.4 shard_map.74.refs_0_
  69.6 1.2 shard_map.75.refs_0_
  70.8 1.2 shard_map.76.refs_0_
  72.5 1.2 shard_map.77.refs_2_
  73.7 1.3 collective-permute-start.21
  75.6 1.4 collective-permute-done.22.refs_5_
  78.5 1.0 collective-permute-start.23
  80.3 1.1 collective-permute-start.24
  82.2 1.4 collective-permute-start.25
  84.5 4.1 %collective-permute-done.24.got_ref.refs_1_ = bf16[16,4224]{1,0:T(8,128)(2,1)S(1)} collective-permute-done((bf16[16,4224]{1,0:T(8,128)(2,1)S(1)}, bf16[16,4224]{1,0:T(8,128)(2,1)S(1)}, u32[]{:S(2)}, u32[]{:S(2)}) %collective-permute-start.24) | collective-permute-done | bytes 135200 | tf_op jit(solution)/shard_map/ppermute | solution.py:296
  88.7 2.7 %collective-permute-start.26 = (bf16[16,4224]{1,0:T(8,128)(2,1)S(1)}, bf16[16,4224]{1,0:T(8,128)(2,1)S(1)}, u32[]{:S(2)}, u32[]{:S(2)}) collective-permute-start(bf16[16,4224]{1,0:T(8,128)(2,1)S(1)} %shard_map.85.refs_2_), channel_id=1, source_target_pairs={{0,24},{4,28},{8,16},{12,20},{16,8},{20,12},{24,0},{28,4},{1,25},{... | collective-permute-start | bytes 405512 | tf_op jit(solution)/shard_map/ppermute | solution.py:296
  91.3 4.3 %collective-permute-done.26.refs_3_ = bf16[16,4224]{1,0:T(8,128)(2,1)S(1)} collective-permute-done((bf16[16,4224]{1,0:T(8,128)(2,1)S(1)}, bf16[16,4224]{1,0:T(8,128)(2,1)S(1)}, u32[]{:S(2)}, u32[]{:S(2)}) %collective-permute-start.26) | collective-permute-done | bytes 135200 | tf_op jit(solution)/shard_map/ppermute | solution.py:296
  95.8 1.2 collective-permute-start.29
  97.9 1.5 collective-permute-start.27
  99.3 1.2 shard_map.87.refs_0_
  101.0 1.2 shard_map.88.refs_0_
  102.2 1.2 shard_map.89.refs_0_
  103.7 1.2 shard_map.90.refs_2_
  104.9 1.3 collective-permute-start.31
  106.8 1.3 collective-permute-done.32.refs_5_
  109.7 1.2 collective-permute-start.33
  111.7 0.9 collective-permute-start.34
  113.4 1.5 collective-permute-start.35
  115.7 4.3 %collective-permute-done.34.got_ref.refs_1_ = bf16[16,4224]{1,0:T(8,128)(2,1)S(1)} collective-permute-done((bf16[16,4224]{1,0:T(8,128)(2,1)S(1)}, bf16[16,4224]{1,0:T(8,128)(2,1)S(1)}, u32[]{:S(2)}, u32[]{:S(2)}) %collective-permute-start.34) | collective-permute-done | bytes 135200 | tf_op jit(solution)/shard_map/ppermute | solution.py:296
  120.1 3.0 %collective-permute-start.36 = (bf16[16,4224]{1,0:T(8,128)(2,1)S(1)}, bf16[16,4224]{1,0:T(8,128)(2,1)S(1)}, u32[]{:S(2)}, u32[]{:S(2)}) collective-permute-start(bf16[16,4224]{1,0:T(8,128)(2,1)S(1)} %shard_map.98.refs_2_), channel_id=1, source_target_pairs={{0,24},{4,28},{8,16},{12,20},{16,8},{20,12},{24,0},{28,4},{1,25},{... | collective-permute-start | bytes 405512 | tf_op jit(solution)/shard_map/ppermute | solution.py:296
  123.1 4.0 %collective-permute-done.36.refs_3_ = bf16[16,4224]{1,0:T(8,128)(2,1)S(1)} collective-permute-done((bf16[16,4224]{1,0:T(8,128)(2,1)S(1)}, bf16[16,4224]{1,0:T(8,128)(2,1)S(1)}, u32[]{:S(2)}, u32[]{:S(2)}) %collective-permute-start.36) | collective-permute-done | bytes 135200 | tf_op jit(solution)/shard_map/ppermute | solution.py:296
  127.9 0.9 collective-permute-start.39
  129.5 1.9 %collective-permute-start.37 = (bf16[16,4096]{1,0:T(8,128)(2,1)S(1)}, bf16[16,4096]{1,0:T(8,128)(2,1)S(1)}, u32[]{:S(2)}, u32[]{:S(2)}) collective-permute-start(bf16[16,4096]{1,0:T(8,128)(2,1)S(1)} %get-tuple-element.68.v_ref.refs_19_), channel_id=1, source_target_pairs={{0,12},{4,8},{8,4},{12,0},{16,28},{20,24},{24,20},{28,16},{1,13},{... | collective-permute-start | bytes 393224 | tf_op jit(solution)/shard_map/ppermute | solution.py:296
  131.4 1.4 shard_map.100.refs_0_
  132.9 1.2 shard_map.101.refs_0_
  134.1 1.2 shard_map.102.refs_0_
  135.7 1.2 shard_map.103.refs_2_
  136.9 1.3 collective-permute-start.41
  138.8 1.3 collective-permute-done.42.refs_5_
  140.9 1.5 %collective-permute-start.46 = (f32[16,128]{1,0:T(8,128)S(1)}, f32[16,128]{1,0:T(8,128)S(1)}, u32[]{:S(2)}, u32[]{:S(2)}) collective-permute-start(f32[16,128]{1,0:T(8,128)S(1)} %get-tuple-element.80.mine_ref), channel_id=1, source_target_pairs={{0,12},{1,29},{2,14},{3,31},{4,8},{5,25},{6,10},{7,27},{8,4},{9,21... | collective-permute-start | bytes 24584 | tf_op jit(solution)/shard_map/ppermute | solution.py:336
  143.3 1.1 collective-permute-start.44
  144.4 2.1 %collective-permute-start.43 = (f32[16,128]{1,0:T(8,128)S(1)}, f32[16,128]{1,0:T(8,128)S(1)}, u32[]{:S(2)}, u32[]{:S(2)}) collective-permute-start(f32[16,128]{1,0:T(8,128)S(1)} %get-tuple-element.80.mine_ref), channel_id=1, source_target_pairs={{0,16},{1,17},{2,18},{3,19},{4,20},{5,21},{6,22},{7,23},{8,24},{9,... | collective-permute-start | bytes 24584 | tf_op jit(solution)/shard_map/ppermute | solution.py:336
  147.0 2.0 %collective-permute-done.43.refs_0_ = f32[16,128]{1,0:T(8,128)S(1)} collective-permute-done((f32[16,128]{1,0:T(8,128)S(1)}, f32[16,128]{1,0:T(8,128)S(1)}, u32[]{:S(2)}, u32[]{:S(2)}) %collective-permute-start.43) | collective-permute-done | bytes 8224 | tf_op jit(solution)/shard_map/ppermute | solution.py:336
  150.2 1.7 %shard_map.107 = (f32[16,16384]{1,0:T(8,128)}, f32[16,512]{1,0:T(8,128)}) custom-call(f32[16,128]{1,0:T(8,128)S(1)} %get-tuple-element.69.gamma_ref, f32[16,16384]{1,0:T(8,128)S(1)} %get-tuple-element.77.direction_ref, f32[16,16384]{1,0:T(8,128)S(1)} %get-tuple-element.78.base_ref, f32[16,512]{1,0:T(8,128)S(1)} %get-tuple-element.79.residual_ref, ...), custom_call_target="tpu_custom_call" | custom-call | bytes 1024 | tf_op jit(solution)/shard_map/pallas_call | solution.py:25
  (96 shorter events, 31.7 us)
Async XLA Ops:
  0.6 2.5 %copy-start = (f32[16,16384]{1,0:T(8,128)S(1)}, f32[16,16384]{1,0:T(8,128)}, u32[]{:S(2)}) copy-start(f32[16,16384]{1,0:T(8,128)} %start_ref.3) | copy-start | bytes 3145732
  3.1 11.4 %copy-start.2 = (f32[16,512]{1,0:T(8,128)S(1)}, f32[16,512]{1,0:T(8,128)}, u32[]{:S(2)}) copy-start(f32[16,512]{1,0:T(8,128)} %targets_ref.1) | copy-start | bytes 98308
  8.3 3.9 %collective-permute-start.2 = (bf16[16,512]{1,0:T(8,128)(2,1)S(1)}, bf16[16,512]{1,0:T(8,128)(2,1)S(1)}, u32[]{:S(2)}, u32[]{:S(2)}) collective-permute-start(bf16[16,512]{1,0:T(8,128)(2,1)S(1)} %get-tuple-element.43.refs_0_), channel_id=1, source_target_pairs={{0,3},{1,2},{2,1},{3,0},{4,7},{5,6},{6,5},{7,4},{8,11},{9,10},{10,... | collective-permute-start | bytes 49160 | tf_op jit(solution)/shard_map/ppermute | solution.py:296
  10.8 3.7 %collective-permute-start.1 = (bf16[16,512]{1,0:T(8,128)(2,1)S(1)}, bf16[16,512]{1,0:T(8,128)(2,1)S(1)}, u32[]{:S(2)}, u32[]{:S(2)}) collective-permute-start(bf16[16,512]{1,0:T(8,128)(2,1)S(1)} %get-tuple-element.43.refs_0_), channel_id=1, source_target_pairs={{0,2},{1,3},{2,0},{3,1},{4,6},{5,7},{6,4},{7,5},{8,10},{9,11},{10,... | collective-permute-start | bytes 49160 | tf_op jit(solution)/shard_map/ppermute | solution.py:296
  11.4 3.1 %collective-permute-start = (bf16[16,512]{1,0:T(8,128)(2,1)S(1)}, bf16[16,512]{1,0:T(8,128)(2,1)S(1)}, u32[]{:S(2)}, u32[]{:S(2)}) collective-permute-start(bf16[16,512]{1,0:T(8,128)(2,1)S(1)} %get-tuple-element.43.refs_0_), channel_id=1, source_target_pairs={{0,1},{1,0},{2,3},{3,2},{4,5},{5,4},{6,7},{7,6},{8,9},{9,8},{10,11... | collective-permute-start | bytes 49160 | tf_op jit(solution)/shard_map/ppermute | solution.py:296
  15.4 5.9 %collective-permute-start.3 = (bf16[16,4224]{1,0:T(8,128)(2,1)S(1)}, bf16[16,4224]{1,0:T(8,128)(2,1)S(1)}, u32[]{:S(2)}, u32[]{:S(2)}) collective-permute-start(bf16[16,4224]{1,0:T(8,128)(2,1)S(1)} %shard_map.54), channel_id=1, source_target_pairs={{0,8},{4,12},{8,0},{12,4},{16,24},{20,28},{24,16},{28,20},{1,9},{5... | collective-permute-start | bytes 405512 | tf_op jit(solution)/shard_map/ppermute | solution.py:296
  17.7 7.0 %collective-permute-start.4 = (bf16[16,4224]{1,0:T(8,128)(2,1)S(1)}, bf16[16,4224]{1,0:T(8,128)(2,1)S(1)}, u32[]{:S(2)}, u32[]{:S(2)}) collective-permute-start(bf16[16,4224]{1,0:T(8,128)(2,1)S(1)} %shard_map.56), channel_id=1, source_target_pairs={{0,4},{4,0},{8,12},{12,8},{16,20},{20,16},{24,28},{28,24},{1,5},{5... | collective-permute-start | bytes 405512 | tf_op jit(solution)/shard_map/ppermute | solution.py:296
  20.0 5.9 %collective-permute-start.5 = (bf16[16,4224]{1,0:T(8,128)(2,1)S(1)}, bf16[16,4224]{1,0:T(8,128)(2,1)S(1)}, u32[]{:S(2)}, u32[]{:S(2)}) collective-permute-start(bf16[16,4224]{1,0:T(8,128)(2,1)S(1)} %shard_map.58), channel_id=1, source_target_pairs={{0,12},{4,8},{8,4},{12,0},{16,28},{20,24},{24,20},{28,16},{1,13},{... | collective-permute-start | bytes 405512 | tf_op jit(solution)/shard_map/ppermute | solution.py:296
  26.1 7.0 %collective-permute-start.6 = (bf16[16,4224]{1,0:T(8,128)(2,1)S(1)}, bf16[16,4224]{1,0:T(8,128)(2,1)S(1)}, u32[]{:S(2)}, u32[]{:S(2)}) collective-permute-start(bf16[16,4224]{1,0:T(8,128)(2,1)S(1)} %shard_map.59.refs_0_), channel_id=1, source_target_pairs={{0,24},{4,28},{8,16},{12,20},{16,8},{20,12},{24,0},{28,4},{1,25},{... | collective-permute-start | bytes 405512 | tf_op jit(solution)/shard_map/ppermute | solution.py:296
  33.6 5.0 %collective-permute-start.9 = (bf16[16,4096]{1,0:T(8,128)(2,1)S(1)}, bf16[16,4096]{1,0:T(8,128)(2,1)S(1)}, u32[]{:S(2)}, u32[]{:S(2)}) collective-permute-start(bf16[16,4096]{1,0:T(8,128)(2,1)S(1)} %get-tuple-element.47.v_ref.refs_7_), channel_id=1, source_target_pairs={{0,4},{4,0},{8,12},{12,8},{16,20},{20,16},{24,28},{28,24},{1,5},{5... | collective-permute-start | bytes 393224 | tf_op jit(solution)/shard_map/ppermute | solution.py:296
  34.9 5.0 %collective-permute-start.8 = (bf16[16,4096]{1,0:T(8,128)(2,1)S(1)}, bf16[16,4096]{1,0:T(8,128)(2,1)S(1)}, u32[]{:S(2)}, u32[]{:S(2)}) collective-permute-start(bf16[16,4096]{1,0:T(8,128)(2,1)S(1)} %get-tuple-element.47.v_ref.refs_7_), channel_id=1, source_target_pairs={{0,8},{4,12},{8,0},{12,4},{16,24},{20,28},{24,16},{28,20},{1,9},{5... | collective-permute-start | bytes 393224 | tf_op jit(solution)/shard_map/ppermute | solution.py:296
  35.6 5.9 %collective-permute-start.7 = (bf16[16,4096]{1,0:T(8,128)(2,1)S(1)}, bf16[16,4096]{1,0:T(8,128)(2,1)S(1)}, u32[]{:S(2)}, u32[]{:S(2)}) collective-permute-start(bf16[16,4096]{1,0:T(8,128)(2,1)S(1)} %get-tuple-element.47.v_ref.refs_7_), channel_id=1, source_target_pairs={{0,12},{4,8},{8,4},{12,0},{16,28},{20,24},{24,20},{28,16},{1,13},{... | collective-permute-start | bytes 393224 | tf_op jit(solution)/shard_map/ppermute | solution.py:296
  42.7 3.2 %collective-permute-start.12 = (bf16[16,640]{1,0:T(8,128)(2,1)S(1)}, bf16[16,640]{1,0:T(8,128)(2,1)S(1)}, u32[]{:S(2)}, u32[]{:S(2)}) collective-permute-start(bf16[16,640]{1,0:T(8,128)(2,1)S(1)} %shard_map.64.refs_0_), channel_id=1, source_target_pairs={{0,3},{1,2},{2,1},{3,0},{4,7},{5,6},{6,5},{7,4},{8,11},{9,10},{10,... | collective-permute-start | bytes 61448 | tf_op jit(solution)/shard_map/ppermute | solution.py:296
  42.7 3.9 %collective-permute-start.11 = (bf16[16,640]{1,0:T(8,128)(2,1)S(1)}, bf16[16,640]{1,0:T(8,128)(2,1)S(1)}, u32[]{:S(2)}, u32[]{:S(2)}) collective-permute-start(bf16[16,640]{1,0:T(8,128)(2,1)S(1)} %shard_map.64.refs_0_), channel_id=1, source_target_pairs={{0,2},{1,3},{2,0},{3,1},{4,6},{5,7},{6,4},{7,5},{8,10},{9,11},{10,... | collective-permute-start | bytes 61448 | tf_op jit(solution)/shard_map/ppermute | solution.py:296
  43.4 3.1 %collective-permute-start.10 = (bf16[16,640]{1,0:T(8,128)(2,1)S(1)}, bf16[16,640]{1,0:T(8,128)(2,1)S(1)}, u32[]{:S(2)}, u32[]{:S(2)}) collective-permute-start(bf16[16,640]{1,0:T(8,128)(2,1)S(1)} %shard_map.64.refs_0_), channel_id=1, source_target_pairs={{0,1},{1,0},{2,3},{3,2},{4,5},{5,4},{6,7},{7,6},{8,9},{9,8},{10,11... | collective-permute-start | bytes 61448 | tf_op jit(solution)/shard_map/ppermute | solution.py:296
  47.4 5.9 %collective-permute-start.13 = (bf16[16,4224]{1,0:T(8,128)(2,1)S(1)}, bf16[16,4224]{1,0:T(8,128)(2,1)S(1)}, u32[]{:S(2)}, u32[]{:S(2)}) collective-permute-start(bf16[16,4224]{1,0:T(8,128)(2,1)S(1)} %shard_map.67), channel_id=1, source_target_pairs={{0,8},{4,12},{8,0},{12,4},{16,24},{20,28},{24,16},{28,20},{1,9},{5... | collective-permute-start | bytes 405512 | tf_op jit(solution)/shard_map/ppermute | solution.py:296
  49.5 7.9 %collective-permute-start.14 = (bf16[16,4224]{1,0:T(8,128)(2,1)S(1)}, bf16[16,4224]{1,0:T(8,128)(2,1)S(1)}, u32[]{:S(2)}, u32[]{:S(2)}) collective-permute-start(bf16[16,4224]{1,0:T(8,128)(2,1)S(1)} %shard_map.69), channel_id=1, source_target_pairs={{0,4},{4,0},{8,12},{12,8},{16,20},{20,16},{24,28},{28,24},{1,5},{5... | collective-permute-start | bytes 405512 | tf_op jit(solution)/shard_map/ppermute | solution.py:296
  51.1 6.4 %collective-permute-start.15 = (bf16[16,4224]{1,0:T(8,128)(2,1)S(1)}, bf16[16,4224]{1,0:T(8,128)(2,1)S(1)}, u32[]{:S(2)}, u32[]{:S(2)}) collective-permute-start(bf16[16,4224]{1,0:T(8,128)(2,1)S(1)} %shard_map.71), channel_id=1, source_target_pairs={{0,12},{4,8},{8,4},{12,0},{16,28},{20,24},{24,20},{28,16},{1,13},{... | collective-permute-start | bytes 405512 | tf_op jit(solution)/shard_map/ppermute | solution.py:296
  57.6 6.8 %collective-permute-start.16 = (bf16[16,4224]{1,0:T(8,128)(2,1)S(1)}, bf16[16,4224]{1,0:T(8,128)(2,1)S(1)}, u32[]{:S(2)}, u32[]{:S(2)}) collective-permute-start(bf16[16,4224]{1,0:T(8,128)(2,1)S(1)} %shard_map.72.refs_2_), channel_id=1, source_target_pairs={{0,24},{4,28},{8,16},{12,20},{16,8},{20,12},{24,0},{28,4},{1,25},{... | collective-permute-start | bytes 405512 | tf_op jit(solution)/shard_map/ppermute | solution.py:296
  64.6 5.0 %collective-permute-start.19 = (bf16[16,4096]{1,0:T(8,128)(2,1)S(1)}, bf16[16,4096]{1,0:T(8,128)(2,1)S(1)}, u32[]{:S(2)}, u32[]{:S(2)}) collective-permute-start(bf16[16,4096]{1,0:T(8,128)(2,1)S(1)} %get-tuple-element.54.v_ref.refs_11_), channel_id=1, source_target_pairs={{0,4},{4,0},{8,12},{12,8},{16,20},{20,16},{24,28},{28,24},{1,5},{5... | collective-permute-start | bytes 393224 | tf_op jit(solution)/shard_map/ppermute | solution.py:296
  65.6 5.3 %collective-permute-start.18 = (bf16[16,4096]{1,0:T(8,128)(2,1)S(1)}, bf16[16,4096]{1,0:T(8,128)(2,1)S(1)}, u32[]{:S(2)}, u32[]{:S(2)}) collective-permute-start(bf16[16,4096]{1,0:T(8,128)(2,1)S(1)} %get-tuple-element.54.v_ref.refs_11_), channel_id=1, source_target_pairs={{0,8},{4,12},{8,0},{12,4},{16,24},{20,28},{24,16},{28,20},{1,9},{5... | collective-permute-start | bytes 393224 | tf_op jit(solution)/shard_map/ppermute | solution.py:296
  66.3 6.2 %collective-permute-start.17 = (bf16[16,4096]{1,0:T(8,128)(2,1)S(1)}, bf16[16,4096]{1,0:T(8,128)(2,1)S(1)}, u32[]{:S(2)}, u32[]{:S(2)}) collective-permute-start(bf16[16,4096]{1,0:T(8,128)(2,1)S(1)} %get-tuple-element.54.v_ref.refs_11_), channel_id=1, source_target_pairs={{0,12},{4,8},{8,4},{12,0},{16,28},{20,24},{24,20},{28,16},{1,13},{... | collective-permute-start | bytes 393224 | tf_op jit(solution)/shard_map/ppermute | solution.py:296
  73.7 3.2 %collective-permute-start.22 = (bf16[16,640]{1,0:T(8,128)(2,1)S(1)}, bf16[16,640]{1,0:T(8,128)(2,1)S(1)}, u32[]{:S(2)}, u32[]{:S(2)}) collective-permute-start(bf16[16,640]{1,0:T(8,128)(2,1)S(1)} %shard_map.77.refs_2_), channel_id=1, source_target_pairs={{0,3},{1,2},{2,1},{3,0},{4,7},{5,6},{6,5},{7,4},{8,11},{9,10},{10,... | collective-permute-start | bytes 61448 | tf_op jit(solution)/shard_map/ppermute | solution.py:296
  73.7 3.9 %collective-permute-start.21 = (bf16[16,640]{1,0:T(8,128)(2,1)S(1)}, bf16[16,640]{1,0:T(8,128)(2,1)S(1)}, u32[]{:S(2)}, u32[]{:S(2)}) collective-permute-start(bf16[16,640]{1,0:T(8,128)(2,1)S(1)} %shard_map.77.refs_2_), channel_id=1, source_target_pairs={{0,2},{1,3},{2,0},{3,1},{4,6},{5,7},{6,4},{7,5},{8,10},{9,11},{10,... | collective-permute-start | bytes 61448 | tf_op jit(solution)/shard_map/ppermute | solution.py:296
  75.0 2.5 %collective-permute-start.20 = (bf16[16,640]{1,0:T(8,128)(2,1)S(1)}, bf16[16,640]{1,0:T(8,128)(2,1)S(1)}, u32[]{:S(2)}, u32[]{:S(2)}) collective-permute-start(bf16[16,640]{1,0:T(8,128)(2,1)S(1)} %shard_map.77.refs_2_), channel_id=1, source_target_pairs={{0,1},{1,0},{2,3},{3,2},{4,5},{5,4},{6,7},{7,6},{8,9},{9,8},{10,11... | collective-permute-start | bytes 61448 | tf_op jit(solution)/shard_map/ppermute | solution.py:296
  78.5 5.9 %collective-permute-start.23 = (bf16[16,4224]{1,0:T(8,128)(2,1)S(1)}, bf16[16,4224]{1,0:T(8,128)(2,1)S(1)}, u32[]{:S(2)}, u32[]{:S(2)}) collective-permute-start(bf16[16,4224]{1,0:T(8,128)(2,1)S(1)} %shard_map.80), channel_id=1, source_target_pairs={{0,8},{4,12},{8,0},{12,4},{16,24},{20,28},{24,16},{28,20},{1,9},{5... | collective-permute-start | bytes 405512 | tf_op jit(solution)/shard_map/ppermute | solution.py:296
  80.3 8.2 %collective-permute-start.24 = (bf16[16,4224]{1,0:T(8,128)(2,1)S(1)}, bf16[16,4224]{1,0:T(8,128)(2,1)S(1)}, u32[]{:S(2)}, u32[]{:S(2)}) collective-permute-start(bf16[16,4224]{1,0:T(8,128)(2,1)S(1)} %shard_map.82), channel_id=1, source_target_pairs={{0,4},{4,0},{8,12},{12,8},{16,20},{20,16},{24,28},{28,24},{1,5},{5... | collective-permute-start | bytes 405512 | tf_op jit(solution)/shard_map/ppermute | solution.py:296
  82.2 6.3 %collective-permute-start.25 = (bf16[16,4224]{1,0:T(8,128)(2,1)S(1)}, bf16[16,4224]{1,0:T(8,128)(2,1)S(1)}, u32[]{:S(2)}, u32[]{:S(2)}) collective-permute-start(bf16[16,4224]{1,0:T(8,128)(2,1)S(1)} %shard_map.84), channel_id=1, source_target_pairs={{0,12},{4,8},{8,4},{12,0},{16,28},{20,24},{24,20},{28,16},{1,13},{... | collective-permute-start | bytes 405512 | tf_op jit(solution)/shard_map/ppermute | solution.py:296
  88.7 7.0 %collective-permute-start.26 = (bf16[16,4224]{1,0:T(8,128)(2,1)S(1)}, bf16[16,4224]{1,0:T(8,128)(2,1)S(1)}, u32[]{:S(2)}, u32[]{:S(2)}) collective-permute-start(bf16[16,4224]{1,0:T(8,128)(2,1)S(1)} %shard_map.85.refs_2_), channel_id=1, source_target_pairs={{0,24},{4,28},{8,16},{12,20},{16,8},{20,12},{24,0},{28,4},{1,25},{... | collective-permute-start | bytes 405512 | tf_op jit(solution)/shard_map/ppermute | solution.py:296
  95.8 5.3 %collective-permute-start.29 = (bf16[16,4096]{1,0:T(8,128)(2,1)S(1)}, bf16[16,4096]{1,0:T(8,128)(2,1)S(1)}, u32[]{:S(2)}, u32[]{:S(2)}) collective-permute-start(bf16[16,4096]{1,0:T(8,128)(2,1)S(1)} %get-tuple-element.61.v_ref.refs_15_), channel_id=1, source_target_pairs={{0,4},{4,0},{8,12},{12,8},{16,20},{20,16},{24,28},{28,24},{1,5},{5... | collective-permute-start | bytes 393224 | tf_op jit(solution)/shard_map/ppermute | solution.py:296
  97.0 5.2 %collective-permute-start.28 = (bf16[16,4096]{1,0:T(8,128)(2,1)S(1)}, bf16[16,4096]{1,0:T(8,128)(2,1)S(1)}, u32[]{:S(2)}, u32[]{:S(2)}) collective-permute-start(bf16[16,4096]{1,0:T(8,128)(2,1)S(1)} %get-tuple-element.61.v_ref.refs_15_), channel_id=1, source_target_pairs={{0,8},{4,12},{8,0},{12,4},{16,24},{20,28},{24,16},{28,20},{1,9},{5... | collective-permute-start | bytes 393224 | tf_op jit(solution)/shard_map/ppermute | solution.py:296
  97.9 5.9 %collective-permute-start.27 = (bf16[16,4096]{1,0:T(8,128)(2,1)S(1)}, bf16[16,4096]{1,0:T(8,128)(2,1)S(1)}, u32[]{:S(2)}, u32[]{:S(2)}) collective-permute-start(bf16[16,4096]{1,0:T(8,128)(2,1)S(1)} %get-tuple-element.61.v_ref.refs_15_), channel_id=1, source_target_pairs={{0,12},{4,8},{8,4},{12,0},{16,28},{20,24},{24,20},{28,16},{1,13},{... | collective-permute-start | bytes 393224 | tf_op jit(solution)/shard_map/ppermute | solution.py:296
  104.9 3.2 %collective-permute-start.32 = (bf16[16,640]{1,0:T(8,128)(2,1)S(1)}, bf16[16,640]{1,0:T(8,128)(2,1)S(1)}, u32[]{:S(2)}, u32[]{:S(2)}) collective-permute-start(bf16[16,640]{1,0:T(8,128)(2,1)S(1)} %shard_map.90.refs_2_), channel_id=1, source_target_pairs={{0,3},{1,2},{2,1},{3,0},{4,7},{5,6},{6,5},{7,4},{8,11},{9,10},{10,... | collective-permute-start | bytes 61448 | tf_op jit(solution)/shard_map/ppermute | solution.py:296
  104.9 3.9 %collective-permute-start.31 = (bf16[16,640]{1,0:T(8,128)(2,1)S(1)}, bf16[16,640]{1,0:T(8,128)(2,1)S(1)}, u32[]{:S(2)}, u32[]{:S(2)}) collective-permute-start(bf16[16,640]{1,0:T(8,128)(2,1)S(1)} %shard_map.90.refs_2_), channel_id=1, source_target_pairs={{0,2},{1,3},{2,0},{3,1},{4,6},{5,7},{6,4},{7,5},{8,10},{9,11},{10,... | collective-permute-start | bytes 61448 | tf_op jit(solution)/shard_map/ppermute | solution.py:296
  106.2 2.6 %collective-permute-start.30 = (bf16[16,640]{1,0:T(8,128)(2,1)S(1)}, bf16[16,640]{1,0:T(8,128)(2,1)S(1)}, u32[]{:S(2)}, u32[]{:S(2)}) collective-permute-start(bf16[16,640]{1,0:T(8,128)(2,1)S(1)} %shard_map.90.refs_2_), channel_id=1, source_target_pairs={{0,1},{1,0},{2,3},{3,2},{4,5},{5,4},{6,7},{7,6},{8,9},{9,8},{10,11... | collective-permute-start | bytes 61448 | tf_op jit(solution)/shard_map/ppermute | solution.py:296
  109.7 5.9 %collective-permute-start.33 = (bf16[16,4224]{1,0:T(8,128)(2,1)S(1)}, bf16[16,4224]{1,0:T(8,128)(2,1)S(1)}, u32[]{:S(2)}, u32[]{:S(2)}) collective-permute-start(bf16[16,4224]{1,0:T(8,128)(2,1)S(1)} %shard_map.93), channel_id=1, source_target_pairs={{0,8},{4,12},{8,0},{12,4},{16,24},{20,28},{24,16},{28,20},{1,9},{5... | collective-permute-start | bytes 405512 | tf_op jit(solution)/shard_map/ppermute | solution.py:296
  111.7 8.2 %collective-permute-start.34 = (bf16[16,4224]{1,0:T(8,128)(2,1)S(1)}, bf16[16,4224]{1,0:T(8,128)(2,1)S(1)}, u32[]{:S(2)}, u32[]{:S(2)}) collective-permute-start(bf16[16,4224]{1,0:T(8,128)(2,1)S(1)} %shard_map.95), channel_id=1, source_target_pairs={{0,4},{4,0},{8,12},{12,8},{16,20},{20,16},{24,28},{28,24},{1,5},{5... | collective-permute-start | bytes 405512 | tf_op jit(solution)/shard_map/ppermute | solution.py:296
  113.4 6.6 %collective-permute-start.35 = (bf16[16,4224]{1,0:T(8,128)(2,1)S(1)}, bf16[16,4224]{1,0:T(8,128)(2,1)S(1)}, u32[]{:S(2)}, u32[]{:S(2)}) collective-permute-start(bf16[16,4224]{1,0:T(8,128)(2,1)S(1)} %shard_map.97), channel_id=1, source_target_pairs={{0,12},{4,8},{8,4},{12,0},{16,28},{20,24},{24,20},{28,16},{1,13},{... | collective-permute-start | bytes 405512 | tf_op jit(solution)/shard_map/ppermute | solution.py:296
  120.1 7.0 %collective-permute-start.36 = (bf16[16,4224]{1,0:T(8,128)(2,1)S(1)}, bf16[16,4224]{1,0:T(8,128)(2,1)S(1)}, u32[]{:S(2)}, u32[]{:S(2)}) collective-permute-start(bf16[16,4224]{1,0:T(8,128)(2,1)S(1)} %shard_map.98.refs_2_), channel_id=1, source_target_pairs={{0,24},{4,28},{8,16},{12,20},{16,8},{20,12},{24,0},{28,4},{1,25},{... | collective-permute-start | bytes 405512 | tf_op jit(solution)/shard_map/ppermute | solution.py:296
  127.9 5.0 %collective-permute-start.39 = (bf16[16,4096]{1,0:T(8,128)(2,1)S(1)}, bf16[16,4096]{1,0:T(8,128)(2,1)S(1)}, u32[]{:S(2)}, u32[]{:S(2)}) collective-permute-start(bf16[16,4096]{1,0:T(8,128)(2,1)S(1)} %get-tuple-element.68.v_ref.refs_19_), channel_id=1, source_target_pairs={{0,4},{4,0},{8,12},{12,8},{16,20},{20,16},{24,28},{28,24},{1,5},{5... | collective-permute-start | bytes 393224 | tf_op jit(solution)/shard_map/ppermute | solution.py:296
  128.8 5.3 %collective-permute-start.38 = (bf16[16,4096]{1,0:T(8,128)(2,1)S(1)}, bf16[16,4096]{1,0:T(8,128)(2,1)S(1)}, u32[]{:S(2)}, u32[]{:S(2)}) collective-permute-start(bf16[16,4096]{1,0:T(8,128)(2,1)S(1)} %get-tuple-element.68.v_ref.refs_19_), channel_id=1, source_target_pairs={{0,8},{4,12},{8,0},{12,4},{16,24},{20,28},{24,16},{28,20},{1,9},{5... | collective-permute-start | bytes 393224 | tf_op jit(solution)/shard_map/ppermute | solution.py:296
  129.5 6.2 %collective-permute-start.37 = (bf16[16,4096]{1,0:T(8,128)(2,1)S(1)}, bf16[16,4096]{1,0:T(8,128)(2,1)S(1)}, u32[]{:S(2)}, u32[]{:S(2)}) collective-permute-start(bf16[16,4096]{1,0:T(8,128)(2,1)S(1)} %get-tuple-element.68.v_ref.refs_19_), channel_id=1, source_target_pairs={{0,12},{4,8},{8,4},{12,0},{16,28},{20,24},{24,20},{28,16},{1,13},{... | collective-permute-start | bytes 393224 | tf_op jit(solution)/shard_map/ppermute | solution.py:296
  134.1 15.0 %copy-start.1 = (f32[16,16384]{1,0:T(8,128)S(1)}, f32[16,16384]{1,0:T(8,128)}, u32[]{:S(2)}) copy-start(f32[16,16384]{1,0:T(8,128)} %start_ref.3) | copy-start | bytes 3145732
  136.9 3.2 %collective-permute-start.42 = (bf16[16,640]{1,0:T(8,128)(2,1)S(1)}, bf16[16,640]{1,0:T(8,128)(2,1)S(1)}, u32[]{:S(2)}, u32[]{:S(2)}) collective-permute-start(bf16[16,640]{1,0:T(8,128)(2,1)S(1)} %shard_map.103.refs_2_), channel_id=1, source_target_pairs={{0,3},{1,2},{2,1},{3,0},{4,7},{5,6},{6,5},{7,4},{8,11},{9,10},{10,... | collective-permute-start | bytes 61448 | tf_op jit(solution)/shard_map/ppermute | solution.py:296
  136.9 3.9 %collective-permute-start.41 = (bf16[16,640]{1,0:T(8,128)(2,1)S(1)}, bf16[16,640]{1,0:T(8,128)(2,1)S(1)}, u32[]{:S(2)}, u32[]{:S(2)}) collective-permute-start(bf16[16,640]{1,0:T(8,128)(2,1)S(1)} %shard_map.103.refs_2_), channel_id=1, source_target_pairs={{0,2},{1,3},{2,0},{3,1},{4,6},{5,7},{6,4},{7,5},{8,10},{9,11},{10,... | collective-permute-start | bytes 61448 | tf_op jit(solution)/shard_map/ppermute | solution.py:296
  138.2 2.6 %collective-permute-start.40 = (bf16[16,640]{1,0:T(8,128)(2,1)S(1)}, bf16[16,640]{1,0:T(8,128)(2,1)S(1)}, u32[]{:S(2)}, u32[]{:S(2)}) collective-permute-start(bf16[16,640]{1,0:T(8,128)(2,1)S(1)} %shard_map.103.refs_2_), channel_id=1, source_target_pairs={{0,1},{1,0},{2,3},{3,2},{4,5},{5,4},{6,7},{7,6},{8,9},{9,8},{10,11... | collective-permute-start | bytes 61448 | tf_op jit(solution)/shard_map/ppermute | solution.py:296
  140.9 5.6 %collective-permute-start.46 = (f32[16,128]{1,0:T(8,128)S(1)}, f32[16,128]{1,0:T(8,128)S(1)}, u32[]{:S(2)}, u32[]{:S(2)}) collective-permute-start(f32[16,128]{1,0:T(8,128)S(1)} %get-tuple-element.80.mine_ref), channel_id=1, source_target_pairs={{0,12},{1,29},{2,14},{3,31},{4,8},{5,25},{6,10},{7,27},{8,4},{9,21... | collective-permute-start | bytes 24584 | tf_op jit(solution)/shard_map/ppermute | solution.py:336
  142.5 4.1 %collective-permute-start.45 = (f32[16,128]{1,0:T(8,128)S(1)}, f32[16,128]{1,0:T(8,128)S(1)}, u32[]{:S(2)}, u32[]{:S(2)}) collective-permute-start(f32[16,128]{1,0:T(8,128)S(1)} %get-tuple-element.80.mine_ref), channel_id=1, source_target_pairs={{0,8},{1,25},{2,10},{3,27},{4,12},{5,29},{6,14},{7,31},{8,0},{9,17... | collective-permute-start | bytes 24584 | tf_op jit(solution)/shard_map/ppermute | solution.py:336
  143.3 3.7 %collective-permute-start.44 = (f32[16,128]{1,0:T(8,128)S(1)}, f32[16,128]{1,0:T(8,128)S(1)}, u32[]{:S(2)}, u32[]{:S(2)}) collective-permute-start(f32[16,128]{1,0:T(8,128)S(1)} %get-tuple-element.80.mine_ref), channel_id=1, source_target_pairs={{0,4},{1,21},{2,6},{3,23},{4,0},{5,17},{6,2},{7,19},{8,12},{9,29},... | collective-permute-start | bytes 24584 | tf_op jit(solution)/shard_map/ppermute | solution.py:336
  144.4 4.5 %collective-permute-start.43 = (f32[16,128]{1,0:T(8,128)S(1)}, f32[16,128]{1,0:T(8,128)S(1)}, u32[]{:S(2)}, u32[]{:S(2)}) collective-permute-start(f32[16,128]{1,0:T(8,128)S(1)} %get-tuple-element.80.mine_ref), channel_id=1, source_target_pairs={{0,16},{1,17},{2,18},{3,19},{4,20},{5,21},{6,22},{7,23},{8,24},{9,... | collective-permute-start | bytes 24584 | tf_op jit(solution)/shard_map/ppermute | solution.py:336
  149.0 1.2 collective-permute-start.47

commit v6 on v5

--- a/solution.py
+++ b/solution.py
@@ -9,6 +9,7 @@
 
 ITERS = 4
 EARLY = 4
+LIMIT = 8
 ADD_FLOPS = 1 << 28
 LANES = 128
 F32 = jnp.float32
@@ -21,7 +22,7 @@
     return jax.ShapeDtypeStruct(sizes, dtype)
 
 
-def call(body, out, args, specs=None, scratch=(), flops=0, aliases=None, out_specs=None):
+def call(body, out, args, specs=None, scratch=(), flops=0, aliases=None, out_specs=None, limit=LIMIT):
     return pl.pallas_call(
         body,
         out_shape=out,
@@ -29,7 +30,7 @@
         out_specs=out_specs or jax.tree.map(lambda _: VMEM, out),
         input_output_aliases=aliases or {},
         scratch_shapes=scratch,
-        compiler_params=pltpu.CompilerParams(vmem_limit_bytes=24 << 20),
+        compiler_params=pltpu.CompilerParams(vmem_limit_bytes=limit << 20),
         cost_estimate=pl.CostEstimate(flops=flops, bytes_accessed=1024, transcendentals=0),
     )(*args)
 
@@ -102,7 +103,7 @@
     first = pieces * EARLY // 16
     whole = shape(rows, columns, dtype=BF16)
     sems = [pltpu.SemaphoreType.DMA((pieces,))]
-    early = call(functools.partial(early_kernel, chunk, first), whole, (operator,), [ANY], sems)
+    early = call(functools.partial(early_kernel, chunk, first), whole, (operator,), [ANY], sems, limit=24)
     return call(
         functools.partial(load_kernel, chunk, first, pieces),
         (whole, shape(start.shape[0], rows, dtype=BF16)),
@@ -110,6 +111,7 @@
         [ANY, VMEM, VMEM],
         sems,
         aliases={2: 0},
+        limit=24,
     )
 
 
@@ -150,13 +152,27 @@
     )
 
 
-def forward_kernel(n_obs, near, distance, op_ref, v_ref, *refs):
+def turn_kernel(n_obs, near, distance, op_ref, out_ref):
+    width = out_ref.shape[0]
+    chunk = min(512, width)
+    base = place(n_obs, near, distance) * width
+    for first in range(0, width, chunk):
+        at = pl.ds(pl.multiple_of(base + first, chunk), chunk)
+        out_ref[first : first + chunk, :] = op_ref[:, at].T
+
+
+def turn(n_obs, near, distance, op):
+    rows, columns = op.shape
+    return call(
+        functools.partial(turn_kernel, n_obs, near, distance), shape(columns // near, rows, dtype=BF16), (op,)
+    )
+
+
+def forward_kernel(turned_ref, v_ref, *refs):
     out_ref = refs[-1]
-    width = v_ref.shape[1]
-    rows = op_ref.shape[0]
+    width, rows = turned_ref.shape
     v = v_ref[...]
-    at = pl.ds(pl.multiple_of(place(n_obs, near, distance) * width, width), width)
-    image = lax.dot_general(v, op_ref[:, at], (((1,), (1,)), ((), ())), preferred_element_type=F32)
+    image = jnp.dot(v, turned_ref[...], preferred_element_type=F32)
     wide = v.astype(F32)
     square = wide * wide
     norm = square[:, :LANES]
@@ -171,13 +187,9 @@
     out_ref[:, rows:] = norm
 
 
-def forward(n_obs, near, distance, dtype, op, v, *total):
-    scen, width = v.shape
-    rows = op.shape[0]
+def forward(dtype, turned, v, *total):
     return call(
-        functools.partial(forward_kernel, n_obs, near, distance),
-        shape(scen, rows + LANES, dtype=dtype),
-        (op, v, *total),
+        forward_kernel, shape(v.shape[0], turned.shape[1] + LANES, dtype=dtype), (turned, v, *total)
     )
 
 
@@ -234,8 +246,10 @@
         out_ref[:, width:] = pack_norm(tree([unpack_norm(ref[:, width:]) for ref in got_refs]))
 
 
-def gradient_kernel(later, *refs):
+def gradient_kernel(later, before, *refs):
     *ins, gradient_ref, rounded_ref, alpha_ref = refs
+    if not later:
+        ins = ins[before:]
     if later:
         old_ref, gamma_ref, *ins = ins
     width = gradient_ref.shape[1]
@@ -269,27 +283,25 @@
             solution_ref[:, at] = solution
 
 
-def last_kernel(parts, chunk, gamma_ref, direction_ref, base_ref, residual_ref, *refs):
-    *ins, out_hbm, out_residual_ref, out_ref, sems = refs
+def last_kernel(parts, gamma_ref, direction_ref, base_ref, residual_ref, *refs):
+    *ins, out_ref, out_residual_ref = refs
     norms = ins[:parts]
     alphas = ins[parts : parts + ITERS - 1]
     images = ins[parts + ITERS - 1 :]
     alpha = gamma_ref[...] / tree([ref[...] for ref in norms])
-    wide = jnp.concatenate([alpha] * (chunk // LANES), axis=1)
-    copies = []
-    for k in range(out_ref.shape[1] // chunk):
-        at = pl.ds(k * chunk, chunk)
-        out_ref[:, at] = base_ref[:, at] + wide * direction_ref[:, at]
-        copies.append(pltpu.make_async_copy(out_ref.at[:, at], out_hbm.at[:, at], sems.at[k]))
-        copies[-1].start()
+
+    def step(k, _):
+        at = pl.ds(pl.multiple_of(k * LANES, LANES), LANES)
+        out_ref[:, at] = base_ref[:, at] + alpha * direction_ref[:, at]
+        return 0
+
+    lax.fori_loop(0, out_ref.shape[1] // LANES, step, 0, unroll=8)
     residual = residual_ref[...]
     rows = residual.shape[1]
     for index in range(ITERS):
         factor = alpha if index == ITERS - 1 else alphas[index][...]
         residual -= jnp.concatenate([factor] * (rows // LANES), axis=1) * images[index][...]
     out_residual_ref[...] = residual
-    for copy in copies:
-        copy.wait()
 
 
 def exchange(value, axis, size, distance):
@@ -365,12 +377,13 @@
 
     def image_parts(mine):
         got = {d: exchange(mine, "obs", n_obs, d) for d in range(1, near)}
-        total = forward(n_obs, near, 0, F32, op, mine)
+        total = forward(F32, turned[0], mine)
         for d in got:
-            total = forward(n_obs, near, d, BF16 if d == near - 1 else F32, op, got[d], total)
+            total = forward(BF16 if d == near - 1 else F32, turned[d], got[d], total)
         return parts_over(total, "par", n_par, True), [mine] + [got[d] for d in range(1, near)]
 
     op, first = load(operator, start)
+    turned = [turn(n_obs, near, d, op) for d in range(near)]
     packed_lanes = shape(scen, LANES, dtype=BF16)
     residual, w, norm, packed = call(
         first_kernel, (image_shape, term_shape, lanes, packed_lanes), (targets, *parts_over(first, "par", n_par, False))
@@ -380,9 +393,10 @@
     for index in range(ITERS):
         parts = gradient_parts(w, norm, packed)
         gradient, rounded, alpha = call(
-            functools.partial(gradient_kernel, index > 0),
+            functools.partial(gradient_kernel, index > 0, near),
             (shape(scen, width), shape(scen, width, dtype=BF16), lanes),
-            ((gradient, gamma) if index else ()) + tuple(parts),
+            ((gradient, gamma) if index else tuple(turned)) + tuple(parts),
+            None if index else [ANY] * near + [VMEM] * len(parts),
         )
         alphas += [alpha] if index else []
         parts, got = image_parts(rounded)
@@ -404,13 +418,10 @@
         (shape(scen, columns), shape(scen, columns)),
         (start, *alphas, *betas, *pieces),
     )
-    chunk = min(2048, columns)
     return call(
-        functools.partial(last_kernel, len(norms), chunk),
+        functools.partial(last_kernel, len(norms)),
         (shape(scen, columns), image_shape),
         (gamma, direction, base, residual, *norms, *alphas, *images),
-        scratch=[pltpu.VMEM((scen, columns), F32), pltpu.SemaphoreType.DMA((columns // chunk,))],
-        out_specs=(ANY, VMEM),
     )
 
 

time: 152 us -> 150 us (0.987)
  Pallas kernels: 44.9 us -> 40.3 us
  waiting for transfers between devices: 50.8 us -> 54.3 us
    pallas_call x58 -> x62, Pallas kernels: 44.9 us -> 40.3 us  [call(): pl.pallas_call(body, out_shape=out, in_specs=specs if specs is not None e...]
    ppermute x44, waiting for transfers between devices: 48.4 us -> 51.7 us  [exchange(): return lax.ppermute(value, axis, [(i, i ^ distance) for i in range(size)])]
  transfers between devices with their start and end apart: 48 -> 48, of which waited for: 31 -> 32; matrix products, arithmetic and copies ran while one was open for 0% -> 0% of each run, Pallas kernels for 16% -> 15%
where the time goes in v6:
time: 150 us
  waiting for transfers between devices  54.3 us (36%)
  starting transfers between devices  54.2 us (36%)
  Pallas kernels  40.3 us (27%)
    ppermute x44, waiting for transfers between devices, exchange(): return lax.ppermute(value, axis, [(i, i ^ distance) for i in range(size)])  51.7 us
    ppermute x44, starting transfers between devices, exchange(): return lax.ppermute(value, axis, [(i, i ^ distance) for i in range(size)])  48.8 us
    pallas_call x62, Pallas kernels, call(): pl.pallas_call(body, out_shape=out, in_specs=specs if specs is not None e...  40.3 us
    ppermute x4, starting transfers between devices, norm_parts(): got.append(lax.ppermute(norm, ('obs', 'par'), pairs))  5.4 us
  transfers between devices with their start and end apart: 48, of which 32 were waited for; matrix products, arithmetic and copies ran while one was open for 0% of the time, Pallas kernels for 15%

profile of v6, /device:TPU:0, one launch (start us, length us, event | category | flops | bytes accessed | tf_op | source)
XLA Modules:
  0.0 149.7 jit_solution(3437707339818277946)
XLA Ops:
  0.6 2.4 %shard_map.50.early_ref = bf16[512,16384]{1,0:T(8,128)(2,1)S(1)} custom-call(bf16[512,16384]{1,0:T(8,128)(2,1)} %op_hbm.3), custom_call_target="tpu_custom_call" | custom-call | bytes 1024 | tf_op jit(solution)/shard_map/pallas_call | solution.py:26
  3.1 5.2 %shard_map.51 = (bf16[512,16384]{1,0:T(8,128)(2,1)S(1)}, bf16[16,512]{1,0:T(8,128)(2,1)S(1)}) custom-call(bf16[512,16384]{1,0:T(8,128)(2,1)} %op_hbm.3, f32[16,16384]{1,0:T(8,128)S(1)} %copy-done, bf16[512,16384]{1,0:T(8,128)(2,1)S(1)} %shard_map.50.early_ref), custom_call_target="tpu_custom_call", output_to_operand_aliasing={{0}: (2, {})} | custom-call | bytes 1024 | tf_op jit(solution)/shard_map/pallas_call | solution.py:26
  8.3 2.5 %collective-permute-start.2 = (bf16[16,512]{1,0:T(8,128)(2,1)S(1)}, bf16[16,512]{1,0:T(8,128)(2,1)S(1)}, u32[]{:S(2)}, u32[]{:S(2)}) collective-permute-start(bf16[16,512]{1,0:T(8,128)(2,1)S(1)} %get-tuple-element.43.refs_0_), channel_id=1, source_target_pairs={{0,3},{1,2},{2,1},{3,0},{4,7},{5,6},{6,5},{7,4},{8,11},{9,10},{10,... | collective-permute-start | bytes 49160 | tf_op jit(solution)/shard_map/ppermute | solution.py:308
  12.2 2.3 %collective-permute-done.1.refs_2_ = bf16[16,512]{1,0:T(8,128)(2,1)S(1)} collective-permute-done((bf16[16,512]{1,0:T(8,128)(2,1)S(1)}, bf16[16,512]{1,0:T(8,128)(2,1)S(1)}, u32[]{:S(2)}, u32[]{:S(2)}) %collective-permute-start.1) | collective-permute-done | bytes 16416 | tf_op jit(solution)/shard_map/ppermute | solution.py:308
  14.6 0.8 shard_map.58
  15.4 1.6 %collective-permute-start.3 = (bf16[16,4224]{1,0:T(8,128)(2,1)S(1)}, bf16[16,4224]{1,0:T(8,128)(2,1)S(1)}, u32[]{:S(2)}, u32[]{:S(2)}) collective-permute-start(bf16[16,4224]{1,0:T(8,128)(2,1)S(1)} %shard_map.58), channel_id=1, source_target_pairs={{0,8},{4,12},{8,0},{12,4},{16,24},{20,28},{24,16},{28,20},{1,9},{5... | collective-permute-start | bytes 405512 | tf_op jit(solution)/shard_map/ppermute | solution.py:308
  17.7 1.5 %collective-permute-start.4 = (bf16[16,4224]{1,0:T(8,128)(2,1)S(1)}, bf16[16,4224]{1,0:T(8,128)(2,1)S(1)}, u32[]{:S(2)}, u32[]{:S(2)}) collective-permute-start(bf16[16,4224]{1,0:T(8,128)(2,1)S(1)} %shard_map.60), channel_id=1, source_target_pairs={{0,4},{4,0},{8,12},{12,8},{16,20},{20,16},{24,28},{28,24},{1,5},{5... | collective-permute-start | bytes 405512 | tf_op jit(solution)/shard_map/ppermute | solution.py:308
  21.3 3.4 %collective-permute-done.4.got_ref.refs_1_ = bf16[16,4224]{1,0:T(8,128)(2,1)S(1)} collective-permute-done((bf16[16,4224]{1,0:T(8,128)(2,1)S(1)}, bf16[16,4224]{1,0:T(8,128)(2,1)S(1)}, u32[]{:S(2)}, u32[]{:S(2)}) %collective-permute-start.4) | collective-permute-done | bytes 135200 | tf_op jit(solution)/shard_map/ppermute | solution.py:308
  24.7 1.2 collective-permute-done.5.refs_2_
  26.1 2.5 %collective-permute-start.6 = (bf16[16,4224]{1,0:T(8,128)(2,1)S(1)}, bf16[16,4224]{1,0:T(8,128)(2,1)S(1)}, u32[]{:S(2)}, u32[]{:S(2)}) collective-permute-start(bf16[16,4224]{1,0:T(8,128)(2,1)S(1)} %shard_map.63.refs_4_), channel_id=1, source_target_pairs={{0,24},{4,28},{8,16},{12,20},{16,8},{20,12},{24,0},{28,4},{1,25},{... | collective-permute-start | bytes 405512 | tf_op jit(solution)/shard_map/ppermute | solution.py:308
  28.6 1.1 shard_map.55.refs_2_.turned_ref
  29.7 1.1 shard_map.54.refs_1_.turned_ref
  30.9 1.1 shard_map.53.refs_0_.turned_ref
  32.0 1.1 shard_map.52.refs_3_.turned_ref
  33.8 1.2 collective-permute-start.9
  35.7 1.6 %collective-permute-start.7 = (bf16[16,4096]{1,0:T(8,128)(2,1)S(1)}, bf16[16,4096]{1,0:T(8,128)(2,1)S(1)}, u32[]{:S(2)}, u32[]{:S(2)}) collective-permute-start(bf16[16,4096]{1,0:T(8,128)(2,1)S(1)} %get-tuple-element.47.v_ref.refs_7_), channel_id=1, source_target_pairs={{0,12},{4,8},{8,4},{12,0},{16,28},{20,24},{24,20},{28,16},{1,13},{... | collective-permute-start | bytes 393224 | tf_op jit(solution)/shard_map/ppermute | solution.py:308
  37.9 1.5 %collective-permute-done.9.v_ref.refs_8_ = bf16[16,4096]{1,0:T(8,128)(2,1)S(1)} collective-permute-done((bf16[16,4096]{1,0:T(8,128)(2,1)S(1)}, bf16[16,4096]{1,0:T(8,128)(2,1)S(1)}, u32[]{:S(2)}, u32[]{:S(2)}) %collective-permute-start.9) | collective-permute-done | bytes 131104 | tf_op jit(solution)/shard_map/ppermute | solution.py:308
  40.7 0.9 collective-permute-done.7.v_ref.refs_10_
  43.0 1.2 collective-permute-start.10
  44.2 1.3 collective-permute-done.12.refs_3_
  46.2 0.8 shard_map.71
  47.0 1.3 collective-permute-start.13
  48.4 0.9 shard_map.73
  49.3 0.8 collective-permute-start.14
  50.9 1.4 collective-permute-start.15
  53.2 4.1 %collective-permute-done.14.got_ref.refs_1_ = bf16[16,4224]{1,0:T(8,128)(2,1)S(1)} collective-permute-done((bf16[16,4224]{1,0:T(8,128)(2,1)S(1)}, bf16[16,4224]{1,0:T(8,128)(2,1)S(1)}, u32[]{:S(2)}, u32[]{:S(2)}) %collective-permute-start.14) | collective-permute-done | bytes 135200 | tf_op jit(solution)/shard_map/ppermute | solution.py:308
  57.4 2.4 %collective-permute-start.16 = (bf16[16,4224]{1,0:T(8,128)(2,1)S(1)}, bf16[16,4224]{1,0:T(8,128)(2,1)S(1)}, u32[]{:S(2)}, u32[]{:S(2)}) collective-permute-start(bf16[16,4224]{1,0:T(8,128)(2,1)S(1)} %shard_map.76.refs_2_), channel_id=1, source_target_pairs={{0,24},{4,28},{8,16},{12,20},{16,8},{20,12},{24,0},{28,4},{1,25},{... | collective-permute-start | bytes 405512 | tf_op jit(solution)/shard_map/ppermute | solution.py:308
  59.7 4.5 %collective-permute-done.16.refs_3_ = bf16[16,4224]{1,0:T(8,128)(2,1)S(1)} collective-permute-done((bf16[16,4224]{1,0:T(8,128)(2,1)S(1)}, bf16[16,4224]{1,0:T(8,128)(2,1)S(1)}, u32[]{:S(2)}, u32[]{:S(2)}) %collective-permute-start.16) | collective-permute-done | bytes 135200 | tf_op jit(solution)/shard_map/ppermute | solution.py:308
  64.4 1.0 collective-permute-start.19
  66.1 1.9 %collective-permute-start.17 = (bf16[16,4096]{1,0:T(8,128)(2,1)S(1)}, bf16[16,4096]{1,0:T(8,128)(2,1)S(1)}, u32[]{:S(2)}, u32[]{:S(2)}) collective-permute-start(bf16[16,4096]{1,0:T(8,128)(2,1)S(1)} %get-tuple-element.54.v_ref.refs_11_), channel_id=1, source_target_pairs={{0,12},{4,8},{8,4},{12,0},{16,28},{20,24},{24,20},{28,16},{1,13},{... | collective-permute-start | bytes 393224 | tf_op jit(solution)/shard_map/ppermute | solution.py:308
  68.6 0.8 collective-permute-done.19.v_ref.refs_12_
  70.9 1.3 collective-permute-done.17.v_ref.refs_14_
  72.9 1.3 collective-permute-start.21
  74.8 1.4 collective-permute-done.22.refs_5_
  77.7 1.0 collective-permute-start.23
  79.5 1.2 collective-permute-start.24
  81.4 1.4 collective-permute-start.25
  83.7 4.0 %collective-permute-done.24.got_ref.refs_1_ = bf16[16,4224]{1,0:T(8,128)(2,1)S(1)} collective-permute-done((bf16[16,4224]{1,0:T(8,128)(2,1)S(1)}, bf16[16,4224]{1,0:T(8,128)(2,1)S(1)}, u32[]{:S(2)}, u32[]{:S(2)}) %collective-permute-start.24) | collective-permute-done | bytes 135200 | tf_op jit(solution)/shard_map/ppermute | solution.py:308
  87.9 2.6 %collective-permute-start.26 = (bf16[16,4224]{1,0:T(8,128)(2,1)S(1)}, bf16[16,4224]{1,0:T(8,128)(2,1)S(1)}, u32[]{:S(2)}, u32[]{:S(2)}) collective-permute-start(bf16[16,4224]{1,0:T(8,128)(2,1)S(1)} %shard_map.89.refs_2_), channel_id=1, source_target_pairs={{0,24},{4,28},{8,16},{12,20},{16,8},{20,12},{24,0},{28,4},{1,25},{... | collective-permute-start | bytes 405512 | tf_op jit(solution)/shard_map/ppermute | solution.py:308
  90.5 4.4 %collective-permute-done.26.refs_3_ = bf16[16,4224]{1,0:T(8,128)(2,1)S(1)} collective-permute-done((bf16[16,4224]{1,0:T(8,128)(2,1)S(1)}, bf16[16,4224]{1,0:T(8,128)(2,1)S(1)}, u32[]{:S(2)}, u32[]{:S(2)}) %collective-permute-start.26) | collective-permute-done | bytes 135200 | tf_op jit(solution)/shard_map/ppermute | solution.py:308
  95.0 1.2 collective-permute-start.29
  96.9 1.6 %collective-permute-start.27 = (bf16[16,4096]{1,0:T(8,128)(2,1)S(1)}, bf16[16,4096]{1,0:T(8,128)(2,1)S(1)}, u32[]{:S(2)}, u32[]{:S(2)}) collective-permute-start(bf16[16,4096]{1,0:T(8,128)(2,1)S(1)} %get-tuple-element.61.v_ref.refs_15_), channel_id=1, source_target_pairs={{0,12},{4,8},{8,4},{12,0},{16,28},{20,24},{24,20},{28,16},{1,13},{... | collective-permute-start | bytes 393224 | tf_op jit(solution)/shard_map/ppermute | solution.py:308
  99.2 1.1 collective-permute-done.29.v_ref.refs_16_
  101.8 1.0 collective-permute-done.27.v_ref.refs_18_
  103.5 1.3 collective-permute-start.31
  105.4 1.4 collective-permute-done.32.refs_5_
  108.4 1.3 collective-permute-start.33
  112.0 1.4 collective-permute-start.35
  114.3 4.4 %collective-permute-done.34.got_ref.refs_1_ = bf16[16,4224]{1,0:T(8,128)(2,1)S(1)} collective-permute-done((bf16[16,4224]{1,0:T(8,128)(2,1)S(1)}, bf16[16,4224]{1,0:T(8,128)(2,1)S(1)}, u32[]{:S(2)}, u32[]{:S(2)}) %collective-permute-start.34) | collective-permute-done | bytes 135200 | tf_op jit(solution)/shard_map/ppermute | solution.py:308
  118.9 2.5 %collective-permute-start.36 = (bf16[16,4224]{1,0:T(8,128)(2,1)S(1)}, bf16[16,4224]{1,0:T(8,128)(2,1)S(1)}, u32[]{:S(2)}, u32[]{:S(2)}) collective-permute-start(bf16[16,4224]{1,0:T(8,128)(2,1)S(1)} %shard_map.102.refs_2_), channel_id=1, source_target_pairs={{0,24},{4,28},{8,16},{12,20},{16,8},{20,12},{24,0},{28,4},{1,25},{... | collective-permute-start | bytes 405512 | tf_op jit(solution)/shard_map/ppermute | solution.py:308
  121.4 4.5 %collective-permute-done.36.refs_3_ = bf16[16,4224]{1,0:T(8,128)(2,1)S(1)} collective-permute-done((bf16[16,4224]{1,0:T(8,128)(2,1)S(1)}, bf16[16,4224]{1,0:T(8,128)(2,1)S(1)}, u32[]{:S(2)}, u32[]{:S(2)}) %collective-permute-start.36) | collective-permute-done | bytes 135200 | tf_op jit(solution)/shard_map/ppermute | solution.py:308
  125.8 0.8 shard_map.103
  126.7 0.9 collective-permute-start.39
  128.3 1.9 %collective-permute-start.37 = (bf16[16,4096]{1,0:T(8,128)(2,1)S(1)}, bf16[16,4096]{1,0:T(8,128)(2,1)S(1)}, u32[]{:S(2)}, u32[]{:S(2)}) collective-permute-start(bf16[16,4096]{1,0:T(8,128)(2,1)S(1)} %get-tuple-element.68.v_ref.refs_19_), channel_id=1, source_target_pairs={{0,12},{4,8},{8,4},{12,0},{16,28},{20,24},{24,20},{28,16},{1,13},{... | collective-permute-start | bytes 393224 | tf_op jit(solution)/shard_map/ppermute | solution.py:308
  130.8 0.9 collective-permute-done.39.v_ref.refs_20_
  133.1 1.4 collective-permute-done.37.v_ref.refs_22_
  135.1 1.2 collective-permute-start.41
  137.0 1.3 collective-permute-done.42.refs_5_
  139.2 1.5 %collective-permute-start.46 = (f32[16,128]{1,0:T(8,128)S(1)}, f32[16,128]{1,0:T(8,128)S(1)}, u32[]{:S(2)}, u32[]{:S(2)}) collective-permute-start(f32[16,128]{1,0:T(8,128)S(1)} %get-tuple-element.80.mine_ref), channel_id=1, source_target_pairs={{0,12},{1,29},{2,14},{3,31},{4,8},{5,25},{6,10},{7,27},{8,4},{9,21... | collective-permute-start | bytes 24584 | tf_op jit(solution)/shard_map/ppermute | solution.py:348
  140.7 0.8 collective-permute-start.45
  141.5 1.2 collective-permute-start.44
  142.6 1.9 %collective-permute-start.43 = (f32[16,128]{1,0:T(8,128)S(1)}, f32[16,128]{1,0:T(8,128)S(1)}, u32[]{:S(2)}, u32[]{:S(2)}) collective-permute-start(f32[16,128]{1,0:T(8,128)S(1)} %get-tuple-element.80.mine_ref), channel_id=1, source_target_pairs={{0,16},{1,17},{2,18},{3,19},{4,20},{5,21},{6,22},{7,23},{8,24},{9,... | collective-permute-start | bytes 24584 | tf_op jit(solution)/shard_map/ppermute | solution.py:348
  145.1 2.1 %collective-permute-done.43.refs_0_ = f32[16,128]{1,0:T(8,128)S(1)} collective-permute-done((f32[16,128]{1,0:T(8,128)S(1)}, f32[16,128]{1,0:T(8,128)S(1)}, u32[]{:S(2)}, u32[]{:S(2)}) %collective-permute-start.43) | collective-permute-done | bytes 8224 | tf_op jit(solution)/shard_map/ppermute | solution.py:348
  148.4 1.4 shard_map.111
  (98 shorter events, 35.9 us)
Async XLA Ops:
  0.6 2.5 %copy-start = (f32[16,16384]{1,0:T(8,128)S(1)}, f32[16,16384]{1,0:T(8,128)}, u32[]{:S(2)}) copy-start(f32[16,16384]{1,0:T(8,128)} %start_ref.3) | copy-start | bytes 3145732
  3.1 11.4 %copy-start.1 = (f32[16,512]{1,0:T(8,128)S(1)}, f32[16,512]{1,0:T(8,128)}, u32[]{:S(2)}) copy-start(f32[16,512]{1,0:T(8,128)} %targets_ref.1) | copy-start | bytes 98308
  8.3 3.9 %collective-permute-start.2 = (bf16[16,512]{1,0:T(8,128)(2,1)S(1)}, bf16[16,512]{1,0:T(8,128)(2,1)S(1)}, u32[]{:S(2)}, u32[]{:S(2)}) collective-permute-start(bf16[16,512]{1,0:T(8,128)(2,1)S(1)} %get-tuple-element.43.refs_0_), channel_id=1, source_target_pairs={{0,3},{1,2},{2,1},{3,0},{4,7},{5,6},{6,5},{7,4},{8,11},{9,10},{10,... | collective-permute-start | bytes 49160 | tf_op jit(solution)/shard_map/ppermute | solution.py:308
  10.8 3.7 %collective-permute-start.1 = (bf16[16,512]{1,0:T(8,128)(2,1)S(1)}, bf16[16,512]{1,0:T(8,128)(2,1)S(1)}, u32[]{:S(2)}, u32[]{:S(2)}) collective-permute-start(bf16[16,512]{1,0:T(8,128)(2,1)S(1)} %get-tuple-element.43.refs_0_), channel_id=1, source_target_pairs={{0,2},{1,3},{2,0},{3,1},{4,6},{5,7},{6,4},{7,5},{8,10},{9,11},{10,... | collective-permute-start | bytes 49160 | tf_op jit(solution)/shard_map/ppermute | solution.py:308
  11.4 3.1 %collective-permute-start = (bf16[16,512]{1,0:T(8,128)(2,1)S(1)}, bf16[16,512]{1,0:T(8,128)(2,1)S(1)}, u32[]{:S(2)}, u32[]{:S(2)}) collective-permute-start(bf16[16,512]{1,0:T(8,128)(2,1)S(1)} %get-tuple-element.43.refs_0_), channel_id=1, source_target_pairs={{0,1},{1,0},{2,3},{3,2},{4,5},{5,4},{6,7},{7,6},{8,9},{9,8},{10,11... | collective-permute-start | bytes 49160 | tf_op jit(solution)/shard_map/ppermute | solution.py:308
  15.4 5.9 %collective-permute-start.3 = (bf16[16,4224]{1,0:T(8,128)(2,1)S(1)}, bf16[16,4224]{1,0:T(8,128)(2,1)S(1)}, u32[]{:S(2)}, u32[]{:S(2)}) collective-permute-start(bf16[16,4224]{1,0:T(8,128)(2,1)S(1)} %shard_map.58), channel_id=1, source_target_pairs={{0,8},{4,12},{8,0},{12,4},{16,24},{20,28},{24,16},{28,20},{1,9},{5... | collective-permute-start | bytes 405512 | tf_op jit(solution)/shard_map/ppermute | solution.py:308
  17.7 7.0 %collective-permute-start.4 = (bf16[16,4224]{1,0:T(8,128)(2,1)S(1)}, bf16[16,4224]{1,0:T(8,128)(2,1)S(1)}, u32[]{:S(2)}, u32[]{:S(2)}) collective-permute-start(bf16[16,4224]{1,0:T(8,128)(2,1)S(1)} %shard_map.60), channel_id=1, source_target_pairs={{0,4},{4,0},{8,12},{12,8},{16,20},{20,16},{24,28},{28,24},{1,5},{5... | collective-permute-start | bytes 405512 | tf_op jit(solution)/shard_map/ppermute | solution.py:308
  20.0 5.9 %collective-permute-start.5 = (bf16[16,4224]{1,0:T(8,128)(2,1)S(1)}, bf16[16,4224]{1,0:T(8,128)(2,1)S(1)}, u32[]{:S(2)}, u32[]{:S(2)}) collective-permute-start(bf16[16,4224]{1,0:T(8,128)(2,1)S(1)} %shard_map.62), channel_id=1, source_target_pairs={{0,12},{4,8},{8,4},{12,0},{16,28},{20,24},{24,20},{28,16},{1,13},{... | collective-permute-start | bytes 405512 | tf_op jit(solution)/shard_map/ppermute | solution.py:308
  26.1 7.1 %collective-permute-start.6 = (bf16[16,4224]{1,0:T(8,128)(2,1)S(1)}, bf16[16,4224]{1,0:T(8,128)(2,1)S(1)}, u32[]{:S(2)}, u32[]{:S(2)}) collective-permute-start(bf16[16,4224]{1,0:T(8,128)(2,1)S(1)} %shard_map.63.refs_4_), channel_id=1, source_target_pairs={{0,24},{4,28},{8,16},{12,20},{16,8},{20,12},{24,0},{28,4},{1,25},{... | collective-permute-start | bytes 405512 | tf_op jit(solution)/shard_map/ppermute | solution.py:308
  33.8 5.6 %collective-permute-start.9 = (bf16[16,4096]{1,0:T(8,128)(2,1)S(1)}, bf16[16,4096]{1,0:T(8,128)(2,1)S(1)}, u32[]{:S(2)}, u32[]{:S(2)}) collective-permute-start(bf16[16,4096]{1,0:T(8,128)(2,1)S(1)} %get-tuple-element.47.v_ref.refs_7_), channel_id=1, source_target_pairs={{0,4},{4,0},{8,12},{12,8},{16,20},{20,16},{24,28},{28,24},{1,5},{5... | collective-permute-start | bytes 393224 | tf_op jit(solution)/shard_map/ppermute | solution.py:308
  35.0 5.0 %collective-permute-start.8 = (bf16[16,4096]{1,0:T(8,128)(2,1)S(1)}, bf16[16,4096]{1,0:T(8,128)(2,1)S(1)}, u32[]{:S(2)}, u32[]{:S(2)}) collective-permute-start(bf16[16,4096]{1,0:T(8,128)(2,1)S(1)} %get-tuple-element.47.v_ref.refs_7_), channel_id=1, source_target_pairs={{0,8},{4,12},{8,0},{12,4},{16,24},{20,28},{24,16},{28,20},{1,9},{5... | collective-permute-start | bytes 393224 | tf_op jit(solution)/shard_map/ppermute | solution.py:308
  35.7 5.9 %collective-permute-start.7 = (bf16[16,4096]{1,0:T(8,128)(2,1)S(1)}, bf16[16,4096]{1,0:T(8,128)(2,1)S(1)}, u32[]{:S(2)}, u32[]{:S(2)}) collective-permute-start(bf16[16,4096]{1,0:T(8,128)(2,1)S(1)} %get-tuple-element.47.v_ref.refs_7_), channel_id=1, source_target_pairs={{0,12},{4,8},{8,4},{12,0},{16,28},{20,24},{24,20},{28,16},{1,13},{... | collective-permute-start | bytes 393224 | tf_op jit(solution)/shard_map/ppermute | solution.py:308
  42.3 3.2 %collective-permute-start.12 = (bf16[16,640]{1,0:T(8,128)(2,1)S(1)}, bf16[16,640]{1,0:T(8,128)(2,1)S(1)}, u32[]{:S(2)}, u32[]{:S(2)}) collective-permute-start(bf16[16,640]{1,0:T(8,128)(2,1)S(1)} %shard_map.68.refs_0_), channel_id=1, source_target_pairs={{0,3},{1,2},{2,1},{3,0},{4,7},{5,6},{6,5},{7,4},{8,11},{9,10},{10,... | collective-permute-start | bytes 61448 | tf_op jit(solution)/shard_map/ppermute | solution.py:308
  42.3 3.8 %collective-permute-start.11 = (bf16[16,640]{1,0:T(8,128)(2,1)S(1)}, bf16[16,640]{1,0:T(8,128)(2,1)S(1)}, u32[]{:S(2)}, u32[]{:S(2)}) collective-permute-start(bf16[16,640]{1,0:T(8,128)(2,1)S(1)} %shard_map.68.refs_0_), channel_id=1, source_target_pairs={{0,2},{1,3},{2,0},{3,1},{4,6},{5,7},{6,4},{7,5},{8,10},{9,11},{10,... | collective-permute-start | bytes 61448 | tf_op jit(solution)/shard_map/ppermute | solution.py:308
  43.0 3.1 %collective-permute-start.10 = (bf16[16,640]{1,0:T(8,128)(2,1)S(1)}, bf16[16,640]{1,0:T(8,128)(2,1)S(1)}, u32[]{:S(2)}, u32[]{:S(2)}) collective-permute-start(bf16[16,640]{1,0:T(8,128)(2,1)S(1)} %shard_map.68.refs_0_), channel_id=1, source_target_pairs={{0,1},{1,0},{2,3},{3,2},{4,5},{5,4},{6,7},{7,6},{8,9},{9,8},{10,11... | collective-permute-start | bytes 61448 | tf_op jit(solution)/shard_map/ppermute | solution.py:308
  47.0 6.1 %collective-permute-start.13 = (bf16[16,4224]{1,0:T(8,128)(2,1)S(1)}, bf16[16,4224]{1,0:T(8,128)(2,1)S(1)}, u32[]{:S(2)}, u32[]{:S(2)}) collective-permute-start(bf16[16,4224]{1,0:T(8,128)(2,1)S(1)} %shard_map.71), channel_id=1, source_target_pairs={{0,8},{4,12},{8,0},{12,4},{16,24},{20,28},{24,16},{28,20},{1,9},{5... | collective-permute-start | bytes 405512 | tf_op jit(solution)/shard_map/ppermute | solution.py:308
  49.3 7.9 %collective-permute-start.14 = (bf16[16,4224]{1,0:T(8,128)(2,1)S(1)}, bf16[16,4224]{1,0:T(8,128)(2,1)S(1)}, u32[]{:S(2)}, u32[]{:S(2)}) collective-permute-start(bf16[16,4224]{1,0:T(8,128)(2,1)S(1)} %shard_map.73), channel_id=1, source_target_pairs={{0,4},{4,0},{8,12},{12,8},{16,20},{20,16},{24,28},{28,24},{1,5},{5... | collective-permute-start | bytes 405512 | tf_op jit(solution)/shard_map/ppermute | solution.py:308
  50.9 6.4 %collective-permute-start.15 = (bf16[16,4224]{1,0:T(8,128)(2,1)S(1)}, bf16[16,4224]{1,0:T(8,128)(2,1)S(1)}, u32[]{:S(2)}, u32[]{:S(2)}) collective-permute-start(bf16[16,4224]{1,0:T(8,128)(2,1)S(1)} %shard_map.75), channel_id=1, source_target_pairs={{0,12},{4,8},{8,4},{12,0},{16,28},{20,24},{24,20},{28,16},{1,13},{... | collective-permute-start | bytes 405512 | tf_op jit(solution)/shard_map/ppermute | solution.py:308
  57.4 6.8 %collective-permute-start.16 = (bf16[16,4224]{1,0:T(8,128)(2,1)S(1)}, bf16[16,4224]{1,0:T(8,128)(2,1)S(1)}, u32[]{:S(2)}, u32[]{:S(2)}) collective-permute-start(bf16[16,4224]{1,0:T(8,128)(2,1)S(1)} %shard_map.76.refs_2_), channel_id=1, source_target_pairs={{0,24},{4,28},{8,16},{12,20},{16,8},{20,12},{24,0},{28,4},{1,25},{... | collective-permute-start | bytes 405512 | tf_op jit(solution)/shard_map/ppermute | solution.py:308
  64.4 5.0 %collective-permute-start.19 = (bf16[16,4096]{1,0:T(8,128)(2,1)S(1)}, bf16[16,4096]{1,0:T(8,128)(2,1)S(1)}, u32[]{:S(2)}, u32[]{:S(2)}) collective-permute-start(bf16[16,4096]{1,0:T(8,128)(2,1)S(1)} %get-tuple-element.54.v_ref.refs_11_), channel_id=1, source_target_pairs={{0,4},{4,0},{8,12},{12,8},{16,20},{20,16},{24,28},{28,24},{1,5},{5... | collective-permute-start | bytes 393224 | tf_op jit(solution)/shard_map/ppermute | solution.py:308
  65.3 5.0 %collective-permute-start.18 = (bf16[16,4096]{1,0:T(8,128)(2,1)S(1)}, bf16[16,4096]{1,0:T(8,128)(2,1)S(1)}, u32[]{:S(2)}, u32[]{:S(2)}) collective-permute-start(bf16[16,4096]{1,0:T(8,128)(2,1)S(1)} %get-tuple-element.54.v_ref.refs_11_), channel_id=1, source_target_pairs={{0,8},{4,12},{8,0},{12,4},{16,24},{20,28},{24,16},{28,20},{1,9},{5... | collective-permute-start | bytes 393224 | tf_op jit(solution)/shard_map/ppermute | solution.py:308
  66.1 6.2 %collective-permute-start.17 = (bf16[16,4096]{1,0:T(8,128)(2,1)S(1)}, bf16[16,4096]{1,0:T(8,128)(2,1)S(1)}, u32[]{:S(2)}, u32[]{:S(2)}) collective-permute-start(bf16[16,4096]{1,0:T(8,128)(2,1)S(1)} %get-tuple-element.54.v_ref.refs_11_), channel_id=1, source_target_pairs={{0,12},{4,8},{8,4},{12,0},{16,28},{20,24},{24,20},{28,16},{1,13},{... | collective-permute-start | bytes 393224 | tf_op jit(solution)/shard_map/ppermute | solution.py:308
  72.9 3.2 %collective-permute-start.22 = (bf16[16,640]{1,0:T(8,128)(2,1)S(1)}, bf16[16,640]{1,0:T(8,128)(2,1)S(1)}, u32[]{:S(2)}, u32[]{:S(2)}) collective-permute-start(bf16[16,640]{1,0:T(8,128)(2,1)S(1)} %shard_map.81.refs_2_), channel_id=1, source_target_pairs={{0,3},{1,2},{2,1},{3,0},{4,7},{5,6},{6,5},{7,4},{8,11},{9,10},{10,... | collective-permute-start | bytes 61448 | tf_op jit(solution)/shard_map/ppermute | solution.py:308
  72.9 3.8 %collective-permute-start.21 = (bf16[16,640]{1,0:T(8,128)(2,1)S(1)}, bf16[16,640]{1,0:T(8,128)(2,1)S(1)}, u32[]{:S(2)}, u32[]{:S(2)}) collective-permute-start(bf16[16,640]{1,0:T(8,128)(2,1)S(1)} %shard_map.81.refs_2_), channel_id=1, source_target_pairs={{0,2},{1,3},{2,0},{3,1},{4,6},{5,7},{6,4},{7,5},{8,10},{9,11},{10,... | collective-permute-start | bytes 61448 | tf_op jit(solution)/shard_map/ppermute | solution.py:308
  74.2 2.5 %collective-permute-start.20 = (bf16[16,640]{1,0:T(8,128)(2,1)S(1)}, bf16[16,640]{1,0:T(8,128)(2,1)S(1)}, u32[]{:S(2)}, u32[]{:S(2)}) collective-permute-start(bf16[16,640]{1,0:T(8,128)(2,1)S(1)} %shard_map.81.refs_2_), channel_id=1, source_target_pairs={{0,1},{1,0},{2,3},{3,2},{4,5},{5,4},{6,7},{7,6},{8,9},{9,8},{10,11... | collective-permute-start | bytes 61448 | tf_op jit(solution)/shard_map/ppermute | solution.py:308
  77.7 5.9 %collective-permute-start.23 = (bf16[16,4224]{1,0:T(8,128)(2,1)S(1)}, bf16[16,4224]{1,0:T(8,128)(2,1)S(1)}, u32[]{:S(2)}, u32[]{:S(2)}) collective-permute-start(bf16[16,4224]{1,0:T(8,128)(2,1)S(1)} %shard_map.84), channel_id=1, source_target_pairs={{0,8},{4,12},{8,0},{12,4},{16,24},{20,28},{24,16},{28,20},{1,9},{5... | collective-permute-start | bytes 405512 | tf_op jit(solution)/shard_map/ppermute | solution.py:308
  79.5 8.2 %collective-permute-start.24 = (bf16[16,4224]{1,0:T(8,128)(2,1)S(1)}, bf16[16,4224]{1,0:T(8,128)(2,1)S(1)}, u32[]{:S(2)}, u32[]{:S(2)}) collective-permute-start(bf16[16,4224]{1,0:T(8,128)(2,1)S(1)} %shard_map.86), channel_id=1, source_target_pairs={{0,4},{4,0},{8,12},{12,8},{16,20},{20,16},{24,28},{28,24},{1,5},{5... | collective-permute-start | bytes 405512 | tf_op jit(solution)/shard_map/ppermute | solution.py:308
  81.4 6.3 %collective-permute-start.25 = (bf16[16,4224]{1,0:T(8,128)(2,1)S(1)}, bf16[16,4224]{1,0:T(8,128)(2,1)S(1)}, u32[]{:S(2)}, u32[]{:S(2)}) collective-permute-start(bf16[16,4224]{1,0:T(8,128)(2,1)S(1)} %shard_map.88), channel_id=1, source_target_pairs={{0,12},{4,8},{8,4},{12,0},{16,28},{20,24},{24,20},{28,16},{1,13},{... | collective-permute-start | bytes 405512 | tf_op jit(solution)/shard_map/ppermute | solution.py:308
  87.9 7.0 %collective-permute-start.26 = (bf16[16,4224]{1,0:T(8,128)(2,1)S(1)}, bf16[16,4224]{1,0:T(8,128)(2,1)S(1)}, u32[]{:S(2)}, u32[]{:S(2)}) collective-permute-start(bf16[16,4224]{1,0:T(8,128)(2,1)S(1)} %shard_map.89.refs_2_), channel_id=1, source_target_pairs={{0,24},{4,28},{8,16},{12,20},{16,8},{20,12},{24,0},{28,4},{1,25},{... | collective-permute-start | bytes 405512 | tf_op jit(solution)/shard_map/ppermute | solution.py:308
  95.0 5.3 %collective-permute-start.29 = (bf16[16,4096]{1,0:T(8,128)(2,1)S(1)}, bf16[16,4096]{1,0:T(8,128)(2,1)S(1)}, u32[]{:S(2)}, u32[]{:S(2)}) collective-permute-start(bf16[16,4096]{1,0:T(8,128)(2,1)S(1)} %get-tuple-element.61.v_ref.refs_15_), channel_id=1, source_target_pairs={{0,4},{4,0},{8,12},{12,8},{16,20},{20,16},{24,28},{28,24},{1,5},{5... | collective-permute-start | bytes 393224 | tf_op jit(solution)/shard_map/ppermute | solution.py:308
  96.2 5.0 %collective-permute-start.28 = (bf16[16,4096]{1,0:T(8,128)(2,1)S(1)}, bf16[16,4096]{1,0:T(8,128)(2,1)S(1)}, u32[]{:S(2)}, u32[]{:S(2)}) collective-permute-start(bf16[16,4096]{1,0:T(8,128)(2,1)S(1)} %get-tuple-element.61.v_ref.refs_15_), channel_id=1, source_target_pairs={{0,8},{4,12},{8,0},{12,4},{16,24},{20,28},{24,16},{28,20},{1,9},{5... | collective-permute-start | bytes 393224 | tf_op jit(solution)/shard_map/ppermute | solution.py:308
  96.9 5.9 %collective-permute-start.27 = (bf16[16,4096]{1,0:T(8,128)(2,1)S(1)}, bf16[16,4096]{1,0:T(8,128)(2,1)S(1)}, u32[]{:S(2)}, u32[]{:S(2)}) collective-permute-start(bf16[16,4096]{1,0:T(8,128)(2,1)S(1)} %get-tuple-element.61.v_ref.refs_15_), channel_id=1, source_target_pairs={{0,12},{4,8},{8,4},{12,0},{16,28},{20,24},{24,20},{28,16},{1,13},{... | collective-permute-start | bytes 393224 | tf_op jit(solution)/shard_map/ppermute | solution.py:308
  103.5 3.3 %collective-permute-start.32 = (bf16[16,640]{1,0:T(8,128)(2,1)S(1)}, bf16[16,640]{1,0:T(8,128)(2,1)S(1)}, u32[]{:S(2)}, u32[]{:S(2)}) collective-permute-start(bf16[16,640]{1,0:T(8,128)(2,1)S(1)} %shard_map.94.refs_2_), channel_id=1, source_target_pairs={{0,3},{1,2},{2,1},{3,0},{4,7},{5,6},{6,5},{7,4},{8,11},{9,10},{10,... | collective-permute-start | bytes 61448 | tf_op jit(solution)/shard_map/ppermute | solution.py:308
  103.5 3.8 %collective-permute-start.31 = (bf16[16,640]{1,0:T(8,128)(2,1)S(1)}, bf16[16,640]{1,0:T(8,128)(2,1)S(1)}, u32[]{:S(2)}, u32[]{:S(2)}) collective-permute-start(bf16[16,640]{1,0:T(8,128)(2,1)S(1)} %shard_map.94.refs_2_), channel_id=1, source_target_pairs={{0,2},{1,3},{2,0},{3,1},{4,6},{5,7},{6,4},{7,5},{8,10},{9,11},{10,... | collective-permute-start | bytes 61448 | tf_op jit(solution)/shard_map/ppermute | solution.py:308
  104.9 2.5 %collective-permute-start.30 = (bf16[16,640]{1,0:T(8,128)(2,1)S(1)}, bf16[16,640]{1,0:T(8,128)(2,1)S(1)}, u32[]{:S(2)}, u32[]{:S(2)}) collective-permute-start(bf16[16,640]{1,0:T(8,128)(2,1)S(1)} %shard_map.94.refs_2_), channel_id=1, source_target_pairs={{0,1},{1,0},{2,3},{3,2},{4,5},{5,4},{6,7},{7,6},{8,9},{9,8},{10,11... | collective-permute-start | bytes 61448 | tf_op jit(solution)/shard_map/ppermute | solution.py:308
  108.4 5.9 %collective-permute-start.33 = (bf16[16,4224]{1,0:T(8,128)(2,1)S(1)}, bf16[16,4224]{1,0:T(8,128)(2,1)S(1)}, u32[]{:S(2)}, u32[]{:S(2)}) collective-permute-start(bf16[16,4224]{1,0:T(8,128)(2,1)S(1)} %shard_map.97), channel_id=1, source_target_pairs={{0,8},{4,12},{8,0},{12,4},{16,24},{20,28},{24,16},{28,20},{1,9},{5... | collective-permute-start | bytes 405512 | tf_op jit(solution)/shard_map/ppermute | solution.py:308
  110.5 8.2 %collective-permute-start.34 = (bf16[16,4224]{1,0:T(8,128)(2,1)S(1)}, bf16[16,4224]{1,0:T(8,128)(2,1)S(1)}, u32[]{:S(2)}, u32[]{:S(2)}) collective-permute-start(bf16[16,4224]{1,0:T(8,128)(2,1)S(1)} %shard_map.99), channel_id=1, source_target_pairs={{0,4},{4,0},{8,12},{12,8},{16,20},{20,16},{24,28},{28,24},{1,5},{5... | collective-permute-start | bytes 405512 | tf_op jit(solution)/shard_map/ppermute | solution.py:308
  112.0 6.7 %collective-permute-start.35 = (bf16[16,4224]{1,0:T(8,128)(2,1)S(1)}, bf16[16,4224]{1,0:T(8,128)(2,1)S(1)}, u32[]{:S(2)}, u32[]{:S(2)}) collective-permute-start(bf16[16,4224]{1,0:T(8,128)(2,1)S(1)} %shard_map.101), channel_id=1, source_target_pairs={{0,12},{4,8},{8,4},{12,0},{16,28},{20,24},{24,20},{28,16},{1,13},{... | collective-permute-start | bytes 405512 | tf_op jit(solution)/shard_map/ppermute | solution.py:308
  118.9 7.0 %collective-permute-start.36 = (bf16[16,4224]{1,0:T(8,128)(2,1)S(1)}, bf16[16,4224]{1,0:T(8,128)(2,1)S(1)}, u32[]{:S(2)}, u32[]{:S(2)}) collective-permute-start(bf16[16,4224]{1,0:T(8,128)(2,1)S(1)} %shard_map.102.refs_2_), channel_id=1, source_target_pairs={{0,24},{4,28},{8,16},{12,20},{16,8},{20,12},{24,0},{28,4},{1,25},{... | collective-permute-start | bytes 405512 | tf_op jit(solution)/shard_map/ppermute | solution.py:308
  126.7 5.0 %collective-permute-start.39 = (bf16[16,4096]{1,0:T(8,128)(2,1)S(1)}, bf16[16,4096]{1,0:T(8,128)(2,1)S(1)}, u32[]{:S(2)}, u32[]{:S(2)}) collective-permute-start(bf16[16,4096]{1,0:T(8,128)(2,1)S(1)} %get-tuple-element.68.v_ref.refs_19_), channel_id=1, source_target_pairs={{0,4},{4,0},{8,12},{12,8},{16,20},{20,16},{24,28},{28,24},{1,5},{5... | collective-permute-start | bytes 393224 | tf_op jit(solution)/shard_map/ppermute | solution.py:308
  127.5 5.0 %collective-permute-start.38 = (bf16[16,4096]{1,0:T(8,128)(2,1)S(1)}, bf16[16,4096]{1,0:T(8,128)(2,1)S(1)}, u32[]{:S(2)}, u32[]{:S(2)}) collective-permute-start(bf16[16,4096]{1,0:T(8,128)(2,1)S(1)} %get-tuple-element.68.v_ref.refs_19_), channel_id=1, source_target_pairs={{0,8},{4,12},{8,0},{12,4},{16,24},{20,28},{24,16},{28,20},{1,9},{5... | collective-permute-start | bytes 393224 | tf_op jit(solution)/shard_map/ppermute | solution.py:308
  128.3 6.2 %collective-permute-start.37 = (bf16[16,4096]{1,0:T(8,128)(2,1)S(1)}, bf16[16,4096]{1,0:T(8,128)(2,1)S(1)}, u32[]{:S(2)}, u32[]{:S(2)}) collective-permute-start(bf16[16,4096]{1,0:T(8,128)(2,1)S(1)} %get-tuple-element.68.v_ref.refs_19_), channel_id=1, source_target_pairs={{0,12},{4,8},{8,4},{12,0},{16,28},{20,24},{24,20},{28,16},{1,13},{... | collective-permute-start | bytes 393224 | tf_op jit(solution)/shard_map/ppermute | solution.py:308
  135.1 3.2 %collective-permute-start.42 = (bf16[16,640]{1,0:T(8,128)(2,1)S(1)}, bf16[16,640]{1,0:T(8,128)(2,1)S(1)}, u32[]{:S(2)}, u32[]{:S(2)}) collective-permute-start(bf16[16,640]{1,0:T(8,128)(2,1)S(1)} %shard_map.107.refs_2_), channel_id=1, source_target_pairs={{0,3},{1,2},{2,1},{3,0},{4,7},{5,6},{6,5},{7,4},{8,11},{9,10},{10,... | collective-permute-start | bytes 61448 | tf_op jit(solution)/shard_map/ppermute | solution.py:308
  135.1 3.8 %collective-permute-start.41 = (bf16[16,640]{1,0:T(8,128)(2,1)S(1)}, bf16[16,640]{1,0:T(8,128)(2,1)S(1)}, u32[]{:S(2)}, u32[]{:S(2)}) collective-permute-start(bf16[16,640]{1,0:T(8,128)(2,1)S(1)} %shard_map.107.refs_2_), channel_id=1, source_target_pairs={{0,2},{1,3},{2,0},{3,1},{4,6},{5,7},{6,4},{7,5},{8,10},{9,11},{10,... | collective-permute-start | bytes 61448 | tf_op jit(solution)/shard_map/ppermute | solution.py:308
  136.4 2.6 %collective-permute-start.40 = (bf16[16,640]{1,0:T(8,128)(2,1)S(1)}, bf16[16,640]{1,0:T(8,128)(2,1)S(1)}, u32[]{:S(2)}, u32[]{:S(2)}) collective-permute-start(bf16[16,640]{1,0:T(8,128)(2,1)S(1)} %shard_map.107.refs_2_), channel_id=1, source_target_pairs={{0,1},{1,0},{2,3},{3,2},{4,5},{5,4},{6,7},{7,6},{8,9},{9,8},{10,11... | collective-permute-start | bytes 61448 | tf_op jit(solution)/shard_map/ppermute | solution.py:308
  139.2 5.4 %collective-permute-start.46 = (f32[16,128]{1,0:T(8,128)S(1)}, f32[16,128]{1,0:T(8,128)S(1)}, u32[]{:S(2)}, u32[]{:S(2)}) collective-permute-start(f32[16,128]{1,0:T(8,128)S(1)} %get-tuple-element.80.mine_ref), channel_id=1, source_target_pairs={{0,12},{1,29},{2,14},{3,31},{4,8},{5,25},{6,10},{7,27},{8,4},{9,21... | collective-permute-start | bytes 24584 | tf_op jit(solution)/shard_map/ppermute | solution.py:348
  140.7 3.9 %collective-permute-start.45 = (f32[16,128]{1,0:T(8,128)S(1)}, f32[16,128]{1,0:T(8,128)S(1)}, u32[]{:S(2)}, u32[]{:S(2)}) collective-permute-start(f32[16,128]{1,0:T(8,128)S(1)} %get-tuple-element.80.mine_ref), channel_id=1, source_target_pairs={{0,8},{1,25},{2,10},{3,27},{4,12},{5,29},{6,14},{7,31},{8,0},{9,17... | collective-permute-start | bytes 24584 | tf_op jit(solution)/shard_map/ppermute | solution.py:348
  141.5 3.7 %collective-permute-start.44 = (f32[16,128]{1,0:T(8,128)S(1)}, f32[16,128]{1,0:T(8,128)S(1)}, u32[]{:S(2)}, u32[]{:S(2)}) collective-permute-start(f32[16,128]{1,0:T(8,128)S(1)} %get-tuple-element.80.mine_ref), channel_id=1, source_target_pairs={{0,4},{1,21},{2,6},{3,23},{4,0},{5,17},{6,2},{7,19},{8,12},{9,29},... | collective-permute-start | bytes 24584 | tf_op jit(solution)/shard_map/ppermute | solution.py:348
  142.6 4.5 %collective-permute-start.43 = (f32[16,128]{1,0:T(8,128)S(1)}, f32[16,128]{1,0:T(8,128)S(1)}, u32[]{:S(2)}, u32[]{:S(2)}) collective-permute-start(f32[16,128]{1,0:T(8,128)S(1)} %get-tuple-element.80.mine_ref), channel_id=1, source_target_pairs={{0,16},{1,17},{2,18},{3,19},{4,20},{5,21},{6,22},{7,23},{8,24},{9,... | collective-permute-start | bytes 24584 | tf_op jit(solution)/shard_map/ppermute | solution.py:348
  147.2 1.2 collective-permute-start.47

commit v7 on v6

--- a/solution.py
+++ b/solution.py
@@ -178,19 +178,24 @@
     norm = square[:, :LANES]
     for k in range(1, width // LANES):
         norm += square[:, k * LANES : (k + 1) * LANES]
+    norms = [norm]
     for sum_ref in refs[:-1]:
         image += sum_ref[:, :rows]
-        norm += sum_ref[:, rows:]
+        norms = [sum_ref[:, at : at + LANES] for at in range(rows, sum_ref.shape[1], LANES)] + norms
     if out_ref.dtype == BF16:
-        norm = pack_norm(lane_total(norm))
+        norms = [pack_norm(lane_total(tree(norms)))]
     out_ref[:, :rows] = image.astype(out_ref.dtype)
-    out_ref[:, rows:] = norm
-
-
-def forward(dtype, turned, v, *total):
-    return call(
-        forward_kernel, shape(v.shape[0], turned.shape[1] + LANES, dtype=dtype), (turned, v, *total)
-    )
+    for k, norm in enumerate(norms):
+        out_ref[:, rows + k * LANES : rows + (k + 1) * LANES] = norm
+
+
+def forward(last, turned, v, *total):
+    scen, rows = v.shape[0], turned.shape[1]
+    if last:
+        out = shape(scen, rows + LANES, dtype=BF16)
+    else:
+        out = shape(scen, (total[0].shape[1] if total else rows) + LANES)
+    return call(forward_kernel, out, (turned, v, *total))
 
 
 def first_kernel(targets_ref, *refs):
@@ -377,9 +382,9 @@
 
     def image_parts(mine):
         got = {d: exchange(mine, "obs", n_obs, d) for d in range(1, near)}
-        total = forward(F32, turned[0], mine)
+        total = forward(near == 1, turned[0], mine)
         for d in got:
-            total = forward(BF16 if d == near - 1 else F32, turned[d], got[d], total)
+            total = forward(d == near - 1, turned[d], got[d], total)
         return parts_over(total, "par", n_par, True), [mine] + [got[d] for d in range(1, near)]
 
     op, first = load(operator, start)

time: 150 us -> 150 us (level)
  no operation moved by 1% of the time
where the time goes in v7:
time: 150 us
  waiting for transfers between devices  54.3 us (36%)
  starting transfers between devices  54.2 us (36%)
  Pallas kernels  40.2 us (27%)
    ppermute x44, waiting for transfers between devices, exchange(): return lax.ppermute(value, axis, [(i, i ^ distance) for i in range(size)])  51.7 us
    ppermute x44, starting transfers between devices, exchange(): return lax.ppermute(value, axis, [(i, i ^ distance) for i in range(size)])  48.8 us
    pallas_call x62, Pallas kernels, call(): pl.pallas_call(body, out_shape=out, in_specs=specs if specs is not None e...  40.2 us
    ppermute x4, starting transfers between devices, norm_parts(): got.append(lax.ppermute(norm, ('obs', 'par'), pairs))  5.4 us
  transfers between devices with their start and end apart: 48, of which 32 were waited for; matrix products, arithmetic and copies ran while one was open for 0% of the time, Pallas kernels for 15%

profile of v7, /device:TPU:0, one launch (start us, length us, event | category | flops | bytes accessed | tf_op | source)
XLA Modules:
  0.0 149.7 jit_solution(8750920444192235472)
XLA Ops:
  0.6 2.4 %shard_map.50.early_ref = bf16[512,16384]{1,0:T(8,128)(2,1)S(1)} custom-call(bf16[512,16384]{1,0:T(8,128)(2,1)} %op_hbm.3), custom_call_target="tpu_custom_call" | custom-call | bytes 1024 | tf_op jit(solution)/shard_map/pallas_call | solution.py:26
  3.1 5.2 %shard_map.51 = (bf16[512,16384]{1,0:T(8,128)(2,1)S(1)}, bf16[16,512]{1,0:T(8,128)(2,1)S(1)}) custom-call(bf16[512,16384]{1,0:T(8,128)(2,1)} %op_hbm.3, f32[16,16384]{1,0:T(8,128)S(1)} %copy-done, bf16[512,16384]{1,0:T(8,128)(2,1)S(1)} %shard_map.50.early_ref), custom_call_target="tpu_custom_call", output_to_operand_aliasing={{0}: (2, {})} | custom-call | bytes 1024 | tf_op jit(solution)/shard_map/pallas_call | solution.py:26
  8.3 2.5 %collective-permute-start.2 = (bf16[16,512]{1,0:T(8,128)(2,1)S(1)}, bf16[16,512]{1,0:T(8,128)(2,1)S(1)}, u32[]{:S(2)}, u32[]{:S(2)}) collective-permute-start(bf16[16,512]{1,0:T(8,128)(2,1)S(1)} %get-tuple-element.43.refs_0_), channel_id=1, source_target_pairs={{0,3},{1,2},{2,1},{3,0},{4,7},{5,6},{6,5},{7,4},{8,11},{9,10},{10,... | collective-permute-start | bytes 49160 | tf_op jit(solution)/shard_map/ppermute | solution.py:313
  12.2 2.3 %collective-permute-done.1.refs_2_ = bf16[16,512]{1,0:T(8,128)(2,1)S(1)} collective-permute-done((bf16[16,512]{1,0:T(8,128)(2,1)S(1)}, bf16[16,512]{1,0:T(8,128)(2,1)S(1)}, u32[]{:S(2)}, u32[]{:S(2)}) %collective-permute-start.1) | collective-permute-done | bytes 16416 | tf_op jit(solution)/shard_map/ppermute | solution.py:313
  14.6 0.8 shard_map.58
  15.4 1.6 %collective-permute-start.3 = (bf16[16,4224]{1,0:T(8,128)(2,1)S(1)}, bf16[16,4224]{1,0:T(8,128)(2,1)S(1)}, u32[]{:S(2)}, u32[]{:S(2)}) collective-permute-start(bf16[16,4224]{1,0:T(8,128)(2,1)S(1)} %shard_map.58), channel_id=1, source_target_pairs={{0,8},{4,12},{8,0},{12,4},{16,24},{20,28},{24,16},{28,20},{1,9},{5... | collective-permute-start | bytes 405512 | tf_op jit(solution)/shard_map/ppermute | solution.py:313
  17.7 1.5 %collective-permute-start.4 = (bf16[16,4224]{1,0:T(8,128)(2,1)S(1)}, bf16[16,4224]{1,0:T(8,128)(2,1)S(1)}, u32[]{:S(2)}, u32[]{:S(2)}) collective-permute-start(bf16[16,4224]{1,0:T(8,128)(2,1)S(1)} %shard_map.60), channel_id=1, source_target_pairs={{0,4},{4,0},{8,12},{12,8},{16,20},{20,16},{24,28},{28,24},{1,5},{5... | collective-permute-start | bytes 405512 | tf_op jit(solution)/shard_map/ppermute | solution.py:313
  21.3 3.4 %collective-permute-done.4.got_ref.refs_1_ = bf16[16,4224]{1,0:T(8,128)(2,1)S(1)} collective-permute-done((bf16[16,4224]{1,0:T(8,128)(2,1)S(1)}, bf16[16,4224]{1,0:T(8,128)(2,1)S(1)}, u32[]{:S(2)}, u32[]{:S(2)}) %collective-permute-start.4) | collective-permute-done | bytes 135200 | tf_op jit(solution)/shard_map/ppermute | solution.py:313
  24.7 1.2 collective-permute-done.5.refs_2_
  26.1 2.5 %collective-permute-start.6 = (bf16[16,4224]{1,0:T(8,128)(2,1)S(1)}, bf16[16,4224]{1,0:T(8,128)(2,1)S(1)}, u32[]{:S(2)}, u32[]{:S(2)}) collective-permute-start(bf16[16,4224]{1,0:T(8,128)(2,1)S(1)} %shard_map.63.refs_4_), channel_id=1, source_target_pairs={{0,24},{4,28},{8,16},{12,20},{16,8},{20,12},{24,0},{28,4},{1,25},{... | collective-permute-start | bytes 405512 | tf_op jit(solution)/shard_map/ppermute | solution.py:313
  28.6 1.1 shard_map.55.refs_2_.turned_ref
  29.7 1.1 shard_map.54.refs_1_.turned_ref
  30.9 1.1 shard_map.53.refs_0_.turned_ref
  32.0 1.1 shard_map.52.refs_3_.turned_ref
  33.8 1.2 collective-permute-start.9
  35.7 1.6 %collective-permute-start.7 = (bf16[16,4096]{1,0:T(8,128)(2,1)S(1)}, bf16[16,4096]{1,0:T(8,128)(2,1)S(1)}, u32[]{:S(2)}, u32[]{:S(2)}) collective-permute-start(bf16[16,4096]{1,0:T(8,128)(2,1)S(1)} %get-tuple-element.47.v_ref.refs_7_), channel_id=1, source_target_pairs={{0,12},{4,8},{8,4},{12,0},{16,28},{20,24},{24,20},{28,16},{1,13},{... | collective-permute-start | bytes 393224 | tf_op jit(solution)/shard_map/ppermute | solution.py:313
  37.9 1.5 %collective-permute-done.9.v_ref.refs_8_ = bf16[16,4096]{1,0:T(8,128)(2,1)S(1)} collective-permute-done((bf16[16,4096]{1,0:T(8,128)(2,1)S(1)}, bf16[16,4096]{1,0:T(8,128)(2,1)S(1)}, u32[]{:S(2)}, u32[]{:S(2)}) %collective-permute-start.9) | collective-permute-done | bytes 131104 | tf_op jit(solution)/shard_map/ppermute | solution.py:313
  40.7 0.9 collective-permute-done.7.v_ref.refs_10_
  43.0 1.2 collective-permute-start.10
  44.2 1.3 collective-permute-done.12.refs_3_
  46.2 0.8 shard_map.71
  47.0 1.3 collective-permute-start.13
  48.4 0.9 shard_map.73
  49.3 0.8 collective-permute-start.14
  50.9 1.4 collective-permute-start.15
  53.2 4.1 %collective-permute-done.14.got_ref.refs_1_ = bf16[16,4224]{1,0:T(8,128)(2,1)S(1)} collective-permute-done((bf16[16,4224]{1,0:T(8,128)(2,1)S(1)}, bf16[16,4224]{1,0:T(8,128)(2,1)S(1)}, u32[]{:S(2)}, u32[]{:S(2)}) %collective-permute-start.14) | collective-permute-done | bytes 135200 | tf_op jit(solution)/shard_map/ppermute | solution.py:313
  57.4 2.4 %collective-permute-start.16 = (bf16[16,4224]{1,0:T(8,128)(2,1)S(1)}, bf16[16,4224]{1,0:T(8,128)(2,1)S(1)}, u32[]{:S(2)}, u32[]{:S(2)}) collective-permute-start(bf16[16,4224]{1,0:T(8,128)(2,1)S(1)} %shard_map.76.refs_2_), channel_id=1, source_target_pairs={{0,24},{4,28},{8,16},{12,20},{16,8},{20,12},{24,0},{28,4},{1,25},{... | collective-permute-start | bytes 405512 | tf_op jit(solution)/shard_map/ppermute | solution.py:313
  59.7 4.5 %collective-permute-done.16.refs_3_ = bf16[16,4224]{1,0:T(8,128)(2,1)S(1)} collective-permute-done((bf16[16,4224]{1,0:T(8,128)(2,1)S(1)}, bf16[16,4224]{1,0:T(8,128)(2,1)S(1)}, u32[]{:S(2)}, u32[]{:S(2)}) %collective-permute-start.16) | collective-permute-done | bytes 135200 | tf_op jit(solution)/shard_map/ppermute | solution.py:313
  64.4 1.0 collective-permute-start.19
  66.1 1.9 %collective-permute-start.17 = (bf16[16,4096]{1,0:T(8,128)(2,1)S(1)}, bf16[16,4096]{1,0:T(8,128)(2,1)S(1)}, u32[]{:S(2)}, u32[]{:S(2)}) collective-permute-start(bf16[16,4096]{1,0:T(8,128)(2,1)S(1)} %get-tuple-element.54.v_ref.refs_11_), channel_id=1, source_target_pairs={{0,12},{4,8},{8,4},{12,0},{16,28},{20,24},{24,20},{28,16},{1,13},{... | collective-permute-start | bytes 393224 | tf_op jit(solution)/shard_map/ppermute | solution.py:313
  68.6 0.8 collective-permute-done.19.v_ref.refs_12_
  70.9 1.3 collective-permute-done.17.v_ref.refs_14_
  72.9 1.3 collective-permute-start.21
  74.8 1.4 collective-permute-done.22.refs_5_
  77.7 1.0 collective-permute-start.23
  79.5 1.2 collective-permute-start.24
  81.4 1.4 collective-permute-start.25
  83.7 4.0 %collective-permute-done.24.got_ref.refs_1_ = bf16[16,4224]{1,0:T(8,128)(2,1)S(1)} collective-permute-done((bf16[16,4224]{1,0:T(8,128)(2,1)S(1)}, bf16[16,4224]{1,0:T(8,128)(2,1)S(1)}, u32[]{:S(2)}, u32[]{:S(2)}) %collective-permute-start.24) | collective-permute-done | bytes 135200 | tf_op jit(solution)/shard_map/ppermute | solution.py:313
  87.9 2.6 %collective-permute-start.26 = (bf16[16,4224]{1,0:T(8,128)(2,1)S(1)}, bf16[16,4224]{1,0:T(8,128)(2,1)S(1)}, u32[]{:S(2)}, u32[]{:S(2)}) collective-permute-start(bf16[16,4224]{1,0:T(8,128)(2,1)S(1)} %shard_map.89.refs_2_), channel_id=1, source_target_pairs={{0,24},{4,28},{8,16},{12,20},{16,8},{20,12},{24,0},{28,4},{1,25},{... | collective-permute-start | bytes 405512 | tf_op jit(solution)/shard_map/ppermute | solution.py:313
  90.5 4.4 %collective-permute-done.26.refs_3_ = bf16[16,4224]{1,0:T(8,128)(2,1)S(1)} collective-permute-done((bf16[16,4224]{1,0:T(8,128)(2,1)S(1)}, bf16[16,4224]{1,0:T(8,128)(2,1)S(1)}, u32[]{:S(2)}, u32[]{:S(2)}) %collective-permute-start.26) | collective-permute-done | bytes 135200 | tf_op jit(solution)/shard_map/ppermute | solution.py:313
  95.0 1.2 collective-permute-start.29
  96.9 1.6 %collective-permute-start.27 = (bf16[16,4096]{1,0:T(8,128)(2,1)S(1)}, bf16[16,4096]{1,0:T(8,128)(2,1)S(1)}, u32[]{:S(2)}, u32[]{:S(2)}) collective-permute-start(bf16[16,4096]{1,0:T(8,128)(2,1)S(1)} %get-tuple-element.61.v_ref.refs_15_), channel_id=1, source_target_pairs={{0,12},{4,8},{8,4},{12,0},{16,28},{20,24},{24,20},{28,16},{1,13},{... | collective-permute-start | bytes 393224 | tf_op jit(solution)/shard_map/ppermute | solution.py:313
  99.2 1.1 collective-permute-done.29.v_ref.refs_16_
  101.8 1.0 collective-permute-done.27.v_ref.refs_18_
  103.5 1.3 collective-permute-start.31
  105.4 1.4 collective-permute-done.32.refs_5_
  108.4 1.3 collective-permute-start.33
  110.5 0.8 collective-permute-start.34
  112.0 1.4 collective-permute-start.35
  114.3 4.4 %collective-permute-done.34.got_ref.refs_1_ = bf16[16,4224]{1,0:T(8,128)(2,1)S(1)} collective-permute-done((bf16[16,4224]{1,0:T(8,128)(2,1)S(1)}, bf16[16,4224]{1,0:T(8,128)(2,1)S(1)}, u32[]{:S(2)}, u32[]{:S(2)}) %collective-permute-start.34) | collective-permute-done | bytes 135200 | tf_op jit(solution)/shard_map/ppermute | solution.py:313
  118.9 2.5 %collective-permute-start.36 = (bf16[16,4224]{1,0:T(8,128)(2,1)S(1)}, bf16[16,4224]{1,0:T(8,128)(2,1)S(1)}, u32[]{:S(2)}, u32[]{:S(2)}) collective-permute-start(bf16[16,4224]{1,0:T(8,128)(2,1)S(1)} %shard_map.102.refs_2_), channel_id=1, source_target_pairs={{0,24},{4,28},{8,16},{12,20},{16,8},{20,12},{24,0},{28,4},{1,25},{... | collective-permute-start | bytes 405512 | tf_op jit(solution)/shard_map/ppermute | solution.py:313
  121.4 4.5 %collective-permute-done.36.refs_3_ = bf16[16,4224]{1,0:T(8,128)(2,1)S(1)} collective-permute-done((bf16[16,4224]{1,0:T(8,128)(2,1)S(1)}, bf16[16,4224]{1,0:T(8,128)(2,1)S(1)}, u32[]{:S(2)}, u32[]{:S(2)}) %collective-permute-start.36) | collective-permute-done | bytes 135200 | tf_op jit(solution)/shard_map/ppermute | solution.py:313
  125.8 0.8 shard_map.103
  126.7 0.9 collective-permute-start.39
  128.3 1.9 %collective-permute-start.37 = (bf16[16,4096]{1,0:T(8,128)(2,1)S(1)}, bf16[16,4096]{1,0:T(8,128)(2,1)S(1)}, u32[]{:S(2)}, u32[]{:S(2)}) collective-permute-start(bf16[16,4096]{1,0:T(8,128)(2,1)S(1)} %get-tuple-element.68.v_ref.refs_19_), channel_id=1, source_target_pairs={{0,12},{4,8},{8,4},{12,0},{16,28},{20,24},{24,20},{28,16},{1,13},{... | collective-permute-start | bytes 393224 | tf_op jit(solution)/shard_map/ppermute | solution.py:313
  130.8 0.9 collective-permute-done.39.v_ref.refs_20_
  133.1 1.4 collective-permute-done.37.v_ref.refs_22_
  135.1 1.2 collective-permute-start.41
  137.0 1.3 collective-permute-done.42.refs_5_
  139.2 1.5 %collective-permute-start.46 = (f32[16,128]{1,0:T(8,128)S(1)}, f32[16,128]{1,0:T(8,128)S(1)}, u32[]{:S(2)}, u32[]{:S(2)}) collective-permute-start(f32[16,128]{1,0:T(8,128)S(1)} %get-tuple-element.80.mine_ref), channel_id=1, source_target_pairs={{0,12},{1,29},{2,14},{3,31},{4,8},{5,25},{6,10},{7,27},{8,4},{9,21... | collective-permute-start | bytes 24584 | tf_op jit(solution)/shard_map/ppermute | solution.py:353
  141.5 1.2 collective-permute-start.44
  142.6 1.9 %collective-permute-start.43 = (f32[16,128]{1,0:T(8,128)S(1)}, f32[16,128]{1,0:T(8,128)S(1)}, u32[]{:S(2)}, u32[]{:S(2)}) collective-permute-start(f32[16,128]{1,0:T(8,128)S(1)} %get-tuple-element.80.mine_ref), channel_id=1, source_target_pairs={{0,16},{1,17},{2,18},{3,19},{4,20},{5,21},{6,22},{7,23},{8,24},{9,... | collective-permute-start | bytes 24584 | tf_op jit(solution)/shard_map/ppermute | solution.py:353
  145.1 2.1 %collective-permute-done.43.refs_0_ = f32[16,128]{1,0:T(8,128)S(1)} collective-permute-done((f32[16,128]{1,0:T(8,128)S(1)}, f32[16,128]{1,0:T(8,128)S(1)}, u32[]{:S(2)}, u32[]{:S(2)}) %collective-permute-start.43) | collective-permute-done | bytes 8224 | tf_op jit(solution)/shard_map/ppermute | solution.py:353
  148.4 1.3 shard_map.111
  (98 shorter events, 35.9 us)
Async XLA Ops:
  0.6 2.5 %copy-start = (f32[16,16384]{1,0:T(8,128)S(1)}, f32[16,16384]{1,0:T(8,128)}, u32[]{:S(2)}) copy-start(f32[16,16384]{1,0:T(8,128)} %start_ref.3) | copy-start | bytes 3145732
  3.1 11.4 %copy-start.1 = (f32[16,512]{1,0:T(8,128)S(1)}, f32[16,512]{1,0:T(8,128)}, u32[]{:S(2)}) copy-start(f32[16,512]{1,0:T(8,128)} %targets_ref.1) | copy-start | bytes 98308
  8.3 3.9 %collective-permute-start.2 = (bf16[16,512]{1,0:T(8,128)(2,1)S(1)}, bf16[16,512]{1,0:T(8,128)(2,1)S(1)}, u32[]{:S(2)}, u32[]{:S(2)}) collective-permute-start(bf16[16,512]{1,0:T(8,128)(2,1)S(1)} %get-tuple-element.43.refs_0_), channel_id=1, source_target_pairs={{0,3},{1,2},{2,1},{3,0},{4,7},{5,6},{6,5},{7,4},{8,11},{9,10},{10,... | collective-permute-start | bytes 49160 | tf_op jit(solution)/shard_map/ppermute | solution.py:313
  10.8 3.7 %collective-permute-start.1 = (bf16[16,512]{1,0:T(8,128)(2,1)S(1)}, bf16[16,512]{1,0:T(8,128)(2,1)S(1)}, u32[]{:S(2)}, u32[]{:S(2)}) collective-permute-start(bf16[16,512]{1,0:T(8,128)(2,1)S(1)} %get-tuple-element.43.refs_0_), channel_id=1, source_target_pairs={{0,2},{1,3},{2,0},{3,1},{4,6},{5,7},{6,4},{7,5},{8,10},{9,11},{10,... | collective-permute-start | bytes 49160 | tf_op jit(solution)/shard_map/ppermute | solution.py:313
  11.4 3.1 %collective-permute-start = (bf16[16,512]{1,0:T(8,128)(2,1)S(1)}, bf16[16,512]{1,0:T(8,128)(2,1)S(1)}, u32[]{:S(2)}, u32[]{:S(2)}) collective-permute-start(bf16[16,512]{1,0:T(8,128)(2,1)S(1)} %get-tuple-element.43.refs_0_), channel_id=1, source_target_pairs={{0,1},{1,0},{2,3},{3,2},{4,5},{5,4},{6,7},{7,6},{8,9},{9,8},{10,11... | collective-permute-start | bytes 49160 | tf_op jit(solution)/shard_map/ppermute | solution.py:313
  15.4 5.9 %collective-permute-start.3 = (bf16[16,4224]{1,0:T(8,128)(2,1)S(1)}, bf16[16,4224]{1,0:T(8,128)(2,1)S(1)}, u32[]{:S(2)}, u32[]{:S(2)}) collective-permute-start(bf16[16,4224]{1,0:T(8,128)(2,1)S(1)} %shard_map.58), channel_id=1, source_target_pairs={{0,8},{4,12},{8,0},{12,4},{16,24},{20,28},{24,16},{28,20},{1,9},{5... | collective-permute-start | bytes 405512 | tf_op jit(solution)/shard_map/ppermute | solution.py:313
  17.7 7.0 %collective-permute-start.4 = (bf16[16,4224]{1,0:T(8,128)(2,1)S(1)}, bf16[16,4224]{1,0:T(8,128)(2,1)S(1)}, u32[]{:S(2)}, u32[]{:S(2)}) collective-permute-start(bf16[16,4224]{1,0:T(8,128)(2,1)S(1)} %shard_map.60), channel_id=1, source_target_pairs={{0,4},{4,0},{8,12},{12,8},{16,20},{20,16},{24,28},{28,24},{1,5},{5... | collective-permute-start | bytes 405512 | tf_op jit(solution)/shard_map/ppermute | solution.py:313
  20.0 5.9 %collective-permute-start.5 = (bf16[16,4224]{1,0:T(8,128)(2,1)S(1)}, bf16[16,4224]{1,0:T(8,128)(2,1)S(1)}, u32[]{:S(2)}, u32[]{:S(2)}) collective-permute-start(bf16[16,4224]{1,0:T(8,128)(2,1)S(1)} %shard_map.62), channel_id=1, source_target_pairs={{0,12},{4,8},{8,4},{12,0},{16,28},{20,24},{24,20},{28,16},{1,13},{... | collective-permute-start | bytes 405512 | tf_op jit(solution)/shard_map/ppermute | solution.py:313
  26.1 7.1 %collective-permute-start.6 = (bf16[16,4224]{1,0:T(8,128)(2,1)S(1)}, bf16[16,4224]{1,0:T(8,128)(2,1)S(1)}, u32[]{:S(2)}, u32[]{:S(2)}) collective-permute-start(bf16[16,4224]{1,0:T(8,128)(2,1)S(1)} %shard_map.63.refs_4_), channel_id=1, source_target_pairs={{0,24},{4,28},{8,16},{12,20},{16,8},{20,12},{24,0},{28,4},{1,25},{... | collective-permute-start | bytes 405512 | tf_op jit(solution)/shard_map/ppermute | solution.py:313
  33.8 5.6 %collective-permute-start.9 = (bf16[16,4096]{1,0:T(8,128)(2,1)S(1)}, bf16[16,4096]{1,0:T(8,128)(2,1)S(1)}, u32[]{:S(2)}, u32[]{:S(2)}) collective-permute-start(bf16[16,4096]{1,0:T(8,128)(2,1)S(1)} %get-tuple-element.47.v_ref.refs_7_), channel_id=1, source_target_pairs={{0,4},{4,0},{8,12},{12,8},{16,20},{20,16},{24,28},{28,24},{1,5},{5... | collective-permute-start | bytes 393224 | tf_op jit(solution)/shard_map/ppermute | solution.py:313
  35.0 5.0 %collective-permute-start.8 = (bf16[16,4096]{1,0:T(8,128)(2,1)S(1)}, bf16[16,4096]{1,0:T(8,128)(2,1)S(1)}, u32[]{:S(2)}, u32[]{:S(2)}) collective-permute-start(bf16[16,4096]{1,0:T(8,128)(2,1)S(1)} %get-tuple-element.47.v_ref.refs_7_), channel_id=1, source_target_pairs={{0,8},{4,12},{8,0},{12,4},{16,24},{20,28},{24,16},{28,20},{1,9},{5... | collective-permute-start | bytes 393224 | tf_op jit(solution)/shard_map/ppermute | solution.py:313
  35.7 5.9 %collective-permute-start.7 = (bf16[16,4096]{1,0:T(8,128)(2,1)S(1)}, bf16[16,4096]{1,0:T(8,128)(2,1)S(1)}, u32[]{:S(2)}, u32[]{:S(2)}) collective-permute-start(bf16[16,4096]{1,0:T(8,128)(2,1)S(1)} %get-tuple-element.47.v_ref.refs_7_), channel_id=1, source_target_pairs={{0,12},{4,8},{8,4},{12,0},{16,28},{20,24},{24,20},{28,16},{1,13},{... | collective-permute-start | bytes 393224 | tf_op jit(solution)/shard_map/ppermute | solution.py:313
  42.3 3.2 %collective-permute-start.12 = (bf16[16,640]{1,0:T(8,128)(2,1)S(1)}, bf16[16,640]{1,0:T(8,128)(2,1)S(1)}, u32[]{:S(2)}, u32[]{:S(2)}) collective-permute-start(bf16[16,640]{1,0:T(8,128)(2,1)S(1)} %shard_map.68.refs_0_), channel_id=1, source_target_pairs={{0,3},{1,2},{2,1},{3,0},{4,7},{5,6},{6,5},{7,4},{8,11},{9,10},{10,... | collective-permute-start | bytes 61448 | tf_op jit(solution)/shard_map/ppermute | solution.py:313
  42.3 3.8 %collective-permute-start.11 = (bf16[16,640]{1,0:T(8,128)(2,1)S(1)}, bf16[16,640]{1,0:T(8,128)(2,1)S(1)}, u32[]{:S(2)}, u32[]{:S(2)}) collective-permute-start(bf16[16,640]{1,0:T(8,128)(2,1)S(1)} %shard_map.68.refs_0_), channel_id=1, source_target_pairs={{0,2},{1,3},{2,0},{3,1},{4,6},{5,7},{6,4},{7,5},{8,10},{9,11},{10,... | collective-permute-start | bytes 61448 | tf_op jit(solution)/shard_map/ppermute | solution.py:313
  43.0 3.1 %collective-permute-start.10 = (bf16[16,640]{1,0:T(8,128)(2,1)S(1)}, bf16[16,640]{1,0:T(8,128)(2,1)S(1)}, u32[]{:S(2)}, u32[]{:S(2)}) collective-permute-start(bf16[16,640]{1,0:T(8,128)(2,1)S(1)} %shard_map.68.refs_0_), channel_id=1, source_target_pairs={{0,1},{1,0},{2,3},{3,2},{4,5},{5,4},{6,7},{7,6},{8,9},{9,8},{10,11... | collective-permute-start | bytes 61448 | tf_op jit(solution)/shard_map/ppermute | solution.py:313
  47.0 6.1 %collective-permute-start.13 = (bf16[16,4224]{1,0:T(8,128)(2,1)S(1)}, bf16[16,4224]{1,0:T(8,128)(2,1)S(1)}, u32[]{:S(2)}, u32[]{:S(2)}) collective-permute-start(bf16[16,4224]{1,0:T(8,128)(2,1)S(1)} %shard_map.71), channel_id=1, source_target_pairs={{0,8},{4,12},{8,0},{12,4},{16,24},{20,28},{24,16},{28,20},{1,9},{5... | collective-permute-start | bytes 405512 | tf_op jit(solution)/shard_map/ppermute | solution.py:313
  49.3 7.9 %collective-permute-start.14 = (bf16[16,4224]{1,0:T(8,128)(2,1)S(1)}, bf16[16,4224]{1,0:T(8,128)(2,1)S(1)}, u32[]{:S(2)}, u32[]{:S(2)}) collective-permute-start(bf16[16,4224]{1,0:T(8,128)(2,1)S(1)} %shard_map.73), channel_id=1, source_target_pairs={{0,4},{4,0},{8,12},{12,8},{16,20},{20,16},{24,28},{28,24},{1,5},{5... | collective-permute-start | bytes 405512 | tf_op jit(solution)/shard_map/ppermute | solution.py:313
  50.9 6.4 %collective-permute-start.15 = (bf16[16,4224]{1,0:T(8,128)(2,1)S(1)}, bf16[16,4224]{1,0:T(8,128)(2,1)S(1)}, u32[]{:S(2)}, u32[]{:S(2)}) collective-permute-start(bf16[16,4224]{1,0:T(8,128)(2,1)S(1)} %shard_map.75), channel_id=1, source_target_pairs={{0,12},{4,8},{8,4},{12,0},{16,28},{20,24},{24,20},{28,16},{1,13},{... | collective-permute-start | bytes 405512 | tf_op jit(solution)/shard_map/ppermute | solution.py:313
  57.4 6.8 %collective-permute-start.16 = (bf16[16,4224]{1,0:T(8,128)(2,1)S(1)}, bf16[16,4224]{1,0:T(8,128)(2,1)S(1)}, u32[]{:S(2)}, u32[]{:S(2)}) collective-permute-start(bf16[16,4224]{1,0:T(8,128)(2,1)S(1)} %shard_map.76.refs_2_), channel_id=1, source_target_pairs={{0,24},{4,28},{8,16},{12,20},{16,8},{20,12},{24,0},{28,4},{1,25},{... | collective-permute-start | bytes 405512 | tf_op jit(solution)/shard_map/ppermute | solution.py:313
  64.4 5.0 %collective-permute-start.19 = (bf16[16,4096]{1,0:T(8,128)(2,1)S(1)}, bf16[16,4096]{1,0:T(8,128)(2,1)S(1)}, u32[]{:S(2)}, u32[]{:S(2)}) collective-permute-start(bf16[16,4096]{1,0:T(8,128)(2,1)S(1)} %get-tuple-element.54.v_ref.refs_11_), channel_id=1, source_target_pairs={{0,4},{4,0},{8,12},{12,8},{16,20},{20,16},{24,28},{28,24},{1,5},{5... | collective-permute-start | bytes 393224 | tf_op jit(solution)/shard_map/ppermute | solution.py:313
  65.3 5.0 %collective-permute-start.18 = (bf16[16,4096]{1,0:T(8,128)(2,1)S(1)}, bf16[16,4096]{1,0:T(8,128)(2,1)S(1)}, u32[]{:S(2)}, u32[]{:S(2)}) collective-permute-start(bf16[16,4096]{1,0:T(8,128)(2,1)S(1)} %get-tuple-element.54.v_ref.refs_11_), channel_id=1, source_target_pairs={{0,8},{4,12},{8,0},{12,4},{16,24},{20,28},{24,16},{28,20},{1,9},{5... | collective-permute-start | bytes 393224 | tf_op jit(solution)/shard_map/ppermute | solution.py:313
  66.1 6.2 %collective-permute-start.17 = (bf16[16,4096]{1,0:T(8,128)(2,1)S(1)}, bf16[16,4096]{1,0:T(8,128)(2,1)S(1)}, u32[]{:S(2)}, u32[]{:S(2)}) collective-permute-start(bf16[16,4096]{1,0:T(8,128)(2,1)S(1)} %get-tuple-element.54.v_ref.refs_11_), channel_id=1, source_target_pairs={{0,12},{4,8},{8,4},{12,0},{16,28},{20,24},{24,20},{28,16},{1,13},{... | collective-permute-start | bytes 393224 | tf_op jit(solution)/shard_map/ppermute | solution.py:313
  72.9 3.2 %collective-permute-start.22 = (bf16[16,640]{1,0:T(8,128)(2,1)S(1)}, bf16[16,640]{1,0:T(8,128)(2,1)S(1)}, u32[]{:S(2)}, u32[]{:S(2)}) collective-permute-start(bf16[16,640]{1,0:T(8,128)(2,1)S(1)} %shard_map.81.refs_2_), channel_id=1, source_target_pairs={{0,3},{1,2},{2,1},{3,0},{4,7},{5,6},{6,5},{7,4},{8,11},{9,10},{10,... | collective-permute-start | bytes 61448 | tf_op jit(solution)/shard_map/ppermute | solution.py:313
  72.9 3.8 %collective-permute-start.21 = (bf16[16,640]{1,0:T(8,128)(2,1)S(1)}, bf16[16,640]{1,0:T(8,128)(2,1)S(1)}, u32[]{:S(2)}, u32[]{:S(2)}) collective-permute-start(bf16[16,640]{1,0:T(8,128)(2,1)S(1)} %shard_map.81.refs_2_), channel_id=1, source_target_pairs={{0,2},{1,3},{2,0},{3,1},{4,6},{5,7},{6,4},{7,5},{8,10},{9,11},{10,... | collective-permute-start | bytes 61448 | tf_op jit(solution)/shard_map/ppermute | solution.py:313
  74.2 2.5 %collective-permute-start.20 = (bf16[16,640]{1,0:T(8,128)(2,1)S(1)}, bf16[16,640]{1,0:T(8,128)(2,1)S(1)}, u32[]{:S(2)}, u32[]{:S(2)}) collective-permute-start(bf16[16,640]{1,0:T(8,128)(2,1)S(1)} %shard_map.81.refs_2_), channel_id=1, source_target_pairs={{0,1},{1,0},{2,3},{3,2},{4,5},{5,4},{6,7},{7,6},{8,9},{9,8},{10,11... | collective-permute-start | bytes 61448 | tf_op jit(solution)/shard_map/ppermute | solution.py:313
  77.7 5.9 %collective-permute-start.23 = (bf16[16,4224]{1,0:T(8,128)(2,1)S(1)}, bf16[16,4224]{1,0:T(8,128)(2,1)S(1)}, u32[]{:S(2)}, u32[]{:S(2)}) collective-permute-start(bf16[16,4224]{1,0:T(8,128)(2,1)S(1)} %shard_map.84), channel_id=1, source_target_pairs={{0,8},{4,12},{8,0},{12,4},{16,24},{20,28},{24,16},{28,20},{1,9},{5... | collective-permute-start | bytes 405512 | tf_op jit(solution)/shard_map/ppermute | solution.py:313
  79.5 8.2 %collective-permute-start.24 = (bf16[16,4224]{1,0:T(8,128)(2,1)S(1)}, bf16[16,4224]{1,0:T(8,128)(2,1)S(1)}, u32[]{:S(2)}, u32[]{:S(2)}) collective-permute-start(bf16[16,4224]{1,0:T(8,128)(2,1)S(1)} %shard_map.86), channel_id=1, source_target_pairs={{0,4},{4,0},{8,12},{12,8},{16,20},{20,16},{24,28},{28,24},{1,5},{5... | collective-permute-start | bytes 405512 | tf_op jit(solution)/shard_map/ppermute | solution.py:313
  81.4 6.3 %collective-permute-start.25 = (bf16[16,4224]{1,0:T(8,128)(2,1)S(1)}, bf16[16,4224]{1,0:T(8,128)(2,1)S(1)}, u32[]{:S(2)}, u32[]{:S(2)}) collective-permute-start(bf16[16,4224]{1,0:T(8,128)(2,1)S(1)} %shard_map.88), channel_id=1, source_target_pairs={{0,12},{4,8},{8,4},{12,0},{16,28},{20,24},{24,20},{28,16},{1,13},{... | collective-permute-start | bytes 405512 | tf_op jit(solution)/shard_map/ppermute | solution.py:313
  87.9 7.0 %collective-permute-start.26 = (bf16[16,4224]{1,0:T(8,128)(2,1)S(1)}, bf16[16,4224]{1,0:T(8,128)(2,1)S(1)}, u32[]{:S(2)}, u32[]{:S(2)}) collective-permute-start(bf16[16,4224]{1,0:T(8,128)(2,1)S(1)} %shard_map.89.refs_2_), channel_id=1, source_target_pairs={{0,24},{4,28},{8,16},{12,20},{16,8},{20,12},{24,0},{28,4},{1,25},{... | collective-permute-start | bytes 405512 | tf_op jit(solution)/shard_map/ppermute | solution.py:313
  95.0 5.3 %collective-permute-start.29 = (bf16[16,4096]{1,0:T(8,128)(2,1)S(1)}, bf16[16,4096]{1,0:T(8,128)(2,1)S(1)}, u32[]{:S(2)}, u32[]{:S(2)}) collective-permute-start(bf16[16,4096]{1,0:T(8,128)(2,1)S(1)} %get-tuple-element.61.v_ref.refs_15_), channel_id=1, source_target_pairs={{0,4},{4,0},{8,12},{12,8},{16,20},{20,16},{24,28},{28,24},{1,5},{5... | collective-permute-start | bytes 393224 | tf_op jit(solution)/shard_map/ppermute | solution.py:313
  96.2 5.0 %collective-permute-start.28 = (bf16[16,4096]{1,0:T(8,128)(2,1)S(1)}, bf16[16,4096]{1,0:T(8,128)(2,1)S(1)}, u32[]{:S(2)}, u32[]{:S(2)}) collective-permute-start(bf16[16,4096]{1,0:T(8,128)(2,1)S(1)} %get-tuple-element.61.v_ref.refs_15_), channel_id=1, source_target_pairs={{0,8},{4,12},{8,0},{12,4},{16,24},{20,28},{24,16},{28,20},{1,9},{5... | collective-permute-start | bytes 393224 | tf_op jit(solution)/shard_map/ppermute | solution.py:313
  96.9 5.9 %collective-permute-start.27 = (bf16[16,4096]{1,0:T(8,128)(2,1)S(1)}, bf16[16,4096]{1,0:T(8,128)(2,1)S(1)}, u32[]{:S(2)}, u32[]{:S(2)}) collective-permute-start(bf16[16,4096]{1,0:T(8,128)(2,1)S(1)} %get-tuple-element.61.v_ref.refs_15_), channel_id=1, source_target_pairs={{0,12},{4,8},{8,4},{12,0},{16,28},{20,24},{24,20},{28,16},{1,13},{... | collective-permute-start | bytes 393224 | tf_op jit(solution)/shard_map/ppermute | solution.py:313
  103.5 3.3 %collective-permute-start.32 = (bf16[16,640]{1,0:T(8,128)(2,1)S(1)}, bf16[16,640]{1,0:T(8,128)(2,1)S(1)}, u32[]{:S(2)}, u32[]{:S(2)}) collective-permute-start(bf16[16,640]{1,0:T(8,128)(2,1)S(1)} %shard_map.94.refs_2_), channel_id=1, source_target_pairs={{0,3},{1,2},{2,1},{3,0},{4,7},{5,6},{6,5},{7,4},{8,11},{9,10},{10,... | collective-permute-start | bytes 61448 | tf_op jit(solution)/shard_map/ppermute | solution.py:313
  103.5 3.8 %collective-permute-start.31 = (bf16[16,640]{1,0:T(8,128)(2,1)S(1)}, bf16[16,640]{1,0:T(8,128)(2,1)S(1)}, u32[]{:S(2)}, u32[]{:S(2)}) collective-permute-start(bf16[16,640]{1,0:T(8,128)(2,1)S(1)} %shard_map.94.refs_2_), channel_id=1, source_target_pairs={{0,2},{1,3},{2,0},{3,1},{4,6},{5,7},{6,4},{7,5},{8,10},{9,11},{10,... | collective-permute-start | bytes 61448 | tf_op jit(solution)/shard_map/ppermute | solution.py:313
  104.9 2.5 %collective-permute-start.30 = (bf16[16,640]{1,0:T(8,128)(2,1)S(1)}, bf16[16,640]{1,0:T(8,128)(2,1)S(1)}, u32[]{:S(2)}, u32[]{:S(2)}) collective-permute-start(bf16[16,640]{1,0:T(8,128)(2,1)S(1)} %shard_map.94.refs_2_), channel_id=1, source_target_pairs={{0,1},{1,0},{2,3},{3,2},{4,5},{5,4},{6,7},{7,6},{8,9},{9,8},{10,11... | collective-permute-start | bytes 61448 | tf_op jit(solution)/shard_map/ppermute | solution.py:313
  108.4 5.9 %collective-permute-start.33 = (bf16[16,4224]{1,0:T(8,128)(2,1)S(1)}, bf16[16,4224]{1,0:T(8,128)(2,1)S(1)}, u32[]{:S(2)}, u32[]{:S(2)}) collective-permute-start(bf16[16,4224]{1,0:T(8,128)(2,1)S(1)} %shard_map.97), channel_id=1, source_target_pairs={{0,8},{4,12},{8,0},{12,4},{16,24},{20,28},{24,16},{28,20},{1,9},{5... | collective-permute-start | bytes 405512 | tf_op jit(solution)/shard_map/ppermute | solution.py:313
  110.5 8.2 %collective-permute-start.34 = (bf16[16,4224]{1,0:T(8,128)(2,1)S(1)}, bf16[16,4224]{1,0:T(8,128)(2,1)S(1)}, u32[]{:S(2)}, u32[]{:S(2)}) collective-permute-start(bf16[16,4224]{1,0:T(8,128)(2,1)S(1)} %shard_map.99), channel_id=1, source_target_pairs={{0,4},{4,0},{8,12},{12,8},{16,20},{20,16},{24,28},{28,24},{1,5},{5... | collective-permute-start | bytes 405512 | tf_op jit(solution)/shard_map/ppermute | solution.py:313
  112.0 6.7 %collective-permute-start.35 = (bf16[16,4224]{1,0:T(8,128)(2,1)S(1)}, bf16[16,4224]{1,0:T(8,128)(2,1)S(1)}, u32[]{:S(2)}, u32[]{:S(2)}) collective-permute-start(bf16[16,4224]{1,0:T(8,128)(2,1)S(1)} %shard_map.101), channel_id=1, source_target_pairs={{0,12},{4,8},{8,4},{12,0},{16,28},{20,24},{24,20},{28,16},{1,13},{... | collective-permute-start | bytes 405512 | tf_op jit(solution)/shard_map/ppermute | solution.py:313
  118.9 7.0 %collective-permute-start.36 = (bf16[16,4224]{1,0:T(8,128)(2,1)S(1)}, bf16[16,4224]{1,0:T(8,128)(2,1)S(1)}, u32[]{:S(2)}, u32[]{:S(2)}) collective-permute-start(bf16[16,4224]{1,0:T(8,128)(2,1)S(1)} %shard_map.102.refs_2_), channel_id=1, source_target_pairs={{0,24},{4,28},{8,16},{12,20},{16,8},{20,12},{24,0},{28,4},{1,25},{... | collective-permute-start | bytes 405512 | tf_op jit(solution)/shard_map/ppermute | solution.py:313
  126.7 5.0 %collective-permute-start.39 = (bf16[16,4096]{1,0:T(8,128)(2,1)S(1)}, bf16[16,4096]{1,0:T(8,128)(2,1)S(1)}, u32[]{:S(2)}, u32[]{:S(2)}) collective-permute-start(bf16[16,4096]{1,0:T(8,128)(2,1)S(1)} %get-tuple-element.68.v_ref.refs_19_), channel_id=1, source_target_pairs={{0,4},{4,0},{8,12},{12,8},{16,20},{20,16},{24,28},{28,24},{1,5},{5... | collective-permute-start | bytes 393224 | tf_op jit(solution)/shard_map/ppermute | solution.py:313
  127.5 5.0 %collective-permute-start.38 = (bf16[16,4096]{1,0:T(8,128)(2,1)S(1)}, bf16[16,4096]{1,0:T(8,128)(2,1)S(1)}, u32[]{:S(2)}, u32[]{:S(2)}) collective-permute-start(bf16[16,4096]{1,0:T(8,128)(2,1)S(1)} %get-tuple-element.68.v_ref.refs_19_), channel_id=1, source_target_pairs={{0,8},{4,12},{8,0},{12,4},{16,24},{20,28},{24,16},{28,20},{1,9},{5... | collective-permute-start | bytes 393224 | tf_op jit(solution)/shard_map/ppermute | solution.py:313
  128.3 6.2 %collective-permute-start.37 = (bf16[16,4096]{1,0:T(8,128)(2,1)S(1)}, bf16[16,4096]{1,0:T(8,128)(2,1)S(1)}, u32[]{:S(2)}, u32[]{:S(2)}) collective-permute-start(bf16[16,4096]{1,0:T(8,128)(2,1)S(1)} %get-tuple-element.68.v_ref.refs_19_), channel_id=1, source_target_pairs={{0,12},{4,8},{8,4},{12,0},{16,28},{20,24},{24,20},{28,16},{1,13},{... | collective-permute-start | bytes 393224 | tf_op jit(solution)/shard_map/ppermute | solution.py:313
  135.1 3.2 %collective-permute-start.42 = (bf16[16,640]{1,0:T(8,128)(2,1)S(1)}, bf16[16,640]{1,0:T(8,128)(2,1)S(1)}, u32[]{:S(2)}, u32[]{:S(2)}) collective-permute-start(bf16[16,640]{1,0:T(8,128)(2,1)S(1)} %shard_map.107.refs_2_), channel_id=1, source_target_pairs={{0,3},{1,2},{2,1},{3,0},{4,7},{5,6},{6,5},{7,4},{8,11},{9,10},{10,... | collective-permute-start | bytes 61448 | tf_op jit(solution)/shard_map/ppermute | solution.py:313
  135.1 3.8 %collective-permute-start.41 = (bf16[16,640]{1,0:T(8,128)(2,1)S(1)}, bf16[16,640]{1,0:T(8,128)(2,1)S(1)}, u32[]{:S(2)}, u32[]{:S(2)}) collective-permute-start(bf16[16,640]{1,0:T(8,128)(2,1)S(1)} %shard_map.107.refs_2_), channel_id=1, source_target_pairs={{0,2},{1,3},{2,0},{3,1},{4,6},{5,7},{6,4},{7,5},{8,10},{9,11},{10,... | collective-permute-start | bytes 61448 | tf_op jit(solution)/shard_map/ppermute | solution.py:313
  136.4 2.6 %collective-permute-start.40 = (bf16[16,640]{1,0:T(8,128)(2,1)S(1)}, bf16[16,640]{1,0:T(8,128)(2,1)S(1)}, u32[]{:S(2)}, u32[]{:S(2)}) collective-permute-start(bf16[16,640]{1,0:T(8,128)(2,1)S(1)} %shard_map.107.refs_2_), channel_id=1, source_target_pairs={{0,1},{1,0},{2,3},{3,2},{4,5},{5,4},{6,7},{7,6},{8,9},{9,8},{10,11... | collective-permute-start | bytes 61448 | tf_op jit(solution)/shard_map/ppermute | solution.py:313
  139.2 5.4 %collective-permute-start.46 = (f32[16,128]{1,0:T(8,128)S(1)}, f32[16,128]{1,0:T(8,128)S(1)}, u32[]{:S(2)}, u32[]{:S(2)}) collective-permute-start(f32[16,128]{1,0:T(8,128)S(1)} %get-tuple-element.80.mine_ref), channel_id=1, source_target_pairs={{0,12},{1,29},{2,14},{3,31},{4,8},{5,25},{6,10},{7,27},{8,4},{9,21... | collective-permute-start | bytes 24584 | tf_op jit(solution)/shard_map/ppermute | solution.py:353
  140.7 3.9 %collective-permute-start.45 = (f32[16,128]{1,0:T(8,128)S(1)}, f32[16,128]{1,0:T(8,128)S(1)}, u32[]{:S(2)}, u32[]{:S(2)}) collective-permute-start(f32[16,128]{1,0:T(8,128)S(1)} %get-tuple-element.80.mine_ref), channel_id=1, source_target_pairs={{0,8},{1,25},{2,10},{3,27},{4,12},{5,29},{6,14},{7,31},{8,0},{9,17... | collective-permute-start | bytes 24584 | tf_op jit(solution)/shard_map/ppermute | solution.py:353
  141.5 3.7 %collective-permute-start.44 = (f32[16,128]{1,0:T(8,128)S(1)}, f32[16,128]{1,0:T(8,128)S(1)}, u32[]{:S(2)}, u32[]{:S(2)}) collective-permute-start(f32[16,128]{1,0:T(8,128)S(1)} %get-tuple-element.80.mine_ref), channel_id=1, source_target_pairs={{0,4},{1,21},{2,6},{3,23},{4,0},{5,17},{6,2},{7,19},{8,12},{9,29},... | collective-permute-start | bytes 24584 | tf_op jit(solution)/shard_map/ppermute | solution.py:353
  142.6 4.5 %collective-permute-start.43 = (f32[16,128]{1,0:T(8,128)S(1)}, f32[16,128]{1,0:T(8,128)S(1)}, u32[]{:S(2)}, u32[]{:S(2)}) collective-permute-start(f32[16,128]{1,0:T(8,128)S(1)} %get-tuple-element.80.mine_ref), channel_id=1, source_target_pairs={{0,16},{1,17},{2,18},{3,19},{4,20},{5,21},{6,22},{7,23},{8,24},{9,... | collective-permute-start | bytes 24584 | tf_op jit(solution)/shard_map/ppermute | solution.py:353
  147.2 1.2 collective-permute-start.47

commit v8 on v7

--- a/solution.py
+++ b/solution.py
@@ -9,6 +9,8 @@
 
 ITERS = 4
 EARLY = 4
+RS_ORDERS = ((2, 1, 3), (2, 1, 3))
+AG_ORDERS = ((3, 2, 1), (1, 2, 3))
 LIMIT = 8
 ADD_FLOPS = 1 << 28
 LANES = 128
@@ -115,12 +117,21 @@
     )
 
 
-def place(n_obs, near, distance):
+def odd():
+    return (lax.axis_index("par") & 1) == 1
+
+
+def place(n_obs, near, distances):
     me = lax.axis_index("obs")
     own = me & (near - 1)
     if mirrored(n_obs, near):
         own = own ^ (((me >> 2) & 1) << 1)
-    return own ^ distance
+    even_one, odd_one = distances
+    return own ^ (even_one if even_one == odd_one else jnp.where(odd(), odd_one, even_one))
+
+
+def slots(near, orders):
+    return list(zip(*orders)) if near == 4 else [(d, d) for d in range(1, near)]
 
 
 def mirrored(n_obs, near):
@@ -234,11 +245,17 @@
     out_ref[...] = sum_ref[...] + got_ref[:, : out_ref.shape[1]].astype(F32)
 
 
+def by_distance(order, member):
+    return sorted(range(len(order)), key=lambda k: order[k][member])
+
+
 def near_kernel(order, sum_ref, norm_ref, *refs):
     *got_refs, out_ref = refs
     width = sum_ref.shape[1]
     total = sum_ref[...] + got_refs[-1][:, :width].astype(F32)
-    norm = tree([norm_ref[...]] + [unpack_norm(ref[:, width:]) for _, ref in sorted(zip(order, got_refs), key=lambda pair: pair[0])])
+    norms = [unpack_norm(ref[:, width:]) for ref in got_refs]
+    even, other = ([norm_ref[...]] + [norms[k] for k in by_distance(order, member)] for member in range(2))
+    norm = jnp.where(odd(), tree(other), tree(even))
     out_ref[:, :width] = total.astype(BF16)
     out_ref[:, width:] = pack_norm(norm)
 
@@ -274,8 +291,8 @@
     alphas = ins[: ITERS - 1]
     betas = ins[ITERS - 1 : 2 * ITERS - 1]
     pieces = ins[2 * ITERS - 1 :]
-    for d in range(near):
-        base = place(n_obs, near, d) * width
+    for d, distances in enumerate([(0, 0)] + slots(near, AG_ORDERS)):
+        base = place(n_obs, near, distances) * width
         for k in range(width // LANES):
             at = pl.ds(pl.multiple_of(base + k * LANES, LANES), LANES)
             here = slice(k * LANES, (k + 1) * LANES)
@@ -311,6 +328,14 @@
 
 def exchange(value, axis, size, distance):
     return lax.ppermute(value, axis, [(i, i ^ distance) for i in range(size)])
+
+
+def exchange_slot(value, n_obs, n_par, distances):
+    pairs = []
+    for at in range(n_obs):
+        for member in range(n_par):
+            pairs.append((at * n_par + member, (at ^ distances[member % 2]) * n_par + member))
+    return lax.ppermute(value, ("obs", "par"), pairs)
 
 
 def stages(size, stride=1):
@@ -364,13 +389,13 @@
     term_shape = shape(2 * scen, rows, dtype=BF16)
 
     def gradient_parts(w, norm, packed):
-        order = (2, 1, 3) if near == 4 else tuple(range(1, near))
-        got = {d: exchange(backward(n_obs, near, d, op, w, packed), "obs", n_obs, d) for d in order}
-        total = backward(n_obs, near, 0, op, w)
-        for d in order[:-1]:
-            total = call(add_kernel, shape(scen, width), (total, got[d]), flops=ADD_FLOPS)
+        order = slots(near, RS_ORDERS)
+        got = [exchange_slot(backward(n_obs, near, d, op, w, packed), n_obs, n_par, d) for d in order]
+        total = backward(n_obs, near, (0, 0), op, w)
+        for piece in got[:-1]:
+            total = call(add_kernel, shape(scen, width), (total, piece), flops=ADD_FLOPS)
         both = shape(scen, width + LANES, dtype=BF16)
-        value = call(functools.partial(near_kernel, order), both, (total, norm, *(got[d] for d in order)))
+        value = call(functools.partial(near_kernel, order), both, (total, norm, *got))
         parts = [value]
         for index, (stride, members) in enumerate(stages(n_obs, near)):
             if index:
@@ -381,14 +406,14 @@
         return parts
 
     def image_parts(mine):
-        got = {d: exchange(mine, "obs", n_obs, d) for d in range(1, near)}
+        got = [exchange_slot(mine, n_obs, n_par, d) for d in slots(near, AG_ORDERS)]
         total = forward(near == 1, turned[0], mine)
-        for d in got:
-            total = forward(d == near - 1, turned[d], got[d], total)
-        return parts_over(total, "par", n_par, True), [mine] + [got[d] for d in range(1, near)]
+        for k, piece in enumerate(got):
+            total = forward(k == len(got) - 1, turned[k + 1], piece, total)
+        return parts_over(total, "par", n_par, True), [mine] + got
 
     op, first = load(operator, start)
-    turned = [turn(n_obs, near, d, op) for d in range(near)]
+    turned = [turn(n_obs, near, d, op) for d in [(0, 0)] + slots(near, AG_ORDERS)]
     packed_lanes = shape(scen, LANES, dtype=BF16)
     residual, w, norm, packed = call(
         first_kernel, (image_shape, term_shape, lanes, packed_lanes), (targets, *parts_over(first, "par", n_par, False))

time: 150 us -> 148 us (0.987)
  waiting for transfers between devices: 54.3 us -> 52.6 us
    ppermute x0 -> x24, starting transfers between devices: none -> 28.2 us  [exchange_slot(): return lax.ppermute(value, ('obs', 'par'), pairs)]
    ppermute x44 -> x20, starting transfers between devices: 48.8 us -> 21 us  [exchange(): return lax.ppermute(value, axis, [(i, i ^ distance) for i in range(size)])]
    ppermute x44 -> x20, waiting for transfers between devices: 51.7 us -> 24.7 us  [exchange(): return lax.ppermute(value, axis, [(i, i ^ distance) for i in range(size)])]
    ppermute x0 -> x24, waiting for transfers between devices: none -> 24.9 us  [exchange_slot(): return lax.ppermute(value, ('obs', 'par'), pairs)]
  transfers between devices with their start and end apart: 48 -> 48, of which waited for: 32 -> 29; matrix products, arithmetic and copies ran while one was open for 0% -> 0% of each run, Pallas kernels for 15% -> 15%
where the time goes in v8:
time: 148 us
  starting transfers between devices  54.3 us (37%)
  waiting for transfers between devices  52.6 us (36%)
  Pallas kernels  40.3 us (27%)
    pallas_call x62, Pallas kernels, call(): pl.pallas_call(body, out_shape=out, in_specs=specs if specs is not None e...  40.3 us
    ppermute x24, starting transfers between devices, exchange_slot(): return lax.ppermute(value, ('obs', 'par'), pairs)  28.2 us
    ppermute x24, waiting for transfers between devices, exchange_slot(): return lax.ppermute(value, ('obs', 'par'), pairs)  24.9 us
    ppermute x20, waiting for transfers between devices, exchange(): return lax.ppermute(value, axis, [(i, i ^ distance) for i in range(size)])  24.7 us
    ppermute x20, starting transfers between devices, exchange(): return lax.ppermute(value, axis, [(i, i ^ distance) for i in range(size)])  21 us
    ppermute x4, starting transfers between devices, norm_parts(): got.append(lax.ppermute(norm, ('obs', 'par'), pairs))  5.06 us
    ppermute x4, waiting for transfers between devices, norm_parts(): got.append(lax.ppermute(norm, ('obs', 'par'), pairs))  2.98 us
  transfers between devices with their start and end apart: 48, of which 29 were waited for; matrix products, arithmetic and copies ran while one was open for 0% of the time, Pallas kernels for 15%

profile of v8, /device:TPU:0, one launch (start us, length us, event | category | flops | bytes accessed | tf_op | source)
XLA Modules:
  0.0 148.1 jit_solution(7218546361486685671)
XLA Ops:
  0.6 2.4 %shard_map.50.early_ref = bf16[512,16384]{1,0:T(8,128)(2,1)S(1)} custom-call(bf16[512,16384]{1,0:T(8,128)(2,1)} %op_hbm.3), custom_call_target="tpu_custom_call" | custom-call | bytes 1024 | tf_op jit(solution)/shard_map/pallas_call | solution.py:28
  3.1 5.2 %shard_map.51 = (bf16[512,16384]{1,0:T(8,128)(2,1)S(1)}, bf16[16,512]{1,0:T(8,128)(2,1)S(1)}) custom-call(bf16[512,16384]{1,0:T(8,128)(2,1)} %op_hbm.3, f32[16,16384]{1,0:T(8,128)S(1)} %copy-done, bf16[512,16384]{1,0:T(8,128)(2,1)S(1)} %shard_map.50.early_ref), custom_call_target="tpu_custom_call", output_to_operand_aliasing={{0}: (2, {})} | custom-call | bytes 1024 | tf_op jit(solution)/shard_map/pallas_call | solution.py:28
  8.3 2.5 %collective-permute-start.2 = (bf16[16,512]{1,0:T(8,128)(2,1)S(1)}, bf16[16,512]{1,0:T(8,128)(2,1)S(1)}, u32[]{:S(2)}, u32[]{:S(2)}) collective-permute-start(bf16[16,512]{1,0:T(8,128)(2,1)S(1)} %get-tuple-element.43.refs_0_), channel_id=1, source_target_pairs={{0,3},{1,2},{2,1},{3,0},{4,7},{5,6},{6,5},{7,4},{8,11},{9,10},{10,... | collective-permute-start | bytes 49160 | tf_op jit(solution)/shard_map/ppermute | solution.py:330
  12.2 2.3 %collective-permute-done.1.refs_2_ = bf16[16,512]{1,0:T(8,128)(2,1)S(1)} collective-permute-done((bf16[16,512]{1,0:T(8,128)(2,1)S(1)}, bf16[16,512]{1,0:T(8,128)(2,1)S(1)}, u32[]{:S(2)}, u32[]{:S(2)}) %collective-permute-start.1) | collective-permute-done | bytes 16416 | tf_op jit(solution)/shard_map/ppermute | solution.py:330
  14.6 0.8 shard_map.58
  15.4 1.6 %collective-permute-start.3 = (bf16[16,4224]{1,0:T(8,128)(2,1)S(1)}, bf16[16,4224]{1,0:T(8,128)(2,1)S(1)}, u32[]{:S(2)}, u32[]{:S(2)}) collective-permute-start(bf16[16,4224]{1,0:T(8,128)(2,1)S(1)} %shard_map.58), channel_id=1, source_target_pairs={{0,8},{1,9},{2,10},{3,11},{4,12},{5,13},{6,14},{7,15},{8,0},{9,1},... | collective-permute-start | bytes 405512 | tf_op jit(solution)/shard_map/ppermute | solution.py:338
  17.7 1.5 %collective-permute-start.4 = (bf16[16,4224]{1,0:T(8,128)(2,1)S(1)}, bf16[16,4224]{1,0:T(8,128)(2,1)S(1)}, u32[]{:S(2)}, u32[]{:S(2)}) collective-permute-start(bf16[16,4224]{1,0:T(8,128)(2,1)S(1)} %shard_map.60), channel_id=1, source_target_pairs={{0,4},{1,5},{2,6},{3,7},{4,0},{5,1},{6,2},{7,3},{8,12},{9,13},{10,... | collective-permute-start | bytes 405512 | tf_op jit(solution)/shard_map/ppermute | solution.py:338
  19.2 0.8 shard_map.62
  21.3 3.4 %collective-permute-done.4.got_ref.refs_1_ = bf16[16,4224]{1,0:T(8,128)(2,1)S(1)} collective-permute-done((bf16[16,4224]{1,0:T(8,128)(2,1)S(1)}, bf16[16,4224]{1,0:T(8,128)(2,1)S(1)}, u32[]{:S(2)}, u32[]{:S(2)}) %collective-permute-start.4) | collective-permute-done | bytes 135200 | tf_op jit(solution)/shard_map/ppermute | solution.py:338
  24.7 1.2 collective-permute-done.5.refs_2_
  26.1 2.5 %collective-permute-start.6 = (bf16[16,4224]{1,0:T(8,128)(2,1)S(1)}, bf16[16,4224]{1,0:T(8,128)(2,1)S(1)}, u32[]{:S(2)}, u32[]{:S(2)}) collective-permute-start(bf16[16,4224]{1,0:T(8,128)(2,1)S(1)} %shard_map.63.refs_4_), channel_id=1, source_target_pairs={{0,24},{4,28},{8,16},{12,20},{16,8},{20,12},{24,0},{28,4},{1,25},{... | collective-permute-start | bytes 405512 | tf_op jit(solution)/shard_map/ppermute | solution.py:330
  28.6 1.1 shard_map.55.refs_2_.turned_ref
  29.7 1.1 shard_map.54.refs_1_.turned_ref
  30.9 1.1 shard_map.53.refs_0_.turned_ref
  32.0 1.1 shard_map.52.refs_3_.turned_ref
  33.8 1.4 collective-permute-start.9
  35.2 1.4 collective-permute-start.8
  37.9 1.7 %collective-permute-done.9.v_ref.refs_8_ = bf16[16,4096]{1,0:T(8,128)(2,1)S(1)} collective-permute-done((bf16[16,4096]{1,0:T(8,128)(2,1)S(1)}, bf16[16,4096]{1,0:T(8,128)(2,1)S(1)}, u32[]{:S(2)}, u32[]{:S(2)}) %collective-permute-start.9) | collective-permute-done | bytes 131104 | tf_op jit(solution)/shard_map/ppermute | solution.py:338
  42.9 1.2 collective-permute-start.10
  44.0 1.3 collective-permute-done.12.refs_3_
  46.1 0.8 shard_map.71
  47.6 0.9 shard_map.73
  48.6 0.8 collective-permute-start.14
  50.2 2.0 %collective-permute-start.15 = (bf16[16,4224]{1,0:T(8,128)(2,1)S(1)}, bf16[16,4224]{1,0:T(8,128)(2,1)S(1)}, u32[]{:S(2)}, u32[]{:S(2)}) collective-permute-start(bf16[16,4224]{1,0:T(8,128)(2,1)S(1)} %shard_map.75), channel_id=1, source_target_pairs={{0,12},{1,13},{2,14},{3,15},{4,8},{5,9},{6,10},{7,11},{8,4},{9,5},... | collective-permute-start | bytes 405512 | tf_op jit(solution)/shard_map/ppermute | solution.py:338
  53.0 3.5 %collective-permute-done.14.got_ref.refs_1_ = bf16[16,4224]{1,0:T(8,128)(2,1)S(1)} collective-permute-done((bf16[16,4224]{1,0:T(8,128)(2,1)S(1)}, bf16[16,4224]{1,0:T(8,128)(2,1)S(1)}, u32[]{:S(2)}, u32[]{:S(2)}) %collective-permute-start.14) | collective-permute-done | bytes 135200 | tf_op jit(solution)/shard_map/ppermute | solution.py:338
  56.6 2.8 %collective-permute-start.16 = (bf16[16,4224]{1,0:T(8,128)(2,1)S(1)}, bf16[16,4224]{1,0:T(8,128)(2,1)S(1)}, u32[]{:S(2)}, u32[]{:S(2)}) collective-permute-start(bf16[16,4224]{1,0:T(8,128)(2,1)S(1)} %shard_map.76.refs_2_), channel_id=1, source_target_pairs={{0,24},{4,28},{8,16},{12,20},{16,8},{20,12},{24,0},{28,4},{1,25},{... | collective-permute-start | bytes 405512 | tf_op jit(solution)/shard_map/ppermute | solution.py:330
  59.4 4.2 %collective-permute-done.16.refs_3_ = bf16[16,4224]{1,0:T(8,128)(2,1)S(1)} collective-permute-done((bf16[16,4224]{1,0:T(8,128)(2,1)S(1)}, bf16[16,4224]{1,0:T(8,128)(2,1)S(1)}, u32[]{:S(2)}, u32[]{:S(2)}) %collective-permute-start.16) | collective-permute-done | bytes 135200 | tf_op jit(solution)/shard_map/ppermute | solution.py:330
  63.7 1.2 collective-permute-start.19
  64.9 1.3 collective-permute-start.18
  66.2 1.1 collective-permute-start.17
  67.9 1.7 %collective-permute-done.19.v_ref.refs_12_ = bf16[16,4096]{1,0:T(8,128)(2,1)S(1)} collective-permute-done((bf16[16,4096]{1,0:T(8,128)(2,1)S(1)}, bf16[16,4096]{1,0:T(8,128)(2,1)S(1)}, u32[]{:S(2)}, u32[]{:S(2)}) %collective-permute-start.19) | collective-permute-done | bytes 131104 | tf_op jit(solution)/shard_map/ppermute | solution.py:338
  71.8 1.2 collective-permute-start.21
  73.7 1.3 collective-permute-done.22.refs_5_
  75.9 0.8 shard_map.84
  78.2 1.2 collective-permute-start.24
  80.3 1.5 %collective-permute-start.25 = (bf16[16,4224]{1,0:T(8,128)(2,1)S(1)}, bf16[16,4224]{1,0:T(8,128)(2,1)S(1)}, u32[]{:S(2)}, u32[]{:S(2)}) collective-permute-start(bf16[16,4224]{1,0:T(8,128)(2,1)S(1)} %shard_map.88), channel_id=1, source_target_pairs={{0,12},{1,13},{2,14},{3,15},{4,8},{5,9},{6,10},{7,11},{8,4},{9,5},... | collective-permute-start | bytes 405512 | tf_op jit(solution)/shard_map/ppermute | solution.py:338
  82.6 4.4 %collective-permute-done.24.got_ref.refs_1_ = bf16[16,4224]{1,0:T(8,128)(2,1)S(1)} collective-permute-done((bf16[16,4224]{1,0:T(8,128)(2,1)S(1)}, bf16[16,4224]{1,0:T(8,128)(2,1)S(1)}, u32[]{:S(2)}, u32[]{:S(2)}) %collective-permute-start.24) | collective-permute-done | bytes 135200 | tf_op jit(solution)/shard_map/ppermute | solution.py:338
  87.2 2.3 %collective-permute-start.26 = (bf16[16,4224]{1,0:T(8,128)(2,1)S(1)}, bf16[16,4224]{1,0:T(8,128)(2,1)S(1)}, u32[]{:S(2)}, u32[]{:S(2)}) collective-permute-start(bf16[16,4224]{1,0:T(8,128)(2,1)S(1)} %shard_map.89.refs_2_), channel_id=1, source_target_pairs={{0,24},{4,28},{8,16},{12,20},{16,8},{20,12},{24,0},{28,4},{1,25},{... | collective-permute-start | bytes 405512 | tf_op jit(solution)/shard_map/ppermute | solution.py:330
  89.5 4.6 %collective-permute-done.26.refs_3_ = bf16[16,4224]{1,0:T(8,128)(2,1)S(1)} collective-permute-done((bf16[16,4224]{1,0:T(8,128)(2,1)S(1)}, bf16[16,4224]{1,0:T(8,128)(2,1)S(1)}, u32[]{:S(2)}, u32[]{:S(2)}) %collective-permute-start.26) | collective-permute-done | bytes 135200 | tf_op jit(solution)/shard_map/ppermute | solution.py:330
  94.3 1.7 %collective-permute-start.29 = (bf16[16,4096]{1,0:T(8,128)(2,1)S(1)}, bf16[16,4096]{1,0:T(8,128)(2,1)S(1)}, u32[]{:S(2)}, u32[]{:S(2)}) collective-permute-start(bf16[16,4096]{1,0:T(8,128)(2,1)S(1)} %get-tuple-element.61.v_ref.refs_15_), channel_id=1, source_target_pairs={{0,12},{1,5},{2,14},{3,7},{4,8},{5,1},{6,10},{7,3},{8,4},{9,13},{1... | collective-permute-start | bytes 393224 | tf_op jit(solution)/shard_map/ppermute | solution.py:338
  96.6 1.2 collective-permute-start.27
  98.5 1.7 %collective-permute-done.29.v_ref.refs_16_ = bf16[16,4096]{1,0:T(8,128)(2,1)S(1)} collective-permute-done((bf16[16,4096]{1,0:T(8,128)(2,1)S(1)}, bf16[16,4096]{1,0:T(8,128)(2,1)S(1)}, u32[]{:S(2)}, u32[]{:S(2)}) %collective-permute-start.29) | collective-permute-done | bytes 131104 | tf_op jit(solution)/shard_map/ppermute | solution.py:338
  102.2 1.1 collective-permute-start.31
  104.1 1.3 collective-permute-done.32.refs_5_
  106.3 0.8 shard_map.97
  107.1 1.3 collective-permute-start.33
  109.2 1.0 collective-permute-start.34
  111.0 1.2 collective-permute-start.35
  113.1 4.1 %collective-permute-done.34.got_ref.refs_1_ = bf16[16,4224]{1,0:T(8,128)(2,1)S(1)} collective-permute-done((bf16[16,4224]{1,0:T(8,128)(2,1)S(1)}, bf16[16,4224]{1,0:T(8,128)(2,1)S(1)}, u32[]{:S(2)}, u32[]{:S(2)}) %collective-permute-start.34) | collective-permute-done | bytes 135200 | tf_op jit(solution)/shard_map/ppermute | solution.py:338
  117.3 2.7 %collective-permute-start.36 = (bf16[16,4224]{1,0:T(8,128)(2,1)S(1)}, bf16[16,4224]{1,0:T(8,128)(2,1)S(1)}, u32[]{:S(2)}, u32[]{:S(2)}) collective-permute-start(bf16[16,4224]{1,0:T(8,128)(2,1)S(1)} %shard_map.102.refs_2_), channel_id=1, source_target_pairs={{0,24},{4,28},{8,16},{12,20},{16,8},{20,12},{24,0},{28,4},{1,25},{... | collective-permute-start | bytes 405512 | tf_op jit(solution)/shard_map/ppermute | solution.py:330
  120.0 4.3 %collective-permute-done.36.refs_3_ = bf16[16,4224]{1,0:T(8,128)(2,1)S(1)} collective-permute-done((bf16[16,4224]{1,0:T(8,128)(2,1)S(1)}, bf16[16,4224]{1,0:T(8,128)(2,1)S(1)}, u32[]{:S(2)}, u32[]{:S(2)}) %collective-permute-start.36) | collective-permute-done | bytes 135200 | tf_op jit(solution)/shard_map/ppermute | solution.py:330
  124.3 0.8 shard_map.103
  125.1 1.4 collective-permute-start.39
  126.5 1.4 collective-permute-start.38
  129.2 1.7 %collective-permute-done.39.v_ref.refs_20_ = bf16[16,4096]{1,0:T(8,128)(2,1)S(1)} collective-permute-done((bf16[16,4096]{1,0:T(8,128)(2,1)S(1)}, bf16[16,4096]{1,0:T(8,128)(2,1)S(1)}, u32[]{:S(2)}, u32[]{:S(2)}) %collective-permute-start.39) | collective-permute-done | bytes 131104 | tf_op jit(solution)/shard_map/ppermute | solution.py:338
  134.3 1.1 collective-permute-start.40
  135.4 1.3 collective-permute-done.42.refs_5_
  137.6 1.3 collective-permute-start.46
  138.8 1.0 collective-permute-start.45
  139.8 1.2 collective-permute-start.44
  141.0 1.6 %collective-permute-start.43 = (f32[16,128]{1,0:T(8,128)S(1)}, f32[16,128]{1,0:T(8,128)S(1)}, u32[]{:S(2)}, u32[]{:S(2)}) collective-permute-start(f32[16,128]{1,0:T(8,128)S(1)} %get-tuple-element.80.mine_ref), channel_id=1, source_target_pairs={{0,16},{1,17},{2,18},{3,19},{4,20},{5,21},{6,22},{7,23},{8,24},{9,... | collective-permute-start | bytes 24584 | tf_op jit(solution)/shard_map/ppermute | solution.py:378
  142.6 0.9 collective-permute-done.44.refs_1_
  143.5 2.1 %collective-permute-done.43.refs_0_ = f32[16,128]{1,0:T(8,128)S(1)} collective-permute-done((f32[16,128]{1,0:T(8,128)S(1)}, f32[16,128]{1,0:T(8,128)S(1)}, u32[]{:S(2)}, u32[]{:S(2)}) %collective-permute-start.43) | collective-permute-done | bytes 8224 | tf_op jit(solution)/shard_map/ppermute | solution.py:378
  146.8 1.3 shard_map.111
  (98 shorter events, 34.3 us)
Async XLA Ops:
  0.6 2.5 %copy-start = (f32[16,16384]{1,0:T(8,128)S(1)}, f32[16,16384]{1,0:T(8,128)}, u32[]{:S(2)}) copy-start(f32[16,16384]{1,0:T(8,128)} %start_ref.3) | copy-start | bytes 3145732
  3.1 11.4 %copy-start.1 = (f32[16,512]{1,0:T(8,128)S(1)}, f32[16,512]{1,0:T(8,128)}, u32[]{:S(2)}) copy-start(f32[16,512]{1,0:T(8,128)} %targets_ref.1) | copy-start | bytes 98308
  8.3 3.9 %collective-permute-start.2 = (bf16[16,512]{1,0:T(8,128)(2,1)S(1)}, bf16[16,512]{1,0:T(8,128)(2,1)S(1)}, u32[]{:S(2)}, u32[]{:S(2)}) collective-permute-start(bf16[16,512]{1,0:T(8,128)(2,1)S(1)} %get-tuple-element.43.refs_0_), channel_id=1, source_target_pairs={{0,3},{1,2},{2,1},{3,0},{4,7},{5,6},{6,5},{7,4},{8,11},{9,10},{10,... | collective-permute-start | bytes 49160 | tf_op jit(solution)/shard_map/ppermute | solution.py:330
  10.8 3.7 %collective-permute-start.1 = (bf16[16,512]{1,0:T(8,128)(2,1)S(1)}, bf16[16,512]{1,0:T(8,128)(2,1)S(1)}, u32[]{:S(2)}, u32[]{:S(2)}) collective-permute-start(bf16[16,512]{1,0:T(8,128)(2,1)S(1)} %get-tuple-element.43.refs_0_), channel_id=1, source_target_pairs={{0,2},{1,3},{2,0},{3,1},{4,6},{5,7},{6,4},{7,5},{8,10},{9,11},{10,... | collective-permute-start | bytes 49160 | tf_op jit(solution)/shard_map/ppermute | solution.py:330
  11.4 3.1 %collective-permute-start = (bf16[16,512]{1,0:T(8,128)(2,1)S(1)}, bf16[16,512]{1,0:T(8,128)(2,1)S(1)}, u32[]{:S(2)}, u32[]{:S(2)}) collective-permute-start(bf16[16,512]{1,0:T(8,128)(2,1)S(1)} %get-tuple-element.43.refs_0_), channel_id=1, source_target_pairs={{0,1},{1,0},{2,3},{3,2},{4,5},{5,4},{6,7},{7,6},{8,9},{9,8},{10,11... | collective-permute-start | bytes 49160 | tf_op jit(solution)/shard_map/ppermute | solution.py:330
  15.4 5.9 %collective-permute-start.3 = (bf16[16,4224]{1,0:T(8,128)(2,1)S(1)}, bf16[16,4224]{1,0:T(8,128)(2,1)S(1)}, u32[]{:S(2)}, u32[]{:S(2)}) collective-permute-start(bf16[16,4224]{1,0:T(8,128)(2,1)S(1)} %shard_map.58), channel_id=1, source_target_pairs={{0,8},{1,9},{2,10},{3,11},{4,12},{5,13},{6,14},{7,15},{8,0},{9,1},... | collective-permute-start | bytes 405512 | tf_op jit(solution)/shard_map/ppermute | solution.py:338
  17.7 7.0 %collective-permute-start.4 = (bf16[16,4224]{1,0:T(8,128)(2,1)S(1)}, bf16[16,4224]{1,0:T(8,128)(2,1)S(1)}, u32[]{:S(2)}, u32[]{:S(2)}) collective-permute-start(bf16[16,4224]{1,0:T(8,128)(2,1)S(1)} %shard_map.60), channel_id=1, source_target_pairs={{0,4},{1,5},{2,6},{3,7},{4,0},{5,1},{6,2},{7,3},{8,12},{9,13},{10,... | collective-permute-start | bytes 405512 | tf_op jit(solution)/shard_map/ppermute | solution.py:338
  20.0 5.9 %collective-permute-start.5 = (bf16[16,4224]{1,0:T(8,128)(2,1)S(1)}, bf16[16,4224]{1,0:T(8,128)(2,1)S(1)}, u32[]{:S(2)}, u32[]{:S(2)}) collective-permute-start(bf16[16,4224]{1,0:T(8,128)(2,1)S(1)} %shard_map.62), channel_id=1, source_target_pairs={{0,12},{1,13},{2,14},{3,15},{4,8},{5,9},{6,10},{7,11},{8,4},{9,5},... | collective-permute-start | bytes 405512 | tf_op jit(solution)/shard_map/ppermute | solution.py:338
  26.1 7.1 %collective-permute-start.6 = (bf16[16,4224]{1,0:T(8,128)(2,1)S(1)}, bf16[16,4224]{1,0:T(8,128)(2,1)S(1)}, u32[]{:S(2)}, u32[]{:S(2)}) collective-permute-start(bf16[16,4224]{1,0:T(8,128)(2,1)S(1)} %shard_map.63.refs_4_), channel_id=1, source_target_pairs={{0,24},{4,28},{8,16},{12,20},{16,8},{20,12},{24,0},{28,4},{1,25},{... | collective-permute-start | bytes 405512 | tf_op jit(solution)/shard_map/ppermute | solution.py:330
  33.8 5.9 %collective-permute-start.9 = (bf16[16,4096]{1,0:T(8,128)(2,1)S(1)}, bf16[16,4096]{1,0:T(8,128)(2,1)S(1)}, u32[]{:S(2)}, u32[]{:S(2)}) collective-permute-start(bf16[16,4096]{1,0:T(8,128)(2,1)S(1)} %get-tuple-element.47.v_ref.refs_7_), channel_id=1, source_target_pairs={{0,12},{1,5},{2,14},{3,7},{4,8},{5,1},{6,10},{7,3},{8,4},{9,13},{1... | collective-permute-start | bytes 393224 | tf_op jit(solution)/shard_map/ppermute | solution.py:338
  35.2 5.7 %collective-permute-start.8 = (bf16[16,4096]{1,0:T(8,128)(2,1)S(1)}, bf16[16,4096]{1,0:T(8,128)(2,1)S(1)}, u32[]{:S(2)}, u32[]{:S(2)}) collective-permute-start(bf16[16,4096]{1,0:T(8,128)(2,1)S(1)} %get-tuple-element.47.v_ref.refs_7_), channel_id=1, source_target_pairs={{0,8},{1,9},{2,10},{3,11},{4,12},{5,13},{6,14},{7,15},{8,0},{9,1},... | collective-permute-start | bytes 393224 | tf_op jit(solution)/shard_map/ppermute | solution.py:338
  36.5 5.0 %collective-permute-start.7 = (bf16[16,4096]{1,0:T(8,128)(2,1)S(1)}, bf16[16,4096]{1,0:T(8,128)(2,1)S(1)}, u32[]{:S(2)}, u32[]{:S(2)}) collective-permute-start(bf16[16,4096]{1,0:T(8,128)(2,1)S(1)} %get-tuple-element.47.v_ref.refs_7_), channel_id=1, source_target_pairs={{0,4},{1,13},{2,6},{3,15},{4,0},{5,9},{6,2},{7,11},{8,12},{9,5},{1... | collective-permute-start | bytes 393224 | tf_op jit(solution)/shard_map/ppermute | solution.py:338
  42.2 3.2 %collective-permute-start.12 = (bf16[16,640]{1,0:T(8,128)(2,1)S(1)}, bf16[16,640]{1,0:T(8,128)(2,1)S(1)}, u32[]{:S(2)}, u32[]{:S(2)}) collective-permute-start(bf16[16,640]{1,0:T(8,128)(2,1)S(1)} %shard_map.68.refs_0_), channel_id=1, source_target_pairs={{0,3},{1,2},{2,1},{3,0},{4,7},{5,6},{6,5},{7,4},{8,11},{9,10},{10,... | collective-permute-start | bytes 61448 | tf_op jit(solution)/shard_map/ppermute | solution.py:330
  42.2 3.8 %collective-permute-start.11 = (bf16[16,640]{1,0:T(8,128)(2,1)S(1)}, bf16[16,640]{1,0:T(8,128)(2,1)S(1)}, u32[]{:S(2)}, u32[]{:S(2)}) collective-permute-start(bf16[16,640]{1,0:T(8,128)(2,1)S(1)} %shard_map.68.refs_0_), channel_id=1, source_target_pairs={{0,2},{1,3},{2,0},{3,1},{4,6},{5,7},{6,4},{7,5},{8,10},{9,11},{10,... | collective-permute-start | bytes 61448 | tf_op jit(solution)/shard_map/ppermute | solution.py:330
  42.9 3.1 %collective-permute-start.10 = (bf16[16,640]{1,0:T(8,128)(2,1)S(1)}, bf16[16,640]{1,0:T(8,128)(2,1)S(1)}, u32[]{:S(2)}, u32[]{:S(2)}) collective-permute-start(bf16[16,640]{1,0:T(8,128)(2,1)S(1)} %shard_map.68.refs_0_), channel_id=1, source_target_pairs={{0,1},{1,0},{2,3},{3,2},{4,5},{5,4},{6,7},{7,6},{8,9},{9,8},{10,11... | collective-permute-start | bytes 61448 | tf_op jit(solution)/shard_map/ppermute | solution.py:330
  46.9 6.1 %collective-permute-start.13 = (bf16[16,4224]{1,0:T(8,128)(2,1)S(1)}, bf16[16,4224]{1,0:T(8,128)(2,1)S(1)}, u32[]{:S(2)}, u32[]{:S(2)}) collective-permute-start(bf16[16,4224]{1,0:T(8,128)(2,1)S(1)} %shard_map.71), channel_id=1, source_target_pairs={{0,8},{1,9},{2,10},{3,11},{4,12},{5,13},{6,14},{7,15},{8,0},{9,1},... | collective-permute-start | bytes 405512 | tf_op jit(solution)/shard_map/ppermute | solution.py:338
  48.6 7.9 %collective-permute-start.14 = (bf16[16,4224]{1,0:T(8,128)(2,1)S(1)}, bf16[16,4224]{1,0:T(8,128)(2,1)S(1)}, u32[]{:S(2)}, u32[]{:S(2)}) collective-permute-start(bf16[16,4224]{1,0:T(8,128)(2,1)S(1)} %shard_map.73), channel_id=1, source_target_pairs={{0,4},{1,5},{2,6},{3,7},{4,0},{5,1},{6,2},{7,3},{8,12},{9,13},{10,... | collective-permute-start | bytes 405512 | tf_op jit(solution)/shard_map/ppermute | solution.py:338
  50.2 6.3 %collective-permute-start.15 = (bf16[16,4224]{1,0:T(8,128)(2,1)S(1)}, bf16[16,4224]{1,0:T(8,128)(2,1)S(1)}, u32[]{:S(2)}, u32[]{:S(2)}) collective-permute-start(bf16[16,4224]{1,0:T(8,128)(2,1)S(1)} %shard_map.75), channel_id=1, source_target_pairs={{0,12},{1,13},{2,14},{3,15},{4,8},{5,9},{6,10},{7,11},{8,4},{9,5},... | collective-permute-start | bytes 405512 | tf_op jit(solution)/shard_map/ppermute | solution.py:338
  56.6 7.0 %collective-permute-start.16 = (bf16[16,4224]{1,0:T(8,128)(2,1)S(1)}, bf16[16,4224]{1,0:T(8,128)(2,1)S(1)}, u32[]{:S(2)}, u32[]{:S(2)}) collective-permute-start(bf16[16,4224]{1,0:T(8,128)(2,1)S(1)} %shard_map.76.refs_2_), channel_id=1, source_target_pairs={{0,24},{4,28},{8,16},{12,20},{16,8},{20,12},{24,0},{28,4},{1,25},{... | collective-permute-start | bytes 405512 | tf_op jit(solution)/shard_map/ppermute | solution.py:330
  63.7 5.9 %collective-permute-start.19 = (bf16[16,4096]{1,0:T(8,128)(2,1)S(1)}, bf16[16,4096]{1,0:T(8,128)(2,1)S(1)}, u32[]{:S(2)}, u32[]{:S(2)}) collective-permute-start(bf16[16,4096]{1,0:T(8,128)(2,1)S(1)} %get-tuple-element.54.v_ref.refs_11_), channel_id=1, source_target_pairs={{0,12},{1,5},{2,14},{3,7},{4,8},{5,1},{6,10},{7,3},{8,4},{9,13},{1... | collective-permute-start | bytes 393224 | tf_op jit(solution)/shard_map/ppermute | solution.py:338
  64.9 5.6 %collective-permute-start.18 = (bf16[16,4096]{1,0:T(8,128)(2,1)S(1)}, bf16[16,4096]{1,0:T(8,128)(2,1)S(1)}, u32[]{:S(2)}, u32[]{:S(2)}) collective-permute-start(bf16[16,4096]{1,0:T(8,128)(2,1)S(1)} %get-tuple-element.54.v_ref.refs_11_), channel_id=1, source_target_pairs={{0,8},{1,9},{2,10},{3,11},{4,12},{5,13},{6,14},{7,15},{8,0},{9,1},... | collective-permute-start | bytes 393224 | tf_op jit(solution)/shard_map/ppermute | solution.py:338
  66.2 5.0 %collective-permute-start.17 = (bf16[16,4096]{1,0:T(8,128)(2,1)S(1)}, bf16[16,4096]{1,0:T(8,128)(2,1)S(1)}, u32[]{:S(2)}, u32[]{:S(2)}) collective-permute-start(bf16[16,4096]{1,0:T(8,128)(2,1)S(1)} %get-tuple-element.54.v_ref.refs_11_), channel_id=1, source_target_pairs={{0,4},{1,13},{2,6},{3,15},{4,0},{5,9},{6,2},{7,11},{8,12},{9,5},{1... | collective-permute-start | bytes 393224 | tf_op jit(solution)/shard_map/ppermute | solution.py:338
  71.8 3.2 %collective-permute-start.22 = (bf16[16,640]{1,0:T(8,128)(2,1)S(1)}, bf16[16,640]{1,0:T(8,128)(2,1)S(1)}, u32[]{:S(2)}, u32[]{:S(2)}) collective-permute-start(bf16[16,640]{1,0:T(8,128)(2,1)S(1)} %shard_map.81.refs_2_), channel_id=1, source_target_pairs={{0,3},{1,2},{2,1},{3,0},{4,7},{5,6},{6,5},{7,4},{8,11},{9,10},{10,... | collective-permute-start | bytes 61448 | tf_op jit(solution)/shard_map/ppermute | solution.py:330
  71.8 3.9 %collective-permute-start.21 = (bf16[16,640]{1,0:T(8,128)(2,1)S(1)}, bf16[16,640]{1,0:T(8,128)(2,1)S(1)}, u32[]{:S(2)}, u32[]{:S(2)}) collective-permute-start(bf16[16,640]{1,0:T(8,128)(2,1)S(1)} %shard_map.81.refs_2_), channel_id=1, source_target_pairs={{0,2},{1,3},{2,0},{3,1},{4,6},{5,7},{6,4},{7,5},{8,10},{9,11},{10,... | collective-permute-start | bytes 61448 | tf_op jit(solution)/shard_map/ppermute | solution.py:330
  73.0 2.7 %collective-permute-start.20 = (bf16[16,640]{1,0:T(8,128)(2,1)S(1)}, bf16[16,640]{1,0:T(8,128)(2,1)S(1)}, u32[]{:S(2)}, u32[]{:S(2)}) collective-permute-start(bf16[16,640]{1,0:T(8,128)(2,1)S(1)} %shard_map.81.refs_2_), channel_id=1, source_target_pairs={{0,1},{1,0},{2,3},{3,2},{4,5},{5,4},{6,7},{7,6},{8,9},{9,8},{10,11... | collective-permute-start | bytes 61448 | tf_op jit(solution)/shard_map/ppermute | solution.py:330
  76.7 5.9 %collective-permute-start.23 = (bf16[16,4224]{1,0:T(8,128)(2,1)S(1)}, bf16[16,4224]{1,0:T(8,128)(2,1)S(1)}, u32[]{:S(2)}, u32[]{:S(2)}) collective-permute-start(bf16[16,4224]{1,0:T(8,128)(2,1)S(1)} %shard_map.84), channel_id=1, source_target_pairs={{0,8},{1,9},{2,10},{3,11},{4,12},{5,13},{6,14},{7,15},{8,0},{9,1},... | collective-permute-start | bytes 405512 | tf_op jit(solution)/shard_map/ppermute | solution.py:338
  78.2 8.8 %collective-permute-start.24 = (bf16[16,4224]{1,0:T(8,128)(2,1)S(1)}, bf16[16,4224]{1,0:T(8,128)(2,1)S(1)}, u32[]{:S(2)}, u32[]{:S(2)}) collective-permute-start(bf16[16,4224]{1,0:T(8,128)(2,1)S(1)} %shard_map.86), channel_id=1, source_target_pairs={{0,4},{1,5},{2,6},{3,7},{4,0},{5,1},{6,2},{7,3},{8,12},{9,13},{10,... | collective-permute-start | bytes 405512 | tf_op jit(solution)/shard_map/ppermute | solution.py:338
  80.3 6.8 %collective-permute-start.25 = (bf16[16,4224]{1,0:T(8,128)(2,1)S(1)}, bf16[16,4224]{1,0:T(8,128)(2,1)S(1)}, u32[]{:S(2)}, u32[]{:S(2)}) collective-permute-start(bf16[16,4224]{1,0:T(8,128)(2,1)S(1)} %shard_map.88), channel_id=1, source_target_pairs={{0,12},{1,13},{2,14},{3,15},{4,8},{5,9},{6,10},{7,11},{8,4},{9,5},... | collective-permute-start | bytes 405512 | tf_op jit(solution)/shard_map/ppermute | solution.py:338
  87.2 7.0 %collective-permute-start.26 = (bf16[16,4224]{1,0:T(8,128)(2,1)S(1)}, bf16[16,4224]{1,0:T(8,128)(2,1)S(1)}, u32[]{:S(2)}, u32[]{:S(2)}) collective-permute-start(bf16[16,4224]{1,0:T(8,128)(2,1)S(1)} %shard_map.89.refs_2_), channel_id=1, source_target_pairs={{0,24},{4,28},{8,16},{12,20},{16,8},{20,12},{24,0},{28,4},{1,25},{... | collective-permute-start | bytes 405512 | tf_op jit(solution)/shard_map/ppermute | solution.py:330
  94.3 5.9 %collective-permute-start.29 = (bf16[16,4096]{1,0:T(8,128)(2,1)S(1)}, bf16[16,4096]{1,0:T(8,128)(2,1)S(1)}, u32[]{:S(2)}, u32[]{:S(2)}) collective-permute-start(bf16[16,4096]{1,0:T(8,128)(2,1)S(1)} %get-tuple-element.61.v_ref.refs_15_), channel_id=1, source_target_pairs={{0,12},{1,5},{2,14},{3,7},{4,8},{5,1},{6,10},{7,3},{8,4},{9,13},{1... | collective-permute-start | bytes 393224 | tf_op jit(solution)/shard_map/ppermute | solution.py:338
  95.9 5.0 %collective-permute-start.28 = (bf16[16,4096]{1,0:T(8,128)(2,1)S(1)}, bf16[16,4096]{1,0:T(8,128)(2,1)S(1)}, u32[]{:S(2)}, u32[]{:S(2)}) collective-permute-start(bf16[16,4096]{1,0:T(8,128)(2,1)S(1)} %get-tuple-element.61.v_ref.refs_15_), channel_id=1, source_target_pairs={{0,8},{1,9},{2,10},{3,11},{4,12},{5,13},{6,14},{7,15},{8,0},{9,1},... | collective-permute-start | bytes 393224 | tf_op jit(solution)/shard_map/ppermute | solution.py:338
  96.6 5.0 %collective-permute-start.27 = (bf16[16,4096]{1,0:T(8,128)(2,1)S(1)}, bf16[16,4096]{1,0:T(8,128)(2,1)S(1)}, u32[]{:S(2)}, u32[]{:S(2)}) collective-permute-start(bf16[16,4096]{1,0:T(8,128)(2,1)S(1)} %get-tuple-element.61.v_ref.refs_15_), channel_id=1, source_target_pairs={{0,4},{1,13},{2,6},{3,15},{4,0},{5,9},{6,2},{7,11},{8,12},{9,5},{1... | collective-permute-start | bytes 393224 | tf_op jit(solution)/shard_map/ppermute | solution.py:338
  102.2 3.2 %collective-permute-start.32 = (bf16[16,640]{1,0:T(8,128)(2,1)S(1)}, bf16[16,640]{1,0:T(8,128)(2,1)S(1)}, u32[]{:S(2)}, u32[]{:S(2)}) collective-permute-start(bf16[16,640]{1,0:T(8,128)(2,1)S(1)} %shard_map.94.refs_2_), channel_id=1, source_target_pairs={{0,3},{1,2},{2,1},{3,0},{4,7},{5,6},{6,5},{7,4},{8,11},{9,10},{10,... | collective-permute-start | bytes 61448 | tf_op jit(solution)/shard_map/ppermute | solution.py:330
  102.2 3.9 %collective-permute-start.31 = (bf16[16,640]{1,0:T(8,128)(2,1)S(1)}, bf16[16,640]{1,0:T(8,128)(2,1)S(1)}, u32[]{:S(2)}, u32[]{:S(2)}) collective-permute-start(bf16[16,640]{1,0:T(8,128)(2,1)S(1)} %shard_map.94.refs_2_), channel_id=1, source_target_pairs={{0,2},{1,3},{2,0},{3,1},{4,6},{5,7},{6,4},{7,5},{8,10},{9,11},{10,... | collective-permute-start | bytes 61448 | tf_op jit(solution)/shard_map/ppermute | solution.py:330
  103.4 2.8 %collective-permute-start.30 = (bf16[16,640]{1,0:T(8,128)(2,1)S(1)}, bf16[16,640]{1,0:T(8,128)(2,1)S(1)}, u32[]{:S(2)}, u32[]{:S(2)}) collective-permute-start(bf16[16,640]{1,0:T(8,128)(2,1)S(1)} %shard_map.94.refs_2_), channel_id=1, source_target_pairs={{0,1},{1,0},{2,3},{3,2},{4,5},{5,4},{6,7},{7,6},{8,9},{9,8},{10,11... | collective-permute-start | bytes 61448 | tf_op jit(solution)/shard_map/ppermute | solution.py:330
  107.1 5.9 %collective-permute-start.33 = (bf16[16,4224]{1,0:T(8,128)(2,1)S(1)}, bf16[16,4224]{1,0:T(8,128)(2,1)S(1)}, u32[]{:S(2)}, u32[]{:S(2)}) collective-permute-start(bf16[16,4224]{1,0:T(8,128)(2,1)S(1)} %shard_map.97), channel_id=1, source_target_pairs={{0,8},{1,9},{2,10},{3,11},{4,12},{5,13},{6,14},{7,15},{8,0},{9,1},... | collective-permute-start | bytes 405512 | tf_op jit(solution)/shard_map/ppermute | solution.py:338
  109.2 7.9 %collective-permute-start.34 = (bf16[16,4224]{1,0:T(8,128)(2,1)S(1)}, bf16[16,4224]{1,0:T(8,128)(2,1)S(1)}, u32[]{:S(2)}, u32[]{:S(2)}) collective-permute-start(bf16[16,4224]{1,0:T(8,128)(2,1)S(1)} %shard_map.99), channel_id=1, source_target_pairs={{0,4},{1,5},{2,6},{3,7},{4,0},{5,1},{6,2},{7,3},{8,12},{9,13},{10,... | collective-permute-start | bytes 405512 | tf_op jit(solution)/shard_map/ppermute | solution.py:338
  111.0 6.2 %collective-permute-start.35 = (bf16[16,4224]{1,0:T(8,128)(2,1)S(1)}, bf16[16,4224]{1,0:T(8,128)(2,1)S(1)}, u32[]{:S(2)}, u32[]{:S(2)}) collective-permute-start(bf16[16,4224]{1,0:T(8,128)(2,1)S(1)} %shard_map.101), channel_id=1, source_target_pairs={{0,12},{1,13},{2,14},{3,15},{4,8},{5,9},{6,10},{7,11},{8,4},{9,5},... | collective-permute-start | bytes 405512 | tf_op jit(solution)/shard_map/ppermute | solution.py:338
  117.3 7.0 %collective-permute-start.36 = (bf16[16,4224]{1,0:T(8,128)(2,1)S(1)}, bf16[16,4224]{1,0:T(8,128)(2,1)S(1)}, u32[]{:S(2)}, u32[]{:S(2)}) collective-permute-start(bf16[16,4224]{1,0:T(8,128)(2,1)S(1)} %shard_map.102.refs_2_), channel_id=1, source_target_pairs={{0,24},{4,28},{8,16},{12,20},{16,8},{20,12},{24,0},{28,4},{1,25},{... | collective-permute-start | bytes 405512 | tf_op jit(solution)/shard_map/ppermute | solution.py:330
  125.1 5.9 %collective-permute-start.39 = (bf16[16,4096]{1,0:T(8,128)(2,1)S(1)}, bf16[16,4096]{1,0:T(8,128)(2,1)S(1)}, u32[]{:S(2)}, u32[]{:S(2)}) collective-permute-start(bf16[16,4096]{1,0:T(8,128)(2,1)S(1)} %get-tuple-element.68.v_ref.refs_19_), channel_id=1, source_target_pairs={{0,12},{1,5},{2,14},{3,7},{4,8},{5,1},{6,10},{7,3},{8,4},{9,13},{1... | collective-permute-start | bytes 393224 | tf_op jit(solution)/shard_map/ppermute | solution.py:338
  126.5 5.7 %collective-permute-start.38 = (bf16[16,4096]{1,0:T(8,128)(2,1)S(1)}, bf16[16,4096]{1,0:T(8,128)(2,1)S(1)}, u32[]{:S(2)}, u32[]{:S(2)}) collective-permute-start(bf16[16,4096]{1,0:T(8,128)(2,1)S(1)} %get-tuple-element.68.v_ref.refs_19_), channel_id=1, source_target_pairs={{0,8},{1,9},{2,10},{3,11},{4,12},{5,13},{6,14},{7,15},{8,0},{9,1},... | collective-permute-start | bytes 393224 | tf_op jit(solution)/shard_map/ppermute | solution.py:338
  127.9 5.0 %collective-permute-start.37 = (bf16[16,4096]{1,0:T(8,128)(2,1)S(1)}, bf16[16,4096]{1,0:T(8,128)(2,1)S(1)}, u32[]{:S(2)}, u32[]{:S(2)}) collective-permute-start(bf16[16,4096]{1,0:T(8,128)(2,1)S(1)} %get-tuple-element.68.v_ref.refs_19_), channel_id=1, source_target_pairs={{0,4},{1,13},{2,6},{3,15},{4,0},{5,9},{6,2},{7,11},{8,12},{9,5},{1... | collective-permute-start | bytes 393224 | tf_op jit(solution)/shard_map/ppermute | solution.py:338
  133.5 3.2 %collective-permute-start.42 = (bf16[16,640]{1,0:T(8,128)(2,1)S(1)}, bf16[16,640]{1,0:T(8,128)(2,1)S(1)}, u32[]{:S(2)}, u32[]{:S(2)}) collective-permute-start(bf16[16,640]{1,0:T(8,128)(2,1)S(1)} %shard_map.107.refs_2_), channel_id=1, source_target_pairs={{0,3},{1,2},{2,1},{3,0},{4,7},{5,6},{6,5},{7,4},{8,11},{9,10},{10,... | collective-permute-start | bytes 61448 | tf_op jit(solution)/shard_map/ppermute | solution.py:330
  133.5 3.9 %collective-permute-start.41 = (bf16[16,640]{1,0:T(8,128)(2,1)S(1)}, bf16[16,640]{1,0:T(8,128)(2,1)S(1)}, u32[]{:S(2)}, u32[]{:S(2)}) collective-permute-start(bf16[16,640]{1,0:T(8,128)(2,1)S(1)} %shard_map.107.refs_2_), channel_id=1, source_target_pairs={{0,2},{1,3},{2,0},{3,1},{4,6},{5,7},{6,4},{7,5},{8,10},{9,11},{10,... | collective-permute-start | bytes 61448 | tf_op jit(solution)/shard_map/ppermute | solution.py:330
  134.3 3.1 %collective-permute-start.40 = (bf16[16,640]{1,0:T(8,128)(2,1)S(1)}, bf16[16,640]{1,0:T(8,128)(2,1)S(1)}, u32[]{:S(2)}, u32[]{:S(2)}) collective-permute-start(bf16[16,640]{1,0:T(8,128)(2,1)S(1)} %shard_map.107.refs_2_), channel_id=1, source_target_pairs={{0,1},{1,0},{2,3},{3,2},{4,5},{5,4},{6,7},{7,6},{8,9},{9,8},{10,11... | collective-permute-start | bytes 61448 | tf_op jit(solution)/shard_map/ppermute | solution.py:330
  137.6 5.1 %collective-permute-start.46 = (f32[16,128]{1,0:T(8,128)S(1)}, f32[16,128]{1,0:T(8,128)S(1)}, u32[]{:S(2)}, u32[]{:S(2)}) collective-permute-start(f32[16,128]{1,0:T(8,128)S(1)} %get-tuple-element.80.mine_ref), channel_id=1, source_target_pairs={{0,12},{1,29},{2,14},{3,31},{4,8},{5,25},{6,10},{7,27},{8,4},{9,21... | collective-permute-start | bytes 24584 | tf_op jit(solution)/shard_map/ppermute | solution.py:378
  138.8 3.8 %collective-permute-start.45 = (f32[16,128]{1,0:T(8,128)S(1)}, f32[16,128]{1,0:T(8,128)S(1)}, u32[]{:S(2)}, u32[]{:S(2)}) collective-permute-start(f32[16,128]{1,0:T(8,128)S(1)} %get-tuple-element.80.mine_ref), channel_id=1, source_target_pairs={{0,8},{1,25},{2,10},{3,27},{4,12},{5,29},{6,14},{7,31},{8,0},{9,17... | collective-permute-start | bytes 24584 | tf_op jit(solution)/shard_map/ppermute | solution.py:378
  139.8 3.7 %collective-permute-start.44 = (f32[16,128]{1,0:T(8,128)S(1)}, f32[16,128]{1,0:T(8,128)S(1)}, u32[]{:S(2)}, u32[]{:S(2)}) collective-permute-start(f32[16,128]{1,0:T(8,128)S(1)} %get-tuple-element.80.mine_ref), channel_id=1, source_target_pairs={{0,4},{1,21},{2,6},{3,23},{4,0},{5,17},{6,2},{7,19},{8,12},{9,29},... | collective-permute-start | bytes 24584 | tf_op jit(solution)/shard_map/ppermute | solution.py:378
  141.0 4.5 %collective-permute-start.43 = (f32[16,128]{1,0:T(8,128)S(1)}, f32[16,128]{1,0:T(8,128)S(1)}, u32[]{:S(2)}, u32[]{:S(2)}) collective-permute-start(f32[16,128]{1,0:T(8,128)S(1)} %get-tuple-element.80.mine_ref), channel_id=1, source_target_pairs={{0,16},{1,17},{2,18},{3,19},{4,20},{5,21},{6,22},{7,23},{8,24},{9,... | collective-permute-start | bytes 24584 | tf_op jit(solution)/shard_map/ppermute | solution.py:378
  145.6 1.2 collective-permute-start.47

commit v9 on v8

--- a/solution.py
+++ b/solution.py
@@ -249,8 +249,8 @@
     return sorted(range(len(order)), key=lambda k: order[k][member])
 
 
-def near_kernel(order, sum_ref, norm_ref, *refs):
-    *got_refs, out_ref = refs
+def near_kernel(order, before, sum_ref, norm_ref, *refs):
+    *got_refs, out_ref = refs[before:]
     width = sum_ref.shape[1]
     total = sum_ref[...] + got_refs[-1][:, :width].astype(F32)
     norms = [unpack_norm(ref[:, width:]) for ref in got_refs]
@@ -388,14 +388,19 @@
     image_shape = shape(scen, rows)
     term_shape = shape(2 * scen, rows, dtype=BF16)
 
-    def gradient_parts(w, norm, packed):
+    def gradient_parts(w, norm, packed, before):
         order = slots(near, RS_ORDERS)
         got = [exchange_slot(backward(n_obs, near, d, op, w, packed), n_obs, n_par, d) for d in order]
         total = backward(n_obs, near, (0, 0), op, w)
         for piece in got[:-1]:
             total = call(add_kernel, shape(scen, width), (total, piece), flops=ADD_FLOPS)
         both = shape(scen, width + LANES, dtype=BF16)
-        value = call(functools.partial(near_kernel, order), both, (total, norm, *got))
+        value = call(
+            functools.partial(near_kernel, order, len(before)),
+            both,
+            (total, norm, *before, *got),
+            [VMEM] * 2 + [ANY] * len(before) + [VMEM] * len(got),
+        )
         parts = [value]
         for index, (stride, members) in enumerate(stages(n_obs, near)):
             if index:
@@ -421,7 +426,7 @@
     images, alphas, betas, pieces = [], [], [], []
     gradient = gamma = None
     for index in range(ITERS):
-        parts = gradient_parts(w, norm, packed)
+        parts = gradient_parts(w, norm, packed, () if index else turned[:2])
         gradient, rounded, alpha = call(
             functools.partial(gradient_kernel, index > 0, near),
             (shape(scen, width), shape(scen, width, dtype=BF16), lanes),

time: 148 us -> 148 us (level)
    ppermute x24, waiting for transfers between devices: 24.9 us -> 22.2 us  [exchange_slot(): return lax.ppermute(value, ('obs', 'par'), pairs)]
    ppermute x20, waiting for transfers between devices: 24.7 us -> 26.6 us  [exchange(): return lax.ppermute(value, axis, [(i, i ^ distance) for i in range(size)])]
  transfers between devices with their start and end apart: 48 -> 48, of which waited for: 29 -> 30; matrix products, arithmetic and copies ran while one was open for 0% -> 0% of each run, Pallas kernels for 15% -> 15%
where the time goes in v9:
time: 148 us
  starting transfers between devices  55.2 us (37%)
  waiting for transfers between devices  51.4 us (35%)
  Pallas kernels  40.2 us (27%)
    pallas_call x62, Pallas kernels, call(): pl.pallas_call(body, out_shape=out, in_specs=specs if specs is not None e...  40.2 us
    ppermute x24, starting transfers between devices, exchange_slot(): return lax.ppermute(value, ('obs', 'par'), pairs)  28.2 us
    ppermute x20, waiting for transfers between devices, exchange(): return lax.ppermute(value, axis, [(i, i ^ distance) for i in range(size)])  26.6 us
    ppermute x24, waiting for transfers between devices, exchange_slot(): return lax.ppermute(value, ('obs', 'par'), pairs)  22.2 us
    ppermute x20, starting transfers between devices, exchange(): return lax.ppermute(value, axis, [(i, i ^ distance) for i in range(size)])  21.6 us
    ppermute x4, starting transfers between devices, norm_parts(): got.append(lax.ppermute(norm, ('obs', 'par'), pairs))  5.46 us
  transfers between devices with their start and end apart: 48, of which 30 were waited for; matrix products, arithmetic and copies ran while one was open for 0% of the time, Pallas kernels for 15%

profile of v9, /device:TPU:0, one launch (start us, length us, event | category | flops | bytes accessed | tf_op | source)
XLA Modules:
  0.0 147.7 jit_solution(12782006873912603051)
XLA Ops:
  0.6 2.4 %shard_map.50.early_ref = bf16[512,16384]{1,0:T(8,128)(2,1)S(1)} custom-call(bf16[512,16384]{1,0:T(8,128)(2,1)} %op_hbm.3), custom_call_target="tpu_custom_call" | custom-call | bytes 1024 | tf_op jit(solution)/shard_map/pallas_call | solution.py:28
  3.1 5.2 %shard_map.51 = (bf16[512,16384]{1,0:T(8,128)(2,1)S(1)}, bf16[16,512]{1,0:T(8,128)(2,1)S(1)}) custom-call(bf16[512,16384]{1,0:T(8,128)(2,1)} %op_hbm.3, f32[16,16384]{1,0:T(8,128)S(1)} %copy-done, bf16[512,16384]{1,0:T(8,128)(2,1)S(1)} %shard_map.50.early_ref), custom_call_target="tpu_custom_call", output_to_operand_aliasing={{0}: (2, {})} | custom-call | bytes 1024 | tf_op jit(solution)/shard_map/pallas_call | solution.py:28
  8.3 2.5 %collective-permute-start.2 = (bf16[16,512]{1,0:T(8,128)(2,1)S(1)}, bf16[16,512]{1,0:T(8,128)(2,1)S(1)}, u32[]{:S(2)}, u32[]{:S(2)}) collective-permute-start(bf16[16,512]{1,0:T(8,128)(2,1)S(1)} %get-tuple-element.43.refs_0_), channel_id=1, source_target_pairs={{0,3},{1,2},{2,1},{3,0},{4,7},{5,6},{6,5},{7,4},{8,11},{9,10},{10,... | collective-permute-start | bytes 49160 | tf_op jit(solution)/shard_map/ppermute | solution.py:330
  12.2 2.3 %collective-permute-done.1.refs_2_ = bf16[16,512]{1,0:T(8,128)(2,1)S(1)} collective-permute-done((bf16[16,512]{1,0:T(8,128)(2,1)S(1)}, bf16[16,512]{1,0:T(8,128)(2,1)S(1)}, u32[]{:S(2)}, u32[]{:S(2)}) %collective-permute-start.1) | collective-permute-done | bytes 16416 | tf_op jit(solution)/shard_map/ppermute | solution.py:330
  14.6 0.8 shard_map.58
  15.4 1.6 %collective-permute-start.3 = (bf16[16,4224]{1,0:T(8,128)(2,1)S(1)}, bf16[16,4224]{1,0:T(8,128)(2,1)S(1)}, u32[]{:S(2)}, u32[]{:S(2)}) collective-permute-start(bf16[16,4224]{1,0:T(8,128)(2,1)S(1)} %shard_map.58), channel_id=1, source_target_pairs={{0,8},{1,9},{2,10},{3,11},{4,12},{5,13},{6,14},{7,15},{8,0},{9,1},... | collective-permute-start | bytes 405512 | tf_op jit(solution)/shard_map/ppermute | solution.py:338
  17.7 1.5 %collective-permute-start.4 = (bf16[16,4224]{1,0:T(8,128)(2,1)S(1)}, bf16[16,4224]{1,0:T(8,128)(2,1)S(1)}, u32[]{:S(2)}, u32[]{:S(2)}) collective-permute-start(bf16[16,4224]{1,0:T(8,128)(2,1)S(1)} %shard_map.60), channel_id=1, source_target_pairs={{0,4},{1,5},{2,6},{3,7},{4,0},{5,1},{6,2},{7,3},{8,12},{9,13},{10,... | collective-permute-start | bytes 405512 | tf_op jit(solution)/shard_map/ppermute | solution.py:338
  20.5 1.1 shard_map.54.refs_1_.turned_ref
  21.6 1.1 shard_map.53.refs_0_.turned_ref
  23.6 1.1 collective-permute-done.4.got_ref.refs_3_
  24.7 1.2 collective-permute-done.5.refs_4_
  26.1 2.5 %collective-permute-start.6 = (bf16[16,4224]{1,0:T(8,128)(2,1)S(1)}, bf16[16,4224]{1,0:T(8,128)(2,1)S(1)}, u32[]{:S(2)}, u32[]{:S(2)}) collective-permute-start(bf16[16,4224]{1,0:T(8,128)(2,1)S(1)} %shard_map.63.refs_4_), channel_id=1, source_target_pairs={{0,24},{4,28},{8,16},{12,20},{16,8},{20,12},{24,0},{28,4},{1,25},{... | collective-permute-start | bytes 405512 | tf_op jit(solution)/shard_map/ppermute | solution.py:330
  28.6 1.1 shard_map.55.refs_2_.turned_ref
  29.7 1.1 shard_map.52.refs_3_.turned_ref
  30.9 2.2 %collective-permute-done.6.refs_5_ = bf16[16,4224]{1,0:T(8,128)(2,1)S(1)} collective-permute-done((bf16[16,4224]{1,0:T(8,128)(2,1)S(1)}, bf16[16,4224]{1,0:T(8,128)(2,1)S(1)}, u32[]{:S(2)}, u32[]{:S(2)}) %collective-permute-start.6) | collective-permute-done | bytes 135200 | tf_op jit(solution)/shard_map/ppermute | solution.py:330
  33.7 1.3 collective-permute-start.9
  35.0 1.4 collective-permute-start.8
  37.8 1.7 %collective-permute-done.9.v_ref.refs_8_ = bf16[16,4096]{1,0:T(8,128)(2,1)S(1)} collective-permute-done((bf16[16,4096]{1,0:T(8,128)(2,1)S(1)}, bf16[16,4096]{1,0:T(8,128)(2,1)S(1)}, u32[]{:S(2)}, u32[]{:S(2)}) %collective-permute-start.9) | collective-permute-done | bytes 131104 | tf_op jit(solution)/shard_map/ppermute | solution.py:338
  42.7 1.2 collective-permute-start.10
  43.9 1.3 collective-permute-done.12.refs_3_
  46.0 0.8 shard_map.71
  47.5 0.9 shard_map.73
  48.4 1.0 collective-permute-start.14
  50.2 1.9 %collective-permute-start.15 = (bf16[16,4224]{1,0:T(8,128)(2,1)S(1)}, bf16[16,4224]{1,0:T(8,128)(2,1)S(1)}, u32[]{:S(2)}, u32[]{:S(2)}) collective-permute-start(bf16[16,4224]{1,0:T(8,128)(2,1)S(1)} %shard_map.75), channel_id=1, source_target_pairs={{0,12},{1,13},{2,14},{3,15},{4,8},{5,9},{6,10},{7,11},{8,4},{9,5},... | collective-permute-start | bytes 405512 | tf_op jit(solution)/shard_map/ppermute | solution.py:338
  52.9 3.5 %collective-permute-done.14.got_ref.refs_1_ = bf16[16,4224]{1,0:T(8,128)(2,1)S(1)} collective-permute-done((bf16[16,4224]{1,0:T(8,128)(2,1)S(1)}, bf16[16,4224]{1,0:T(8,128)(2,1)S(1)}, u32[]{:S(2)}, u32[]{:S(2)}) %collective-permute-start.14) | collective-permute-done | bytes 135200 | tf_op jit(solution)/shard_map/ppermute | solution.py:338
  56.5 3.0 %collective-permute-start.16 = (bf16[16,4224]{1,0:T(8,128)(2,1)S(1)}, bf16[16,4224]{1,0:T(8,128)(2,1)S(1)}, u32[]{:S(2)}, u32[]{:S(2)}) collective-permute-start(bf16[16,4224]{1,0:T(8,128)(2,1)S(1)} %shard_map.76.refs_2_), channel_id=1, source_target_pairs={{0,24},{4,28},{8,16},{12,20},{16,8},{20,12},{24,0},{28,4},{1,25},{... | collective-permute-start | bytes 405512 | tf_op jit(solution)/shard_map/ppermute | solution.py:330
  59.5 4.0 %collective-permute-done.16.refs_3_ = bf16[16,4224]{1,0:T(8,128)(2,1)S(1)} collective-permute-done((bf16[16,4224]{1,0:T(8,128)(2,1)S(1)}, bf16[16,4224]{1,0:T(8,128)(2,1)S(1)}, u32[]{:S(2)}, u32[]{:S(2)}) %collective-permute-start.16) | collective-permute-done | bytes 135200 | tf_op jit(solution)/shard_map/ppermute | solution.py:330
  63.7 2.6 %collective-permute-start.18 = (bf16[16,4096]{1,0:T(8,128)(2,1)S(1)}, bf16[16,4096]{1,0:T(8,128)(2,1)S(1)}, u32[]{:S(2)}, u32[]{:S(2)}) collective-permute-start(bf16[16,4096]{1,0:T(8,128)(2,1)S(1)} %get-tuple-element.54.v_ref.refs_11_), channel_id=1, source_target_pairs={{0,8},{1,9},{2,10},{3,11},{4,12},{5,13},{6,14},{7,15},{8,0},{9,1},... | collective-permute-start | bytes 393224 | tf_op jit(solution)/shard_map/ppermute | solution.py:338
  66.2 0.9 collective-permute-start.17
  67.8 1.7 %collective-permute-done.19.v_ref.refs_12_ = bf16[16,4096]{1,0:T(8,128)(2,1)S(1)} collective-permute-done((bf16[16,4096]{1,0:T(8,128)(2,1)S(1)}, bf16[16,4096]{1,0:T(8,128)(2,1)S(1)}, u32[]{:S(2)}, u32[]{:S(2)}) %collective-permute-start.19) | collective-permute-done | bytes 131104 | tf_op jit(solution)/shard_map/ppermute | solution.py:338
  71.9 1.0 collective-permute-start.21
  72.9 0.9 collective-permute-start.20
  73.8 1.3 collective-permute-done.22.refs_5_
  75.1 0.8 collective-permute-done.21.refs_4_
  78.1 1.2 collective-permute-start.24
  80.1 1.9 %collective-permute-start.25 = (bf16[16,4224]{1,0:T(8,128)(2,1)S(1)}, bf16[16,4224]{1,0:T(8,128)(2,1)S(1)}, u32[]{:S(2)}, u32[]{:S(2)}) collective-permute-start(bf16[16,4224]{1,0:T(8,128)(2,1)S(1)} %shard_map.88), channel_id=1, source_target_pairs={{0,12},{1,13},{2,14},{3,15},{4,8},{5,9},{6,10},{7,11},{8,4},{9,5},... | collective-permute-start | bytes 405512 | tf_op jit(solution)/shard_map/ppermute | solution.py:338
  82.8 4.0 %collective-permute-done.24.got_ref.refs_1_ = bf16[16,4224]{1,0:T(8,128)(2,1)S(1)} collective-permute-done((bf16[16,4224]{1,0:T(8,128)(2,1)S(1)}, bf16[16,4224]{1,0:T(8,128)(2,1)S(1)}, u32[]{:S(2)}, u32[]{:S(2)}) %collective-permute-start.24) | collective-permute-done | bytes 135200 | tf_op jit(solution)/shard_map/ppermute | solution.py:338
  87.0 2.5 %collective-permute-start.26 = (bf16[16,4224]{1,0:T(8,128)(2,1)S(1)}, bf16[16,4224]{1,0:T(8,128)(2,1)S(1)}, u32[]{:S(2)}, u32[]{:S(2)}) collective-permute-start(bf16[16,4224]{1,0:T(8,128)(2,1)S(1)} %shard_map.89.refs_2_), channel_id=1, source_target_pairs={{0,24},{4,28},{8,16},{12,20},{16,8},{20,12},{24,0},{28,4},{1,25},{... | collective-permute-start | bytes 405512 | tf_op jit(solution)/shard_map/ppermute | solution.py:330
  89.5 4.4 %collective-permute-done.26.refs_3_ = bf16[16,4224]{1,0:T(8,128)(2,1)S(1)} collective-permute-done((bf16[16,4224]{1,0:T(8,128)(2,1)S(1)}, bf16[16,4224]{1,0:T(8,128)(2,1)S(1)}, u32[]{:S(2)}, u32[]{:S(2)}) %collective-permute-start.26) | collective-permute-done | bytes 135200 | tf_op jit(solution)/shard_map/ppermute | solution.py:330
  94.1 1.6 %collective-permute-start.29 = (bf16[16,4096]{1,0:T(8,128)(2,1)S(1)}, bf16[16,4096]{1,0:T(8,128)(2,1)S(1)}, u32[]{:S(2)}, u32[]{:S(2)}) collective-permute-start(bf16[16,4096]{1,0:T(8,128)(2,1)S(1)} %get-tuple-element.61.v_ref.refs_15_), channel_id=1, source_target_pairs={{0,12},{1,5},{2,14},{3,7},{4,8},{5,1},{6,10},{7,3},{8,4},{9,13},{1... | collective-permute-start | bytes 393224 | tf_op jit(solution)/shard_map/ppermute | solution.py:338
  96.4 1.2 collective-permute-start.27
  98.3 1.7 %collective-permute-done.29.v_ref.refs_16_ = bf16[16,4096]{1,0:T(8,128)(2,1)S(1)} collective-permute-done((bf16[16,4096]{1,0:T(8,128)(2,1)S(1)}, bf16[16,4096]{1,0:T(8,128)(2,1)S(1)}, u32[]{:S(2)}, u32[]{:S(2)}) %collective-permute-start.29) | collective-permute-done | bytes 131104 | tf_op jit(solution)/shard_map/ppermute | solution.py:338
  102.1 1.1 collective-permute-start.31
  104.0 1.3 collective-permute-done.32.refs_5_
  107.0 1.3 collective-permute-start.33
  109.0 0.9 collective-permute-start.34
  110.7 1.4 collective-permute-start.35
  112.9 4.1 %collective-permute-done.34.got_ref.refs_1_ = bf16[16,4224]{1,0:T(8,128)(2,1)S(1)} collective-permute-done((bf16[16,4224]{1,0:T(8,128)(2,1)S(1)}, bf16[16,4224]{1,0:T(8,128)(2,1)S(1)}, u32[]{:S(2)}, u32[]{:S(2)}) %collective-permute-start.34) | collective-permute-done | bytes 135200 | tf_op jit(solution)/shard_map/ppermute | solution.py:338
  117.1 2.8 %collective-permute-start.36 = (bf16[16,4224]{1,0:T(8,128)(2,1)S(1)}, bf16[16,4224]{1,0:T(8,128)(2,1)S(1)}, u32[]{:S(2)}, u32[]{:S(2)}) collective-permute-start(bf16[16,4224]{1,0:T(8,128)(2,1)S(1)} %shard_map.102.refs_2_), channel_id=1, source_target_pairs={{0,24},{4,28},{8,16},{12,20},{16,8},{20,12},{24,0},{28,4},{1,25},{... | collective-permute-start | bytes 405512 | tf_op jit(solution)/shard_map/ppermute | solution.py:330
  120.0 4.1 %collective-permute-done.36.refs_3_ = bf16[16,4224]{1,0:T(8,128)(2,1)S(1)} collective-permute-done((bf16[16,4224]{1,0:T(8,128)(2,1)S(1)}, bf16[16,4224]{1,0:T(8,128)(2,1)S(1)}, u32[]{:S(2)}, u32[]{:S(2)}) %collective-permute-start.36) | collective-permute-done | bytes 135200 | tf_op jit(solution)/shard_map/ppermute | solution.py:330
  124.1 0.8 shard_map.103
  124.9 1.4 collective-permute-start.39
  126.3 1.1 collective-permute-start.38
  127.4 1.0 collective-permute-start.37
  129.0 1.7 %collective-permute-done.39.v_ref.refs_20_ = bf16[16,4096]{1,0:T(8,128)(2,1)S(1)} collective-permute-done((bf16[16,4096]{1,0:T(8,128)(2,1)S(1)}, bf16[16,4096]{1,0:T(8,128)(2,1)S(1)}, u32[]{:S(2)}, u32[]{:S(2)}) %collective-permute-start.39) | collective-permute-done | bytes 131104 | tf_op jit(solution)/shard_map/ppermute | solution.py:338
  133.0 1.1 collective-permute-start.41
  134.1 0.8 collective-permute-start.40
  134.9 1.3 collective-permute-done.42.refs_5_
  137.2 1.2 collective-permute-start.46
  138.4 1.2 collective-permute-start.45
  139.5 1.1 collective-permute-start.44
  140.7 2.0 %collective-permute-start.43 = (f32[16,128]{1,0:T(8,128)S(1)}, f32[16,128]{1,0:T(8,128)S(1)}, u32[]{:S(2)}, u32[]{:S(2)}) collective-permute-start(f32[16,128]{1,0:T(8,128)S(1)} %get-tuple-element.80.mine_ref), channel_id=1, source_target_pairs={{0,16},{1,17},{2,18},{3,19},{4,20},{5,21},{6,22},{7,23},{8,24},{9,... | collective-permute-start | bytes 24584 | tf_op jit(solution)/shard_map/ppermute | solution.py:378
  143.2 2.0 %collective-permute-done.43.refs_0_ = f32[16,128]{1,0:T(8,128)S(1)} collective-permute-done((f32[16,128]{1,0:T(8,128)S(1)}, f32[16,128]{1,0:T(8,128)S(1)}, u32[]{:S(2)}, u32[]{:S(2)}) %collective-permute-start.43) | collective-permute-done | bytes 8224 | tf_op jit(solution)/shard_map/ppermute | solution.py:378
  146.4 1.4 shard_map.111
  (98 shorter events, 34.1 us)
Async XLA Ops:
  0.6 2.5 %copy-start = (f32[16,16384]{1,0:T(8,128)S(1)}, f32[16,16384]{1,0:T(8,128)}, u32[]{:S(2)}) copy-start(f32[16,16384]{1,0:T(8,128)} %start_ref.3) | copy-start | bytes 3145732
  3.1 11.4 %copy-start.1 = (f32[16,512]{1,0:T(8,128)S(1)}, f32[16,512]{1,0:T(8,128)}, u32[]{:S(2)}) copy-start(f32[16,512]{1,0:T(8,128)} %targets_ref.1) | copy-start | bytes 98308
  8.3 3.9 %collective-permute-start.2 = (bf16[16,512]{1,0:T(8,128)(2,1)S(1)}, bf16[16,512]{1,0:T(8,128)(2,1)S(1)}, u32[]{:S(2)}, u32[]{:S(2)}) collective-permute-start(bf16[16,512]{1,0:T(8,128)(2,1)S(1)} %get-tuple-element.43.refs_0_), channel_id=1, source_target_pairs={{0,3},{1,2},{2,1},{3,0},{4,7},{5,6},{6,5},{7,4},{8,11},{9,10},{10,... | collective-permute-start | bytes 49160 | tf_op jit(solution)/shard_map/ppermute | solution.py:330
  10.8 3.7 %collective-permute-start.1 = (bf16[16,512]{1,0:T(8,128)(2,1)S(1)}, bf16[16,512]{1,0:T(8,128)(2,1)S(1)}, u32[]{:S(2)}, u32[]{:S(2)}) collective-permute-start(bf16[16,512]{1,0:T(8,128)(2,1)S(1)} %get-tuple-element.43.refs_0_), channel_id=1, source_target_pairs={{0,2},{1,3},{2,0},{3,1},{4,6},{5,7},{6,4},{7,5},{8,10},{9,11},{10,... | collective-permute-start | bytes 49160 | tf_op jit(solution)/shard_map/ppermute | solution.py:330
  11.4 3.1 %collective-permute-start = (bf16[16,512]{1,0:T(8,128)(2,1)S(1)}, bf16[16,512]{1,0:T(8,128)(2,1)S(1)}, u32[]{:S(2)}, u32[]{:S(2)}) collective-permute-start(bf16[16,512]{1,0:T(8,128)(2,1)S(1)} %get-tuple-element.43.refs_0_), channel_id=1, source_target_pairs={{0,1},{1,0},{2,3},{3,2},{4,5},{5,4},{6,7},{7,6},{8,9},{9,8},{10,11... | collective-permute-start | bytes 49160 | tf_op jit(solution)/shard_map/ppermute | solution.py:330
  15.4 8.2 %collective-permute-start.3 = (bf16[16,4224]{1,0:T(8,128)(2,1)S(1)}, bf16[16,4224]{1,0:T(8,128)(2,1)S(1)}, u32[]{:S(2)}, u32[]{:S(2)}) collective-permute-start(bf16[16,4224]{1,0:T(8,128)(2,1)S(1)} %shard_map.58), channel_id=1, source_target_pairs={{0,8},{1,9},{2,10},{3,11},{4,12},{5,13},{6,14},{7,15},{8,0},{9,1},... | collective-permute-start | bytes 405512 | tf_op jit(solution)/shard_map/ppermute | solution.py:338
  17.7 7.0 %collective-permute-start.4 = (bf16[16,4224]{1,0:T(8,128)(2,1)S(1)}, bf16[16,4224]{1,0:T(8,128)(2,1)S(1)}, u32[]{:S(2)}, u32[]{:S(2)}) collective-permute-start(bf16[16,4224]{1,0:T(8,128)(2,1)S(1)} %shard_map.60), channel_id=1, source_target_pairs={{0,4},{1,5},{2,6},{3,7},{4,0},{5,1},{6,2},{7,3},{8,12},{9,13},{10,... | collective-permute-start | bytes 405512 | tf_op jit(solution)/shard_map/ppermute | solution.py:338
  20.0 5.9 %collective-permute-start.5 = (bf16[16,4224]{1,0:T(8,128)(2,1)S(1)}, bf16[16,4224]{1,0:T(8,128)(2,1)S(1)}, u32[]{:S(2)}, u32[]{:S(2)}) collective-permute-start(bf16[16,4224]{1,0:T(8,128)(2,1)S(1)} %shard_map.62), channel_id=1, source_target_pairs={{0,12},{1,13},{2,14},{3,15},{4,8},{5,9},{6,10},{7,11},{8,4},{9,5},... | collective-permute-start | bytes 405512 | tf_op jit(solution)/shard_map/ppermute | solution.py:338
  26.1 7.0 %collective-permute-start.6 = (bf16[16,4224]{1,0:T(8,128)(2,1)S(1)}, bf16[16,4224]{1,0:T(8,128)(2,1)S(1)}, u32[]{:S(2)}, u32[]{:S(2)}) collective-permute-start(bf16[16,4224]{1,0:T(8,128)(2,1)S(1)} %shard_map.63.refs_4_), channel_id=1, source_target_pairs={{0,24},{4,28},{8,16},{12,20},{16,8},{20,12},{24,0},{28,4},{1,25},{... | collective-permute-start | bytes 405512 | tf_op jit(solution)/shard_map/ppermute | solution.py:330
  33.7 5.9 %collective-permute-start.9 = (bf16[16,4096]{1,0:T(8,128)(2,1)S(1)}, bf16[16,4096]{1,0:T(8,128)(2,1)S(1)}, u32[]{:S(2)}, u32[]{:S(2)}) collective-permute-start(bf16[16,4096]{1,0:T(8,128)(2,1)S(1)} %get-tuple-element.47.v_ref.refs_7_), channel_id=1, source_target_pairs={{0,12},{1,5},{2,14},{3,7},{4,8},{5,1},{6,10},{7,3},{8,4},{9,13},{1... | collective-permute-start | bytes 393224 | tf_op jit(solution)/shard_map/ppermute | solution.py:338
  35.0 5.7 %collective-permute-start.8 = (bf16[16,4096]{1,0:T(8,128)(2,1)S(1)}, bf16[16,4096]{1,0:T(8,128)(2,1)S(1)}, u32[]{:S(2)}, u32[]{:S(2)}) collective-permute-start(bf16[16,4096]{1,0:T(8,128)(2,1)S(1)} %get-tuple-element.47.v_ref.refs_7_), channel_id=1, source_target_pairs={{0,8},{1,9},{2,10},{3,11},{4,12},{5,13},{6,14},{7,15},{8,0},{9,1},... | collective-permute-start | bytes 393224 | tf_op jit(solution)/shard_map/ppermute | solution.py:338
  36.4 5.0 %collective-permute-start.7 = (bf16[16,4096]{1,0:T(8,128)(2,1)S(1)}, bf16[16,4096]{1,0:T(8,128)(2,1)S(1)}, u32[]{:S(2)}, u32[]{:S(2)}) collective-permute-start(bf16[16,4096]{1,0:T(8,128)(2,1)S(1)} %get-tuple-element.47.v_ref.refs_7_), channel_id=1, source_target_pairs={{0,4},{1,13},{2,6},{3,15},{4,0},{5,9},{6,2},{7,11},{8,12},{9,5},{1... | collective-permute-start | bytes 393224 | tf_op jit(solution)/shard_map/ppermute | solution.py:338
  42.0 3.2 %collective-permute-start.12 = (bf16[16,640]{1,0:T(8,128)(2,1)S(1)}, bf16[16,640]{1,0:T(8,128)(2,1)S(1)}, u32[]{:S(2)}, u32[]{:S(2)}) collective-permute-start(bf16[16,640]{1,0:T(8,128)(2,1)S(1)} %shard_map.68.refs_0_), channel_id=1, source_target_pairs={{0,3},{1,2},{2,1},{3,0},{4,7},{5,6},{6,5},{7,4},{8,11},{9,10},{10,... | collective-permute-start | bytes 61448 | tf_op jit(solution)/shard_map/ppermute | solution.py:330
  42.0 3.8 %collective-permute-start.11 = (bf16[16,640]{1,0:T(8,128)(2,1)S(1)}, bf16[16,640]{1,0:T(8,128)(2,1)S(1)}, u32[]{:S(2)}, u32[]{:S(2)}) collective-permute-start(bf16[16,640]{1,0:T(8,128)(2,1)S(1)} %shard_map.68.refs_0_), channel_id=1, source_target_pairs={{0,2},{1,3},{2,0},{3,1},{4,6},{5,7},{6,4},{7,5},{8,10},{9,11},{10,... | collective-permute-start | bytes 61448 | tf_op jit(solution)/shard_map/ppermute | solution.py:330
  42.7 3.1 %collective-permute-start.10 = (bf16[16,640]{1,0:T(8,128)(2,1)S(1)}, bf16[16,640]{1,0:T(8,128)(2,1)S(1)}, u32[]{:S(2)}, u32[]{:S(2)}) collective-permute-start(bf16[16,640]{1,0:T(8,128)(2,1)S(1)} %shard_map.68.refs_0_), channel_id=1, source_target_pairs={{0,1},{1,0},{2,3},{3,2},{4,5},{5,4},{6,7},{7,6},{8,9},{9,8},{10,11... | collective-permute-start | bytes 61448 | tf_op jit(solution)/shard_map/ppermute | solution.py:330
  46.8 6.1 %collective-permute-start.13 = (bf16[16,4224]{1,0:T(8,128)(2,1)S(1)}, bf16[16,4224]{1,0:T(8,128)(2,1)S(1)}, u32[]{:S(2)}, u32[]{:S(2)}) collective-permute-start(bf16[16,4224]{1,0:T(8,128)(2,1)S(1)} %shard_map.71), channel_id=1, source_target_pairs={{0,8},{1,9},{2,10},{3,11},{4,12},{5,13},{6,14},{7,15},{8,0},{9,1},... | collective-permute-start | bytes 405512 | tf_op jit(solution)/shard_map/ppermute | solution.py:338
  48.4 7.9 %collective-permute-start.14 = (bf16[16,4224]{1,0:T(8,128)(2,1)S(1)}, bf16[16,4224]{1,0:T(8,128)(2,1)S(1)}, u32[]{:S(2)}, u32[]{:S(2)}) collective-permute-start(bf16[16,4224]{1,0:T(8,128)(2,1)S(1)} %shard_map.73), channel_id=1, source_target_pairs={{0,4},{1,5},{2,6},{3,7},{4,0},{5,1},{6,2},{7,3},{8,12},{9,13},{10,... | collective-permute-start | bytes 405512 | tf_op jit(solution)/shard_map/ppermute | solution.py:338
  50.2 6.2 %collective-permute-start.15 = (bf16[16,4224]{1,0:T(8,128)(2,1)S(1)}, bf16[16,4224]{1,0:T(8,128)(2,1)S(1)}, u32[]{:S(2)}, u32[]{:S(2)}) collective-permute-start(bf16[16,4224]{1,0:T(8,128)(2,1)S(1)} %shard_map.75), channel_id=1, source_target_pairs={{0,12},{1,13},{2,14},{3,15},{4,8},{5,9},{6,10},{7,11},{8,4},{9,5},... | collective-permute-start | bytes 405512 | tf_op jit(solution)/shard_map/ppermute | solution.py:338
  56.5 7.0 %collective-permute-start.16 = (bf16[16,4224]{1,0:T(8,128)(2,1)S(1)}, bf16[16,4224]{1,0:T(8,128)(2,1)S(1)}, u32[]{:S(2)}, u32[]{:S(2)}) collective-permute-start(bf16[16,4224]{1,0:T(8,128)(2,1)S(1)} %shard_map.76.refs_2_), channel_id=1, source_target_pairs={{0,24},{4,28},{8,16},{12,20},{16,8},{20,12},{24,0},{28,4},{1,25},{... | collective-permute-start | bytes 405512 | tf_op jit(solution)/shard_map/ppermute | solution.py:330
  63.6 5.9 %collective-permute-start.19 = (bf16[16,4096]{1,0:T(8,128)(2,1)S(1)}, bf16[16,4096]{1,0:T(8,128)(2,1)S(1)}, u32[]{:S(2)}, u32[]{:S(2)}) collective-permute-start(bf16[16,4096]{1,0:T(8,128)(2,1)S(1)} %get-tuple-element.54.v_ref.refs_11_), channel_id=1, source_target_pairs={{0,12},{1,5},{2,14},{3,7},{4,8},{5,1},{6,10},{7,3},{8,4},{9,13},{1... | collective-permute-start | bytes 393224 | tf_op jit(solution)/shard_map/ppermute | solution.py:338
  63.7 6.9 %collective-permute-start.18 = (bf16[16,4096]{1,0:T(8,128)(2,1)S(1)}, bf16[16,4096]{1,0:T(8,128)(2,1)S(1)}, u32[]{:S(2)}, u32[]{:S(2)}) collective-permute-start(bf16[16,4096]{1,0:T(8,128)(2,1)S(1)} %get-tuple-element.54.v_ref.refs_11_), channel_id=1, source_target_pairs={{0,8},{1,9},{2,10},{3,11},{4,12},{5,13},{6,14},{7,15},{8,0},{9,1},... | collective-permute-start | bytes 393224 | tf_op jit(solution)/shard_map/ppermute | solution.py:338
  66.2 5.0 %collective-permute-start.17 = (bf16[16,4096]{1,0:T(8,128)(2,1)S(1)}, bf16[16,4096]{1,0:T(8,128)(2,1)S(1)}, u32[]{:S(2)}, u32[]{:S(2)}) collective-permute-start(bf16[16,4096]{1,0:T(8,128)(2,1)S(1)} %get-tuple-element.54.v_ref.refs_11_), channel_id=1, source_target_pairs={{0,4},{1,13},{2,6},{3,15},{4,0},{5,9},{6,2},{7,11},{8,12},{9,5},{1... | collective-permute-start | bytes 393224 | tf_op jit(solution)/shard_map/ppermute | solution.py:338
  71.9 3.2 %collective-permute-start.22 = (bf16[16,640]{1,0:T(8,128)(2,1)S(1)}, bf16[16,640]{1,0:T(8,128)(2,1)S(1)}, u32[]{:S(2)}, u32[]{:S(2)}) collective-permute-start(bf16[16,640]{1,0:T(8,128)(2,1)S(1)} %shard_map.81.refs_2_), channel_id=1, source_target_pairs={{0,3},{1,2},{2,1},{3,0},{4,7},{5,6},{6,5},{7,4},{8,11},{9,10},{10,... | collective-permute-start | bytes 61448 | tf_op jit(solution)/shard_map/ppermute | solution.py:330
  71.9 4.0 %collective-permute-start.21 = (bf16[16,640]{1,0:T(8,128)(2,1)S(1)}, bf16[16,640]{1,0:T(8,128)(2,1)S(1)}, u32[]{:S(2)}, u32[]{:S(2)}) collective-permute-start(bf16[16,640]{1,0:T(8,128)(2,1)S(1)} %shard_map.81.refs_2_), channel_id=1, source_target_pairs={{0,2},{1,3},{2,0},{3,1},{4,6},{5,7},{6,4},{7,5},{8,10},{9,11},{10,... | collective-permute-start | bytes 61448 | tf_op jit(solution)/shard_map/ppermute | solution.py:330
  72.9 3.0 %collective-permute-start.20 = (bf16[16,640]{1,0:T(8,128)(2,1)S(1)}, bf16[16,640]{1,0:T(8,128)(2,1)S(1)}, u32[]{:S(2)}, u32[]{:S(2)}) collective-permute-start(bf16[16,640]{1,0:T(8,128)(2,1)S(1)} %shard_map.81.refs_2_), channel_id=1, source_target_pairs={{0,1},{1,0},{2,3},{3,2},{4,5},{5,4},{6,7},{7,6},{8,9},{9,8},{10,11... | collective-permute-start | bytes 61448 | tf_op jit(solution)/shard_map/ppermute | solution.py:330
  76.9 5.9 %collective-permute-start.23 = (bf16[16,4224]{1,0:T(8,128)(2,1)S(1)}, bf16[16,4224]{1,0:T(8,128)(2,1)S(1)}, u32[]{:S(2)}, u32[]{:S(2)}) collective-permute-start(bf16[16,4224]{1,0:T(8,128)(2,1)S(1)} %shard_map.84), channel_id=1, source_target_pairs={{0,8},{1,9},{2,10},{3,11},{4,12},{5,13},{6,14},{7,15},{8,0},{9,1},... | collective-permute-start | bytes 405512 | tf_op jit(solution)/shard_map/ppermute | solution.py:338
  78.1 8.7 %collective-permute-start.24 = (bf16[16,4224]{1,0:T(8,128)(2,1)S(1)}, bf16[16,4224]{1,0:T(8,128)(2,1)S(1)}, u32[]{:S(2)}, u32[]{:S(2)}) collective-permute-start(bf16[16,4224]{1,0:T(8,128)(2,1)S(1)} %shard_map.86), channel_id=1, source_target_pairs={{0,4},{1,5},{2,6},{3,7},{4,0},{5,1},{6,2},{7,3},{8,12},{9,13},{10,... | collective-permute-start | bytes 405512 | tf_op jit(solution)/shard_map/ppermute | solution.py:338
  80.1 6.8 %collective-permute-start.25 = (bf16[16,4224]{1,0:T(8,128)(2,1)S(1)}, bf16[16,4224]{1,0:T(8,128)(2,1)S(1)}, u32[]{:S(2)}, u32[]{:S(2)}) collective-permute-start(bf16[16,4224]{1,0:T(8,128)(2,1)S(1)} %shard_map.88), channel_id=1, source_target_pairs={{0,12},{1,13},{2,14},{3,15},{4,8},{5,9},{6,10},{7,11},{8,4},{9,5},... | collective-permute-start | bytes 405512 | tf_op jit(solution)/shard_map/ppermute | solution.py:338
  87.0 7.0 %collective-permute-start.26 = (bf16[16,4224]{1,0:T(8,128)(2,1)S(1)}, bf16[16,4224]{1,0:T(8,128)(2,1)S(1)}, u32[]{:S(2)}, u32[]{:S(2)}) collective-permute-start(bf16[16,4224]{1,0:T(8,128)(2,1)S(1)} %shard_map.89.refs_2_), channel_id=1, source_target_pairs={{0,24},{4,28},{8,16},{12,20},{16,8},{20,12},{24,0},{28,4},{1,25},{... | collective-permute-start | bytes 405512 | tf_op jit(solution)/shard_map/ppermute | solution.py:330
  94.1 5.9 %collective-permute-start.29 = (bf16[16,4096]{1,0:T(8,128)(2,1)S(1)}, bf16[16,4096]{1,0:T(8,128)(2,1)S(1)}, u32[]{:S(2)}, u32[]{:S(2)}) collective-permute-start(bf16[16,4096]{1,0:T(8,128)(2,1)S(1)} %get-tuple-element.61.v_ref.refs_15_), channel_id=1, source_target_pairs={{0,12},{1,5},{2,14},{3,7},{4,8},{5,1},{6,10},{7,3},{8,4},{9,13},{1... | collective-permute-start | bytes 393224 | tf_op jit(solution)/shard_map/ppermute | solution.py:338
  95.7 5.0 %collective-permute-start.28 = (bf16[16,4096]{1,0:T(8,128)(2,1)S(1)}, bf16[16,4096]{1,0:T(8,128)(2,1)S(1)}, u32[]{:S(2)}, u32[]{:S(2)}) collective-permute-start(bf16[16,4096]{1,0:T(8,128)(2,1)S(1)} %get-tuple-element.61.v_ref.refs_15_), channel_id=1, source_target_pairs={{0,8},{1,9},{2,10},{3,11},{4,12},{5,13},{6,14},{7,15},{8,0},{9,1},... | collective-permute-start | bytes 393224 | tf_op jit(solution)/shard_map/ppermute | solution.py:338
  96.4 5.0 %collective-permute-start.27 = (bf16[16,4096]{1,0:T(8,128)(2,1)S(1)}, bf16[16,4096]{1,0:T(8,128)(2,1)S(1)}, u32[]{:S(2)}, u32[]{:S(2)}) collective-permute-start(bf16[16,4096]{1,0:T(8,128)(2,1)S(1)} %get-tuple-element.61.v_ref.refs_15_), channel_id=1, source_target_pairs={{0,4},{1,13},{2,6},{3,15},{4,0},{5,9},{6,2},{7,11},{8,12},{9,5},{1... | collective-permute-start | bytes 393224 | tf_op jit(solution)/shard_map/ppermute | solution.py:338
  102.1 3.2 %collective-permute-start.32 = (bf16[16,640]{1,0:T(8,128)(2,1)S(1)}, bf16[16,640]{1,0:T(8,128)(2,1)S(1)}, u32[]{:S(2)}, u32[]{:S(2)}) collective-permute-start(bf16[16,640]{1,0:T(8,128)(2,1)S(1)} %shard_map.94.refs_2_), channel_id=1, source_target_pairs={{0,3},{1,2},{2,1},{3,0},{4,7},{5,6},{6,5},{7,4},{8,11},{9,10},{10,... | collective-permute-start | bytes 61448 | tf_op jit(solution)/shard_map/ppermute | solution.py:330
  102.1 3.9 %collective-permute-start.31 = (bf16[16,640]{1,0:T(8,128)(2,1)S(1)}, bf16[16,640]{1,0:T(8,128)(2,1)S(1)}, u32[]{:S(2)}, u32[]{:S(2)}) collective-permute-start(bf16[16,640]{1,0:T(8,128)(2,1)S(1)} %shard_map.94.refs_2_), channel_id=1, source_target_pairs={{0,2},{1,3},{2,0},{3,1},{4,6},{5,7},{6,4},{7,5},{8,10},{9,11},{10,... | collective-permute-start | bytes 61448 | tf_op jit(solution)/shard_map/ppermute | solution.py:330
  103.2 2.8 %collective-permute-start.30 = (bf16[16,640]{1,0:T(8,128)(2,1)S(1)}, bf16[16,640]{1,0:T(8,128)(2,1)S(1)}, u32[]{:S(2)}, u32[]{:S(2)}) collective-permute-start(bf16[16,640]{1,0:T(8,128)(2,1)S(1)} %shard_map.94.refs_2_), channel_id=1, source_target_pairs={{0,1},{1,0},{2,3},{3,2},{4,5},{5,4},{6,7},{7,6},{8,9},{9,8},{10,11... | collective-permute-start | bytes 61448 | tf_op jit(solution)/shard_map/ppermute | solution.py:330
  107.0 5.9 %collective-permute-start.33 = (bf16[16,4224]{1,0:T(8,128)(2,1)S(1)}, bf16[16,4224]{1,0:T(8,128)(2,1)S(1)}, u32[]{:S(2)}, u32[]{:S(2)}) collective-permute-start(bf16[16,4224]{1,0:T(8,128)(2,1)S(1)} %shard_map.97), channel_id=1, source_target_pairs={{0,8},{1,9},{2,10},{3,11},{4,12},{5,13},{6,14},{7,15},{8,0},{9,1},... | collective-permute-start | bytes 405512 | tf_op jit(solution)/shard_map/ppermute | solution.py:338
  109.0 7.9 %collective-permute-start.34 = (bf16[16,4224]{1,0:T(8,128)(2,1)S(1)}, bf16[16,4224]{1,0:T(8,128)(2,1)S(1)}, u32[]{:S(2)}, u32[]{:S(2)}) collective-permute-start(bf16[16,4224]{1,0:T(8,128)(2,1)S(1)} %shard_map.99), channel_id=1, source_target_pairs={{0,4},{1,5},{2,6},{3,7},{4,0},{5,1},{6,2},{7,3},{8,12},{9,13},{10,... | collective-permute-start | bytes 405512 | tf_op jit(solution)/shard_map/ppermute | solution.py:338
  110.7 6.3 %collective-permute-start.35 = (bf16[16,4224]{1,0:T(8,128)(2,1)S(1)}, bf16[16,4224]{1,0:T(8,128)(2,1)S(1)}, u32[]{:S(2)}, u32[]{:S(2)}) collective-permute-start(bf16[16,4224]{1,0:T(8,128)(2,1)S(1)} %shard_map.101), channel_id=1, source_target_pairs={{0,12},{1,13},{2,14},{3,15},{4,8},{5,9},{6,10},{7,11},{8,4},{9,5},... | collective-permute-start | bytes 405512 | tf_op jit(solution)/shard_map/ppermute | solution.py:338
  117.1 7.0 %collective-permute-start.36 = (bf16[16,4224]{1,0:T(8,128)(2,1)S(1)}, bf16[16,4224]{1,0:T(8,128)(2,1)S(1)}, u32[]{:S(2)}, u32[]{:S(2)}) collective-permute-start(bf16[16,4224]{1,0:T(8,128)(2,1)S(1)} %shard_map.102.refs_2_), channel_id=1, source_target_pairs={{0,24},{4,28},{8,16},{12,20},{16,8},{20,12},{24,0},{28,4},{1,25},{... | collective-permute-start | bytes 405512 | tf_op jit(solution)/shard_map/ppermute | solution.py:330
  124.9 5.9 %collective-permute-start.39 = (bf16[16,4096]{1,0:T(8,128)(2,1)S(1)}, bf16[16,4096]{1,0:T(8,128)(2,1)S(1)}, u32[]{:S(2)}, u32[]{:S(2)}) collective-permute-start(bf16[16,4096]{1,0:T(8,128)(2,1)S(1)} %get-tuple-element.68.v_ref.refs_19_), channel_id=1, source_target_pairs={{0,12},{1,5},{2,14},{3,7},{4,8},{5,1},{6,10},{7,3},{8,4},{9,13},{1... | collective-permute-start | bytes 393224 | tf_op jit(solution)/shard_map/ppermute | solution.py:338
  126.3 5.4 %collective-permute-start.38 = (bf16[16,4096]{1,0:T(8,128)(2,1)S(1)}, bf16[16,4096]{1,0:T(8,128)(2,1)S(1)}, u32[]{:S(2)}, u32[]{:S(2)}) collective-permute-start(bf16[16,4096]{1,0:T(8,128)(2,1)S(1)} %get-tuple-element.68.v_ref.refs_19_), channel_id=1, source_target_pairs={{0,8},{1,9},{2,10},{3,11},{4,12},{5,13},{6,14},{7,15},{8,0},{9,1},... | collective-permute-start | bytes 393224 | tf_op jit(solution)/shard_map/ppermute | solution.py:338
  127.4 5.0 %collective-permute-start.37 = (bf16[16,4096]{1,0:T(8,128)(2,1)S(1)}, bf16[16,4096]{1,0:T(8,128)(2,1)S(1)}, u32[]{:S(2)}, u32[]{:S(2)}) collective-permute-start(bf16[16,4096]{1,0:T(8,128)(2,1)S(1)} %get-tuple-element.68.v_ref.refs_19_), channel_id=1, source_target_pairs={{0,4},{1,13},{2,6},{3,15},{4,0},{5,9},{6,2},{7,11},{8,12},{9,5},{1... | collective-permute-start | bytes 393224 | tf_op jit(solution)/shard_map/ppermute | solution.py:338
  133.0 3.2 %collective-permute-start.42 = (bf16[16,640]{1,0:T(8,128)(2,1)S(1)}, bf16[16,640]{1,0:T(8,128)(2,1)S(1)}, u32[]{:S(2)}, u32[]{:S(2)}) collective-permute-start(bf16[16,640]{1,0:T(8,128)(2,1)S(1)} %shard_map.107.refs_2_), channel_id=1, source_target_pairs={{0,3},{1,2},{2,1},{3,0},{4,7},{5,6},{6,5},{7,4},{8,11},{9,10},{10,... | collective-permute-start | bytes 61448 | tf_op jit(solution)/shard_map/ppermute | solution.py:330
  133.0 4.0 %collective-permute-start.41 = (bf16[16,640]{1,0:T(8,128)(2,1)S(1)}, bf16[16,640]{1,0:T(8,128)(2,1)S(1)}, u32[]{:S(2)}, u32[]{:S(2)}) collective-permute-start(bf16[16,640]{1,0:T(8,128)(2,1)S(1)} %shard_map.107.refs_2_), channel_id=1, source_target_pairs={{0,2},{1,3},{2,0},{3,1},{4,6},{5,7},{6,4},{7,5},{8,10},{9,11},{10,... | collective-permute-start | bytes 61448 | tf_op jit(solution)/shard_map/ppermute | solution.py:330
  134.1 2.9 %collective-permute-start.40 = (bf16[16,640]{1,0:T(8,128)(2,1)S(1)}, bf16[16,640]{1,0:T(8,128)(2,1)S(1)}, u32[]{:S(2)}, u32[]{:S(2)}) collective-permute-start(bf16[16,640]{1,0:T(8,128)(2,1)S(1)} %shard_map.107.refs_2_), channel_id=1, source_target_pairs={{0,1},{1,0},{2,3},{3,2},{4,5},{5,4},{6,7},{7,6},{8,9},{9,8},{10,11... | collective-permute-start | bytes 61448 | tf_op jit(solution)/shard_map/ppermute | solution.py:330
  137.2 5.5 %collective-permute-start.46 = (f32[16,128]{1,0:T(8,128)S(1)}, f32[16,128]{1,0:T(8,128)S(1)}, u32[]{:S(2)}, u32[]{:S(2)}) collective-permute-start(f32[16,128]{1,0:T(8,128)S(1)} %get-tuple-element.80.mine_ref), channel_id=1, source_target_pairs={{0,12},{1,29},{2,14},{3,31},{4,8},{5,25},{6,10},{7,27},{8,4},{9,21... | collective-permute-start | bytes 24584 | tf_op jit(solution)/shard_map/ppermute | solution.py:378
  138.4 4.3 %collective-permute-start.45 = (f32[16,128]{1,0:T(8,128)S(1)}, f32[16,128]{1,0:T(8,128)S(1)}, u32[]{:S(2)}, u32[]{:S(2)}) collective-permute-start(f32[16,128]{1,0:T(8,128)S(1)} %get-tuple-element.80.mine_ref), channel_id=1, source_target_pairs={{0,8},{1,25},{2,10},{3,27},{4,12},{5,29},{6,14},{7,31},{8,0},{9,17... | collective-permute-start | bytes 24584 | tf_op jit(solution)/shard_map/ppermute | solution.py:378
  139.5 3.7 %collective-permute-start.44 = (f32[16,128]{1,0:T(8,128)S(1)}, f32[16,128]{1,0:T(8,128)S(1)}, u32[]{:S(2)}, u32[]{:S(2)}) collective-permute-start(f32[16,128]{1,0:T(8,128)S(1)} %get-tuple-element.80.mine_ref), channel_id=1, source_target_pairs={{0,4},{1,21},{2,6},{3,23},{4,0},{5,17},{6,2},{7,19},{8,12},{9,29},... | collective-permute-start | bytes 24584 | tf_op jit(solution)/shard_map/ppermute | solution.py:378
  140.7 4.5 %collective-permute-start.43 = (f32[16,128]{1,0:T(8,128)S(1)}, f32[16,128]{1,0:T(8,128)S(1)}, u32[]{:S(2)}, u32[]{:S(2)}) collective-permute-start(f32[16,128]{1,0:T(8,128)S(1)} %get-tuple-element.80.mine_ref), channel_id=1, source_target_pairs={{0,16},{1,17},{2,18},{3,19},{4,20},{5,21},{6,22},{7,23},{8,24},{9,... | collective-permute-start | bytes 24584 | tf_op jit(solution)/shard_map/ppermute | solution.py:378
  145.2 1.2 collective-permute-start.47
